TPU v7x, 32 devices: a whole 2x2x4 slice. The times are simulated.
32 devices in a mesh: groups: 2 (over x), seq: 16 (over z, y, core).
Axes of the slice: x: 2, y: 2, z: 4, core: 2. Of those that a mesh axis runs over, the one named last changes fastest.
Arguments:
- queries: bfloat16 [8192, 1536], P(('groups', 'seq')), parts along dimension 0, may hold values from -5 to 5
- keys: bfloat16 [8192, 1536], P(('groups', 'seq')), parts along dimension 0, may hold values from -5 to 5
- values: bfloat16 [8192, 1536], P(('groups', 'seq')), parts along dimension 0, may hold values from -6 to 6
- frame_index: int32 [64], P(('groups', 'seq')), parts along dimension 0, may hold values from 0 to 15, never falling along the last dimension, each value on 1 to 4 neighbouring positions
- block_mask: int32 [32, 32], replicated, may hold values from 0 to 1, as said below
- out_weight: bfloat16 [1536, 3072], P('seq'), may hold values from -0.15625 to 0.15625
Outputs:
- projected: bfloat16 [8192, 3072], P(('groups', 'seq')), parts along dimension 0
There are 2 independent parts, one for each index of `groups`. A program takes and returns all parts, laid end to end along the dimension named above; an argument that names none is the same for every part. Nothing has to cross between parts.
Inputs may be any that keep to these rules, and one draw needn't show every extreme that they name: `block_mask`: entry (i, j) can be 1 only where |i // B - j // B| <= 4 with B = 2; every diagonal entry is 1; some entry with |i // B - j // B| = 4 is 1.
All inputs are finite; a program needn't handle non-finite values.
Results may differ from a plain program's by a relative error of at most 0.0085.
Values may be sent and summed in bfloat16 or wider, within the bound.
No kernel may reach another device: no remote copies, remote signals or barrier semaphores. Data moves between devices by JAX's collectives and lax.ppermute only.
A program may use at most 128 MiB of HBM per device.

v0:
```python
import math

import jax
import jax.numpy as jnp
from jax import lax
from jax.sharding import PartitionSpec as P

HEADS = 12
HDIM = 128
TCH = 16
BLK = 128
REACH = 4


def as_sent(value):

    def short(part):
        return part.astype(jnp.bfloat16) if part.dtype == jnp.float32 else part

    return jax.tree.map(short, value)


def shifted(value, axis, steps):
    count = lax.axis_size(axis)
    initial, last = (max(0, -steps), min(count, count - steps))
    return lax.ppermute(value, axis, [(source, source + steps) for source in range(initial, last)])


def rotate_time(inputs, frames):
    count = inputs.shape[0]
    tok_frames = jnp.repeat(frames, BLK, total_repeat_length=count).astype(jnp.float32)
    half_ch = TCH // 2
    freqs = jnp.float32(256.0) ** (-jnp.arange(half_ch, dtype=jnp.float32) / half_ch)
    angles = tok_frames[:, None] * freqs[None, :]
    cosine = jnp.cos(angles)[:, None, :]
    sine = jnp.sin(angles)[:, None, :]
    shaped = inputs.astype(jnp.float32).reshape(count, HEADS, HDIM)
    first = shaped[..., :half_ch]
    second = shaped[..., half_ch:TCH]
    turned = jnp.concatenate(
        [first * cosine - second * sine, second * cosine + first * sine, shaped[..., TCH:]], axis=-1
    )
    return turned.reshape(count, HEADS * HDIM).astype(jnp.bfloat16)


def on_device(queries, keys, values, frame_index, block_mask, out_weight):
    tok_count = queries.shape[0]
    per_dev = tok_count // BLK
    position = lax.axis_index("seq")
    ndevices = lax.axis_size("seq")
    scale = 1.0 / math.sqrt(HDIM)
    query_rot = rotate_time(queries, frame_index).reshape(tok_count, HEADS, HDIM)
    key_rot = rotate_time(keys, frame_index)
    my_rows = lax.dynamic_slice_in_dim(block_mask, position * per_dev, per_dev, 0)

    def allowed_for(offset):
        source = position - offset
        inside = (source >= 0) & (source < ndevices)
        col_start = jnp.clip(source, 0, ndevices - 1) * per_dev
        blocks = lax.dynamic_slice_in_dim(my_rows, col_start, per_dev, 1)
        return (blocks > 0) & inside

    def attend(state, pair, blocks_ok):
        peak, totals, accum = state
        key_part, value_part = pair
        allowed = jnp.repeat(jnp.repeat(blocks_ok, BLK, axis=0), BLK, axis=1)
        scores = (
            jnp.einsum(
                "qhd,khd->hqk",
                query_rot,
                key_part.reshape(tok_count, HEADS, HDIM),
                preferred_element_type=jnp.float32,
            )
            * scale
        )
        scores = jnp.where(allowed[None], scores, jnp.float32(-1e30))
        new_peak = jnp.maximum(peak, jnp.max(scores, axis=-1))
        shrink = jnp.exp(peak - new_peak)
        expo = jnp.exp(scores - new_peak[..., None])
        totals = totals * shrink + jnp.sum(expo, axis=-1)
        mixed = jnp.einsum(
            "hqk,khd->hqd",
            expo.astype(jnp.bfloat16),
            value_part.reshape(tok_count, HEADS, HDIM),
            preferred_element_type=jnp.float32,
        )
        accum = accum * shrink[..., None] + mixed
        return (new_peak, totals, accum)

    start_state = (
        jnp.full((HEADS, tok_count), -1e30, jnp.float32),
        jnp.zeros((HEADS, tok_count), jnp.float32),
        jnp.zeros((HEADS, tok_count, HDIM), jnp.float32),
    )
    state = attend(start_state, (key_rot, values), allowed_for(0))
    carried = {1: (key_rot, values), -1: (key_rot, values)}
    for distance in range(1, REACH + 1):
        for heading in (1, -1):
            carried[heading] = shifted(as_sent(carried[heading]), "seq", heading)
            visit_blocks_ok = allowed_for(heading * distance)
            state = attend(state, carried[heading], visit_blocks_ok)
    peak, totals, accum = state
    attended = (
        (accum / totals[..., None])
        .transpose(1, 0, 2)
        .reshape(tok_count, HEADS * HDIM)
        .astype(jnp.bfloat16)
    )
    projected = jnp.dot(
        attended,
        lax.all_gather(out_weight, "seq", axis=0, tiled=True),
        preferred_element_type=jnp.float32,
    )
    return projected.astype(jnp.bfloat16)


def solution(mesh):
    return jax.shard_map(
        on_device,
        mesh=mesh,
        in_specs=(
            P(("groups", "seq"), None),
            P(("groups", "seq"), None),
            P(("groups", "seq"), None),
            P(("groups", "seq")),
            P(),
            P("seq", None),
        ),
        out_specs=P(("groups", "seq"), None),
        check_vma=False,
    )
```

profile of v0, /device:TPU:0, one launch (start us, length us, event | category | flops | bytes accessed | tf_op | source)
XLA Modules:
  0.0 230.3 jit_solution(6153333995660222757)
XLA Ops:
  13.5 2.3 copy.141
  20.1 3.9 %collective-permute-start = (bf16[256,1536]{0,1:T(8,128)(2,1)}, bf16[256,1536]{0,1:T(8,128)(2,1)}, u32[]{:S(2)}, u32[]{:S(2)}) collective-permute-start(bf16[256,1536]{0,1:T(8,128)(2,1)} %bitcast.11), channel_id=1, source_target_pairs={{0,1},{1,2},{2,3},{3,4},{4,5},{5,6},{6,7},{7,8},{8,9},{9,10},{10,1... | collective-permute-start | bytes 2359304 | tf_op jit(solution)/shard_map/ppermute | solution.py:26
  24.1 4.5 %collective-permute-start.1 = (bf16[256,1536]{1,0:T(8,128)(2,1)}, bf16[256,1536]{1,0:T(8,128)(2,1)}, u32[]{:S(2)}, u32[]{:S(2)}) collective-permute-start(bf16[256,1536]{1,0:T(8,128)(2,1)} %param.14), channel_id=1, source_target_pairs={{0,1},{1,2},{2,3},{3,4},{4,5},{5,6},{6,7},{7,8},{8,9},{9,10},{10,1... | collective-permute-start | bytes 2359304 | tf_op jit(solution)/shard_map/ppermute | solution.py:26
  35.0 2.3 fusion
  38.6 30.6 %collective-permute-start.5 = (bf16[256,1536]{1,0:T(8,128)(2,1)}, bf16[256,1536]{1,0:T(8,128)(2,1)}, u32[]{:S(2)}, u32[]{:S(2)}) collective-permute-start(bf16[256,1536]{1,0:T(8,128)(2,1)} %collective-permute-done.1), channel_id=1, source_target_pairs={{0,1},{1,2},{2,3},{3,4},{4,5},{5,6},{6,7},{7,8},{8,9},{9,10},{10,1... | collective-permute-start | bytes 2359304 | tf_op jit(solution)/shard_map/ppermute | solution.py:26
  70.6 4.5 %collective-permute-start.4 = (bf16[256,1536]{0,1:T(8,128)(2,1)}, bf16[256,1536]{0,1:T(8,128)(2,1)S(1)}, u32[]{:S(2)}, u32[]{:S(2)}) collective-permute-start(bf16[256,1536]{0,1:T(8,128)(2,1)} %collective-permute-done), channel_id=1, source_target_pairs={{0,1},{1,2},{2,3},{3,4},{4,5},{5,6},{6,7},{7,8},{8,9},{9,10},{10,1... | collective-permute-start | bytes 2359304 | tf_op jit(solution)/shard_map/ppermute | solution.py:26
  79.0 3.5 %fusion.2 = (f32[12,256]{1,0:T(8,128)S(1)}, f32[12,256,256]{1,2,0:T(8,128)}) fusion(pred[256,256]{0,1:T(8,128)(4,1)S(1)} %bitcast.336, bf16[256,12,128]{2,0,1:T(8,128)(2,1)S(1)} %pad_maximum_fusion, bf16[256,12,128]{0,2,1:T(8,128)(2,1)} %bitcast.17), kind=kOutput, calls=%fused_computation.21 | convolution fusion | flops 203682816 | bytes 4796416 | tf_op jit(solution)/shard_map/qhd,khd->hqk/dot_general | solution.py:68
  83.8 39.3 %collective-permute-start.9 = (bf16[256,1536]{1,0:T(8,128)(2,1)}, bf16[256,1536]{1,0:T(8,128)(2,1)}, u32[]{:S(2)}, u32[]{:S(2)}) collective-permute-start(bf16[256,1536]{1,0:T(8,128)(2,1)} %collective-permute-done.5), channel_id=1, source_target_pairs={{0,1},{1,2},{2,3},{3,4},{4,5},{5,6},{6,7},{7,8},{8,9},{9,10},{10,1... | collective-permute-start | bytes 2359304 | tf_op jit(solution)/shard_map/ppermute | solution.py:26
  124.4 3.5 %fusion.1 = (f32[12,256]{1,0:T(8,128)S(1)}, f32[12,256,256]{1,2,0:T(8,128)}) fusion(pred[256,256]{0,1:T(8,128)(4,1)S(1)} %bitcast.339, bf16[256,12,128]{2,0,1:T(8,128)(2,1)S(1)} %pad_maximum_fusion, bf16[256,12,128]{0,2,1:T(8,128)(2,1)} %bitcast.12), kind=kOutput, calls=%fused_computation.20 | convolution fusion | flops 203682816 | bytes 4796416 | tf_op jit(solution)/shard_map/qhd,khd->hqk/dot_general | solution.py:68
  127.9 2.3 %copy.92 = bf16[256,1536]{0,1:T(8,128)(2,1)} copy(bf16[256,1536]{1,0:T(8,128)(2,1)} %collective-permute-done.1) | data formatting | bytes 1572864 | tf_op jit(solution)/shard_map/ppermute | solution.py:26
  131.6 5.0 %collective-permute-start.8 = (bf16[256,1536]{0,1:T(8,128)(2,1)S(1)}, bf16[256,1536]{0,1:T(8,128)(2,1)}, u32[]{:S(2)}, u32[]{:S(2)}) collective-permute-start(bf16[256,1536]{0,1:T(8,128)(2,1)S(1)} %collective-permute-done.4), channel_id=1, source_target_pairs={{0,1},{1,2},{2,3},{3,4},{4,5},{5,6},{6,7},{7,8},{8,9},{9,10},{10,1... | collective-permute-start | bytes 2359304 | tf_op jit(solution)/shard_map/ppermute | solution.py:26
  136.7 3.5 %fusion.4 = (f32[12,256]{1,0:T(8,128)S(1)}, f32[12,256,256]{1,2,0:T(8,128)}) fusion(pred[256,256]{0,1:T(8,128)(4,1)S(1)} %bitcast.342, bf16[256,12,128]{2,0,1:T(8,128)(2,1)S(1)} %pad_maximum_fusion, bf16[256,12,128]{0,2,1:T(8,128)(2,1)} %bitcast.27), kind=kOutput, calls=%fused_computation.23 | convolution fusion | flops 203682816 | bytes 4796416 | tf_op jit(solution)/shard_map/qhd,khd->hqk/dot_general | solution.py:68
  140.3 2.4 %fusion.3 = (f32[12,256]{1,0:T(8,128)S(1)}, f32[12,256,256]{1,2,0:T(8,128)}) fusion(pred[256,256]{0,1:T(8,128)(4,1)S(1)} %bitcast.345, bf16[256,12,128]{2,0,1:T(8,128)(2,1)S(1)} %pad_maximum_fusion, bf16[256,12,128]{0,2,1:T(8,128)(2,1)S(1)} %bitcast.360), kind=kOutput, calls=%fused_computation.22 | convolution fusion | flops 203682816 | bytes 4796416 | tf_op jit(solution)/shard_map/qhd,khd->hqk/dot_general | solution.py:68
  144.0 4.3 %collective-permute-start.13 = (bf16[256,1536]{1,0:T(8,128)(2,1)}, bf16[256,1536]{1,0:T(8,128)(2,1)}, u32[]{:S(2)}, u32[]{:S(2)}) collective-permute-start(bf16[256,1536]{1,0:T(8,128)(2,1)} %collective-permute-done.9), channel_id=1, source_target_pairs={{0,1},{1,2},{2,3},{3,4},{4,5},{5,6},{6,7},{7,8},{8,9},{9,10},{10,1... | collective-permute-start | bytes 2359304 | tf_op jit(solution)/shard_map/ppermute | solution.py:26
  150.3 2.3 copy.100
  152.6 2.3 %copy.104 = bf16[256,1536]{0,1:T(8,128)(2,1)} copy(bf16[256,1536]{1,0:T(8,128)(2,1)} %collective-permute-done.7) | data formatting | bytes 1572864 | tf_op jit(solution)/shard_map/ppermute | solution.py:26
  154.9 18.6 %collective-permute-start.12 = (bf16[256,1536]{0,1:T(8,128)(2,1)}, bf16[256,1536]{0,1:T(8,128)(2,1)}, u32[]{:S(2)}, u32[]{:S(2)}) collective-permute-start(bf16[256,1536]{0,1:T(8,128)(2,1)} %collective-permute-done.8), channel_id=1, source_target_pairs={{0,1},{1,2},{2,3},{3,4},{4,5},{5,6},{6,7},{7,8},{8,9},{9,10},{10,1... | collective-permute-start | bytes 2359304 | tf_op jit(solution)/shard_map/ppermute | solution.py:26
  174.2 4.1 %fusion.6 = (f32[12,256]{1,0:T(8,128)}, f32[12,256,256]{1,2,0:T(8,128)}) fusion(pred[256,256]{0,1:T(8,128)(4,1)S(1)} %bitcast.348, bf16[256,12,128]{2,0,1:T(8,128)(2,1)S(1)} %pad_maximum_fusion, bf16[256,12,128]{0,2,1:T(8,128)(2,1)} %bitcast.37), kind=kOutput, calls=%fused_computation.25 | convolution fusion | flops 203682816 | bytes 4796416 | tf_op jit(solution)/shard_map/qhd,khd->hqk/dot_general | solution.py:68
  178.4 2.3 copy.108
  180.7 2.3 copy.112
  183.0 4.2 %fusion.5 = (f32[12,256]{1,0:T(8,128)}, f32[12,256,256]{1,2,0:T(8,128)}) fusion(pred[256,256]{0,1:T(8,128)(4,1)S(1)} %bitcast.351, bf16[256,12,128]{2,0,1:T(8,128)(2,1)S(1)} %pad_maximum_fusion, bf16[256,12,128]{0,2,1:T(8,128)(2,1)} %bitcast.32), kind=kOutput, calls=%fused_computation.24 | convolution fusion | flops 203682816 | bytes 4796416 | tf_op jit(solution)/shard_map/qhd,khd->hqk/dot_general | solution.py:68
  187.2 2.3 copy.116
  193.6 2.0 fusion.7
  216.0 7.4 %convolution_convert_fusion = bf16[256,3072]{1,0:T(8,128)(2,1)} fusion(bf16[256,1536]{0,1:T(8,128)(2,1)S(1)} %bitcast.320, bf16[1536,3072]{1,0:T(8,128)(2,1)} %all-gather.2.cloned.1.call-done), kind=kOutput, calls=%fused_computation | convolution fusion | flops 2416705536 | bytes 11796480 | tf_op jit(solution)/shard_map/dot_general | solution.py:109
  (176 shorter events, 56.1 us)
Async XLA Ops:
  6.5 209.5 %all-gather.2.cloned.1.call-start = ((), (), s32[]{:S(2)}) async-start(), calls=%async_computation | async-start | bytes 10027008 | tf_op jit(solution)/shard_map/all_gather | solution.py:111
  16.2 13.7 %copy-start.17 = (bf16[256,1536]{1,0:T(8,128)(2,1)S(1)}, bf16[256,1536]{1,0:T(8,128)(2,1)}, u32[]{:S(2)}) copy-start(bf16[256,1536]{1,0:T(8,128)(2,1)} %param.12) | copy-start | bytes 2359300
  18.9 18.4 %collective-permute-start.2 = (bf16[256,1536]{0,1:T(8,128)(2,1)}, bf16[256,1536]{0,1:T(8,128)(2,1)}, u32[]{:S(2)}, u32[]{:S(2)}) collective-permute-start(bf16[256,1536]{0,1:T(8,128)(2,1)} %bitcast.11), channel_id=1, source_target_pairs={{1,0},{2,1},{3,2},{4,3},{5,4},{6,5},{7,6},{8,7},{9,8},{10,9},{11,1... | collective-permute-start | bytes 2359304 | tf_op jit(solution)/shard_map/ppermute | solution.py:26
  20.1 50.4 %collective-permute-start = (bf16[256,1536]{0,1:T(8,128)(2,1)}, bf16[256,1536]{0,1:T(8,128)(2,1)}, u32[]{:S(2)}, u32[]{:S(2)}) collective-permute-start(bf16[256,1536]{0,1:T(8,128)(2,1)} %bitcast.11), channel_id=1, source_target_pairs={{0,1},{1,2},{2,3},{3,4},{4,5},{5,6},{6,7},{7,8},{8,9},{9,10},{10,1... | collective-permute-start | bytes 2359304 | tf_op jit(solution)/shard_map/ppermute | solution.py:26
  24.1 14.5 %collective-permute-start.1 = (bf16[256,1536]{1,0:T(8,128)(2,1)}, bf16[256,1536]{1,0:T(8,128)(2,1)}, u32[]{:S(2)}, u32[]{:S(2)}) collective-permute-start(bf16[256,1536]{1,0:T(8,128)(2,1)} %param.14), channel_id=1, source_target_pairs={{0,1},{1,2},{2,3},{3,4},{4,5},{5,6},{6,7},{7,8},{8,9},{9,10},{10,1... | collective-permute-start | bytes 2359304 | tf_op jit(solution)/shard_map/ppermute | solution.py:26
  28.6 40.6 %collective-permute-start.3 = (bf16[256,1536]{1,0:T(8,128)(2,1)}, bf16[256,1536]{1,0:T(8,128)(2,1)}, u32[]{:S(2)}, u32[]{:S(2)}) collective-permute-start(bf16[256,1536]{1,0:T(8,128)(2,1)} %param.14), channel_id=1, source_target_pairs={{1,0},{2,1},{3,2},{4,3},{5,4},{6,5},{7,6},{8,7},{9,8},{10,9},{11,1... | collective-permute-start | bytes 2359304 | tf_op jit(solution)/shard_map/ppermute | solution.py:26
  37.3 45.2 %collective-permute-start.6 = (bf16[256,1536]{0,1:T(8,128)(2,1)}, bf16[256,1536]{0,1:T(8,128)(2,1)}, u32[]{:S(2)}, u32[]{:S(2)}) collective-permute-start(bf16[256,1536]{0,1:T(8,128)(2,1)} %collective-permute-done.2), channel_id=1, source_target_pairs={{1,0},{2,1},{3,2},{4,3},{5,4},{6,5},{7,6},{8,7},{9,8},{10,9},{11,1... | collective-permute-start | bytes 2359304 | tf_op jit(solution)/shard_map/ppermute | solution.py:26
  38.6 45.2 %collective-permute-start.5 = (bf16[256,1536]{1,0:T(8,128)(2,1)}, bf16[256,1536]{1,0:T(8,128)(2,1)}, u32[]{:S(2)}, u32[]{:S(2)}) collective-permute-start(bf16[256,1536]{1,0:T(8,128)(2,1)} %collective-permute-done.1), channel_id=1, source_target_pairs={{0,1},{1,2},{2,3},{3,4},{4,5},{5,6},{6,7},{7,8},{8,9},{9,10},{10,1... | collective-permute-start | bytes 2359304 | tf_op jit(solution)/shard_map/ppermute | solution.py:26
  69.2 53.9 %collective-permute-start.7 = (bf16[256,1536]{1,0:T(8,128)(2,1)}, bf16[256,1536]{1,0:T(8,128)(2,1)}, u32[]{:S(2)}, u32[]{:S(2)}) collective-permute-start(bf16[256,1536]{1,0:T(8,128)(2,1)} %collective-permute-done.3), channel_id=1, source_target_pairs={{1,0},{2,1},{3,2},{4,3},{5,4},{6,5},{7,6},{8,7},{9,8},{10,9},{11,1... | collective-permute-start | bytes 2359304 | tf_op jit(solution)/shard_map/ppermute | solution.py:26
  70.6 61.1 %collective-permute-start.4 = (bf16[256,1536]{0,1:T(8,128)(2,1)}, bf16[256,1536]{0,1:T(8,128)(2,1)S(1)}, u32[]{:S(2)}, u32[]{:S(2)}) collective-permute-start(bf16[256,1536]{0,1:T(8,128)(2,1)} %collective-permute-done), channel_id=1, source_target_pairs={{0,1},{1,2},{2,3},{3,4},{4,5},{5,6},{6,7},{7,8},{8,9},{9,10},{10,1... | collective-permute-start | bytes 2359304 | tf_op jit(solution)/shard_map/ppermute | solution.py:26
  82.5 67.1 %copy-start.22 = (f32[12,256]{1,0:T(8,128)}, f32[12,256]{1,0:T(8,128)S(1)}, u32[]{:S(2)}) copy-start(f32[12,256]{1,0:T(8,128)S(1)} %get-tuple-element.77) | copy-start | bytes 36868
  82.5 60.2 %collective-permute-start.10 = (bf16[256,1536]{0,1:T(8,128)(2,1)}, bf16[256,1536]{0,1:T(8,128)(2,1)}, u32[]{:S(2)}, u32[]{:S(2)}) collective-permute-start(bf16[256,1536]{0,1:T(8,128)(2,1)} %collective-permute-done.6), channel_id=1, source_target_pairs={{1,0},{2,1},{3,2},{4,3},{5,4},{6,5},{7,6},{8,7},{9,8},{10,9},{11,1... | collective-permute-start | bytes 2359304 | tf_op jit(solution)/shard_map/ppermute | solution.py:26
  83.8 60.2 %collective-permute-start.9 = (bf16[256,1536]{1,0:T(8,128)(2,1)}, bf16[256,1536]{1,0:T(8,128)(2,1)}, u32[]{:S(2)}, u32[]{:S(2)}) collective-permute-start(bf16[256,1536]{1,0:T(8,128)(2,1)} %collective-permute-done.5), channel_id=1, source_target_pairs={{0,1},{1,2},{2,3},{3,4},{4,5},{5,6},{6,7},{7,8},{8,9},{9,10},{10,1... | collective-permute-start | bytes 2359304 | tf_op jit(solution)/shard_map/ppermute | solution.py:26
  123.1 25.3 %collective-permute-start.11 = (bf16[256,1536]{1,0:T(8,128)(2,1)}, bf16[256,1536]{1,0:T(8,128)(2,1)}, u32[]{:S(2)}, u32[]{:S(2)}) collective-permute-start(bf16[256,1536]{1,0:T(8,128)(2,1)} %collective-permute-done.7), channel_id=1, source_target_pairs={{1,0},{2,1},{3,2},{4,3},{5,4},{6,5},{7,6},{8,7},{9,8},{10,9},{11,1... | collective-permute-start | bytes 2359304 | tf_op jit(solution)/shard_map/ppermute | solution.py:26
  127.9 21.7 %copy-start.18 = (f32[12,256]{1,0:T(8,128)}, f32[12,256]{1,0:T(8,128)S(1)}, u32[]{:S(2)}) copy-start(f32[12,256]{1,0:T(8,128)S(1)} %get-tuple-element.79) | copy-start | bytes 36868
  131.6 23.3 %collective-permute-start.8 = (bf16[256,1536]{0,1:T(8,128)(2,1)S(1)}, bf16[256,1536]{0,1:T(8,128)(2,1)}, u32[]{:S(2)}, u32[]{:S(2)}) collective-permute-start(bf16[256,1536]{0,1:T(8,128)(2,1)S(1)} %collective-permute-done.4), channel_id=1, source_target_pairs={{0,1},{1,2},{2,3},{3,4},{4,5},{5,6},{6,7},{7,8},{8,9},{9,10},{10,1... | collective-permute-start | bytes 2359304 | tf_op jit(solution)/shard_map/ppermute | solution.py:26
  140.2 12.3 %copy-start.24 = (f32[12,256]{1,0:T(8,128)}, f32[12,256]{1,0:T(8,128)S(1)}, u32[]{:S(2)}) copy-start(f32[12,256]{1,0:T(8,128)S(1)} %get-tuple-element.73) | copy-start | bytes 36868
  142.7 30.9 %copy-start.20 = (f32[12,256]{1,0:T(8,128)}, f32[12,256]{1,0:T(8,128)S(1)}, u32[]{:S(2)}) copy-start(f32[12,256]{1,0:T(8,128)S(1)} %get-tuple-element.75) | copy-start | bytes 36868
  142.7 48.3 %collective-permute-start.14 = (bf16[256,1536]{0,1:T(8,128)(2,1)}, bf16[256,1536]{0,1:T(8,128)(2,1)}, u32[]{:S(2)}, u32[]{:S(2)}) collective-permute-start(bf16[256,1536]{0,1:T(8,128)(2,1)} %collective-permute-done.10), channel_id=1, source_target_pairs={{1,0},{2,1},{3,2},{4,3},{5,4},{6,5},{7,6},{8,7},{9,8},{10,9},{11,1... | collective-permute-start | bytes 2359304 | tf_op jit(solution)/shard_map/ppermute | solution.py:26
  144.0 43.2 %collective-permute-start.13 = (bf16[256,1536]{1,0:T(8,128)(2,1)}, bf16[256,1536]{1,0:T(8,128)(2,1)}, u32[]{:S(2)}, u32[]{:S(2)}) collective-permute-start(bf16[256,1536]{1,0:T(8,128)(2,1)} %collective-permute-done.9), channel_id=1, source_target_pairs={{0,1},{1,2},{2,3},{3,4},{4,5},{5,6},{6,7},{7,8},{8,9},{9,10},{10,1... | collective-permute-start | bytes 2359304 | tf_op jit(solution)/shard_map/ppermute | solution.py:26
  148.3 41.2 %collective-permute-start.15 = (bf16[256,1536]{1,0:T(8,128)(2,1)}, bf16[256,1536]{1,0:T(8,128)(2,1)}, u32[]{:S(2)}, u32[]{:S(2)}) collective-permute-start(bf16[256,1536]{1,0:T(8,128)(2,1)} %collective-permute-done.11), channel_id=1, source_target_pairs={{1,0},{2,1},{3,2},{4,3},{5,4},{6,5},{7,6},{8,7},{9,8},{10,9},{11,1... | collective-permute-start | bytes 2359304 | tf_op jit(solution)/shard_map/ppermute | solution.py:26
  154.9 38.7 %collective-permute-start.12 = (bf16[256,1536]{0,1:T(8,128)(2,1)}, bf16[256,1536]{0,1:T(8,128)(2,1)}, u32[]{:S(2)}, u32[]{:S(2)}) collective-permute-start(bf16[256,1536]{0,1:T(8,128)(2,1)} %collective-permute-done.8), channel_id=1, source_target_pairs={{0,1},{1,2},{2,3},{3,4},{4,5},{5,6},{6,7},{7,8},{8,9},{9,10},{10,1... | collective-permute-start | bytes 2359304 | tf_op jit(solution)/shard_map/ppermute | solution.py:26
  174.2 8.7 %copy-start.34 = (pred[1,2,2,128]{3,1,2,0:T(4,128)(4,1)S(1)}, pred[1,2,2,128]{3,1,2,0:T(4,128)(4,1)}, u32[]{:S(2)}) copy-start(pred[1,2,2,128]{3,1,2,0:T(4,128)(4,1)} %copy.163) | copy-start | bytes 1540
  183.0 6.5 %copy-start.15 = (pred[256,2,128]{0,2,1:T(8,128)(4,1)}, pred[256,2,128]{0,2,1:T(8,128)(4,1)S(1)}, u32[]{:S(2)}) copy-start(pred[256,2,128]{0,2,1:T(8,128)(4,1)S(1)} %broadcast_in_dim.201) | copy-start | bytes 196612
  (28 other events, 52.3 us)
Sparse Core Ops, SparseCore 0:
  9.6 128.7 all-gather.1
where the time goes:
time: 233 us; the launch traced here: 230 us
  starting transfers between devices  121 us (52%)
  matrix products  44.1 us (19%)
  local copies, waits for them, and re-layouts  39 us (17%)
  between operations  14.2 us (6%)
  other arithmetic  11.1 us (5%)
    ppermute x16, starting transfers between devices, shifted(): lax.ppermute(value, axis, [(source, source + steps) for source in range(i...  121 us
    dot_general x9, matrix products, attend(): jnp.einsum('qhd,khd->hqk', query_rot, key_part.reshape(tok_count, HEADS,...  27.4 us
    ppermute x8, local copies, waits for them, and re-layouts, shifted(): lax.ppermute(value, axis, [(source, source + steps) for source in range(i...  16.6 us
    unnamed x94, local copies, waits for them, and re-layouts  14.6 us
    dot_general x9, matrix products, attend(): jnp.einsum('hqk,khd->hqd', expo.astype(jnp.bfloat16), value_part.reshape(...  9.2 us
    dot_general x1, matrix products, on_device(): jnp.dot(attended, lax.all_gather(out_weight, 'seq', axis=0, tiled=True),...  7.45 us
    reduce_sum x5, other arithmetic, attend(): totals = totals * shrink + jnp.sum(expo, axis=-1)  6.22 us
  transfers between devices with their start and end apart: 17, of which 0 were waited for; matrix products, arithmetic and copies ran while one was open for 35% of the time, Pallas kernels for 0%

commit v1 on v0

v1 whole, which is shorter than its diff:
```python
import functools
import math

import jax
import jax.numpy as jnp
from jax import lax
from jax.experimental import pallas as pl
from jax.experimental.pallas import tpu as pltpu
from jax.sharding import Mesh
from jax.sharding import PartitionSpec as P

HEADS = 12
HDIM = 128
TCH = 16
BLK = 128
LANES = 4
HL = HEADS // LANES
HC = HL * HDIM
BAND = 18
CH = 2
NEG = -1e30
TO_EXP2 = math.log2(math.e) / math.sqrt(HDIM)


def turn_tables(frame):
    lane = lax.broadcasted_iota(jnp.int32, (8, HDIM), 1)
    half = TCH // 2
    channel = lax.rem(lane, half).astype(jnp.float32)
    angle = frame.astype(jnp.float32) * jnp.exp2(-channel)
    cosine, sine = jnp.cos(angle), jnp.sin(angle)
    same = jnp.where(lane < TCH, cosine, 1.0)
    other = jnp.where(lane < half, -sine, jnp.where(lane < TCH, sine, 0.0))
    return same[:1], other[:1]


def turned(x, same, other):
    x = x.astype(jnp.float32)
    half = TCH // 2
    lane = lax.broadcasted_iota(jnp.int32, x.shape, 1)
    partner = jnp.where(lane < half, pltpu.roll(x, HDIM - half, 1), pltpu.roll(x, half, 1))
    return (x * same + partner * other).astype(jnp.bfloat16)


def turn_rows(frames, x_ref, o_ref):
    for block in range(x_ref.shape[0] // BLK):
        same, other = turn_tables(frames[block])
        rows = slice(block * BLK, (block + 1) * BLK)
        for head in range(HL):
            cols = slice(head * HDIM, (head + 1) * HDIM)
            o_ref[0, rows, cols] = turned(x_ref[rows, cols], same, other)


def pack_kv_kernel(frames, k_ref, v_ref, o_ref):
    turn_rows(frames, k_ref, o_ref)
    o_ref[0, :, HC:] = v_ref[...]


def pack_q_kernel(frames, q_ref, o_ref):
    turn_rows(frames, q_ref, o_ref)


def pack(kernel, frames, arrays, width):
    count = arrays[0].shape[0]
    return pl.pallas_call(
        kernel,
        out_shape=jax.ShapeDtypeStruct((LANES, count, width), jnp.bfloat16),
        grid=(LANES,),
        in_specs=[pl.BlockSpec(memory_space=pltpu.SMEM)]
        + [pl.BlockSpec((count, HC), lambda g: (0, g)) for _ in arrays],
        out_specs=pl.BlockSpec((1, count, width), lambda g: (g, 0, 0)),
    )(frames, *arrays)


def attend_kernel(
    mask, q_ref, here_ref, before_ref, after_ref, o_ref, kv, scores, peak, total, mixed, picks, sems
):
    step = pl.program_id(0)
    plane = lax.axis_index("plane")
    plane_blocks = here_ref.shape[0] // BLK
    nblk = mask.shape[0]
    copies = [
        pltpu.make_async_copy(ref, kv.at[pl.ds(i * here_ref.shape[0], here_ref.shape[0])], sems.at[i])
        for i, ref in enumerate((before_ref, here_ref, after_ref))
    ]

    @pl.when(step == 0)
    def _():
        for copy in copies:
            copy.start()
        for copy in copies:
            copy.wait()

    my_block = plane * plane_blocks + step
    first = (plane - 1) * plane_blocks

    def pick(i, count):
        at = first + i
        inside = (at >= 0) & (at < nblk)
        kept = inside & (mask[my_block, jnp.clip(at, 0, nblk - 1)] > 0)
        picks[count] = i
        return count + kept.astype(jnp.int32)

    count = lax.fori_loop(0, 3 * plane_blocks, pick, jnp.int32(0))
    for extra in range(CH - 1):
        picks[count + extra] = plane_blocks + step
    rounds = lax.div(count + (CH - 1), CH)
    peak[...] = jnp.full(peak.shape, NEG, jnp.float32)
    total[...] = jnp.zeros(total.shape, jnp.float32)
    mixed[...] = jnp.zeros(mixed.shape, jnp.float32)

    def score(r, carry):
        for c in range(CH):
            slot = r * CH + c
            rows = pl.ds(pl.multiple_of(picks[slot] * BLK, BLK), BLK)
            for h in range(HL):
                cols = slice(h * HDIM, (h + 1) * HDIM)
                s = lax.dot_general(
                    q_ref[:, cols],
                    kv[rows, cols],
                    (((1,), (1,)), ((), ())),
                    preferred_element_type=jnp.float32,
                )
                if c > 0:
                    s = jnp.where(slot < count, s, NEG)
                scores[h, slot] = s
                peak[h] = jnp.maximum(peak[h], s)
        return carry

    lax.fori_loop(0, rounds, score, 0)
    for h in range(HL):
        top = jnp.max(peak[h], axis=1, keepdims=True)
        peak[h] = jnp.broadcast_to(top, (BLK, BLK))

    def mix(r, carry):
        rows = [pl.ds(pl.multiple_of(picks[r * CH + c] * BLK, BLK), BLK) for c in range(CH)]
        for h in range(HL):
            vcols = slice(HC + h * HDIM, HC + (h + 1) * HDIM)
            parts = []
            for c in range(CH):
                e = jnp.exp2((scores[h, r * CH + c] - peak[h]) * TO_EXP2)
                total[h] += e
                parts.append(e.astype(jnp.bfloat16))
            mixed[h] += jnp.dot(
                jnp.concatenate(parts, axis=1),
                jnp.concatenate([kv[row, vcols] for row in rows], axis=0),
                preferred_element_type=jnp.float32,
            )
        return carry

    lax.fori_loop(0, rounds, mix, 0)
    for h in range(HL):
        whole = jnp.sum(total[h], axis=1, keepdims=True)
        o_ref[:, h * HDIM : (h + 1) * HDIM] = (mixed[h] / whole).astype(jnp.bfloat16)


def attend(mask, q, here, before, after):
    tokens = q.shape[0]
    slots = -(-BAND // CH) * CH
    hbm = pl.BlockSpec(memory_space=pl.ANY)
    return pl.pallas_call(
        attend_kernel,
        out_shape=jax.ShapeDtypeStruct((tokens, HC), jnp.bfloat16),
        grid=(tokens // BLK,),
        in_specs=[
            pl.BlockSpec(memory_space=pltpu.SMEM),
            pl.BlockSpec((BLK, HC), lambda b: (b, 0)),
            hbm,
            hbm,
            hbm,
        ],
        out_specs=pl.BlockSpec((BLK, HC), lambda b: (b, 0)),
        scratch_shapes=[
            pltpu.VMEM((3 * tokens, 2 * HC), jnp.bfloat16),
            pltpu.VMEM((HL, slots, BLK, BLK), jnp.float32),
            pltpu.VMEM((HL, BLK, BLK), jnp.float32),
            pltpu.VMEM((HL, BLK, BLK), jnp.float32),
            pltpu.VMEM((HL, BLK, HDIM), jnp.float32),
            pltpu.SMEM((3 * tokens // BLK + CH,), jnp.int32),
            pltpu.SemaphoreType.DMA((3,)),
        ],
        compiler_params=pltpu.CompilerParams(vmem_limit_bytes=40 * 1024 * 1024),
    )(mask, q, here, before, after)


def project_kernel(a_ref, w_ref, o_ref):
    acc = jnp.dot(a_ref[0], w_ref[:HC], preferred_element_type=jnp.float32)
    for g in range(1, LANES):
        acc += jnp.dot(a_ref[g], w_ref[g * HC : (g + 1) * HC], preferred_element_type=jnp.float32)
    o_ref[...] = acc.astype(jnp.bfloat16)


def project(attended, weight, width):
    groups, count, depth = attended.shape
    return pl.pallas_call(
        project_kernel,
        out_shape=jax.ShapeDtypeStruct((count, weight.shape[1]), jnp.bfloat16),
        grid=(weight.shape[1] // width,),
        in_specs=[
            pl.BlockSpec((groups, count, depth), lambda n: (0, 0, 0)),
            pl.BlockSpec((weight.shape[0], width), lambda n: (0, n)),
        ],
        out_specs=pl.BlockSpec((count, width), lambda n: (0, n)),
        compiler_params=pltpu.CompilerParams(vmem_limit_bytes=40 * 1024 * 1024),
    )(attended, weight)


def on_device(queries, keys, values, frame_index, block_mask, out_weight):
    count = queries.shape[0]
    planes = lax.axis_size("plane")
    weight = lax.all_gather(out_weight, ("plane", "lane"), axis=0, tiled=True)
    kv = pack(pack_kv_kernel, frame_index, (keys, values), 2 * HC)
    kv = lax.all_to_all(kv, "lane", 0, 0, tiled=True).reshape(LANES * count, 2 * HC)
    before = lax.ppermute(kv, "plane", [(p, p + 1) for p in range(planes - 1)])
    after = lax.ppermute(kv, "plane", [(p + 1, p) for p in range(planes - 1)])
    q = pack(pack_q_kernel, frame_index, (queries,), HC)
    q = lax.all_to_all(q, "lane", 0, 0, tiled=True).reshape(LANES * count, HC)
    attended = attend(block_mask, q, kv, before, after)
    attended = lax.all_to_all(attended.reshape(LANES, count, HC), "lane", 0, 0, tiled=True)
    return project(attended, weight, 512)


def solution(mesh):
    groups, seq = mesh.devices.shape
    split = Mesh(mesh.devices.reshape(groups, seq // LANES, LANES), ("groups", "plane", "lane"))
    tokens = P(("groups", "plane", "lane"), None)
    return jax.shard_map(
        on_device,
        mesh=split,
        in_specs=(
            tokens,
            tokens,
            tokens,
            P(("groups", "plane", "lane")),
            P(),
            P(("plane", "lane"), None),
        ),
        out_specs=tokens,
        check_vma=False,
    )
```

time: 233 us -> 176 us (0.76)
  starting transfers between devices: 121 us -> 5.74 us
  blocking collectives: 0 us -> 68.6 us
  waiting for transfers between devices: 0.77 us -> 47.7 us
  matrix products: 44.1 us -> 0 us
  Pallas kernels: 0 us -> 35.6 us
  local copies, waits for them, and re-layouts: 39 us -> 3.68 us
  other arithmetic: 11.1 us -> 0 us
    ppermute x16 -> x2, starting transfers between devices: 121 us -> 5.73 us  [the longest x1 4.44 us: on_device(): before = lax.ppermute(kv, 'plane', [(p, p + 1) for p in range(planes - 1)])]
    all_to_all x0 -> x3, blocking collectives: none -> 68.6 us  [the longest x1 30.6 us: on_device(): lax.all_to_all(kv, 'lane', 0, 0, tiled=True).reshape(LANES * count, 2 * HC)]
    ppermute x16 -> x2, waiting for transfers between devices: 0.04 us -> 47 us  [the longest x1 34.2 us: on_device(): before = lax.ppermute(kv, 'plane', [(p, p + 1) for p in range(planes - 1)])]
    dot_general x19 -> x0, matrix products: 44.1 us -> none  [the longest x9 27.4 us: attend(): jnp.einsum('qhd,khd->hqk', query_rot, key_part.reshape(tok_count, HEADS,...]
    pallas_call x0 -> x4, Pallas kernels: none -> 35.6 us  [the longest x1 22.4 us: attend(): pl.pallas_call(attend_kernel, out_shape=jax.ShapeDtypeStruct((tokens, HC)...]
    ppermute x8 -> x0, local copies, waits for them, and re-layouts: 16.6 us -> none  [shifted(): lax.ppermute(value, axis, [(source, source + steps) for source in range(i...]
    unnamed x94 -> x4, local copies, waits for them, and re-layouts: 14.6 us -> 3.68 us
    reduce_sum x5 -> x0, other arithmetic: 6.22 us -> none  [attend(): totals = totals * shrink + jnp.sum(expo, axis=-1)]
  transfers between devices with their start and end apart: 17 -> 3, of which waited for: 0 -> 2; matrix products, arithmetic and copies ran while one was open for 35% -> 0% of each run, Pallas kernels for 0% -> 17%
where the time goes in v1:
time: 176 us; the launch traced here: 175 us
  blocking collectives  68.6 us (39%)
  waiting for transfers between devices  47.7 us (27%)
  Pallas kernels  35.6 us (20%)
  between operations  13.4 us (8%)
  starting transfers between devices  5.74 us (3%)
  local copies, waits for them, and re-layouts  3.68 us (2%)
    ppermute x1, waiting for transfers between devices, on_device(): before = lax.ppermute(kv, 'plane', [(p, p + 1) for p in range(planes - 1)])  34.2 us
    all_to_all x1, blocking collectives, on_device(): lax.all_to_all(kv, 'lane', 0, 0, tiled=True).reshape(LANES * count, 2 * HC)  30.6 us
    all_to_all x1, blocking collectives, on_device(): q = lax.all_to_all(q, 'lane', 0, 0, tiled=True).reshape(LANES * count, HC)  23.9 us
    pallas_call x1, Pallas kernels, attend(): pl.pallas_call(attend_kernel, out_shape=jax.ShapeDtypeStruct((tokens, HC)...  22.4 us
    all_to_all x1, blocking collectives, on_device(): lax.all_to_all(attended.reshape(LANES, count, HC), 'lane', 0, 0, tiled=True)  14.1 us
    ppermute x1, waiting for transfers between devices, on_device(): after = lax.ppermute(kv, 'plane', [(p + 1, p) for p in range(planes - 1)])  12.8 us
    pallas_call x2, Pallas kernels, pack(): pl.pallas_call(kernel, out_shape=jax.ShapeDtypeStruct((LANES, count, widt...  7.6 us
    pallas_call x1, Pallas kernels, project(): pl.pallas_call(project_kernel, out_shape=jax.ShapeDtypeStruct((count, wei...  5.61 us
  transfers between devices with their start and end apart: 3, of which 2 were waited for; matrix products, arithmetic and copies ran while one was open for 0% of the time, Pallas kernels for 17%

profile of v1, /device:TPU:0, one launch (start us, length us, event | category | flops | bytes accessed | tf_op | source)
XLA Modules:
  0.0 174.8 jit_solution(4203042811656700601)
XLA Ops:
  6.5 0.0 all-gather.2.cloned.1.call-start
  6.5 0.7 all-gather.2.cloned.1.call-update
  7.3 4.0 %shard_map.65 = bf16[4,256,768]{2,1,0:T(8,128)(2,1)} custom-call(s32[2]{0:T(128)} %frames.3, bf16[256,1536]{1,0:T(8,128)(2,1)} %k_ref.1, bf16[256,1536]{1,0:T(8,128)(2,1)} %v_ref.1), custom_call_target="tpu_custom_call" | custom-call | tf_op jit(solution)/shard_map/pallas_call | solution.py:64
  11.2 30.6 %all_to_all.15 = bf16[4,256,768]{2,1,0:T(8,128)(2,1)S(1)} all-to-all(bf16[4,256,768]{2,1,0:T(8,128)(2,1)} %shard_map.65), channel_id=1, replica_groups=mesh['groups'=2,'plane'=4,'lane'=4] {'lane'}, dimensions={0} | all-to-all | bytes 3145728 | tf_op jit(solution)/shard_map/all_to_all | solution.py:212
  41.9 0.0 copy-start.1
  41.9 4.4 %collective-permute-start = (bf16[1024,768]{1,0:T(8,128)(2,1)S(1)}, bf16[1024,768]{1,0:T(8,128)(2,1)S(1)}, u32[]{:S(2)}, u32[]{:S(2)}) collective-permute-start(bf16[1024,768]{1,0:T(8,128)(2,1)S(1)} %bitcast.3), channel_id=1, source_target_pairs={{0,4},{4,8},{8,12},{1,5},{5,9},{9,13},{2,6},{6,10},{10,14},{3,7},{... | collective-permute-start | bytes 4718600 | tf_op jit(solution)/shard_map/ppermute | solution.py:213
  46.3 1.3 collective-permute-start.1
  47.6 3.6 %shard_map.64 = bf16[4,256,384]{2,1,0:T(8,128)(2,1)} custom-call(s32[2]{0:T(128)} %frames.3, bf16[256,1536]{1,0:T(8,128)(2,1)} %q_ref.1), custom_call_target="tpu_custom_call" | custom-call | tf_op jit(solution)/shard_map/pallas_call | solution.py:64
  51.2 23.9 %all_to_all.16 = bf16[4,256,384]{2,1,0:T(8,128)(2,1)S(1)} all-to-all(bf16[4,256,384]{2,1,0:T(8,128)(2,1)} %shard_map.64), channel_id=1, replica_groups=mesh['groups'=2,'plane'=4,'lane'=4] {'lane'}, dimensions={0} | all-to-all | bytes 1572864 | tf_op jit(solution)/shard_map/all_to_all | solution.py:216
  75.1 34.2 %collective-permute-done.before_ref = bf16[1024,768]{1,0:T(8,128)(2,1)S(1)} collective-permute-done((bf16[1024,768]{1,0:T(8,128)(2,1)S(1)}, bf16[1024,768]{1,0:T(8,128)(2,1)S(1)}, u32[]{:S(2)}, u32[]{:S(2)}) %collective-permute-start) | collective-permute-done | bytes 1572896 | tf_op jit(solution)/shard_map/ppermute | solution.py:213
  109.4 12.8 %collective-permute-done.1.after_ref = bf16[1024,768]{1,0:T(8,128)(2,1)} collective-permute-done((bf16[1024,768]{1,0:T(8,128)(2,1)S(1)}, bf16[1024,768]{1,0:T(8,128)(2,1)}, u32[]{:S(2)}, u32[]{:S(2)}) %collective-permute-start.1) | collective-permute-done | bytes 1572896 | tf_op jit(solution)/shard_map/ppermute | solution.py:214
  122.1 0.0 copy-done.1
  122.1 22.4 %shard_map.66 = bf16[1024,384]{1,0:T(8,128)(2,1)S(1)} custom-call(s32[32,32]{1,0:T(8,128)S(1)} %copy-done.1, bf16[1024,384]{1,0:T(8,128)(2,1)S(1)} %bitcast.6, bf16[1024,768]{1,0:T(8,128)(2,1)S(1)} %bitcast.5, bf16[1024,768]{1,0:T(8,128)(2,1)S(1)} %collective-permute-done.before_ref, bf16[1024,768]{1,0:T(8,128)(2,1)} %collective-permute-done.1.after_ref), custom_call_target="tpu_custom_call" | custom-call | tf_op jit(solution)/shard_map/pallas_call | solution.py:160
  144.6 14.1 %all_to_all.17.a_ref = bf16[4,256,384]{2,1,0:T(8,128)(2,1)S(1)} all-to-all(bf16[4,256,384]{2,1,0:T(8,128)(2,1)S(1)} %bitcast.7), channel_id=1, replica_groups=mesh['groups'=2,'plane'=4,'lane'=4] {'lane'}, dimensions={0} | all-to-all | bytes 1572864 | tf_op jit(solution)/shard_map/all_to_all | solution.py:218
  158.6 0.0 all-gather.2.cloned.1.call-done.w_ref
  158.6 0.0 copy-start
  158.6 3.7 %copy-done = bf16[1536,3072]{1,0:T(8,128)(2,1)S(1)} copy-done((bf16[1536,3072]{1,0:T(8,128)(2,1)S(1)}, bf16[1536,3072]{1,0:T(8,128)(2,1)}, u32[]{:S(2)}) %copy-start) | copy-done | bytes 9437208
  162.3 5.6 %shard_map.67 = bf16[256,3072]{1,0:T(8,128)(2,1)} custom-call(bf16[4,256,384]{2,1,0:T(8,128)(2,1)S(1)} %all_to_all.17.a_ref, bf16[1536,3072]{1,0:T(8,128)(2,1)S(1)} %copy-done), custom_call_target="tpu_custom_call" | custom-call | tf_op jit(solution)/shard_map/pallas_call | solution.py:194
Async XLA Ops:
  6.5 152.1 %all-gather.2.cloned.1.call-start = ((), (), s32[]{:S(2)}) async-start(), calls=%async_computation.3 | async-start | bytes 10027008 | tf_op jit(solution)/shard_map/all_gather | solution.py:210
  41.9 80.3 %copy-start.1 = (s32[32,32]{1,0:T(8,128)S(1)}, s32[32,32]{1,0:T(8,128)}, u32[]{:S(2)}) copy-start(s32[32,32]{1,0:T(8,128)} %mask.1) | copy-start | bytes 12292
  41.9 67.5 %collective-permute-start = (bf16[1024,768]{1,0:T(8,128)(2,1)S(1)}, bf16[1024,768]{1,0:T(8,128)(2,1)S(1)}, u32[]{:S(2)}, u32[]{:S(2)}) collective-permute-start(bf16[1024,768]{1,0:T(8,128)(2,1)S(1)} %bitcast.3), channel_id=1, source_target_pairs={{0,4},{4,8},{8,12},{1,5},{5,9},{9,13},{2,6},{6,10},{10,14},{3,7},{... | collective-permute-start | bytes 4718600 | tf_op jit(solution)/shard_map/ppermute | solution.py:213
  46.3 75.8 %collective-permute-start.1 = (bf16[1024,768]{1,0:T(8,128)(2,1)S(1)}, bf16[1024,768]{1,0:T(8,128)(2,1)}, u32[]{:S(2)}, u32[]{:S(2)}) collective-permute-start(bf16[1024,768]{1,0:T(8,128)(2,1)S(1)} %bitcast.4), channel_id=1, source_target_pairs={{4,0},{8,4},{12,8},{5,1},{9,5},{13,9},{6,2},{10,6},{14,10},{7,3},{... | collective-permute-start | bytes 4718600 | tf_op jit(solution)/shard_map/ppermute | solution.py:214
  158.6 3.7 %copy-start = (bf16[1536,3072]{1,0:T(8,128)(2,1)S(1)}, bf16[1536,3072]{1,0:T(8,128)(2,1)}, u32[]{:S(2)}) copy-start(bf16[1536,3072]{1,0:T(8,128)(2,1)} %all-gather.2.cloned.1.call-done.w_ref) | copy-start | bytes 28311556
Sparse Core Ops, SparseCore 0:
  9.6 108.3 all-gather.1

commit v2 on v1

v2 whole, which is shorter than its diff:
```python
import math

import jax
import jax.numpy as jnp
from jax import lax
from jax.experimental import pallas as pl
from jax.experimental.pallas import tpu as pltpu
from jax.sharding import Mesh
from jax.sharding import PartitionSpec as P

HEADS = 12
HDIM = 128
TCH = 16
BLK = 128
LANES = 4
HL = HEADS // LANES
HC = HL * HDIM
REACH = 4
NEG = -1e30
TO_EXP2 = math.log2(math.e) / math.sqrt(HDIM)


def turn_tables(frames, same, other):
    lane = lax.broadcasted_iota(jnp.int32, (8, HDIM), 1)
    half = TCH // 2
    channel = lax.rem(lane, half).astype(jnp.float32)
    for block in range(same.shape[0]):
        angle = frames[block].astype(jnp.float32) * jnp.exp2(-channel)
        cosine, sine = jnp.cos(angle), jnp.sin(angle)
        same[block] = jnp.where(lane < TCH, cosine, 1.0)
        other[block] = jnp.where(lane < half, -sine, jnp.where(lane < TCH, sine, 0.0))


def turn_rows(frames, x_ref, o_ref, same, other):
    @pl.when(pl.program_id(0) == 0)
    def _():
        turn_tables(frames, same, other)

    half = TCH // 2
    lane = lax.broadcasted_iota(jnp.int32, (BLK, HDIM), 1)
    for block in range(x_ref.shape[0] // BLK):
        rows = slice(block * BLK, (block + 1) * BLK)
        for head in range(HL):
            cols = slice(head * HDIM, (head + 1) * HDIM)
            x = x_ref[rows, cols].astype(jnp.float32)
            partner = jnp.where(lane < half, pltpu.roll(x, HDIM - half, 1), pltpu.roll(x, half, 1))
            o_ref[0, rows, cols] = (x * same[block, :1] + partner * other[block, :1]).astype(jnp.bfloat16)


def pack_kv_kernel(frames, k_ref, v_ref, o_ref, same, other):
    turn_rows(frames, k_ref, o_ref, same, other)
    o_ref[0, :, HC:] = v_ref[...]


def pack_q_kernel(frames, q_ref, o_ref, same, other):
    turn_rows(frames, q_ref, o_ref, same, other)


def pack(kernel, frames, arrays, width):
    count = arrays[0].shape[0]
    table = pltpu.VMEM((count // BLK, 8, HDIM), jnp.float32)
    return pl.pallas_call(
        kernel,
        out_shape=jax.ShapeDtypeStruct((LANES, count, width), jnp.bfloat16),
        grid=(LANES,),
        in_specs=[pl.BlockSpec(memory_space=pltpu.SMEM)]
        + [pl.BlockSpec((count, HC), lambda g: (0, g)) for _ in arrays],
        out_specs=pl.BlockSpec((1, count, width), lambda g: (g, 0, 0)),
        scratch_shapes=[table, table],
    )(frames, *arrays)


def attend_kernel(mask, q_ref, here_ref, before_ref, after_ref, o_ref, kv, scores, weights, sems):
    tile, head = pl.program_id(0), pl.program_id(1)
    plane = lax.axis_index("plane")
    plane_rows = here_ref.shape[0]
    rows = q_ref.shape[0]
    per_dev = rows // BLK
    nblk = mask.shape[0]

    @pl.when((tile == 0) & (head == 0))
    def _():
        copies = [
            pltpu.make_async_copy(ref, kv.at[pl.ds(i * plane_rows, plane_rows)], sems.at[i])
            for i, ref in enumerate((before_ref, here_ref, after_ref))
        ]
        for copy in copies:
            copy.start()
        for copy in copies:
            copy.wait()

    me = plane * LANES + tile
    start = pl.multiple_of(tile * rows, BLK)
    kcols = pl.ds(pl.multiple_of(head * HDIM, HDIM), HDIM)
    vcols = pl.ds(pl.multiple_of(HC + head * HDIM, HDIM), HDIM)
    q = q_ref[...]
    peak = jnp.full((rows, BLK), NEG, jnp.float32)
    for i in range(2 * REACH + 1):
        keys = kv[pl.ds(pl.multiple_of(start + i * rows, BLK), rows), kcols]
        s = lax.dot_general(q, keys, (((1,), (1,)), ((), ())), preferred_element_type=jnp.float32)
        for b in range(per_dev):
            key_block = (me - REACH + i) * per_dev + b
            inside = (key_block >= 0) & (key_block < nblk)
            column = jnp.clip(key_block, 0, nblk - 1)
            parts = []
            for a in range(per_dev):
                kept = inside & (mask[me * per_dev + a, column] > 0)
                bias = jnp.where(kept, 0.0, NEG)
                parts.append(s[a * BLK : (a + 1) * BLK, b * BLK : (b + 1) * BLK] + bias)
            part = jnp.concatenate(parts, axis=0)
            peak = jnp.maximum(peak, part)
            at = i * rows + b * BLK
            scores[:, at : at + BLK] = part
    top = jnp.max(peak, axis=1, keepdims=True)
    total = jnp.zeros((rows, BLK), jnp.float32)
    for j in range((2 * REACH + 1) * per_dev):
        cols = slice(j * BLK, (j + 1) * BLK)
        e = jnp.exp2((scores[:, cols] - top) * TO_EXP2)
        total += e
        weights[:, cols] = e.astype(jnp.bfloat16)
    values = kv[pl.ds(start, (2 * REACH + 1) * rows), vcols]
    mixed = jnp.dot(weights[...], values, preferred_element_type=jnp.float32)
    o_ref[...] = (mixed / jnp.sum(total, axis=1, keepdims=True)).astype(jnp.bfloat16)


def attend(mask, q, here, before, after):
    tokens = q.shape[0]
    rows = tokens // LANES
    span = (2 * REACH + 1) * rows
    hbm = pl.BlockSpec(memory_space=pl.ANY)
    return pl.pallas_call(
        attend_kernel,
        out_shape=jax.ShapeDtypeStruct((tokens, HC), jnp.bfloat16),
        grid=(LANES, HL),
        in_specs=[
            pl.BlockSpec(memory_space=pltpu.SMEM),
            pl.BlockSpec((rows, HDIM), lambda t, h: (t, h)),
            hbm,
            hbm,
            hbm,
        ],
        out_specs=pl.BlockSpec((rows, HDIM), lambda t, h: (t, h)),
        scratch_shapes=[
            pltpu.VMEM((3 * tokens, 2 * HC), jnp.bfloat16),
            pltpu.VMEM((rows, span), jnp.float32),
            pltpu.VMEM((rows, span), jnp.bfloat16),
            pltpu.SemaphoreType.DMA((3,)),
        ],
        compiler_params=pltpu.CompilerParams(vmem_limit_bytes=56 * 1024 * 1024),
    )(mask, q, here, before, after)


def project_kernel(a_ref, w_ref, o_ref):
    acc = jnp.dot(a_ref[0], w_ref[0, 0, :HC], preferred_element_type=jnp.float32)
    for g in range(1, LANES):
        acc += jnp.dot(a_ref[g], w_ref[0, 0, g * HC : (g + 1) * HC], preferred_element_type=jnp.float32)
    o_ref[...] = acc.astype(jnp.bfloat16)


def project(attended, weight):
    lanes, count, depth = attended.shape
    cores, groups, channels, width = weight.shape
    return pl.pallas_call(
        project_kernel,
        out_shape=jax.ShapeDtypeStruct((count, cores * groups * width), jnp.bfloat16),
        grid=(groups, cores),
        in_specs=[
            pl.BlockSpec((lanes, count, depth), lambda g, c: (0, 0, 0)),
            pl.BlockSpec((1, 1, channels, width), lambda g, c: (c, g, 0, 0)),
        ],
        out_specs=pl.BlockSpec((count, width), lambda g, c: (0, g * cores + c)),
        compiler_params=pltpu.CompilerParams(vmem_limit_bytes=56 * 1024 * 1024),
    )(attended, weight)


def gather_weight(own):
    groups = lax.axis_size("groups")
    rows, columns = own.shape
    width = columns // (2 * groups)
    start = lax.axis_index("groups") * 2 * width
    halves = lax.dynamic_slice_in_dim(own, start, 2 * width, 1).reshape(rows, 2, width)
    halves = lax.all_to_all(halves.transpose(1, 0, 2), "core", 0, 0, tiled=True)
    part = lax.all_gather(halves.reshape(2 * rows, width), ("plane", "row"), axis=0, tiled=True)
    return lax.all_gather(lax.all_gather(part, "groups"), "core")


def on_device(queries, keys, values, frame_index, block_mask, out_weight):
    count = queries.shape[0]
    planes = lax.axis_size("plane")
    lane = ("row", "core")
    weight = gather_weight(out_weight)
    kv = pack(pack_kv_kernel, frame_index, (keys, values), 2 * HC)
    kv = lax.all_to_all(kv, lane, 0, 0, tiled=True).reshape(LANES * count, 2 * HC)
    before = lax.ppermute(kv, "plane", [(p, p + 1) for p in range(planes - 1)])
    after = lax.ppermute(kv, "plane", [(p + 1, p) for p in range(planes - 1)])
    q = pack(pack_q_kernel, frame_index, (queries,), HC)
    q = lax.all_to_all(q, lane, 0, 0, tiled=True).reshape(LANES * count, HC)
    attended = attend(block_mask, q, kv, before, after)
    attended = lax.all_to_all(attended.reshape(LANES, count, HC), lane, 0, 0, tiled=True)
    return project(attended, weight)


def solution(mesh):
    groups, seq = mesh.devices.shape
    split = Mesh(
        mesh.devices.reshape(groups, seq // LANES, LANES // 2, 2), ("groups", "plane", "row", "core")
    )
    along = ("plane", "row", "core")
    tokens = P(("groups",) + along, None)
    return jax.shard_map(
        on_device,
        mesh=split,
        in_specs=(tokens, tokens, tokens, P(("groups",) + along), P(), P(along, None)),
        out_specs=tokens,
        check_vma=False,
    )
```

time: 176 us -> 251 us (1.43)
  waiting for transfers between devices: 47.7 us -> 134 us
  blocking collectives: 68.6 us -> 60.1 us
    all_gather x1 -> x3, waiting for transfers between devices: 0.01 us -> 118 us  [the longest x2 62.7 us: gather_weight(): return lax.all_gather(lax.all_gather(part, 'groups'), 'core')]
    ppermute x1, waiting for transfers between devices: 34.2 us -> 11.2 us  [on_device(): before = lax.ppermute(kv, 'plane', [(p, p + 1) for p in range(planes - 1)])]
    all_to_all x3 -> x4, blocking collectives: 68.6 us -> 60.1 us  [the longest x1 23.6 us: on_device(): lax.all_to_all(kv, lane, 0, 0, tiled=True).reshape(LANES * count, 2 * HC)]
    ppermute x1, waiting for transfers between devices: 12.8 us -> 5.35 us  [on_device(): after = lax.ppermute(kv, 'plane', [(p + 1, p) for p in range(planes - 1)])]
    unnamed x4, local copies, waits for them, and re-layouts: 3.68 us -> 1.07 us
  transfers between devices with their start and end apart: 3 -> 5, of which waited for: 2 -> 4; matrix products, arithmetic and copies ran while one was open for 0% -> 0% of each run, Pallas kernels for 17% -> 11%
where the time goes in v2:
time: 251 us
  waiting for transfers between devices  134 us (53%)
  blocking collectives  60.1 us (24%)
  Pallas kernels  36.3 us (14%)
  between operations  13.1 us (5%)
  starting transfers between devices  5.89 us (2%)
    all_gather x2, waiting for transfers between devices, gather_weight(): return lax.all_gather(lax.all_gather(part, 'groups'), 'core')  62.7 us
    all_gather x1, waiting for transfers between devices, gather_weight(): lax.all_gather(halves.reshape(2 * rows, width), ('plane', 'row'), axis=0,...  54.9 us
    all_to_all x1, blocking collectives, on_device(): lax.all_to_all(kv, lane, 0, 0, tiled=True).reshape(LANES * count, 2 * HC)  23.6 us
    pallas_call x1, Pallas kernels, attend(): pl.pallas_call(attend_kernel, out_shape=jax.ShapeDtypeStruct((tokens, HC)...  21 us
    all_to_all x1, blocking collectives, on_device(): lax.all_to_all(attended.reshape(LANES, count, HC), lane, 0, 0, tiled=True)  15.9 us
    all_to_all x1, blocking collectives, on_device(): q = lax.all_to_all(q, lane, 0, 0, tiled=True).reshape(LANES * count, HC)  15.9 us
    ppermute x1, waiting for transfers between devices, on_device(): before = lax.ppermute(kv, 'plane', [(p, p + 1) for p in range(planes - 1)])  11.2 us
    pallas_call x2, Pallas kernels, pack(): pl.pallas_call(kernel, out_shape=jax.ShapeDtypeStruct((LANES, count, widt...  7.75 us
  transfers between devices with their start and end apart: 5, of which 4 were waited for; matrix products, arithmetic and copies ran while one was open for 0% of the time, Pallas kernels for 11%

profile of v2, /device:TPU:0, one launch (start us, length us, event | category | flops | bytes accessed | tf_op | source)
XLA Modules:
  0.0 250.8 jit_solution(18396813077192889724)
XLA Ops:
  6.5 0.0 copy-start
  6.5 0.0 all-gather.6.cloned.1.call-start
  6.5 1.1 copy-done
  7.6 0.1 reshape.18
  7.7 4.7 %all_to_all.20 = bf16[2,96,768]{2,1,0:T(8,128)(2,1)} all-to-all(bf16[2,96,768]{2,1,0:T(8,128)(2,1)S(1)} %copy.8), channel_id=1, replica_groups=mesh['groups'=2,'plane'=4,'row'=2,'core'=2] {'core'}, dimensions={0} | all-to-all | bytes 589824 | tf_op jit(solution)/shard_map/all_to_all | solution.py:182
  12.4 0.0 all-gather.6.cloned.1.call-update
  12.4 0.0 all-gather.8.cloned.1.call-start
  12.5 54.9 %all-gather.6.cloned.1.call-done = bf16[1536,768]{1,0:T(8,128)(2,1)} async-done(((bf16[192,768]{1,0:T(8,128)(2,1)}), bf16[1536,768]{1,0:T(8,128)(2,1)}) %all-gather.6.cloned.1.call-update) | async-done | bytes 2359312 | tf_op jit(solution)/shard_map/all_gather | solution.py:183
  67.4 0.0 all-gather.8.cloned.1.call-update
  67.4 0.0 all-gather.10.cloned.1.call-start
  67.4 62.7 %all-gather.8.cloned.1.call-done = bf16[3072,768]{1,0:T(8,128)(2,1)} async-done(((bf16[1536,768]{1,0:T(8,128)(2,1)}), bf16[3072,768]{1,0:T(8,128)(2,1)}) %all-gather.8.cloned.1.call-update) | async-done | bytes 4718608 | tf_op jit(solution)/shard_map/all_gather | solution.py:184
  130.1 0.0 all-gather.10.cloned.1.call-update
  130.2 4.1 %shard_map.65 = bf16[4,256,768]{2,1,0:T(8,128)(2,1)} custom-call(s32[2]{0:T(128)} %frames.3, bf16[256,1536]{1,0:T(8,128)(2,1)} %k_ref.1, bf16[256,1536]{1,0:T(8,128)(2,1)} %v_ref.1), custom_call_target="tpu_custom_call" | custom-call | tf_op jit(solution)/shard_map/pallas_call | solution.py:62
  134.2 23.6 %all_to_all.21 = bf16[4,256,768]{2,1,0:T(8,128)(2,1)S(1)} all-to-all(bf16[4,256,768]{2,1,0:T(8,128)(2,1)} %shard_map.65), channel_id=1, replica_groups=mesh['groups'=2,'plane'=4,'row'=2,'core'=2] {'row','core'}, dimensions={0} | all-to-all | bytes 3145728 | tf_op jit(solution)/shard_map/all_to_all | solution.py:193
  157.8 4.5 %collective-permute-start = (bf16[1024,768]{1,0:T(8,128)(2,1)S(1)}, bf16[1024,768]{1,0:T(8,128)(2,1)}, u32[]{:S(2)}, u32[]{:S(2)}) collective-permute-start(bf16[1024,768]{1,0:T(8,128)(2,1)S(1)} %bitcast.8), channel_id=1, source_target_pairs={{0,4},{4,8},{8,12},{1,5},{5,9},{9,13},{2,6},{6,10},{10,14},{3,7},{... | collective-permute-start | bytes 4718600 | tf_op jit(solution)/shard_map/ppermute | solution.py:194
  162.4 1.3 collective-permute-start.1
  163.6 3.7 %shard_map.64 = bf16[4,256,384]{2,1,0:T(8,128)(2,1)} custom-call(s32[2]{0:T(128)} %frames.3, bf16[256,1536]{1,0:T(8,128)(2,1)} %q_ref.1), custom_call_target="tpu_custom_call" | custom-call | tf_op jit(solution)/shard_map/pallas_call | solution.py:62
  167.3 15.9 %all_to_all.22 = bf16[4,256,384]{2,1,0:T(8,128)(2,1)} all-to-all(bf16[4,256,384]{2,1,0:T(8,128)(2,1)} %shard_map.64), channel_id=1, replica_groups=mesh['groups'=2,'plane'=4,'row'=2,'core'=2] {'row','core'}, dimensions={0} | all-to-all | bytes 1572864 | tf_op jit(solution)/shard_map/all_to_all | solution.py:197
  183.3 0.0 copy-done.1
  183.3 11.2 %collective-permute-done.before_ref = bf16[1024,768]{1,0:T(8,128)(2,1)} collective-permute-done((bf16[1024,768]{1,0:T(8,128)(2,1)S(1)}, bf16[1024,768]{1,0:T(8,128)(2,1)}, u32[]{:S(2)}, u32[]{:S(2)}) %collective-permute-start) | collective-permute-done | bytes 1572896 | tf_op jit(solution)/shard_map/ppermute | solution.py:194
  194.5 5.4 %collective-permute-done.1.after_ref = bf16[1024,768]{1,0:T(8,128)(2,1)} collective-permute-done((bf16[1024,768]{1,0:T(8,128)(2,1)S(1)}, bf16[1024,768]{1,0:T(8,128)(2,1)}, u32[]{:S(2)}, u32[]{:S(2)}) %collective-permute-start.1) | collective-permute-done | bytes 1572896 | tf_op jit(solution)/shard_map/ppermute | solution.py:195
  199.8 21.0 %shard_map.66 = bf16[1024,384]{1,0:T(8,128)(2,1)} custom-call(s32[32,32]{1,0:T(8,128)} %mask.1, bf16[1024,384]{1,0:T(8,128)(2,1)} %bitcast.12, bf16[1024,768]{1,0:T(8,128)(2,1)} %bitcast.10, bf16[1024,768]{1,0:T(8,128)(2,1)} %collective-permute-done.before_ref, bf16[1024,768]{1,0:T(8,128)(2,1)} %collective-permute-done.1.after_ref), custom_call_target="tpu_custom_call" | custom-call | tf_op jit(solution)/shard_map/pallas_call | solution.py:131
  220.8 15.9 %all_to_all.23.a_ref = bf16[4,256,384]{2,1,0:T(8,128)(2,1)} all-to-all(bf16[4,256,384]{2,1,0:T(8,128)(2,1)} %bitcast.13), channel_id=1, replica_groups=mesh['groups'=2,'plane'=4,'row'=2,'core'=2] {'row','core'}, dimensions={0} | all-to-all | bytes 1572864 | tf_op jit(solution)/shard_map/all_to_all | solution.py:199
  236.8 7.5 %shard_map.67 = bf16[256,3072]{1,0:T(8,128)(2,1)} custom-call(bf16[4,256,384]{2,1,0:T(8,128)(2,1)} %all_to_all.23.a_ref, bf16[2,2,1536,768]{3,2,1,0:T(8,128)(2,1)} %bitcast.7), custom_call_target="tpu_custom_call" | custom-call | tf_op jit(solution)/shard_map/pallas_call | solution.py:163
  (4 shorter events, 0.1 us)
Async XLA Ops:
  6.5 1.1 copy-start
  6.5 60.8 %all-gather.6.cloned.1.call-start = ((), (), s32[]{:S(2)}) async-start(), calls=%async_computation.4 | async-start | bytes 2654208 | tf_op jit(solution)/shard_map/all_gather | solution.py:183
  12.4 117.7 %all-gather.8.cloned.1.call-start = ((), (), s32[]{:S(2)}) async-start(), calls=%async_computation.5 | async-start | bytes 7077888 | tf_op jit(solution)/shard_map/all_gather | solution.py:184
  67.4 169.4 %all-gather.10.cloned.1.call-start = ((), (), s32[]{:S(2)}) async-start(), calls=%async_computation.6 | async-start | bytes 14155776 | tf_op jit(solution)/shard_map/all_gather | solution.py:184
  157.8 25.4 %copy-start.1 = (bf16[4,256,768]{2,1,0:T(8,128)(2,1)}, bf16[4,256,768]{2,1,0:T(8,128)(2,1)S(1)}, u32[]{:S(2)}) copy-start(bf16[4,256,768]{2,1,0:T(8,128)(2,1)S(1)} %all_to_all.21) | copy-start | bytes 4718596
  157.8 36.7 %collective-permute-start = (bf16[1024,768]{1,0:T(8,128)(2,1)S(1)}, bf16[1024,768]{1,0:T(8,128)(2,1)}, u32[]{:S(2)}, u32[]{:S(2)}) collective-permute-start(bf16[1024,768]{1,0:T(8,128)(2,1)S(1)} %bitcast.8), channel_id=1, source_target_pairs={{0,4},{4,8},{8,12},{1,5},{5,9},{9,13},{2,6},{6,10},{10,14},{3,7},{... | collective-permute-start | bytes 4718600 | tf_op jit(solution)/shard_map/ppermute | solution.py:194
  162.4 37.5 %collective-permute-start.1 = (bf16[1024,768]{1,0:T(8,128)(2,1)S(1)}, bf16[1024,768]{1,0:T(8,128)(2,1)}, u32[]{:S(2)}, u32[]{:S(2)}) collective-permute-start(bf16[1024,768]{1,0:T(8,128)(2,1)S(1)} %bitcast.9), channel_id=1, source_target_pairs={{4,0},{8,4},{12,8},{5,1},{9,5},{13,9},{6,2},{10,6},{14,10},{7,3},{... | collective-permute-start | bytes 4718600 | tf_op jit(solution)/shard_map/ppermute | solution.py:195
Sparse Core Ops, SparseCore 0:
  12.6 54.7 all-gather.5
  68.9 61.1 all-gather.7
  131.7 21.8 all-gather.9

commit v3 on v2

v3 whole, which is shorter than its diff:
```python
import math

import jax
import jax.numpy as jnp
from jax import lax
from jax.experimental import pallas as pl
from jax.experimental.pallas import tpu as pltpu
from jax.sharding import Mesh
from jax.sharding import PartitionSpec as P

HEADS = 12
HDIM = 128
TCH = 16
BLK = 128
LANES = 4
HL = HEADS // LANES
HC = HL * HDIM
REACH = 4
NEG = -1e30
TO_EXP2 = math.log2(math.e) / math.sqrt(HDIM)


def turn_tables(frames, same, other):
    lane = lax.broadcasted_iota(jnp.int32, (8, HDIM), 1)
    half = TCH // 2
    channel = lax.rem(lane, half).astype(jnp.float32)
    for block in range(same.shape[0]):
        angle = frames[block].astype(jnp.float32) * jnp.exp2(-channel)
        cosine, sine = jnp.cos(angle), jnp.sin(angle)
        same[block] = jnp.where(lane < TCH, cosine, 1.0)
        other[block] = jnp.where(lane < half, -sine, jnp.where(lane < TCH, sine, 0.0))


def lane_of(step):
    row, core = lax.axis_index("row"), lax.axis_index("core")
    return lax.bitwise_xor(row, step // 2) * 2 + lax.bitwise_xor(core, step % 2)


def turn_into(frames, x_ref, outs, same, other):
    turn_tables(frames, same, other)
    half = TCH // 2
    lane = lax.broadcasted_iota(jnp.int32, (BLK, HDIM), 1)
    for step in range(LANES):
        for head in range(HL):
            start = pl.multiple_of(lane_of(step) * HC + head * HDIM, HDIM)
            for block in range(x_ref.shape[0] // BLK):
                rows = slice(block * BLK, (block + 1) * BLK)
                x = x_ref[rows, pl.ds(start, HDIM)].astype(jnp.float32)
                partner = jnp.where(lane < half, pltpu.roll(x, HDIM - half, 1), pltpu.roll(x, half, 1))
                turned = x * same[block, :1] + partner * other[block, :1]
                outs[step][rows, head * HDIM : (head + 1) * HDIM] = turned.astype(jnp.bfloat16)


def pack_kv_kernel(frames, k_ref, v_ref, *rest):
    outs, tables = rest[:LANES], rest[LANES:]
    turn_into(frames, k_ref, outs, *tables)
    for step in range(LANES):
        start = pl.multiple_of(lane_of(step) * HC, HDIM)
        outs[step][:, HC:] = v_ref[:, pl.ds(start, HC)]


def pack_q_kernel(frames, q_ref, *rest):
    turn_into(frames, q_ref, rest[:LANES], *rest[LANES:])


def pack(kernel, frames, arrays, width):
    count = arrays[0].shape[0]
    table = pltpu.VMEM((count // BLK, 8, HDIM), jnp.float32)
    return pl.pallas_call(
        kernel,
        out_shape=[jax.ShapeDtypeStruct((count, width), jnp.bfloat16)] * LANES,
        in_specs=[pl.BlockSpec(memory_space=pltpu.SMEM)]
        + [pl.BlockSpec(memory_space=pltpu.VMEM) for _ in arrays],
        out_specs=[pl.BlockSpec(memory_space=pltpu.VMEM)] * LANES,
        scratch_shapes=[table, table],
        compiler_params=pltpu.CompilerParams(vmem_limit_bytes=56 * 1024 * 1024),
    )(frames, *arrays)


def attend_kernel(mask, *refs):
    q_refs, kv_refs, rest = refs[:LANES], refs[LANES : 4 * LANES], refs[4 * LANES :]
    o_ref, q_all, kv, scores, weights, sems = rest
    tile = pl.program_id(0)
    plane = lax.axis_index("plane")
    rows = o_ref.shape[0]
    per_dev = rows // BLK
    nblk = mask.shape[0]

    @pl.when(tile == 0)
    def _():
        copies = []
        for step in range(LANES):
            at = pl.multiple_of(lane_of(step) * rows, BLK)
            copies.append((q_refs[step], q_all.at[pl.ds(at, rows)]))
        for part in range(3):
            for step in range(LANES):
                at = pl.multiple_of((part * LANES + lane_of(step)) * rows, BLK)
                copies.append((kv_refs[part * LANES + step], kv.at[pl.ds(at, rows)]))
        started = [
            pltpu.make_async_copy(source, target, sems.at[i]) for i, (source, target) in enumerate(copies)
        ]
        for copy in started:
            copy.start()
        for copy in started:
            copy.wait()

    me = plane * LANES + tile
    start = pl.multiple_of(tile * rows, BLK)
    biases = []
    for j in range((2 * REACH + 1) * per_dev):
        key_block = (me - REACH) * per_dev + j
        inside = (key_block >= 0) & (key_block < nblk)
        column = jnp.clip(key_block, 0, nblk - 1)
        biases.append(
            [jnp.where(inside & (mask[me * per_dev + a, column] > 0), 0.0, NEG) for a in range(per_dev)]
        )
    for h in range(HL):
        kcols = slice(h * HDIM, (h + 1) * HDIM)
        vcols = slice(HC + h * HDIM, HC + (h + 1) * HDIM)
        q = q_all[pl.ds(start, rows), kcols]
        peak = jnp.full((rows, BLK), NEG, jnp.float32)
        for i in range(2 * REACH + 1):
            keys = kv[pl.ds(pl.multiple_of(start + i * rows, BLK), rows), kcols]
            s = lax.dot_general(q, keys, (((1,), (1,)), ((), ())), preferred_element_type=jnp.float32)
            for b in range(per_dev):
                j = i * per_dev + b
                parts = [
                    s[a * BLK : (a + 1) * BLK, b * BLK : (b + 1) * BLK] + biases[j][a]
                    for a in range(per_dev)
                ]
                part = jnp.concatenate(parts, axis=0)
                peak = jnp.maximum(peak, part)
                scores[h, :, j * BLK : (j + 1) * BLK] = part
        top = jnp.max(peak, axis=1, keepdims=True)
        total = jnp.zeros((rows, BLK), jnp.float32)
        for j in range((2 * REACH + 1) * per_dev):
            cols = slice(j * BLK, (j + 1) * BLK)
            e = jnp.exp2((scores[h, :, cols] - top) * TO_EXP2)
            total += e
            weights[h, :, cols] = e.astype(jnp.bfloat16)
        values = kv[pl.ds(start, (2 * REACH + 1) * rows), vcols]
        mixed = jnp.dot(weights[h], values, preferred_element_type=jnp.float32)
        o_ref[:, kcols] = (mixed / jnp.sum(total, axis=1, keepdims=True)).astype(jnp.bfloat16)


def attend(mask, q, kv):
    rows = q[0].shape[0]
    span = (2 * REACH + 1) * rows
    hbm = pl.BlockSpec(memory_space=pl.ANY)
    return pl.pallas_call(
        attend_kernel,
        out_shape=jax.ShapeDtypeStruct((LANES * rows, HC), jnp.bfloat16),
        grid=(LANES,),
        in_specs=[pl.BlockSpec(memory_space=pltpu.SMEM)] + [hbm] * (4 * LANES),
        out_specs=pl.BlockSpec((rows, HC), lambda t: (t, 0)),
        scratch_shapes=[
            pltpu.VMEM((LANES * rows, HC), jnp.bfloat16),
            pltpu.VMEM((3 * LANES * rows, 2 * HC), jnp.bfloat16),
            pltpu.VMEM((HL, rows, span), jnp.float32),
            pltpu.VMEM((HL, rows, span), jnp.bfloat16),
            pltpu.SemaphoreType.DMA((4 * LANES,)),
        ],
        compiler_params=pltpu.CompilerParams(vmem_limit_bytes=56 * 1024 * 1024),
    )(mask, *q, *kv)


def project_kernel(shard, groups, a_ref, *refs):
    w_refs, (o_ref, by_shard) = refs[:-2], refs[-2:]
    step = pl.program_id(0)
    depth = by_shard.shape[2]
    width = w_refs[0].shape[2]
    columns = o_ref.shape[1] // groups

    @pl.when(step == 0)
    def _():
        for lane in range(LANES):
            parts = []
            for plane in range(depth // shard):
                channel = (plane * LANES + lane) * shard
                whole = a_ref[channel // HC]
                parts.append(whole[:, channel % HC : channel % HC + shard])
            by_shard[lane] = jnp.concatenate(parts, axis=1)

    row = lax.axis_index("row")
    mine = lax.axis_index("groups")
    for dx in range(groups):
        acc = None
        for dr in range(2):
            for core in range(2):
                part = jnp.dot(
                    by_shard[lax.bitwise_xor(row, dr) * 2 + core],
                    w_refs[dx * 2 + dr][core],
                    preferred_element_type=jnp.float32,
                )
                acc = part if acc is None else acc + part
        block = lax.rem(mine + groups - dx, groups)
        at = pl.multiple_of(block * columns + step * width, HDIM)
        o_ref[:, pl.ds(at, width)] = acc.astype(jnp.bfloat16)


def project(attended, weights, shard):
    lanes, count, depth = attended.shape
    groups = len(weights) // 2
    columns = weights[0].shape[2]
    steps = 3
    return pl.pallas_call(
        lambda *refs: project_kernel(shard, groups, *refs),
        out_shape=jax.ShapeDtypeStruct((count, groups * columns), jnp.bfloat16),
        grid=(steps,),
        in_specs=[pl.BlockSpec((lanes, count, depth), lambda n: (0, 0, 0))]
        + [pl.BlockSpec((2, depth, columns // steps), lambda n: (0, 0, n)) for _ in weights],
        out_specs=pl.BlockSpec((count, groups * columns), lambda n: (0, 0)),
        scratch_shapes=[pltpu.VMEM((lanes, count, depth), jnp.bfloat16)],
        compiler_params=pltpu.CompilerParams(vmem_limit_bytes=56 * 1024 * 1024),
    )(attended, *weights)


def after(x, *others):
    return lax.optimization_barrier((x, *others))[0]


def on_device(queries, keys, values, frame_index, block_mask, out_weight):
    count = queries.shape[0]
    planes, groups = lax.axis_size("plane"), lax.axis_size("groups")
    seq = ("plane", "row", "core")
    lane = ("row", "core")

    def index(p, r, c):
        return (p * 2 + r) * 2 + c

    every = [(p, r, c) for p in range(planes) for r in range(2) for c in range(2)]

    def to_lane(x, dr, dc):
        return lax.ppermute(x, seq, [(index(p, r, c), index(p, r ^ dr, c ^ dc)) for p, r, c in every])

    def to_plane(x, dp, dc):
        pairs = [
            (index(p, r, c), index(p + dp, r, c ^ dc)) for p, r, c in every if 0 <= p + dp < planes
        ]
        return lax.ppermute(x, seq, pairs)

    columns = out_weight.shape[1] // groups
    half = lax.dynamic_slice_in_dim(out_weight, lax.axis_index("groups") * columns, columns, 1)
    strip = lax.all_gather(half, "plane", axis=0, tiled=True)

    kv = pack(pack_kv_kernel, frame_index, (keys, values), 2 * HC)
    across = [to_lane(kv[2], 1, 0), to_lane(kv[3], 1, 1)]
    early = {(dp, dc): to_plane(kv[dc], dp, dc) for dc in range(2) for dp in (1, -1)}
    here = [kv[0], to_lane(kv[1], 0, 1)] + across
    q = pack(pack_q_kernel, frame_index, (after(queries, kv[0]),), HC)
    late = {(dp, dc): to_plane(across[dc], dp, 0) for dc in range(2) for dp in (1, -1)}
    q = [q[0]] + [to_lane(after(q[d], *across), d // 2, d % 2) for d in range(1, LANES)]
    lower = [early[1, 0], early[1, 1], late[1, 0], late[1, 1]]
    upper = [early[-1, 0], early[-1, 1], late[-1, 0], late[-1, 1]]

    def round_groups(x, dx):
        return lax.ppermute(x, "groups", [(g, (g + dx) % groups) for g in range(groups)])

    strip = after(strip, *across, *early.values(), here[1])
    other = lax.ppermute(strip, "row", [(0, 1), (1, 0)])
    arrived = [*late.values(), *q[1:]]
    other = after(other, *arrived)
    strips = {(0, 0): strip, (0, 1): other}
    for dx in range(1, groups):
        strips[dx, 0] = after(round_groups(strip, dx), *arrived)
        strips[dx, 1] = round_groups(other, dx)
    attended = attend(block_mask, q, lower + here + upper)
    for dx in range(1, groups):
        strips[dx, 1] = after(strips[dx, 1], attended)
    weights = [lax.all_gather(strips[dx, dr], "core") for dx in range(groups) for dr in range(2)]
    attended = lax.all_to_all(attended.reshape(LANES, count, HC), lane, 0, 0, tiled=True)
    return project(attended, weights, out_weight.shape[0])


def solution(mesh):
    groups, seq = mesh.devices.shape
    split = Mesh(
        mesh.devices.reshape(groups, seq // LANES, LANES // 2, 2), ("groups", "plane", "row", "core")
    )
    along = ("plane", "row", "core")
    tokens = P(("groups",) + along, None)
    return jax.shard_map(
        on_device,
        mesh=split,
        in_specs=(tokens, tokens, tokens, P(("groups",) + along), P(), P(along, None)),
        out_specs=tokens,
        check_vma=False,
    )
```

time: 251 us -> 175 us (0.70)
  waiting for transfers between devices: 134 us -> 79.5 us
  blocking collectives: 60.1 us -> 14.8 us
  starting transfers between devices: 5.89 us -> 30.9 us
  Pallas kernels: 36.3 us -> 32.2 us
  local copies, waits for them, and re-layouts: 1.19 us -> 4.22 us
    all_gather x3 -> x5, waiting for transfers between devices: 118 us -> 0.27 us  [the longest x1 0.25 us: on_device(): strip = lax.all_gather(half, 'plane', axis=0, tiled=True)]
    ppermute x2 -> x17, waiting for transfers between devices: 16.6 us -> 79.2 us  [the longest x8 31.2 us: to_plane(): return lax.ppermute(x, seq, pairs)]
    all_to_all x3 -> x0, blocking collectives: 44.2 us -> none  [the longest x1 23.6 us: on_device(): lax.all_to_all(kv, lane, 0, 0, tiled=True).reshape(LANES * count, 2 * HC)]
    ppermute x2 -> x17, starting transfers between devices: 5.81 us -> 30.7 us  [the longest x8 22.1 us: to_plane(): return lax.ppermute(x, seq, pairs)]
    pallas_call x4, Pallas kernels: 36.3 us -> 32.2 us  [the longest x1 18.5 us: attend(): pl.pallas_call(attend_kernel, out_shape=jax.ShapeDtypeStruct((LANES * row...]
  transfers between devices with their start and end apart: 5 -> 22, of which waited for: 4 -> 12; matrix products, arithmetic and copies ran while one was open for 0% -> 0% of each run, Pallas kernels for 11% -> 14%
where the time goes in v3:
time: 175 us
  waiting for transfers between devices  79.5 us (45%)
  Pallas kernels  32.2 us (18%)
  starting transfers between devices  30.9 us (18%)
  blocking collectives  14.8 us (8%)
  between operations  13.3 us (8%)
  local copies, waits for them, and re-layouts  4.22 us (2%)
    ppermute x8, waiting for transfers between devices, to_plane(): return lax.ppermute(x, seq, pairs)  31.2 us
    ppermute x1, waiting for transfers between devices, on_device(): other = lax.ppermute(strip, 'row', [(0, 1), (1, 0)])  26.5 us
    ppermute x8, starting transfers between devices, to_plane(): return lax.ppermute(x, seq, pairs)  22.1 us
    pallas_call x1, Pallas kernels, attend(): pl.pallas_call(attend_kernel, out_shape=jax.ShapeDtypeStruct((LANES * row...  18.5 us
    all_to_all x1, blocking collectives, on_device(): lax.all_to_all(attended.reshape(LANES, count, HC), lane, 0, 0, tiled=True)  14.8 us
    ppermute x6, waiting for transfers between devices, to_lane(): lax.ppermute(x, seq, [(index(p, r, c), index(p, r ^ dr, c ^ dc)) for p, r...  14.3 us
    pallas_call x1, Pallas kernels, project(): pl.pallas_call(lambda *refs: project_kernel(shard, groups, *refs), out_sh...  8.24 us
    ppermute x2, waiting for transfers between devices, round_groups(): lax.ppermute(x, 'groups', [(g, (g + dx) % groups) for g in range(groups)])  7.13 us
  transfers between devices with their start and end apart: 22, of which 12 were waited for; matrix products, arithmetic and copies ran while one was open for 0% of the time, Pallas kernels for 14%

profile of v3, /device:TPU:0, one launch (start us, length us, event | category | flops | bytes accessed | tf_op | source)
XLA Modules:
  0.0 175.0 jit_solution(8467436968620630604)
XLA Ops:
  8.4 3.1 %shard_map.64 = (bf16[256,768]{1,0:T(8,128)(2,1)}, bf16[256,768]{1,0:T(8,128)(2,1)}, bf16[256,768]{1,0:T(8,128)(2,1)}, bf16[256,768]{1,0:T(8,128)(2,1)}) custom-call(s32[2]{0:T(128)} %frames.3, bf16[256,1536]{1,0:T(8,128)(2,1)} %k_ref.1, bf16[256,1536]{1,0:T(8,128)(2,1)} %v_ref.1), custom_call_target="tpu_custom_call" | custom-call | tf_op jit(solution)/shard_map/pallas_call | solution.py:69
  11.5 3.0 %collective-permute-start = (bf16[256,768]{1,0:T(8,128)(2,1)}, bf16[256,768]{1,0:T(8,128)(2,1)S(1)}, u32[]{:S(2)}, u32[]{:S(2)}) collective-permute-start(bf16[256,768]{1,0:T(8,128)(2,1)} %get-tuple-element.25), channel_id=1, source_target_pairs={{0,2},{1,3},{2,0},{3,1},{4,6},{5,7},{6,4},{7,5},{8,10},{9,11},{10,... | collective-permute-start | bytes 1179656 | tf_op jit(solution)/shard_map/ppermute | solution.py:234
  14.4 1.3 collective-permute-start.11
  15.9 4.3 %collective-permute-start.6 = (bf16[256,768]{1,0:T(8,128)(2,1)}, bf16[256,768]{1,0:T(8,128)(2,1)S(1)}, u32[]{:S(2)}, u32[]{:S(2)}) collective-permute-start(bf16[256,768]{1,0:T(8,128)(2,1)} %get-tuple-element.32), channel_id=1, source_target_pairs={{0,5},{1,4},{2,7},{3,6},{4,9},{5,8},{6,11},{7,10},{8,13},{9,12},{1... | collective-permute-start | bytes 1179656 | tf_op jit(solution)/shard_map/ppermute | solution.py:240
  20.2 4.4 %collective-permute-done.refs_10_ = bf16[256,768]{1,0:T(8,128)(2,1)S(1)} collective-permute-done((bf16[256,768]{1,0:T(8,128)(2,1)}, bf16[256,768]{1,0:T(8,128)(2,1)S(1)}, u32[]{:S(2)}, u32[]{:S(2)}) %collective-permute-start) | collective-permute-done | bytes 393248 | tf_op jit(solution)/shard_map/ppermute | solution.py:234
  24.6 1.3 collective-permute-start.10
  25.9 5.7 %collective-permute-done.1.refs_11_ = bf16[256,768]{1,0:T(8,128)(2,1)S(1)} collective-permute-done((bf16[256,768]{1,0:T(8,128)(2,1)}, bf16[256,768]{1,0:T(8,128)(2,1)S(1)}, u32[]{:S(2)}, u32[]{:S(2)}) %collective-permute-start.1) | collective-permute-done | bytes 393248 | tf_op jit(solution)/shard_map/ppermute | solution.py:234
  31.6 3.5 %collective-permute-start.5 = (bf16[256,768]{1,0:T(8,128)(2,1)}, bf16[256,768]{1,0:T(8,128)(2,1)S(1)}, u32[]{:S(2)}, u32[]{:S(2)}) collective-permute-start(bf16[256,768]{1,0:T(8,128)(2,1)} %get-tuple-element.21.refs_8_), channel_id=1, source_target_pairs={{0,4},{1,5},{2,6},{3,7},{4,8},{5,9},{6,10},{7,11},{8,12},{9,13},{1... | collective-permute-start | bytes 1179656 | tf_op jit(solution)/shard_map/ppermute | solution.py:240
  35.1 4.5 %collective-permute-done.11.refs_13_ = bf16[256,768]{1,0:T(8,128)(2,1)S(1)} collective-permute-done((bf16[256,768]{1,0:T(8,128)(2,1)}, bf16[256,768]{1,0:T(8,128)(2,1)S(1)}, u32[]{:S(2)}, u32[]{:S(2)}) %collective-permute-start.11) | collective-permute-done | bytes 393248 | tf_op jit(solution)/shard_map/ppermute | solution.py:240
  39.5 15.9 %collective-permute-done.10.refs_12_ = bf16[256,768]{1,0:T(8,128)(2,1)S(1)} collective-permute-done((bf16[256,768]{1,0:T(8,128)(2,1)}, bf16[256,768]{1,0:T(8,128)(2,1)S(1)}, u32[]{:S(2)}, u32[]{:S(2)}) %collective-permute-start.10) | collective-permute-done | bytes 393248 | tf_op jit(solution)/shard_map/ppermute | solution.py:240
  56.4 1.6 collective-permute-start.15
  57.9 2.5 %shard_map.65 = (bf16[256,384]{1,0:T(8,128)(2,1)}, bf16[256,384]{1,0:T(8,128)(2,1)}, bf16[256,384]{1,0:T(8,128)(2,1)}, bf16[256,384]{1,0:T(8,128)(2,1)}) custom-call(s32[2]{0:T(128)} %frames.3, bf16[256,1536]{1,0:T(8,128)(2,1)} %q_ref), custom_call_target="tpu_custom_call" | custom-call | tf_op jit(solution)/shard_map/pallas_call | solution.py:69
  63.5 4.2 %collective-permute-done.4.refs_3_ = bf16[256,384]{1,0:T(8,128)(2,1)S(1)} collective-permute-done((bf16[256,384]{1,0:T(8,128)(2,1)}, bf16[256,384]{1,0:T(8,128)(2,1)S(1)}, u32[]{:S(2)}, u32[]{:S(2)}) %collective-permute-start.4) | collective-permute-done | bytes 196640 | tf_op jit(solution)/shard_map/ppermute | solution.py:234
  67.7 4.3 %collective-permute-start.7 = (bf16[256,768]{1,0:T(8,128)(2,1)S(1)}, bf16[256,768]{1,0:T(8,128)(2,1)S(1)}, u32[]{:S(2)}, u32[]{:S(2)}) collective-permute-start(bf16[256,768]{1,0:T(8,128)(2,1)S(1)} %collective-permute-done.refs_10_), channel_id=1, source_target_pairs={{0,4},{1,5},{2,6},{3,7},{4,8},{5,9},{6,10},{7,11},{8,12},{9,13},{1... | collective-permute-start | bytes 1179656 | tf_op jit(solution)/shard_map/ppermute | solution.py:240
  72.1 1.3 collective-permute-start.13
  73.4 4.9 %collective-permute-start.8 = (bf16[256,768]{1,0:T(8,128)(2,1)S(1)}, bf16[256,768]{1,0:T(8,128)(2,1)S(1)}, u32[]{:S(2)}, u32[]{:S(2)}) collective-permute-start(bf16[256,768]{1,0:T(8,128)(2,1)S(1)} %collective-permute-done.1.refs_11_), channel_id=1, source_target_pairs={{0,4},{1,5},{2,6},{3,7},{4,8},{5,9},{6,10},{7,11},{8,12},{9,13},{1... | collective-permute-start | bytes 1179656 | tf_op jit(solution)/shard_map/ppermute | solution.py:240
  78.3 3.1 %collective-permute-done.7.refs_6_ = bf16[256,768]{1,0:T(8,128)(2,1)S(1)} collective-permute-done((bf16[256,768]{1,0:T(8,128)(2,1)S(1)}, bf16[256,768]{1,0:T(8,128)(2,1)S(1)}, u32[]{:S(2)}, u32[]{:S(2)}) %collective-permute-start.7) | collective-permute-done | bytes 393248 | tf_op jit(solution)/shard_map/ppermute | solution.py:240
  81.4 4.3 %collective-permute-done.13.refs_15_ = bf16[256,768]{1,0:T(8,128)(2,1)S(1)} collective-permute-done((bf16[256,768]{1,0:T(8,128)(2,1)S(1)}, bf16[256,768]{1,0:T(8,128)(2,1)S(1)}, u32[]{:S(2)}, u32[]{:S(2)}) %collective-permute-start.13) | collective-permute-done | bytes 393248 | tf_op jit(solution)/shard_map/ppermute | solution.py:240
  85.7 3.5 %collective-permute-done.8.refs_7_ = bf16[256,768]{1,0:T(8,128)(2,1)S(1)} collective-permute-done((bf16[256,768]{1,0:T(8,128)(2,1)S(1)}, bf16[256,768]{1,0:T(8,128)(2,1)S(1)}, u32[]{:S(2)}, u32[]{:S(2)}) %collective-permute-start.8) | collective-permute-done | bytes 393248 | tf_op jit(solution)/shard_map/ppermute | solution.py:240
  91.1 26.5 %collective-permute-done.14 = bf16[384,1536]{1,0:T(8,128)(2,1)} collective-permute-done((bf16[384,1536]{1,0:T(8,128)(2,1)S(1)}, bf16[384,1536]{1,0:T(8,128)(2,1)}, u32[]{:S(2)}, u32[]{:S(2)}) %collective-permute-start.14) | collective-permute-done | bytes 1179680 | tf_op jit(solution)/shard_map/ppermute | solution.py:260
  118.7 18.5 %shard_map.66 = bf16[1024,384]{1,0:T(8,128)(2,1)} custom-call(s32[32,32]{1,0:T(8,128)} %mask.1, bf16[256,384]{1,0:T(8,128)(2,1)} %get-tuple-element.23.refs_0_, bf16[256,384]{1,0:T(8,128)(2,1)} %collective-permute-done.2.refs_1_, bf16[256,384]{1,0:T(8,128)(2,1)} %collective-permute-done.3.refs_2_, bf16[256,384]{1,0:T(8,128)(2,1)} %copy-done.15, ...), custom_call_target="tpu_custom_call" | custom-call | tf_op jit(solution)/shard_map/pallas_call | solution.py:150
  137.2 7.1 %collective-permute-done.16 = bf16[384,1536]{1,0:T(8,128)(2,1)S(1)} collective-permute-done((bf16[384,1536]{1,0:T(8,128)(2,1)}, bf16[384,1536]{1,0:T(8,128)(2,1)S(1)}, u32[]{:S(2)}, u32[]{:S(2)}) %collective-permute-start.16) | collective-permute-done | bytes 1179680 | tf_op jit(solution)/shard_map/ppermute | solution.py:257
  145.4 14.8 %all_to_all.5.refs_0_ = bf16[4,256,384]{2,1,0:T(8,128)(2,1)} all-to-all(bf16[4,256,384]{2,1,0:T(8,128)(2,1)S(1)} %bitcast.5), channel_id=1, replica_groups=mesh['groups'=2,'plane'=4,'row'=2,'core'=2] {'row','core'}, dimensions={0} | all-to-all | bytes 1572864 | tf_op jit(solution)/shard_map/all_to_all | solution.py:271
  160.2 8.2 %shard_map.67 = bf16[256,3072]{1,0:T(8,128)(2,1)} custom-call(bf16[4,256,384]{2,1,0:T(8,128)(2,1)} %all_to_all.5.refs_0_, bf16[2,384,1536]{2,1,0:T(8,128)(2,1)} %bitcast.6, bf16[2,384,1536]{2,1,0:T(8,128)(2,1)} %bitcast.8, bf16[2,384,1536]{2,1,0:T(8,128)(2,1)} %bitcast.7, bf16[2,384,1536]{2,1,0:T(8,128)(2,1)} %bitcast.9), custom_call_target="tpu_custom_call" | custom-call | tf_op jit(solution)/shard_map/pallas_call | solution.py:206
  (63 shorter events, 10.2 us)
Async XLA Ops:
  6.5 49.1 %all-gather.10.cloned.1.call-start = ((), (), s32[]{:S(2)}) async-start(), calls=%async_computation.1 | async-start | bytes 1474560 | tf_op jit(solution)/shard_map/all_gather | solution.py:244
  8.3 151.8 %all-gather.12.cloned.1.call-start = ((), (), s32[]{:S(2)}) async-start(), calls=%async_computation.2 | async-start | bytes 3538944 | tf_op jit(solution)/shard_map/all_gather | solution.py:270
  11.5 13.1 %collective-permute-start = (bf16[256,768]{1,0:T(8,128)(2,1)}, bf16[256,768]{1,0:T(8,128)(2,1)S(1)}, u32[]{:S(2)}, u32[]{:S(2)}) collective-permute-start(bf16[256,768]{1,0:T(8,128)(2,1)} %get-tuple-element.25), channel_id=1, source_target_pairs={{0,2},{1,3},{2,0},{3,1},{4,6},{5,7},{6,4},{7,5},{8,10},{9,11},{10,... | collective-permute-start | bytes 1179656 | tf_op jit(solution)/shard_map/ppermute | solution.py:234
  14.4 17.1 %collective-permute-start.1 = (bf16[256,768]{1,0:T(8,128)(2,1)}, bf16[256,768]{1,0:T(8,128)(2,1)S(1)}, u32[]{:S(2)}, u32[]{:S(2)}) collective-permute-start(bf16[256,768]{1,0:T(8,128)(2,1)} %get-tuple-element.26), channel_id=1, source_target_pairs={{0,3},{1,2},{2,1},{3,0},{4,7},{5,6},{6,5},{7,4},{8,11},{9,10},{10,... | collective-permute-start | bytes 1179656 | tf_op jit(solution)/shard_map/ppermute | solution.py:234
  14.4 25.1 %collective-permute-start.11 = (bf16[256,768]{1,0:T(8,128)(2,1)}, bf16[256,768]{1,0:T(8,128)(2,1)S(1)}, u32[]{:S(2)}, u32[]{:S(2)}) collective-permute-start(bf16[256,768]{1,0:T(8,128)(2,1)} %get-tuple-element.32), channel_id=1, source_target_pairs={{4,1},{5,0},{6,3},{7,2},{8,5},{9,4},{10,7},{11,6},{12,9},{13,8},{1... | collective-permute-start | bytes 1179656 | tf_op jit(solution)/shard_map/ppermute | solution.py:240
  15.7 23.8 %collective-permute-start.9 = (bf16[256,768]{1,0:T(8,128)(2,1)}, bf16[256,768]{1,0:T(8,128)(2,1)S(1)}, u32[]{:S(2)}, u32[]{:S(2)}) collective-permute-start(bf16[256,768]{1,0:T(8,128)(2,1)} %get-tuple-element.32), channel_id=1, source_target_pairs={{0,1},{1,0},{2,3},{3,2},{4,5},{5,4},{6,7},{7,6},{8,9},{9,8},{10,11... | collective-permute-start | bytes 1179656 | tf_op jit(solution)/shard_map/ppermute | solution.py:234
  15.9 23.6 %collective-permute-start.6 = (bf16[256,768]{1,0:T(8,128)(2,1)}, bf16[256,768]{1,0:T(8,128)(2,1)S(1)}, u32[]{:S(2)}, u32[]{:S(2)}) collective-permute-start(bf16[256,768]{1,0:T(8,128)(2,1)} %get-tuple-element.32), channel_id=1, source_target_pairs={{0,5},{1,4},{2,7},{3,6},{4,9},{5,8},{6,11},{7,10},{8,13},{9,12},{1... | collective-permute-start | bytes 1179656 | tf_op jit(solution)/shard_map/ppermute | solution.py:240
  24.6 65.4 %copy-start.4 = (bf16[256,768]{1,0:T(8,128)(2,1)}, bf16[256,768]{1,0:T(8,128)(2,1)S(1)}, u32[]{:S(2)}) copy-start(bf16[256,768]{1,0:T(8,128)(2,1)S(1)} %collective-permute-done.refs_10_) | copy-start | bytes 1179652
  24.6 30.8 %collective-permute-start.10 = (bf16[256,768]{1,0:T(8,128)(2,1)}, bf16[256,768]{1,0:T(8,128)(2,1)S(1)}, u32[]{:S(2)}, u32[]{:S(2)}) collective-permute-start(bf16[256,768]{1,0:T(8,128)(2,1)} %get-tuple-element.21.refs_8_), channel_id=1, source_target_pairs={{4,0},{5,1},{6,2},{7,3},{8,4},{9,5},{10,6},{11,7},{12,8},{13,9},{1... | collective-permute-start | bytes 1179656 | tf_op jit(solution)/shard_map/ppermute | solution.py:240
  31.6 58.5 %copy-start.5 = (bf16[256,768]{1,0:T(8,128)(2,1)}, bf16[256,768]{1,0:T(8,128)(2,1)S(1)}, u32[]{:S(2)}) copy-start(bf16[256,768]{1,0:T(8,128)(2,1)S(1)} %collective-permute-done.1.refs_11_) | copy-start | bytes 1179652
  31.6 23.8 %collective-permute-start.5 = (bf16[256,768]{1,0:T(8,128)(2,1)}, bf16[256,768]{1,0:T(8,128)(2,1)S(1)}, u32[]{:S(2)}, u32[]{:S(2)}) collective-permute-start(bf16[256,768]{1,0:T(8,128)(2,1)} %get-tuple-element.21.refs_8_), channel_id=1, source_target_pairs={{0,4},{1,5},{2,6},{3,7},{4,8},{5,9},{6,10},{7,11},{8,12},{9,13},{1... | collective-permute-start | bytes 1179656 | tf_op jit(solution)/shard_map/ppermute | solution.py:240
  56.3 103.9 %all-gather.16.cloned.1.call-start = ((), (), s32[]{:S(2)}) async-start(), calls=%async_computation.4 | async-start | bytes 3538944 | tf_op jit(solution)/shard_map/all_gather | solution.py:270
  56.4 33.6 %collective-permute-start.15 = (bf16[384,1536]{1,0:T(8,128)(2,1)}, bf16[384,1536]{1,0:T(8,128)(2,1)}, u32[]{:S(2)}, u32[]{:S(2)}) collective-permute-start(bf16[384,1536]{1,0:T(8,128)(2,1)} %all-gather.10.cloned.1.call-done), channel_id=1, source_target_pairs={{0,16},{16,0},{1,17},{17,1},{2,18},{18,2},{3,19},{19,3},{4,20},{20... | collective-permute-start | bytes 3538952 | tf_op jit(solution)/shard_map/ppermute | solution.py:257
  60.4 7.3 %collective-permute-start.4 = (bf16[256,384]{1,0:T(8,128)(2,1)}, bf16[256,384]{1,0:T(8,128)(2,1)S(1)}, u32[]{:S(2)}, u32[]{:S(2)}) collective-permute-start(bf16[256,384]{1,0:T(8,128)(2,1)} %get-tuple-element.31), channel_id=1, source_target_pairs={{0,3},{1,2},{2,1},{3,0},{4,7},{5,6},{6,5},{7,4},{8,11},{9,10},{10,... | collective-permute-start | bytes 589832 | tf_op jit(solution)/shard_map/ppermute | solution.py:234
  60.7 11.4 %collective-permute-start.3 = (bf16[256,384]{1,0:T(8,128)(2,1)}, bf16[256,384]{1,0:T(8,128)(2,1)}, u32[]{:S(2)}, u32[]{:S(2)}) collective-permute-start(bf16[256,384]{1,0:T(8,128)(2,1)} %get-tuple-element.29), channel_id=1, source_target_pairs={{0,2},{1,3},{2,0},{3,1},{4,6},{5,7},{6,4},{7,5},{8,10},{9,11},{10,... | collective-permute-start | bytes 589832 | tf_op jit(solution)/shard_map/ppermute | solution.py:234
  61.9 11.5 %collective-permute-start.2 = (bf16[256,384]{1,0:T(8,128)(2,1)}, bf16[256,384]{1,0:T(8,128)(2,1)}, u32[]{:S(2)}, u32[]{:S(2)}) collective-permute-start(bf16[256,384]{1,0:T(8,128)(2,1)} %get-tuple-element.27), channel_id=1, source_target_pairs={{0,1},{1,0},{2,3},{3,2},{4,5},{5,4},{6,7},{7,6},{8,9},{9,8},{10,11... | collective-permute-start | bytes 589832 | tf_op jit(solution)/shard_map/ppermute | solution.py:234
  62.2 16.1 %collective-permute-start.12 = (bf16[256,768]{1,0:T(8,128)(2,1)S(1)}, bf16[256,768]{1,0:T(8,128)(2,1)S(1)}, u32[]{:S(2)}, u32[]{:S(2)}) collective-permute-start(bf16[256,768]{1,0:T(8,128)(2,1)S(1)} %collective-permute-done.refs_10_), channel_id=1, source_target_pairs={{4,0},{5,1},{6,2},{7,3},{8,4},{9,5},{10,6},{11,7},{12,8},{13,9},{1... | collective-permute-start | bytes 1179656 | tf_op jit(solution)/shard_map/ppermute | solution.py:240
  67.7 13.7 %collective-permute-start.7 = (bf16[256,768]{1,0:T(8,128)(2,1)S(1)}, bf16[256,768]{1,0:T(8,128)(2,1)S(1)}, u32[]{:S(2)}, u32[]{:S(2)}) collective-permute-start(bf16[256,768]{1,0:T(8,128)(2,1)S(1)} %collective-permute-done.refs_10_), channel_id=1, source_target_pairs={{0,4},{1,5},{2,6},{3,7},{4,8},{5,9},{6,10},{7,11},{8,12},{9,13},{1... | collective-permute-start | bytes 1179656 | tf_op jit(solution)/shard_map/ppermute | solution.py:240
  72.1 13.6 %collective-permute-start.13 = (bf16[256,768]{1,0:T(8,128)(2,1)S(1)}, bf16[256,768]{1,0:T(8,128)(2,1)S(1)}, u32[]{:S(2)}, u32[]{:S(2)}) collective-permute-start(bf16[256,768]{1,0:T(8,128)(2,1)S(1)} %collective-permute-done.1.refs_11_), channel_id=1, source_target_pairs={{4,0},{5,1},{6,2},{7,3},{8,4},{9,5},{10,6},{11,7},{12,8},{13,9},{1... | collective-permute-start | bytes 1179656 | tf_op jit(solution)/shard_map/ppermute | solution.py:240
  73.4 15.8 %collective-permute-start.8 = (bf16[256,768]{1,0:T(8,128)(2,1)S(1)}, bf16[256,768]{1,0:T(8,128)(2,1)S(1)}, u32[]{:S(2)}, u32[]{:S(2)}) collective-permute-start(bf16[256,768]{1,0:T(8,128)(2,1)S(1)} %collective-permute-done.1.refs_11_), channel_id=1, source_target_pairs={{0,4},{1,5},{2,6},{3,7},{4,8},{5,9},{6,10},{7,11},{8,12},{9,13},{1... | collective-permute-start | bytes 1179656 | tf_op jit(solution)/shard_map/ppermute | solution.py:240
  90.0 70.1 %all-gather.14.cloned.1.call-start = ((), (), s32[]{:S(2)}) async-start(), calls=%async_computation.3 | async-start | bytes 3538944 | tf_op jit(solution)/shard_map/all_gather | solution.py:270
  90.1 27.5 %collective-permute-start.14 = (bf16[384,1536]{1,0:T(8,128)(2,1)S(1)}, bf16[384,1536]{1,0:T(8,128)(2,1)}, u32[]{:S(2)}, u32[]{:S(2)}) collective-permute-start(bf16[384,1536]{1,0:T(8,128)(2,1)S(1)} %copy-done.2), channel_id=1, source_target_pairs={{0,2},{2,0},{1,3},{3,1},{4,6},{6,4},{5,7},{7,5},{8,10},{10,8},{9,1... | collective-permute-start | bytes 3538952 | tf_op jit(solution)/shard_map/ppermute | solution.py:260
  117.6 42.6 %all-gather.18.cloned.1.call-start = ((), (), s32[]{:S(2)}) async-start(), calls=%async_computation.5 | async-start | bytes 3538944 | tf_op jit(solution)/shard_map/all_gather | solution.py:270
  117.7 26.7 %collective-permute-start.16 = (bf16[384,1536]{1,0:T(8,128)(2,1)}, bf16[384,1536]{1,0:T(8,128)(2,1)S(1)}, u32[]{:S(2)}, u32[]{:S(2)}) collective-permute-start(bf16[384,1536]{1,0:T(8,128)(2,1)} %collective-permute-done.14), channel_id=1, source_target_pairs={{0,16},{16,0},{1,17},{17,1},{2,18},{18,2},{3,19},{19,3},{4,20},{20... | collective-permute-start | bytes 3538952 | tf_op jit(solution)/shard_map/ppermute | solution.py:257
  (14 other events, 236.8 us)
Sparse Core Ops, SparseCore 0:
  8.9 46.6 all-gather.9
  57.2 12.3 all-gather.11
  90.1 11.9 all-gather.15
  117.7 11.5 all-gather.13
  145.5 11.3 all-gather.17

commit v4 on v3

v4 whole, which is shorter than its diff:
```python
import math

import jax
import jax.numpy as jnp
from jax import lax
from jax.experimental import pallas as pl
from jax.experimental.pallas import tpu as pltpu
from jax.sharding import Mesh
from jax.sharding import PartitionSpec as P

HEADS = 12
HDIM = 128
TCH = 16
BLK = 128
LANES = 4
HL = HEADS // LANES
HC = HL * HDIM
REACH = 4
NEG = -1e30
TO_EXP2 = math.log2(math.e) / math.sqrt(HDIM)


def turn_tables(frames, same, other):
    lane = lax.broadcasted_iota(jnp.int32, (8, HDIM), 1)
    half = TCH // 2
    channel = lax.rem(lane, half).astype(jnp.float32)
    for block in range(same.shape[0]):
        angle = frames[block].astype(jnp.float32) * jnp.exp2(-channel)
        cosine, sine = jnp.cos(angle), jnp.sin(angle)
        same[block] = jnp.where(lane < TCH, cosine, 1.0)
        other[block] = jnp.where(lane < half, -sine, jnp.where(lane < TCH, sine, 0.0))


def lane_of(step):
    row, core = lax.axis_index("row"), lax.axis_index("core")
    return lax.bitwise_xor(row, step // 2) * 2 + lax.bitwise_xor(core, step % 2)


def turn_into(frames, x_ref, outs, same, other):
    turn_tables(frames, same, other)
    half = TCH // 2
    lane = lax.broadcasted_iota(jnp.int32, (BLK, HDIM), 1)
    for step in range(LANES):
        for head in range(HL):
            start = pl.multiple_of(lane_of(step) * HC + head * HDIM, HDIM)
            for block in range(x_ref.shape[0] // BLK):
                rows = slice(block * BLK, (block + 1) * BLK)
                x = x_ref[rows, pl.ds(start, HDIM)].astype(jnp.float32)
                partner = jnp.where(lane < half, pltpu.roll(x, HDIM - half, 1), pltpu.roll(x, half, 1))
                turned = x * same[block, :1] + partner * other[block, :1]
                outs[step][rows, head * HDIM : (head + 1) * HDIM] = turned.astype(jnp.bfloat16)


def pack_kv_kernel(frames, k_ref, v_ref, *rest):
    outs, tables = rest[:LANES], rest[LANES:]
    turn_into(frames, k_ref, outs, *tables)
    for step in range(LANES):
        start = pl.multiple_of(lane_of(step) * HC, HDIM)
        outs[step][:, HC:] = v_ref[:, pl.ds(start, HC)]


def pack_q_kernel(frames, q_ref, *rest):
    turn_into(frames, q_ref, rest[:LANES], *rest[LANES:])


def pack(kernel, frames, arrays, width):
    count = arrays[0].shape[0]
    table = pltpu.VMEM((count // BLK, 8, HDIM), jnp.float32)
    return pl.pallas_call(
        kernel,
        out_shape=[jax.ShapeDtypeStruct((count, width), jnp.bfloat16)] * LANES,
        in_specs=[pl.BlockSpec(memory_space=pltpu.SMEM)]
        + [pl.BlockSpec(memory_space=pltpu.VMEM) for _ in arrays],
        out_specs=[pl.BlockSpec(memory_space=pltpu.VMEM)] * LANES,
        scratch_shapes=[table, table],
        compiler_params=pltpu.CompilerParams(vmem_limit_bytes=56 * 1024 * 1024),
    )(frames, *arrays)


def attend_kernel(tiles, mask, *refs):
    q_refs, kv_refs, rest = refs[: len(tiles)], refs[len(tiles) : len(tiles) + 3 * LANES], refs[len(tiles) + 3 * LANES :]
    o_refs, (kv, scores, weights, sems) = rest[: len(tiles)], rest[len(tiles) :]
    plane = lax.axis_index("plane")
    rows = o_refs[0].shape[0]
    per_dev = rows // BLK
    nblk = mask.shape[0]
    span = 2 * REACH + 1

    copies = []
    for part in range(3):
        for step in range(LANES):
            at = pl.multiple_of((part * LANES + lane_of(step)) * rows, BLK)
            i = part * LANES + step
            copies.append(pltpu.make_async_copy(kv_refs[i], kv.at[pl.ds(at, rows)], sems.at[i]))
    for copy in copies:
        copy.start()
    for copy in copies:
        copy.wait()

    for t, step in enumerate(tiles):
        tile = lane_of(step)
        me = plane * LANES + tile
        start = pl.multiple_of(tile * rows, BLK)
        biases = []
        for j in range(span * per_dev):
            key_block = (me - REACH) * per_dev + j
            inside = (key_block >= 0) & (key_block < nblk)
            column = jnp.clip(key_block, 0, nblk - 1)
            biases.append(
                [jnp.where(inside & (mask[me * per_dev + a, column] > 0), 0.0, NEG) for a in range(per_dev)]
            )

        def one_head(h, carry):
            kcols = pl.ds(pl.multiple_of(h * HDIM, HDIM), HDIM)
            vcols = pl.ds(pl.multiple_of(HC + h * HDIM, HDIM), HDIM)
            sums = []
            for a in range(per_dev):
                block = slice(a * BLK, (a + 1) * BLK)
                q = q_refs[t][block, kcols]
                peak = jnp.full((BLK, BLK), NEG, jnp.float32)
                for i in range(span):
                    keys = kv[pl.ds(pl.multiple_of(start + i * rows, BLK), rows), kcols]
                    s = lax.dot_general(q, keys, (((1,), (1,)), ((), ())), preferred_element_type=jnp.float32)
                    for b in range(per_dev):
                        j = i * per_dev + b
                        part = s[:, b * BLK : (b + 1) * BLK] + biases[j][a]
                        peak = jnp.maximum(peak, part)
                        scores[block, j * BLK : (j + 1) * BLK] = part
                top = jnp.broadcast_to(jnp.max(peak, axis=1, keepdims=True), (BLK, BLK))
                total = jnp.zeros((BLK, BLK), jnp.float32)
                for j in range(span * per_dev):
                    cols = slice(j * BLK, (j + 1) * BLK)
                    e = jnp.exp2((scores[block, cols] - top) * TO_EXP2)
                    total += e
                    weights[block, cols] = e.astype(jnp.bfloat16)
                sums.append(jnp.sum(total, axis=1, keepdims=True))
            values = kv[pl.ds(start, span * rows), vcols]
            mixed = jnp.dot(weights[...], values, preferred_element_type=jnp.float32)
            o_refs[t][:, kcols] = (mixed / jnp.concatenate(sums, axis=0)).astype(jnp.bfloat16)
            return carry

        lax.fori_loop(0, HL, one_head, 0)


def attend(tiles, mask, q, kv):
    rows = kv[0].shape[0]
    span = (2 * REACH + 1) * rows
    vmem = pl.BlockSpec(memory_space=pltpu.VMEM)
    return pl.pallas_call(
        lambda *refs: attend_kernel(tiles, *refs),
        out_shape=[jax.ShapeDtypeStruct((rows, HC), jnp.bfloat16)] * len(tiles),
        in_specs=[pl.BlockSpec(memory_space=pltpu.SMEM)]
        + [vmem] * len(tiles)
        + [pl.BlockSpec(memory_space=pl.ANY)] * (3 * LANES),
        out_specs=[vmem] * len(tiles),
        scratch_shapes=[
            pltpu.VMEM((3 * LANES * rows, 2 * HC), jnp.bfloat16),
            pltpu.VMEM((rows, span), jnp.float32),
            pltpu.VMEM((rows, span), jnp.bfloat16),
            pltpu.SemaphoreType.DMA((3 * LANES,)),
        ],
        compiler_params=pltpu.CompilerParams(vmem_limit_bytes=56 * 1024 * 1024),
    )(mask, *[q[t] for t in tiles], *kv)


def project_kernel(order, a_refs, w_ref, o_ref, by_lane, by_shard):
    depth = by_shard.shape[1]
    shard = depth // len(order)

    @pl.when(pl.program_id(0) == 0)
    def _():
        for step in range(LANES):
            by_lane[lane_of(step)] = a_refs[step][...]
        parts = []
        for place in order:
            lane, at = place * shard // HC, place * shard % HC
            parts.append(by_lane[lane][:, at : at + shard])
        by_shard[...] = jnp.concatenate(parts, axis=1)

    o_ref[...] = jnp.dot(by_shard[...], w_ref[...], preferred_element_type=jnp.float32).astype(jnp.bfloat16)


def project(attended, weight, order, steps):
    count, depth = attended[0].shape
    channels, columns = weight.shape
    width = columns // steps
    whole = pl.BlockSpec((count, depth), lambda n: (0, 0))
    return pl.pallas_call(
        lambda *refs: project_kernel(order, refs[:LANES], *refs[LANES:]),
        out_shape=jax.ShapeDtypeStruct((count, columns), jnp.bfloat16),
        grid=(steps,),
        in_specs=[whole] * LANES + [pl.BlockSpec((channels, width), lambda n: (0, n))],
        out_specs=pl.BlockSpec((count, width), lambda n: (0, n)),
        scratch_shapes=[
            pltpu.VMEM((LANES, count, depth), jnp.bfloat16),
            pltpu.VMEM((count, channels), jnp.bfloat16),
        ],
        compiler_params=pltpu.CompilerParams(vmem_limit_bytes=56 * 1024 * 1024),
    )(*attended, weight)


def after(x, *others):
    return lax.optimization_barrier((x, *others))[0]


def on_device(queries, keys, values, frame_index, block_mask, out_weight):
    count = queries.shape[0]
    planes = lax.axis_size("plane")
    seq = ("plane", "row", "core")

    def index(p, r, c):
        return (p * 2 + r) * 2 + c

    every = [(p, r, c) for p in range(planes) for r in range(2) for c in range(2)]

    def to_lane(x, dr, dc):
        return lax.ppermute(x, seq, [(index(p, r, c), index(p, r ^ dr, c ^ dc)) for p, r, c in every])

    def to_plane(x, dp, dc):
        pairs = [
            (index(p, r, c), index(p + dp, r, c ^ dc)) for p, r, c in every if 0 <= p + dp < planes
        ]
        return lax.ppermute(x, seq, pairs)

    walk = [(p, 0) for p in range(planes)] + [(p, 1) for p in reversed(range(planes))]
    order = [index(p, r, c) for p, r in walk for c in range(2)]
    weight = lax.all_gather(out_weight, seq, axis=0, tiled=True, axis_index_groups=[order])

    kv = pack(pack_kv_kernel, frame_index, (keys, values), 2 * HC)
    across = [to_lane(kv[2], 1, 0), to_lane(kv[3], 1, 1)]
    early = {(dp, dc): to_plane(kv[dc], dp, dc) for dc in range(2) for dp in (1, -1)}
    here = [kv[0], to_lane(kv[1], 0, 1)] + across
    q = pack(pack_q_kernel, frame_index, (after(queries, kv[0]),), HC)
    late = {(dp, dc): to_plane(across[dc], dp, 0) for dc in range(2) for dp in (1, -1)}
    q = [q[0]] + [to_lane(after(q[d], *across), d // 2, d % 2) for d in range(1, LANES)]
    lower = [early[1, 0], early[1, 1], late[1, 0], late[1, 1]]
    upper = [early[-1, 0], early[-1, 1], late[-1, 0], late[-1, 1]]

    pieces = lower + here + upper
    attended = dict(zip((2, 3), attend((2, 3), block_mask, q, pieces)))
    back = {d: to_lane(attended[d], 1, d % 2) for d in (2, 3)}
    attended = dict(zip((0, 1), attend((0, 1), after(block_mask, attended[2]), q, pieces)))
    mixed = [attended[0], to_lane(attended[1], 0, 1), back[2], back[3]]
    return project(mixed, weight, order, 6)


def solution(mesh):
    groups, seq = mesh.devices.shape
    split = Mesh(
        mesh.devices.reshape(groups, seq // LANES, LANES // 2, 2), ("groups", "plane", "row", "core")
    )
    along = ("plane", "row", "core")
    tokens = P(("groups",) + along, None)
    return jax.shard_map(
        on_device,
        mesh=split,
        in_specs=(tokens, tokens, tokens, P(("groups",) + along), P(), P(along, None)),
        out_specs=tokens,
        check_vma=False,
    )
```

time: 175 us -> 146 us (0.83)
  waiting for transfers between devices: 79.5 us -> 63.9 us
  blocking collectives: 14.8 us -> 0 us
  Pallas kernels: 32.2 us -> 37.9 us
  starting transfers between devices: 30.9 us -> 27.7 us
  local copies, waits for them, and re-layouts: 4.22 us -> 2.16 us
    ppermute x3 -> x0, waiting for transfers between devices: 33.7 us -> none  [the longest x1 26.5 us: on_device(): other = lax.ppermute(strip, 'row', [(0, 1), (1, 0)])]
    ppermute x6 -> x9, waiting for transfers between devices: 14.3 us -> 38.9 us  [to_lane(): lax.ppermute(x, seq, [(index(p, r, c), index(p, r ^ dr, c ^ dc)) for p, r...]
    all_to_all x1 -> x0, blocking collectives: 14.8 us -> none  [on_device(): lax.all_to_all(attended.reshape(LANES, count, HC), lane, 0, 0, tiled=True)]
    ppermute x8, waiting for transfers between devices: 31.2 us -> 24.2 us  [to_plane(): return lax.ppermute(x, seq, pairs)]
    pallas_call x2 -> x3, Pallas kernels: 26.7 us -> 32.2 us  [the longest x2 24.1 us: attend(): pl.pallas_call(lambda *refs: attend_kernel(tiles, *refs), out_shape=[jax....]
    ppermute x6 -> x9, starting transfers between devices: 5.04 us -> 9.65 us  [to_lane(): lax.ppermute(x, seq, [(index(p, r, c), index(p, r ^ dr, c ^ dc)) for p, r...]
    ppermute x8, starting transfers between devices: 22.1 us -> 18 us  [to_plane(): return lax.ppermute(x, seq, pairs)]
    ppermute x3 -> x0, starting transfers between devices: 3.6 us -> none  [the longest x2 2.62 us: round_groups(): lax.ppermute(x, 'groups', [(g, (g + dx) % groups) for g in range(groups)])]
  transfers between devices with their start and end apart: 22 -> 18, of which waited for: 12 -> 8; matrix products, arithmetic and copies ran while one was open for 0% -> 0% of each run, Pallas kernels for 14% -> 21%
where the time goes in v4:
time: 146 us; the launch traced here: 145 us
  waiting for transfers between devices  63.9 us (44%)
  Pallas kernels  37.9 us (26%)
  starting transfers between devices  27.7 us (19%)
  between operations  13.6 us (9%)
  local copies, waits for them, and re-layouts  2.16 us (1%)
    ppermute x9, waiting for transfers between devices, to_lane(): lax.ppermute(x, seq, [(index(p, r, c), index(p, r ^ dr, c ^ dc)) for p, r...  38.9 us
    ppermute x8, waiting for transfers between devices, to_plane(): return lax.ppermute(x, seq, pairs)  24.2 us
    pallas_call x2, Pallas kernels, attend(): pl.pallas_call(lambda *refs: attend_kernel(tiles, *refs), out_shape=[jax....  24.1 us
    ppermute x8, starting transfers between devices, to_plane(): return lax.ppermute(x, seq, pairs)  18 us
    ppermute x9, starting transfers between devices, to_lane(): lax.ppermute(x, seq, [(index(p, r, c), index(p, r ^ dr, c ^ dc)) for p, r...  9.65 us
    pallas_call x1, Pallas kernels, project(): pl.pallas_call(lambda *refs: project_kernel(order, refs[:LANES], *refs[LA...  8.15 us
    pallas_call x2, Pallas kernels, pack(): pl.pallas_call(kernel, out_shape=[jax.ShapeDtypeStruct((count, width), jn...  5.7 us
  transfers between devices with their start and end apart: 18, of which 8 were waited for; matrix products, arithmetic and copies ran while one was open for 0% of the time, Pallas kernels for 21%

profile of v4, /device:TPU:0, one launch (start us, length us, event | category | flops | bytes accessed | tf_op | source)
XLA Modules:
  0.0 145.2 jit_solution(13244568994176705141)
XLA Ops:
  7.3 3.1 %shard_map.64 = (bf16[256,768]{1,0:T(8,128)(2,1)}, bf16[256,768]{1,0:T(8,128)(2,1)}, bf16[256,768]{1,0:T(8,128)(2,1)}, bf16[256,768]{1,0:T(8,128)(2,1)}) custom-call(s32[2]{0:T(128)} %frames.3, bf16[256,1536]{1,0:T(8,128)(2,1)} %k_ref.1, bf16[256,1536]{1,0:T(8,128)(2,1)} %v_ref.1), custom_call_target="tpu_custom_call" | custom-call | tf_op jit(solution)/shard_map/pallas_call | solution.py:69
  10.3 3.0 %collective-permute-start = (bf16[256,768]{1,0:T(8,128)(2,1)}, bf16[256,768]{1,0:T(8,128)(2,1)S(1)}, u32[]{:S(2)}, u32[]{:S(2)}) collective-permute-start(bf16[256,768]{1,0:T(8,128)(2,1)} %get-tuple-element.25), channel_id=1, source_target_pairs={{0,2},{1,3},{2,0},{3,1},{4,6},{5,7},{6,4},{7,5},{8,10},{9,11},{10,... | collective-permute-start | bytes 1179656 | tf_op jit(solution)/shard_map/ppermute | solution.py:217
  13.3 3.5 %collective-permute-start.4 = (bf16[256,768]{1,0:T(8,128)(2,1)}, bf16[256,768]{1,0:T(8,128)(2,1)S(1)}, u32[]{:S(2)}, u32[]{:S(2)}) collective-permute-start(bf16[256,768]{1,0:T(8,128)(2,1)} %get-tuple-element.22.refs_7_), channel_id=1, source_target_pairs={{0,4},{1,5},{2,6},{3,7},{4,8},{5,9},{6,10},{7,11},{8,12},{9,13},{1... | collective-permute-start | bytes 1179656 | tf_op jit(solution)/shard_map/ppermute | solution.py:223
  16.8 1.3 collective-permute-start.9
  18.1 1.3 collective-permute-start.10
  19.4 8.6 %collective-permute-done.refs_9_ = bf16[256,768]{1,0:T(8,128)(2,1)S(1)} collective-permute-done((bf16[256,768]{1,0:T(8,128)(2,1)}, bf16[256,768]{1,0:T(8,128)(2,1)S(1)}, u32[]{:S(2)}, u32[]{:S(2)}) %collective-permute-start) | collective-permute-done | bytes 393248 | tf_op jit(solution)/shard_map/ppermute | solution.py:217
  28.0 1.3 collective-permute-start.5
  29.3 14.4 %collective-permute-done.1.refs_10_ = bf16[256,768]{1,0:T(8,128)(2,1)S(1)} collective-permute-done((bf16[256,768]{1,0:T(8,128)(2,1)}, bf16[256,768]{1,0:T(8,128)(2,1)S(1)}, u32[]{:S(2)}, u32[]{:S(2)}) %collective-permute-start.1) | collective-permute-done | bytes 393248 | tf_op jit(solution)/shard_map/ppermute | solution.py:217
  43.7 2.6 %shard_map.65 = (bf16[256,384]{1,0:T(8,128)(2,1)}, bf16[256,384]{1,0:T(8,128)(2,1)}, bf16[256,384]{1,0:T(8,128)(2,1)}, bf16[256,384]{1,0:T(8,128)(2,1)}) custom-call(s32[2]{0:T(128)} %frames.3, bf16[256,1536]{1,0:T(8,128)(2,1)} %q_ref), custom_call_target="tpu_custom_call" | custom-call | tf_op jit(solution)/shard_map/pallas_call | solution.py:69
  46.3 2.2 %collective-permute-start.3 = (bf16[256,384]{1,0:T(8,128)(2,1)}, bf16[256,384]{1,0:T(8,128)(2,1)S(1)}, u32[]{:S(2)}, u32[]{:S(2)}) collective-permute-start(bf16[256,384]{1,0:T(8,128)(2,1)} %get-tuple-element.29), channel_id=1, source_target_pairs={{0,3},{1,2},{2,1},{3,0},{4,7},{5,6},{6,5},{7,4},{8,11},{9,10},{10,... | collective-permute-start | bytes 589832 | tf_op jit(solution)/shard_map/ppermute | solution.py:217
  48.6 1.3 collective-permute-start.11
  49.9 5.3 %collective-permute-done.10.refs_12_ = bf16[256,768]{1,0:T(8,128)(2,1)S(1)} collective-permute-done((bf16[256,768]{1,0:T(8,128)(2,1)}, bf16[256,768]{1,0:T(8,128)(2,1)S(1)}, u32[]{:S(2)}, u32[]{:S(2)}) %collective-permute-start.10) | collective-permute-done | bytes 393248 | tf_op jit(solution)/shard_map/ppermute | solution.py:223
  56.5 4.6 %collective-permute-start.6 = (bf16[256,768]{1,0:T(8,128)(2,1)S(1)}, bf16[256,768]{1,0:T(8,128)(2,1)S(1)}, u32[]{:S(2)}, u32[]{:S(2)}) collective-permute-start(bf16[256,768]{1,0:T(8,128)(2,1)S(1)} %collective-permute-done.refs_9_), channel_id=1, source_target_pairs={{0,4},{1,5},{2,6},{3,7},{4,8},{5,9},{6,10},{7,11},{8,12},{9,13},{1... | collective-permute-start | bytes 1179656 | tf_op jit(solution)/shard_map/ppermute | solution.py:223
  61.1 3.5 %collective-permute-start.7 = (bf16[256,768]{1,0:T(8,128)(2,1)S(1)}, bf16[256,768]{1,0:T(8,128)(2,1)S(1)}, u32[]{:S(2)}, u32[]{:S(2)}) collective-permute-start(bf16[256,768]{1,0:T(8,128)(2,1)S(1)} %collective-permute-done.1.refs_10_), channel_id=1, source_target_pairs={{0,4},{1,5},{2,6},{3,7},{4,8},{5,9},{6,10},{7,11},{8,12},{9,13},{1... | collective-permute-start | bytes 1179656 | tf_op jit(solution)/shard_map/ppermute | solution.py:223
  64.6 1.7 %collective-permute-start.2 = (bf16[256,384]{1,0:T(8,128)(2,1)}, bf16[256,384]{1,0:T(8,128)(2,1)S(1)}, u32[]{:S(2)}, u32[]{:S(2)}) collective-permute-start(bf16[256,384]{1,0:T(8,128)(2,1)} %get-tuple-element.27), channel_id=1, source_target_pairs={{0,2},{1,3},{2,0},{3,1},{4,6},{5,7},{6,4},{7,5},{8,10},{9,11},{10,... | collective-permute-start | bytes 589832 | tf_op jit(solution)/shard_map/ppermute | solution.py:217
  66.3 9.1 %collective-permute-done.2.refs_1_ = bf16[256,384]{1,0:T(8,128)(2,1)S(1)} collective-permute-done((bf16[256,384]{1,0:T(8,128)(2,1)}, bf16[256,384]{1,0:T(8,128)(2,1)S(1)}, u32[]{:S(2)}, u32[]{:S(2)}) %collective-permute-start.2) | collective-permute-done | bytes 196640 | tf_op jit(solution)/shard_map/ppermute | solution.py:217
  75.5 14.1 %collective-permute-done.12.refs_14_ = bf16[256,768]{1,0:T(8,128)(2,1)S(1)} collective-permute-done((bf16[256,768]{1,0:T(8,128)(2,1)S(1)}, bf16[256,768]{1,0:T(8,128)(2,1)S(1)}, u32[]{:S(2)}, u32[]{:S(2)}) %collective-permute-start.12) | collective-permute-done | bytes 393248 | tf_op jit(solution)/shard_map/ppermute | solution.py:223
  89.6 4.8 %collective-permute-done.7.refs_6_ = bf16[256,768]{1,0:T(8,128)(2,1)S(1)} collective-permute-done((bf16[256,768]{1,0:T(8,128)(2,1)S(1)}, bf16[256,768]{1,0:T(8,128)(2,1)S(1)}, u32[]{:S(2)}, u32[]{:S(2)}) %collective-permute-start.7) | collective-permute-done | bytes 393248 | tf_op jit(solution)/shard_map/ppermute | solution.py:223
  95.3 12.1 %shard_map.66 = (bf16[256,384]{1,0:T(8,128)(2,1)}, bf16[256,384]{1,0:T(8,128)(2,1)}) custom-call(s32[32,32]{1,0:T(8,128)} %refs_0_.2, bf16[256,384]{1,0:T(8,128)(2,1)} %copy-done.13, bf16[256,384]{1,0:T(8,128)(2,1)} %copy-done.11, bf16[256,768]{1,0:T(8,128)(2,1)} %copy-done.2, bf16[256,768]{1,0:T(8,128)(2,1)} %copy-done.5, bf16[256,768]{1,0:T(8,128)(2,1)} %copy-done.9, ...), custom_call_target="tpu_custom_call" | custom-call | tf_op jit(solution)/shard_map/pallas_call | solution.py:149
  107.4 2.5 %collective-permute-start.15 = (bf16[256,384]{1,0:T(8,128)(2,1)}, bf16[256,384]{1,0:T(8,128)(2,1)S(1)}, u32[]{:S(2)}, u32[]{:S(2)}) collective-permute-start(bf16[256,384]{1,0:T(8,128)(2,1)} %get-tuple-element.31), channel_id=1, source_target_pairs={{0,2},{1,3},{2,0},{3,1},{4,6},{5,7},{6,4},{7,5},{8,10},{9,11},{10,... | collective-permute-start | bytes 589832 | tf_op jit(solution)/shard_map/ppermute | solution.py:217
  110.6 12.0 %shard_map.67 = (bf16[256,384]{1,0:T(8,128)(2,1)}, bf16[256,384]{1,0:T(8,128)(2,1)}) custom-call(s32[32,32]{1,0:T(8,128)} %refs_0_.2, bf16[256,384]{1,0:T(8,128)(2,1)} %get-tuple-element.33.refs_1_, bf16[256,384]{1,0:T(8,128)(2,1)} %copy-done.12, bf16[256,768]{1,0:T(8,128)(2,1)} %copy-done.2, bf16[256,768]{1,0:T(8,128)(2,1)} %copy-done.5, ...), custom_call_target="tpu_custom_call" | custom-call | tf_op jit(solution)/shard_map/pallas_call | solution.py:149
  122.8 1.5 %collective-permute-done.14.refs_1_ = bf16[256,384]{1,0:T(8,128)(2,1)S(1)} collective-permute-done((bf16[256,384]{1,0:T(8,128)(2,1)}, bf16[256,384]{1,0:T(8,128)(2,1)S(1)}, u32[]{:S(2)}, u32[]{:S(2)}) %collective-permute-start.14) | collective-permute-done | bytes 196640 | tf_op jit(solution)/shard_map/ppermute | solution.py:217
  124.3 5.3 %collective-permute-done.16.refs_3_ = bf16[256,384]{1,0:T(8,128)(2,1)S(1)} collective-permute-done((bf16[256,384]{1,0:T(8,128)(2,1)}, bf16[256,384]{1,0:T(8,128)(2,1)S(1)}, u32[]{:S(2)}, u32[]{:S(2)}) %collective-permute-start.16) | collective-permute-done | bytes 196640 | tf_op jit(solution)/shard_map/ppermute | solution.py:217
  130.2 8.1 %shard_map.68 = bf16[256,3072]{1,0:T(8,128)(2,1)} custom-call(bf16[256,384]{1,0:T(8,128)(2,1)} %get-tuple-element.36.refs_0_, bf16[256,384]{1,0:T(8,128)(2,1)} %copy-done.15, bf16[256,384]{1,0:T(8,128)(2,1)} %copy-done.14, bf16[256,384]{1,0:T(8,128)(2,1)} %copy-done.16, bf16[1536,3072]{1,0:T(8,128)(2,1)} %all-gather.2.cloned.1.call-done.refs_4_), custom_call_target="tpu_custom_call" | custom-call | tf_op jit(solution)/shard_map/pallas_call | solution.py:188
  (52 shorter events, 4.4 us)
Async XLA Ops:
  6.5 123.0 %all-gather.2.cloned.1.call-start = ((), (), s32[]{:S(2)}) async-start(), calls=%async_computation | async-start | bytes 10027008 | tf_op jit(solution)/shard_map/all_gather | solution.py:227
  10.3 17.7 %collective-permute-start = (bf16[256,768]{1,0:T(8,128)(2,1)}, bf16[256,768]{1,0:T(8,128)(2,1)S(1)}, u32[]{:S(2)}, u32[]{:S(2)}) collective-permute-start(bf16[256,768]{1,0:T(8,128)(2,1)} %get-tuple-element.25), channel_id=1, source_target_pairs={{0,2},{1,3},{2,0},{3,1},{4,6},{5,7},{6,4},{7,5},{8,10},{9,11},{10,... | collective-permute-start | bytes 1179656 | tf_op jit(solution)/shard_map/ppermute | solution.py:217
  13.3 30.4 %collective-permute-start.1 = (bf16[256,768]{1,0:T(8,128)(2,1)}, bf16[256,768]{1,0:T(8,128)(2,1)S(1)}, u32[]{:S(2)}, u32[]{:S(2)}) collective-permute-start(bf16[256,768]{1,0:T(8,128)(2,1)} %get-tuple-element.26), channel_id=1, source_target_pairs={{0,3},{1,2},{2,1},{3,0},{4,7},{5,6},{6,5},{7,4},{8,11},{9,10},{10,... | collective-permute-start | bytes 1179656 | tf_op jit(solution)/shard_map/ppermute | solution.py:217
  13.3 33.0 %collective-permute-start.4 = (bf16[256,768]{1,0:T(8,128)(2,1)}, bf16[256,768]{1,0:T(8,128)(2,1)S(1)}, u32[]{:S(2)}, u32[]{:S(2)}) collective-permute-start(bf16[256,768]{1,0:T(8,128)(2,1)} %get-tuple-element.22.refs_7_), channel_id=1, source_target_pairs={{0,4},{1,5},{2,6},{3,7},{4,8},{5,9},{6,10},{7,11},{8,12},{9,13},{1... | collective-permute-start | bytes 1179656 | tf_op jit(solution)/shard_map/ppermute | solution.py:223
  16.8 31.8 %collective-permute-start.9 = (bf16[256,768]{1,0:T(8,128)(2,1)}, bf16[256,768]{1,0:T(8,128)(2,1)S(1)}, u32[]{:S(2)}, u32[]{:S(2)}) collective-permute-start(bf16[256,768]{1,0:T(8,128)(2,1)} %get-tuple-element.22.refs_7_), channel_id=1, source_target_pairs={{4,0},{5,1},{6,2},{7,3},{8,4},{9,5},{10,6},{11,7},{12,8},{13,9},{1... | collective-permute-start | bytes 1179656 | tf_op jit(solution)/shard_map/ppermute | solution.py:223
  18.1 37.0 %collective-permute-start.10 = (bf16[256,768]{1,0:T(8,128)(2,1)}, bf16[256,768]{1,0:T(8,128)(2,1)S(1)}, u32[]{:S(2)}, u32[]{:S(2)}) collective-permute-start(bf16[256,768]{1,0:T(8,128)(2,1)} %get-tuple-element.30), channel_id=1, source_target_pairs={{4,1},{5,0},{6,3},{7,2},{8,5},{9,4},{10,7},{11,6},{12,9},{13,8},{1... | collective-permute-start | bytes 1179656 | tf_op jit(solution)/shard_map/ppermute | solution.py:223
  28.0 66.4 %copy-start = (bf16[256,768]{1,0:T(8,128)(2,1)}, bf16[256,768]{1,0:T(8,128)(2,1)S(1)}, u32[]{:S(2)}) copy-start(bf16[256,768]{1,0:T(8,128)(2,1)S(1)} %collective-permute-done.refs_9_) | copy-start | bytes 1179652
  28.0 28.4 %collective-permute-start.5 = (bf16[256,768]{1,0:T(8,128)(2,1)}, bf16[256,768]{1,0:T(8,128)(2,1)S(1)}, u32[]{:S(2)}, u32[]{:S(2)}) collective-permute-start(bf16[256,768]{1,0:T(8,128)(2,1)} %get-tuple-element.30), channel_id=1, source_target_pairs={{0,5},{1,4},{2,7},{3,6},{4,9},{5,8},{6,11},{7,10},{8,13},{9,12},{1... | collective-permute-start | bytes 1179656 | tf_op jit(solution)/shard_map/ppermute | solution.py:223
  43.7 50.7 %copy-start.1 = (bf16[256,768]{1,0:T(8,128)(2,1)}, bf16[256,768]{1,0:T(8,128)(2,1)S(1)}, u32[]{:S(2)}) copy-start(bf16[256,768]{1,0:T(8,128)(2,1)S(1)} %collective-permute-done.1.refs_10_) | copy-start | bytes 1179652
  43.7 17.3 %collective-permute-start.8 = (bf16[256,768]{1,0:T(8,128)(2,1)}, bf16[256,768]{1,0:T(8,128)(2,1)S(1)}, u32[]{:S(2)}, u32[]{:S(2)}) collective-permute-start(bf16[256,768]{1,0:T(8,128)(2,1)} %get-tuple-element.30), channel_id=1, source_target_pairs={{0,1},{1,0},{2,3},{3,2},{4,5},{5,4},{6,7},{7,6},{8,9},{9,8},{10,11... | collective-permute-start | bytes 1179656 | tf_op jit(solution)/shard_map/ppermute | solution.py:217
  46.3 48.1 %copy-start.2 = (bf16[256,768]{1,0:T(8,128)(2,1)}, bf16[256,768]{1,0:T(8,128)(2,1)S(1)}, u32[]{:S(2)}) copy-start(bf16[256,768]{1,0:T(8,128)(2,1)S(1)} %collective-permute-done.4.refs_3_) | copy-start | bytes 1179652
  46.3 18.2 %collective-permute-start.3 = (bf16[256,384]{1,0:T(8,128)(2,1)}, bf16[256,384]{1,0:T(8,128)(2,1)S(1)}, u32[]{:S(2)}, u32[]{:S(2)}) collective-permute-start(bf16[256,384]{1,0:T(8,128)(2,1)} %get-tuple-element.29), channel_id=1, source_target_pairs={{0,3},{1,2},{2,1},{3,0},{4,7},{5,6},{6,5},{7,4},{8,11},{9,10},{10,... | collective-permute-start | bytes 589832 | tf_op jit(solution)/shard_map/ppermute | solution.py:217
  48.6 45.9 %copy-start.3 = (bf16[256,768]{1,0:T(8,128)(2,1)}, bf16[256,768]{1,0:T(8,128)(2,1)S(1)}, u32[]{:S(2)}) copy-start(bf16[256,768]{1,0:T(8,128)(2,1)S(1)} %collective-permute-done.9.refs_11_) | copy-start | bytes 1179652
  48.6 26.9 %collective-permute-start.11 = (bf16[256,768]{1,0:T(8,128)(2,1)S(1)}, bf16[256,768]{1,0:T(8,128)(2,1)S(1)}, u32[]{:S(2)}, u32[]{:S(2)}) collective-permute-start(bf16[256,768]{1,0:T(8,128)(2,1)S(1)} %collective-permute-done.refs_9_), channel_id=1, source_target_pairs={{4,0},{5,1},{6,2},{7,3},{8,4},{9,5},{10,6},{11,7},{12,8},{13,9},{1... | collective-permute-start | bytes 1179656 | tf_op jit(solution)/shard_map/ppermute | solution.py:223
  55.1 39.3 %copy-start.4 = (bf16[256,768]{1,0:T(8,128)(2,1)}, bf16[256,768]{1,0:T(8,128)(2,1)S(1)}, u32[]{:S(2)}) copy-start(bf16[256,768]{1,0:T(8,128)(2,1)S(1)} %collective-permute-done.10.refs_12_) | copy-start | bytes 1179652
  55.1 34.4 %collective-permute-start.12 = (bf16[256,768]{1,0:T(8,128)(2,1)S(1)}, bf16[256,768]{1,0:T(8,128)(2,1)S(1)}, u32[]{:S(2)}, u32[]{:S(2)}) collective-permute-start(bf16[256,768]{1,0:T(8,128)(2,1)S(1)} %collective-permute-done.1.refs_10_), channel_id=1, source_target_pairs={{4,0},{5,1},{6,2},{7,3},{8,4},{9,5},{10,6},{11,7},{12,8},{13,9},{1... | collective-permute-start | bytes 1179656 | tf_op jit(solution)/shard_map/ppermute | solution.py:223
  56.4 38.0 %copy-start.5 = (bf16[256,768]{1,0:T(8,128)(2,1)}, bf16[256,768]{1,0:T(8,128)(2,1)S(1)}, u32[]{:S(2)}) copy-start(bf16[256,768]{1,0:T(8,128)(2,1)S(1)} %collective-permute-done.5.refs_4_) | copy-start | bytes 1179652
  56.5 33.1 %collective-permute-start.6 = (bf16[256,768]{1,0:T(8,128)(2,1)S(1)}, bf16[256,768]{1,0:T(8,128)(2,1)S(1)}, u32[]{:S(2)}, u32[]{:S(2)}) collective-permute-start(bf16[256,768]{1,0:T(8,128)(2,1)S(1)} %collective-permute-done.refs_9_), channel_id=1, source_target_pairs={{0,4},{1,5},{2,6},{3,7},{4,8},{5,9},{6,10},{7,11},{8,12},{9,13},{1... | collective-permute-start | bytes 1179656 | tf_op jit(solution)/shard_map/ppermute | solution.py:223
  61.1 33.4 %collective-permute-start.7 = (bf16[256,768]{1,0:T(8,128)(2,1)S(1)}, bf16[256,768]{1,0:T(8,128)(2,1)S(1)}, u32[]{:S(2)}, u32[]{:S(2)}) collective-permute-start(bf16[256,768]{1,0:T(8,128)(2,1)S(1)} %collective-permute-done.1.refs_10_), channel_id=1, source_target_pairs={{0,4},{1,5},{2,6},{3,7},{4,8},{5,9},{6,10},{7,11},{8,12},{9,13},{1... | collective-permute-start | bytes 1179656 | tf_op jit(solution)/shard_map/ppermute | solution.py:223
  64.6 10.9 %collective-permute-start.2 = (bf16[256,384]{1,0:T(8,128)(2,1)}, bf16[256,384]{1,0:T(8,128)(2,1)S(1)}, u32[]{:S(2)}, u32[]{:S(2)}) collective-permute-start(bf16[256,384]{1,0:T(8,128)(2,1)} %get-tuple-element.27), channel_id=1, source_target_pairs={{0,2},{1,3},{2,0},{3,1},{4,6},{5,7},{6,4},{7,5},{8,10},{9,11},{10,... | collective-permute-start | bytes 589832 | tf_op jit(solution)/shard_map/ppermute | solution.py:217
  75.4 34.4 %collective-permute-start.13 = (bf16[256,384]{1,0:T(8,128)(2,1)}, bf16[256,384]{1,0:T(8,128)(2,1)S(1)}, u32[]{:S(2)}, u32[]{:S(2)}) collective-permute-start(bf16[256,384]{1,0:T(8,128)(2,1)} %get-tuple-element.35), channel_id=1, source_target_pairs={{0,1},{1,0},{2,3},{3,2},{4,5},{5,4},{6,7},{7,6},{8,9},{9,8},{10,11... | collective-permute-start | bytes 589832 | tf_op jit(solution)/shard_map/ppermute | solution.py:217
  107.4 16.9 %collective-permute-start.15 = (bf16[256,384]{1,0:T(8,128)(2,1)}, bf16[256,384]{1,0:T(8,128)(2,1)S(1)}, u32[]{:S(2)}, u32[]{:S(2)}) collective-permute-start(bf16[256,384]{1,0:T(8,128)(2,1)} %get-tuple-element.31), channel_id=1, source_target_pairs={{0,2},{1,3},{2,0},{3,1},{4,6},{5,7},{6,4},{7,5},{8,10},{9,11},{10,... | collective-permute-start | bytes 589832 | tf_op jit(solution)/shard_map/ppermute | solution.py:217
  122.6 1.7 %collective-permute-start.14 = (bf16[256,384]{1,0:T(8,128)(2,1)}, bf16[256,384]{1,0:T(8,128)(2,1)S(1)}, u32[]{:S(2)}, u32[]{:S(2)}) collective-permute-start(bf16[256,384]{1,0:T(8,128)(2,1)} %get-tuple-element.37), channel_id=1, source_target_pairs={{0,1},{1,0},{2,3},{3,2},{4,5},{5,4},{6,7},{7,6},{8,9},{9,8},{10,11... | collective-permute-start | bytes 589832 | tf_op jit(solution)/shard_map/ppermute | solution.py:217
  122.7 6.9 %collective-permute-start.16 = (bf16[256,384]{1,0:T(8,128)(2,1)}, bf16[256,384]{1,0:T(8,128)(2,1)S(1)}, u32[]{:S(2)}, u32[]{:S(2)}) collective-permute-start(bf16[256,384]{1,0:T(8,128)(2,1)} %get-tuple-element.38), channel_id=1, source_target_pairs={{0,3},{1,2},{2,1},{3,0},{4,7},{5,6},{6,5},{7,4},{8,11},{9,10},{10,... | collective-permute-start | bytes 589832 | tf_op jit(solution)/shard_map/ppermute | solution.py:217
  (11 other events, 123.9 us)
Sparse Core Ops, SparseCore 0:
  9.0 90.9 all-gather.1

commit v5 on v4

v5 whole, which is shorter than its diff:
```python
import math

import jax
import jax.numpy as jnp
from jax import lax
from jax.experimental import pallas as pl
from jax.experimental.pallas import tpu as pltpu
from jax.sharding import Mesh
from jax.sharding import PartitionSpec as P

HEADS = 12
HDIM = 128
TCH = 16
BLK = 128
LANES = 4
HL = HEADS // LANES
HC = HL * HDIM
REACH = 4
NEG = -1e30
TO_EXP2 = math.log2(math.e) / math.sqrt(HDIM)


def turn_tables(frames, same, other):
    lane = lax.broadcasted_iota(jnp.int32, (8, HDIM), 1)
    half = TCH // 2
    channel = lax.rem(lane, half).astype(jnp.float32)
    for block in range(same.shape[0]):
        angle = frames[block].astype(jnp.float32) * jnp.exp2(-channel)
        cosine, sine = jnp.cos(angle), jnp.sin(angle)
        same[block] = jnp.where(lane < TCH, cosine, 1.0)
        other[block] = jnp.where(lane < half, -sine, jnp.where(lane < TCH, sine, 0.0))


def lane_of(step):
    mine = lax.axis_index("row") * 2 + lax.axis_index("core")
    return lax.bitwise_xor(mine, step)


def turn_into(frames, x_ref, outs, same, other):
    turn_tables(frames, same, other)
    half = TCH // 2
    lane = lax.broadcasted_iota(jnp.int32, (BLK, HDIM), 1)
    for step in range(LANES):
        for head in range(HL):
            start = pl.multiple_of(lane_of(step) * HC + head * HDIM, HDIM)
            for block in range(x_ref.shape[0] // BLK):
                rows = slice(block * BLK, (block + 1) * BLK)
                x = x_ref[rows, pl.ds(start, HDIM)].astype(jnp.float32)
                partner = jnp.where(lane < half, pltpu.roll(x, HDIM - half, 1), pltpu.roll(x, half, 1))
                turned = x * same[block, :1] + partner * other[block, :1]
                outs[step][rows, head * HDIM : (head + 1) * HDIM] = turned.astype(jnp.bfloat16)


def pack_kv_kernel(frames, k_ref, v_ref, *rest):
    outs, tables = rest[:LANES], rest[LANES:]
    turn_into(frames, k_ref, outs, *tables)
    for step in range(LANES):
        start = pl.multiple_of(lane_of(step) * HC, HDIM)
        outs[step][:, HC:] = v_ref[:, pl.ds(start, HC)]


def pack_q_kernel(frames, q_ref, *rest):
    turn_into(frames, q_ref, rest[:LANES], *rest[LANES:])


def pack(kernel, frames, arrays, width):
    count = arrays[0].shape[0]
    table = pltpu.VMEM((count // BLK, 8, HDIM), jnp.float32)
    return pl.pallas_call(
        kernel,
        out_shape=[jax.ShapeDtypeStruct((count, width), jnp.bfloat16)] * LANES,
        in_specs=[pl.BlockSpec(memory_space=pltpu.SMEM)]
        + [pl.BlockSpec(memory_space=pltpu.VMEM) for _ in arrays],
        out_specs=[pl.BlockSpec(memory_space=pltpu.VMEM)] * LANES,
        scratch_shapes=[table, table],
        compiler_params=pltpu.CompilerParams(vmem_limit_bytes=56 * 1024 * 1024),
    )(frames, *arrays)


def biases_of(mask, me, devices, per_dev):
    nblk = mask.shape[0]
    biases = []
    for device in devices:
        for b in range(per_dev):
            key_block = device * per_dev + b
            inside = (key_block >= 0) & (key_block < nblk)
            column = jnp.clip(key_block, 0, nblk - 1)
            biases.append(
                [jnp.where(inside & (mask[me * per_dev + a, column] > 0), 0.0, NEG) for a in range(per_dev)]
            )
    return biases


def attend_head(h, q, kv, starts, biases, scores, weights, state):
    rows = q.shape[0]
    per_dev = rows // BLK
    kcols = slice(h * HDIM, (h + 1) * HDIM)
    vcols = slice(HC + h * HDIM, HC + (h + 1) * HDIM)
    peak = jnp.full((rows, BLK), NEG, jnp.float32)
    for i, start in enumerate(starts):
        keys = kv[pl.ds(start, rows), kcols]
        s = lax.dot_general(q, keys, (((1,), (1,)), ((), ())), preferred_element_type=jnp.float32)
        for b in range(per_dev):
            j = i * per_dev + b
            parts = [
                s[a * BLK : (a + 1) * BLK, b * BLK : (b + 1) * BLK] + biases[j][a] for a in range(per_dev)
            ]
            part = jnp.concatenate(parts, axis=0)
            peak = jnp.maximum(peak, part)
            scores[h, :, j * BLK : (j + 1) * BLK] = part
    top = jnp.max(peak, axis=1, keepdims=True)
    if state is not None:
        top = jnp.maximum(top, state[0])
    total = jnp.zeros((rows, BLK), jnp.float32)
    for j in range(len(starts) * per_dev):
        cols = slice(j * BLK, (j + 1) * BLK)
        e = jnp.exp2((scores[h, :, cols] - top) * TO_EXP2)
        total += e
        weights[h, :, cols] = e.astype(jnp.bfloat16)
    mixed = None
    for i, start in enumerate(starts):
        part = jnp.dot(
            weights[h, :, i * rows : (i + 1) * rows],
            kv[pl.ds(start, rows), vcols],
            preferred_element_type=jnp.float32,
        )
        mixed = part if mixed is None else mixed + part
    total = jnp.sum(total, axis=1, keepdims=True)
    if state is not None:
        shrink = jnp.exp2((state[0] - top) * TO_EXP2)
        total += state[1] * shrink
        mixed += state[2] * shrink
    return top, total, mixed


def fetch(pairs, sems):
    copies = [pltpu.make_async_copy(source, target, sems.at[i]) for i, (source, target) in enumerate(pairs)]
    for copy in copies:
        copy.start()
    for copy in copies:
        copy.wait()


def begin_kernel(mask, *refs):
    q_refs, kv_refs, rest = refs[:LANES], refs[LANES : 3 * LANES], refs[3 * LANES :]
    accs, stats, (q_all, kv, scores, weights, sems) = rest[:2], rest[2:4], rest[4:]
    rows = q_all.shape[1]
    per_dev = rows // BLK
    plane = lax.axis_index("plane")
    pairs = [(q_refs[step], q_all.at[step]) for step in range(LANES)]
    places = [LANES + lane_of(step) for step in range(LANES)]
    places += [part * LANES + lane_of(step) for part in (0, 2) for step in range(2)]
    for ref, place in zip(kv_refs, places):
        pairs.append((ref, kv.at[pl.ds(pl.multiple_of(place * rows, BLK), rows)]))
    fetch(pairs, sems)
    for group in range(2):

        def one_tile(core, carry):
            step = 2 * group + core
            tile = lane_of(step)
            me = plane * LANES + tile
            devices = [plane * LANES + lane for lane in range(LANES)]
            devices += chunk_devices_at(group, tile, False)
            starts = [pl.multiple_of((d - (plane - 1) * LANES) * rows, BLK) for d in devices]
            biases = biases_of(mask, me, devices, per_dev)
            for h in range(HL):
                cols = slice(h * HDIM, (h + 1) * HDIM)
                q = q_all[step, :, cols]
                top, total, mixed = attend_head(h, q, kv, starts, biases, scores, weights, None)
                accs[group][core, :, cols] = mixed
                stats[group][core, :, h : h + 1] = top
                stats[group][core, :, HL + h : HL + h + 1] = total
            return carry

        lax.fori_loop(0, 2, one_tile, 0)


def chunk_devices_at(group, tile, late):
    plane = lax.axis_index("plane")
    me = plane * LANES + tile
    row, core = lax.div(tile, 2), lax.rem(tile, 2)
    if late == (group == 1):
        return [me - REACH, me + REACH, jnp.where(core == 0, me - REACH + 1, me + REACH - 1)]
    first = jnp.where(row == 0, (plane - 1) * LANES + 2, (plane + 1) * LANES)
    return [first, first + 1]


def finish_kernel(group, mask, q_a, q_b, acc, stat, *refs):
    kv_refs, o_refs, (kv, scores, weights, sems) = refs[:LANES], refs[LANES : LANES + 2], refs[LANES + 2 :]
    rows = q_a.shape[0]
    per_dev = rows // BLK
    plane = lax.axis_index("plane")
    places = [part * LANES + lane_of(step) for part in (0, 2) for step in (2, 3)]
    fetch(
        [
            (ref, kv.at[pl.ds(pl.multiple_of(place * rows, BLK), rows)])
            for ref, place in zip(kv_refs, places)
        ],
        sems,
    )
    for core, (q_ref, o_ref) in enumerate(zip((q_a, q_b), o_refs)):
        tile = lane_of(2 * group + core)
        me = plane * LANES + tile
        devices = chunk_devices_at(group, tile, True)
        starts = [pl.multiple_of((d - (plane - 1) * LANES) * rows, BLK) for d in devices]
        biases = biases_of(mask, me, devices, per_dev)
        for h in range(HL):
            cols = slice(h * HDIM, (h + 1) * HDIM)
            state = (stat[core, :, h : h + 1], stat[core, :, HL + h : HL + h + 1], acc[core, :, cols])
            _, total, mixed = attend_head(h, q_ref[:, cols], kv, starts, biases, scores, weights, state)
            o_ref[:, cols] = (mixed / total).astype(jnp.bfloat16)


def attend_begin(mask, q, kv):
    rows = kv[0].shape[0]
    span = 7 * rows
    vmem = pl.BlockSpec(memory_space=pltpu.VMEM)
    return pl.pallas_call(
        begin_kernel,
        out_shape=[jax.ShapeDtypeStruct((2, rows, HC), jnp.float32)] * 2
        + [jax.ShapeDtypeStruct((2, rows, HDIM), jnp.float32)] * 2,
        in_specs=[pl.BlockSpec(memory_space=pltpu.SMEM)] + [pl.BlockSpec(memory_space=pl.ANY)] * (3 * LANES),
        out_specs=[vmem] * 4,
        scratch_shapes=[
            pltpu.VMEM((LANES, rows, HC), jnp.bfloat16),
            pltpu.VMEM((3 * LANES * rows, 2 * HC), jnp.bfloat16),
            pltpu.VMEM((HL, rows, span), jnp.float32),
            pltpu.VMEM((HL, rows, span), jnp.bfloat16),
            pltpu.SemaphoreType.DMA((3 * LANES,)),
        ],
        compiler_params=pltpu.CompilerParams(vmem_limit_bytes=56 * 1024 * 1024),
    )(mask, *q, *kv)


def attend_finish(group, mask, q, acc, stat, kv):
    rows = kv[0].shape[0]
    span = 3 * rows
    vmem = pl.BlockSpec(memory_space=pltpu.VMEM)
    return pl.pallas_call(
        lambda *refs: finish_kernel(group, *refs),
        out_shape=[jax.ShapeDtypeStruct((rows, HC), jnp.bfloat16)] * 2,
        in_specs=[pl.BlockSpec(memory_space=pltpu.SMEM)]
        + [vmem] * 4
        + [pl.BlockSpec(memory_space=pl.ANY)] * LANES,
        out_specs=[vmem] * 2,
        scratch_shapes=[
            pltpu.VMEM((3 * LANES * rows, 2 * HC), jnp.bfloat16),
            pltpu.VMEM((HL, rows, span), jnp.float32),
            pltpu.VMEM((HL, rows, span), jnp.bfloat16),
            pltpu.SemaphoreType.DMA((LANES,)),
        ],
        compiler_params=pltpu.CompilerParams(vmem_limit_bytes=56 * 1024 * 1024),
    )(mask, *q, acc, stat, *kv)


def project_kernel(order, groups, a_refs, w_refs, o_ref, by_lane, by_shard):
    step = pl.program_id(0)
    depth = by_shard.shape[1]
    shard = depth // len(order)

    @pl.when(step == 0)
    def _():
        for d in range(LANES):
            by_lane[lane_of(d)] = a_refs[d][...]
        parts = []
        for place in order:
            lane, at = place * shard // HC, place * shard % HC
            parts.append(by_lane[lane][:, at : at + shard])
        by_shard[...] = jnp.concatenate(parts, axis=1)

    mine, core = lax.axis_index("groups"), lax.axis_index("core")
    widths = [w.shape[1] for w in w_refs]
    steps = o_ref.shape[1] // (widths[0] + groups * widths[1])
    direct, strip, half = widths[0] * steps, widths[1] * steps, widths[1] * steps // 2
    places = [0, direct + mine * strip]
    for dx in range(1, groups):
        start = direct + lax.rem(mine + groups - dx, groups) * strip
        places += [start + core * half, start + (1 - core) * half]
    for w_ref, place, width in zip(w_refs, places, widths):
        out = jnp.dot(by_shard[...], w_ref[...], preferred_element_type=jnp.float32)
        at = pl.multiple_of(place + step * width, HDIM)
        o_ref[:, pl.ds(at, width)] = out.astype(jnp.bfloat16)


def project(attended, weights, order, groups):
    count, depth = attended[0].shape
    channels = weights[0].shape[0]
    steps = weights[-1].shape[1] // HDIM
    columns = weights[0].shape[1] + groups * weights[1].shape[1]
    whole = pl.BlockSpec((count, depth), lambda n: (0, 0))
    return pl.pallas_call(
        lambda *refs: project_kernel(order, groups, refs[:LANES], refs[LANES:-3], *refs[-3:]),
        out_shape=jax.ShapeDtypeStruct((count, columns), jnp.bfloat16),
        grid=(steps,),
        in_specs=[whole] * LANES
        + [pl.BlockSpec((channels, w.shape[1] // steps), lambda n: (0, n)) for w in weights],
        out_specs=pl.BlockSpec((count, columns), lambda n: (0, 0)),
        scratch_shapes=[
            pltpu.VMEM((LANES, count, depth), jnp.bfloat16),
            pltpu.VMEM((count, channels), jnp.bfloat16),
        ],
        compiler_params=pltpu.CompilerParams(vmem_limit_bytes=56 * 1024 * 1024),
    )(*attended, *weights)


def after(x, *others):
    return lax.optimization_barrier((x, *others))[0]


def on_device(queries, keys, values, frame_index, block_mask, out_weight):
    count = queries.shape[0]
    planes, groups = lax.axis_size("plane"), lax.axis_size("groups")
    seq = ("plane", "row", "core")

    def index(p, r, c):
        return (p * 2 + r) * 2 + c

    every = [(p, r, c) for p in range(planes) for r in range(2) for c in range(2)]

    def to_lane(x, dr, dc):
        return lax.ppermute(x, seq, [(index(p, r, c), index(p, r ^ dr, c ^ dc)) for p, r, c in every])

    def to_plane(x, dp, dc):
        pairs = [
            (index(p, r, c), index(p + dp, r, c ^ dc)) for p, r, c in every if 0 <= p + dp < planes
        ]
        return lax.ppermute(x, seq, pairs)

    walk = [(p, 0) for p in range(planes)] + [(p, 1) for p in reversed(range(planes))]
    order = [index(p, r, c) for p, r in walk for c in range(2)]

    def gather(part):
        return lax.all_gather(part, seq, axis=0, tiled=True, axis_index_groups=[order])

    columns = out_weight.shape[1]
    strip = 2 * columns // 3 // (groups * 2 * HDIM) * 2 * HDIM
    direct = columns - groups * strip
    strip_at = direct + lax.axis_index("groups") * strip
    own_strip = gather(lax.dynamic_slice_in_dim(out_weight, strip_at, strip, 1))

    kv = pack(pack_kv_kernel, frame_index, (keys, values), 2 * HC)
    across = [to_lane(kv[2], 1, 0), to_lane(kv[3], 1, 1)]
    early = {(dp, dc): to_plane(kv[dc], dp, dc) for dc in range(2) for dp in (1, -1)}
    here = [kv[0], to_lane(kv[1], 0, 1)] + across
    q = pack(pack_q_kernel, frame_index, (after(queries, across[0]),), HC)
    late = {(dp, dc): to_plane(across[dc], dp, 0) for dc in range(2) for dp in (1, -1)}
    q = [q[0]] + [to_lane(after(q[d], *across), d // 2, d % 2) for d in range(1, LANES)]

    own_strip = after(own_strip, *early.values())
    half = strip // 2
    core_at = lax.axis_index("core") * half
    sent = lax.dynamic_slice_in_dim(own_strip, core_at, half, 1)
    halves = [
        lax.ppermute(sent, "groups", [(g, (g + dx) % groups) for g in range(groups)])
        for dx in range(1, groups)
    ]
    begun = attend_begin(
        after(block_mask, sent), q, here + [early[dp, dc] for dp in (1, -1) for dc in range(2)]
    )
    late = [after(late[dp, dc], begun[0]) for dp in (1, -1) for dc in range(2)]
    direct_strip = gather(after(out_weight[:, :direct], *late))
    mixed = attend_finish(1, block_mask, q[2:], begun[1], begun[3], late)
    back = [to_lane(mixed[d], 1, d) for d in range(2)]
    mixed = attend_finish(0, after(block_mask, mixed[0]), q[:2], begun[0], begun[2], late)
    mixed = [mixed[0], to_lane(mixed[1], 0, 1)] + back
    weights = [direct_strip, own_strip]
    for x in halves:
        x = after(x, mixed[0])
        weights += [x, lax.ppermute(x, "core", [(0, 1), (1, 0)])]
    return project(mixed, weights, order, groups)


def solution(mesh):
    groups, seq = mesh.devices.shape
    split = Mesh(
        mesh.devices.reshape(groups, seq // LANES, LANES // 2, 2), ("groups", "plane", "row", "core")
    )
    along = ("plane", "row", "core")
    tokens = P(("groups",) + along, None)
    return jax.shard_map(
        on_device,
        mesh=split,
        in_specs=(tokens, tokens, tokens, P(("groups",) + along), P(), P(along, None)),
        out_specs=tokens,
        check_vma=False,
    )
```

time: 146 us -> 148 us (1.014)
  waiting for transfers between devices: 63.9 us -> 52.4 us
  starting transfers between devices: 27.7 us -> 32.9 us
  local copies, waits for them, and re-layouts: 2.16 us -> 6.32 us
  Pallas kernels: 37.9 us -> 41.6 us
    ppermute x8, waiting for transfers between devices: 24.2 us -> 0.67 us  [to_plane(): return lax.ppermute(x, seq, pairs)]
    ppermute x0 -> x2, waiting for transfers between devices: none -> 19.4 us  [the longest x1 19.3 us: on_device(): lax.ppermute(sent, 'groups', [(g, (g + dx) % groups) for g in range(group...]
    ppermute x9, waiting for transfers between devices: 38.9 us -> 32.3 us  [to_lane(): lax.ppermute(x, seq, [(index(p, r, c), index(p, r ^ dr, c ^ dc)) for p, r...]
    pallas_call x3 -> x4, Pallas kernels: 32.2 us -> 36.1 us  [the longest x1 14.2 us: attend_begin(): pl.pallas_call(begin_kernel, out_shape=[jax.ShapeDtypeStruct((2, rows, HC...]
    ppermute x8, starting transfers between devices: 18 us -> 21.5 us  [to_plane(): return lax.ppermute(x, seq, pairs)]
    slice x0 -> x1, local copies, waits for them, and re-layouts: none -> 1.83 us  [on_device(): direct_strip = gather(after(out_weight[:, :direct], *late))]
    ppermute x0 -> x2, starting transfers between devices: none -> 1.78 us  [the longest x1 1.77 us: on_device(): lax.ppermute(sent, 'groups', [(g, (g + dx) % groups) for g in range(group...]
    dynamic_slice x0 -> x1, local copies, waits for them, and re-layouts: none -> 1.51 us  [on_device(): sent = lax.dynamic_slice_in_dim(own_strip, core_at, half, 1)]
  transfers between devices with their start and end apart: 18 -> 21, of which waited for: 8 -> 8; matrix products, arithmetic and copies ran while one was open for 0% -> 1% of each run, Pallas kernels for 21% -> 23%
where the time goes in v5:
time: 148 us; the launch traced here: 147 us
  waiting for transfers between devices  52.4 us (35%)
  Pallas kernels  41.6 us (28%)
  starting transfers between devices  32.9 us (22%)
  between operations  13.7 us (9%)
  local copies, waits for them, and re-layouts  6.32 us (4%)
    ppermute x9, waiting for transfers between devices, to_lane(): lax.ppermute(x, seq, [(index(p, r, c), index(p, r ^ dr, c ^ dc)) for p, r...  32.3 us
    ppermute x8, starting transfers between devices, to_plane(): return lax.ppermute(x, seq, pairs)  21.5 us
    ppermute x1, waiting for transfers between devices, on_device(): lax.ppermute(sent, 'groups', [(g, (g + dx) % groups) for g in range(group...  19.3 us
    pallas_call x1, Pallas kernels, attend_begin(): pl.pallas_call(begin_kernel, out_shape=[jax.ShapeDtypeStruct((2, rows, HC...  14.2 us
    pallas_call x2, Pallas kernels, attend_finish(): pl.pallas_call(lambda *refs: finish_kernel(group, *refs), out_shape=[jax....  13.5 us
    ppermute x9, starting transfers between devices, to_lane(): lax.ppermute(x, seq, [(index(p, r, c), index(p, r ^ dr, c ^ dc)) for p, r...  9.51 us
    pallas_call x1, Pallas kernels, project(): pl.pallas_call(lambda *refs: project_kernel(order, groups, refs[:LANES],...  8.33 us
    pallas_call x2, Pallas kernels, pack(): pl.pallas_call(kernel, out_shape=[jax.ShapeDtypeStruct((count, width), jn...  5.54 us
  transfers between devices with their start and end apart: 21, of which 8 were waited for; matrix products, arithmetic and copies ran while one was open for 1% of the time, Pallas kernels for 23%

profile of v5, /device:TPU:0, one launch (start us, length us, event | category | flops | bytes accessed | tf_op | source)
XLA Modules:
  0.0 146.9 jit_solution(8843586812472971876)
XLA Ops:
  6.5 1.8 %fusion = (bf16[96,1024]{1,0:T(8,128)(2,1)}, bf16[96,1024]{1,0:T(8,128)(2,1)}) fusion(bf16[96,3072]{1,0:T(8,128)(2,1)} %param.11, s32[]{:T(128)S(6)} %select_n.6), kind=kLoop, calls=%fused_computation.2 | loop fusion | bytes 786436 | tf_op jit(solution)/shard_map/slice | solution.py:361
  8.4 3.1 %shard_map.64 = (bf16[256,768]{1,0:T(8,128)(2,1)}, bf16[256,768]{1,0:T(8,128)(2,1)}, bf16[256,768]{1,0:T(8,128)(2,1)}, bf16[256,768]{1,0:T(8,128)(2,1)}) custom-call(s32[2]{0:T(128)} %frames.3, bf16[256,1536]{1,0:T(8,128)(2,1)} %k_ref.1, bf16[256,1536]{1,0:T(8,128)(2,1)} %v_ref.1), custom_call_target="tpu_custom_call" | custom-call | tf_op jit(solution)/shard_map/pallas_call | solution.py:69
  11.5 3.0 %collective-permute-start = (bf16[256,768]{1,0:T(8,128)(2,1)}, bf16[256,768]{1,0:T(8,128)(2,1)}, u32[]{:S(2)}, u32[]{:S(2)}) collective-permute-start(bf16[256,768]{1,0:T(8,128)(2,1)} %get-tuple-element.34), channel_id=1, source_target_pairs={{0,2},{1,3},{2,0},{3,1},{4,6},{5,7},{6,4},{7,5},{8,10},{9,11},{10,... | collective-permute-start | bytes 1179656 | tf_op jit(solution)/shard_map/ppermute | solution.py:321
  14.5 3.5 %collective-permute-start.4 = (bf16[256,768]{1,0:T(8,128)(2,1)}, bf16[256,768]{1,0:T(8,128)(2,1)S(1)}, u32[]{:S(2)}, u32[]{:S(2)}) collective-permute-start(bf16[256,768]{1,0:T(8,128)(2,1)} %get-tuple-element.41.refs_4_), channel_id=1, source_target_pairs={{0,4},{1,5},{2,6},{3,7},{4,8},{5,9},{6,10},{7,11},{8,12},{9,13},{1... | collective-permute-start | bytes 1179656 | tf_op jit(solution)/shard_map/ppermute | solution.py:327
  19.3 4.2 %collective-permute-start.6 = (bf16[256,768]{1,0:T(8,128)(2,1)}, bf16[256,768]{1,0:T(8,128)(2,1)S(1)}, u32[]{:S(2)}, u32[]{:S(2)}) collective-permute-start(bf16[256,768]{1,0:T(8,128)(2,1)} %get-tuple-element.42), channel_id=1, source_target_pairs={{0,5},{1,4},{2,7},{3,6},{4,9},{5,8},{6,11},{7,10},{8,13},{9,12},{1... | collective-permute-start | bytes 1179656 | tf_op jit(solution)/shard_map/ppermute | solution.py:327
  23.5 6.9 %collective-permute-done.refs_6_ = bf16[256,768]{1,0:T(8,128)(2,1)} collective-permute-done((bf16[256,768]{1,0:T(8,128)(2,1)}, bf16[256,768]{1,0:T(8,128)(2,1)}, u32[]{:S(2)}, u32[]{:S(2)}) %collective-permute-start) | collective-permute-done | bytes 393248 | tf_op jit(solution)/shard_map/ppermute | solution.py:321
  31.7 13.4 %collective-permute-done.1.refs_7_ = bf16[256,768]{1,0:T(8,128)(2,1)} collective-permute-done((bf16[256,768]{1,0:T(8,128)(2,1)}, bf16[256,768]{1,0:T(8,128)(2,1)}, u32[]{:S(2)}, u32[]{:S(2)}) %collective-permute-start.1) | collective-permute-done | bytes 393248 | tf_op jit(solution)/shard_map/ppermute | solution.py:321
  45.1 2.5 %shard_map.65 = (bf16[256,384]{1,0:T(8,128)(2,1)}, bf16[256,384]{1,0:T(8,128)(2,1)}, bf16[256,384]{1,0:T(8,128)(2,1)}, bf16[256,384]{1,0:T(8,128)(2,1)}) custom-call(s32[2]{0:T(128)} %frames.3, bf16[256,1536]{1,0:T(8,128)(2,1)} %q_ref), custom_call_target="tpu_custom_call" | custom-call | tf_op jit(solution)/shard_map/pallas_call | solution.py:69
  48.1 2.2 %collective-permute-start.3 = (bf16[256,384]{1,0:T(8,128)(2,1)}, bf16[256,384]{1,0:T(8,128)(2,1)S(1)}, u32[]{:S(2)}, u32[]{:S(2)}) collective-permute-start(bf16[256,384]{1,0:T(8,128)(2,1)} %get-tuple-element.40), channel_id=1, source_target_pairs={{0,3},{1,2},{2,1},{3,0},{4,7},{5,6},{6,5},{7,4},{8,11},{9,10},{10,... | collective-permute-start | bytes 589832 | tf_op jit(solution)/shard_map/ppermute | solution.py:321
  53.6 4.6 %collective-permute-start.11 = (bf16[256,768]{1,0:T(8,128)(2,1)}, bf16[256,768]{1,0:T(8,128)(2,1)S(1)}, u32[]{:S(2)}, u32[]{:S(2)}) collective-permute-start(bf16[256,768]{1,0:T(8,128)(2,1)} %collective-permute-done.1.refs_7_), channel_id=1, source_target_pairs={{0,4},{1,5},{2,6},{3,7},{4,8},{5,9},{6,10},{7,11},{8,12},{9,13},{1... | collective-permute-start | bytes 1179656 | tf_op jit(solution)/shard_map/ppermute | solution.py:327
  58.2 4.1 %collective-permute-start.10 = (bf16[256,768]{1,0:T(8,128)(2,1)}, bf16[256,768]{1,0:T(8,128)(2,1)S(1)}, u32[]{:S(2)}, u32[]{:S(2)}) collective-permute-start(bf16[256,768]{1,0:T(8,128)(2,1)} %collective-permute-done.refs_6_), channel_id=1, source_target_pairs={{0,4},{1,5},{2,6},{3,7},{4,8},{5,9},{6,10},{7,11},{8,12},{9,13},{1... | collective-permute-start | bytes 1179656 | tf_op jit(solution)/shard_map/ppermute | solution.py:327
  62.4 1.6 %collective-permute-start.2 = (bf16[256,384]{1,0:T(8,128)(2,1)}, bf16[256,384]{1,0:T(8,128)(2,1)S(1)}, u32[]{:S(2)}, u32[]{:S(2)}) collective-permute-start(bf16[256,384]{1,0:T(8,128)(2,1)} %get-tuple-element.38), channel_id=1, source_target_pairs={{0,2},{1,3},{2,0},{3,1},{4,6},{5,7},{6,4},{7,5},{8,10},{9,11},{10,... | collective-permute-start | bytes 589832 | tf_op jit(solution)/shard_map/ppermute | solution.py:321
  63.9 1.5 %constant_dynamic-slice_fusion = bf16[1536,512]{1,0:T(8,128)(2,1)S(1)} fusion(bf16[1536,1024]{1,0:T(8,128)(2,1)} %all-gather.3.cloned.1.call-done.refs_5_, s32[]{:T(128)S(6)} %select_n.7), kind=kLoop, calls=%fused_computation | loop fusion | bytes 3145732 | tf_op jit(solution)/shard_map/dynamic_slice | solution.py:352
  65.5 3.1 %collective-permute-done.2.refs_2_.refs_1_ = bf16[256,384]{1,0:T(8,128)(2,1)S(1)} collective-permute-done((bf16[256,384]{1,0:T(8,128)(2,1)}, bf16[256,384]{1,0:T(8,128)(2,1)S(1)}, u32[]{:S(2)}, u32[]{:S(2)}) %collective-permute-start.2) | collective-permute-done | bytes 196640 | tf_op jit(solution)/shard_map/ppermute | solution.py:321
  69.2 14.2 %shard_map.66 = (f32[2,256,384]{2,1,0:T(8,128)}, f32[2,256,384]{2,1,0:T(8,128)}, f32[2,256,128]{2,1,0:T(8,128)}, f32[2,256,128]{2,1,0:T(8,128)}) custom-call(s32[32,32]{1,0:T(8,128)} %refs_0_.2, bf16[256,384]{1,0:T(8,128)(2,1)} %get-tuple-element.45.refs_0_.refs_1_, bf16[256,384]{1,0:T(8,128)(2,1)} %copy-done.6, bf16[256,384]{1,0:T(8,128)(2,1)} %copy-done.8, ...), custom_call_target="tpu_custom_call" | custom-call | tf_op jit(solution)/shard_map/pallas_call | solution.py:218
  84.6 1.8 %collective-permute-start.17 = (bf16[1536,512]{1,0:T(8,128)(2,1)S(1)}, bf16[1536,512]{1,0:T(8,128)(2,1)S(1)}, u32[]{:S(2)}, u32[]{:S(2)}) collective-permute-start(bf16[1536,512]{1,0:T(8,128)(2,1)S(1)} %constant_dynamic-slice_fusion), channel_id=1, source_target_pairs={{0,16},{16,0},{1,17},{17,1},{2,18},{18,2},{3,19},{19,3},{4,20},{20... | collective-permute-start | bytes 4718600 | tf_op jit(solution)/shard_map/ppermute | solution.py:354
  86.4 7.0 %shard_map.67 = (bf16[256,384]{1,0:T(8,128)(2,1)}, bf16[256,384]{1,0:T(8,128)(2,1)}) custom-call(s32[32,32]{1,0:T(8,128)} %refs_0_.2, bf16[256,384]{1,0:T(8,128)(2,1)} %copy-done.8, bf16[256,384]{1,0:T(8,128)(2,1)} %copy-done.7, f32[2,256,384]{2,1,0:T(8,128)} %get-tuple-element.48.refs_3_, f32[2,256,128]{2,1,0:T(8,128)} %get-tuple-element.49.refs_4_, ...), custom_call_target="tpu_custom_call" | custom-call | tf_op jit(solution)/shard_map/pallas_call | solution.py:239
  93.5 6.4 %shard_map.68 = (bf16[256,384]{1,0:T(8,128)(2,1)}, bf16[256,384]{1,0:T(8,128)(2,1)}) custom-call(s32[32,32]{1,0:T(8,128)} %refs_0_.2, bf16[256,384]{1,0:T(8,128)(2,1)} %get-tuple-element.45.refs_0_.refs_1_, bf16[256,384]{1,0:T(8,128)(2,1)} %copy-done.6, f32[2,256,384]{2,1,0:T(8,128)} %get-tuple-element.50.refs_3_, f32[2,256,128]{2,1,0:T(8,128)} %get-tuple-element.57.refs_4_, ...), custom_call_target="tpu_custom_call" | custom-call | tf_op jit(solution)/shard_map/pallas_call | solution.py:239
  99.9 19.3 %collective-permute-done.17.refs_6_ = bf16[1536,512]{1,0:T(8,128)(2,1)S(1)} collective-permute-done((bf16[1536,512]{1,0:T(8,128)(2,1)S(1)}, bf16[1536,512]{1,0:T(8,128)(2,1)S(1)}, u32[]{:S(2)}, u32[]{:S(2)}) %collective-permute-start.17) | collective-permute-done | bytes 1572896 | tf_op jit(solution)/shard_map/ppermute | solution.py:354
  119.3 1.8 %collective-permute-start.15 = (bf16[256,384]{1,0:T(8,128)(2,1)S(1)}, bf16[256,384]{1,0:T(8,128)(2,1)S(1)}, u32[]{:S(2)}, u32[]{:S(2)}) collective-permute-start(bf16[256,384]{1,0:T(8,128)(2,1)S(1)} %copy-done.16), channel_id=1, source_target_pairs={{0,2},{1,3},{2,0},{3,1},{4,6},{5,7},{6,4},{7,5},{8,10},{9,11},{10,... | collective-permute-start | bytes 589832 | tf_op jit(solution)/shard_map/ppermute | solution.py:321
  121.5 1.7 %collective-permute-done.14.refs_1_ = bf16[256,384]{1,0:T(8,128)(2,1)S(1)} collective-permute-done((bf16[256,384]{1,0:T(8,128)(2,1)}, bf16[256,384]{1,0:T(8,128)(2,1)S(1)}, u32[]{:S(2)}, u32[]{:S(2)}) %collective-permute-start.14) | collective-permute-done | bytes 196640 | tf_op jit(solution)/shard_map/ppermute | solution.py:321
  123.2 3.9 %collective-permute-done.15.refs_2_ = bf16[256,384]{1,0:T(8,128)(2,1)S(1)} collective-permute-done((bf16[256,384]{1,0:T(8,128)(2,1)S(1)}, bf16[256,384]{1,0:T(8,128)(2,1)S(1)}, u32[]{:S(2)}, u32[]{:S(2)}) %collective-permute-start.15) | collective-permute-done | bytes 196640 | tf_op jit(solution)/shard_map/ppermute | solution.py:321
  127.1 3.5 %collective-permute-done.16.refs_3_ = bf16[256,384]{1,0:T(8,128)(2,1)} collective-permute-done((bf16[256,384]{1,0:T(8,128)(2,1)S(1)}, bf16[256,384]{1,0:T(8,128)(2,1)}, u32[]{:S(2)}, u32[]{:S(2)}) %collective-permute-start.16) | collective-permute-done | bytes 196640 | tf_op jit(solution)/shard_map/ppermute | solution.py:321
  131.7 8.3 %shard_map.69 = bf16[256,3072]{1,0:T(8,128)(2,1)} custom-call(bf16[256,384]{1,0:T(8,128)(2,1)} %get-tuple-element.58.refs_0_, bf16[256,384]{1,0:T(8,128)(2,1)} %copy-done.14, bf16[256,384]{1,0:T(8,128)(2,1)} %copy-done.13, bf16[256,384]{1,0:T(8,128)(2,1)} %collective-permute-done.16.refs_3_, bf16[1536,1024]{1,0:T(8,128)(2,1)} %all-gather.5.cloned.1.call-done.refs_4_, ...), custom_call_target="tpu_custom_call" | custom-call | tf_op jit(solution)/shard_map/pallas_call | solution.py:291
  (62 shorter events, 9.8 us)
Async XLA Ops:
  6.5 55.8 %all-gather.3.cloned.1.call-start = ((), (), s32[]{:S(2)}) async-start(), calls=%async_computation | async-start | bytes 3342336 | tf_op jit(solution)/shard_map/all_gather | solution.py:333
  8.4 122.1 %all-gather.5.cloned.1.call-start = ((), (), s32[]{:S(2)}) async-start(), calls=%async_computation.1 | async-start | bytes 3342336 | tf_op jit(solution)/shard_map/all_gather | solution.py:333
  11.5 18.9 %collective-permute-start = (bf16[256,768]{1,0:T(8,128)(2,1)}, bf16[256,768]{1,0:T(8,128)(2,1)}, u32[]{:S(2)}, u32[]{:S(2)}) collective-permute-start(bf16[256,768]{1,0:T(8,128)(2,1)} %get-tuple-element.34), channel_id=1, source_target_pairs={{0,2},{1,3},{2,0},{3,1},{4,6},{5,7},{6,4},{7,5},{8,10},{9,11},{10,... | collective-permute-start | bytes 1179656 | tf_op jit(solution)/shard_map/ppermute | solution.py:321
  14.5 30.6 %collective-permute-start.1 = (bf16[256,768]{1,0:T(8,128)(2,1)}, bf16[256,768]{1,0:T(8,128)(2,1)}, u32[]{:S(2)}, u32[]{:S(2)}) collective-permute-start(bf16[256,768]{1,0:T(8,128)(2,1)} %get-tuple-element.37), channel_id=1, source_target_pairs={{0,3},{1,2},{2,1},{3,0},{4,7},{5,6},{6,5},{7,4},{8,11},{9,10},{10,... | collective-permute-start | bytes 1179656 | tf_op jit(solution)/shard_map/ppermute | solution.py:321
  14.5 33.0 %collective-permute-start.4 = (bf16[256,768]{1,0:T(8,128)(2,1)}, bf16[256,768]{1,0:T(8,128)(2,1)S(1)}, u32[]{:S(2)}, u32[]{:S(2)}) collective-permute-start(bf16[256,768]{1,0:T(8,128)(2,1)} %get-tuple-element.41.refs_4_), channel_id=1, source_target_pairs={{0,4},{1,5},{2,6},{3,7},{4,8},{5,9},{6,10},{7,11},{8,12},{9,13},{1... | collective-permute-start | bytes 1179656 | tf_op jit(solution)/shard_map/ppermute | solution.py:327
  18.0 30.1 %collective-permute-start.5 = (bf16[256,768]{1,0:T(8,128)(2,1)}, bf16[256,768]{1,0:T(8,128)(2,1)S(1)}, u32[]{:S(2)}, u32[]{:S(2)}) collective-permute-start(bf16[256,768]{1,0:T(8,128)(2,1)} %get-tuple-element.41.refs_4_), channel_id=1, source_target_pairs={{4,0},{5,1},{6,2},{7,3},{8,4},{9,5},{10,6},{11,7},{12,8},{13,9},{1... | collective-permute-start | bytes 1179656 | tf_op jit(solution)/shard_map/ppermute | solution.py:327
  19.3 31.0 %collective-permute-start.6 = (bf16[256,768]{1,0:T(8,128)(2,1)}, bf16[256,768]{1,0:T(8,128)(2,1)S(1)}, u32[]{:S(2)}, u32[]{:S(2)}) collective-permute-start(bf16[256,768]{1,0:T(8,128)(2,1)} %get-tuple-element.42), channel_id=1, source_target_pairs={{0,5},{1,4},{2,7},{3,6},{4,9},{5,8},{6,11},{7,10},{8,13},{9,12},{1... | collective-permute-start | bytes 1179656 | tf_op jit(solution)/shard_map/ppermute | solution.py:327
  30.4 21.9 %collective-permute-start.7 = (bf16[256,768]{1,0:T(8,128)(2,1)}, bf16[256,768]{1,0:T(8,128)(2,1)S(1)}, u32[]{:S(2)}, u32[]{:S(2)}) collective-permute-start(bf16[256,768]{1,0:T(8,128)(2,1)} %get-tuple-element.42), channel_id=1, source_target_pairs={{4,1},{5,0},{6,3},{7,2},{8,5},{9,4},{10,7},{11,6},{12,9},{13,8},{1... | collective-permute-start | bytes 1179656 | tf_op jit(solution)/shard_map/ppermute | solution.py:327
  45.1 8.5 %collective-permute-start.9 = (bf16[256,768]{1,0:T(8,128)(2,1)}, bf16[256,768]{1,0:T(8,128)(2,1)}, u32[]{:S(2)}, u32[]{:S(2)}) collective-permute-start(bf16[256,768]{1,0:T(8,128)(2,1)} %get-tuple-element.42), channel_id=1, source_target_pairs={{0,1},{1,0},{2,3},{3,2},{4,5},{5,4},{6,7},{7,6},{8,9},{9,8},{10,11... | collective-permute-start | bytes 1179656 | tf_op jit(solution)/shard_map/ppermute | solution.py:321
  47.5 10.6 %collective-permute-start.8 = (bf16[256,384]{1,0:T(8,128)(2,1)}, bf16[256,384]{1,0:T(8,128)(2,1)S(1)}, u32[]{:S(2)}, u32[]{:S(2)}) collective-permute-start(bf16[256,384]{1,0:T(8,128)(2,1)} %get-tuple-element.47), channel_id=1, source_target_pairs={{0,1},{1,0},{2,3},{3,2},{4,5},{5,4},{6,7},{7,6},{8,9},{9,8},{10,11... | collective-permute-start | bytes 589832 | tf_op jit(solution)/shard_map/ppermute | solution.py:321
  48.1 14.3 %collective-permute-start.3 = (bf16[256,384]{1,0:T(8,128)(2,1)}, bf16[256,384]{1,0:T(8,128)(2,1)S(1)}, u32[]{:S(2)}, u32[]{:S(2)}) collective-permute-start(bf16[256,384]{1,0:T(8,128)(2,1)} %get-tuple-element.40), channel_id=1, source_target_pairs={{0,3},{1,2},{2,1},{3,0},{4,7},{5,6},{6,5},{7,4},{8,11},{9,10},{10,... | collective-permute-start | bytes 589832 | tf_op jit(solution)/shard_map/ppermute | solution.py:321
  50.3 33.1 %collective-permute-start.13 = (bf16[256,768]{1,0:T(8,128)(2,1)}, bf16[256,768]{1,0:T(8,128)(2,1)S(1)}, u32[]{:S(2)}, u32[]{:S(2)}) collective-permute-start(bf16[256,768]{1,0:T(8,128)(2,1)} %collective-permute-done.1.refs_7_), channel_id=1, source_target_pairs={{4,0},{5,1},{6,2},{7,3},{8,4},{9,5},{10,6},{11,7},{12,8},{13,9},{1... | collective-permute-start | bytes 1179656 | tf_op jit(solution)/shard_map/ppermute | solution.py:327
  52.3 31.2 %collective-permute-start.12 = (bf16[256,768]{1,0:T(8,128)(2,1)}, bf16[256,768]{1,0:T(8,128)(2,1)S(1)}, u32[]{:S(2)}, u32[]{:S(2)}) collective-permute-start(bf16[256,768]{1,0:T(8,128)(2,1)} %collective-permute-done.refs_6_), channel_id=1, source_target_pairs={{4,0},{5,1},{6,2},{7,3},{8,4},{9,5},{10,6},{11,7},{12,8},{13,9},{1... | collective-permute-start | bytes 1179656 | tf_op jit(solution)/shard_map/ppermute | solution.py:327
  53.6 29.9 %collective-permute-start.11 = (bf16[256,768]{1,0:T(8,128)(2,1)}, bf16[256,768]{1,0:T(8,128)(2,1)S(1)}, u32[]{:S(2)}, u32[]{:S(2)}) collective-permute-start(bf16[256,768]{1,0:T(8,128)(2,1)} %collective-permute-done.1.refs_7_), channel_id=1, source_target_pairs={{0,4},{1,5},{2,6},{3,7},{4,8},{5,9},{6,10},{7,11},{8,12},{9,13},{1... | collective-permute-start | bytes 1179656 | tf_op jit(solution)/shard_map/ppermute | solution.py:327
  58.2 25.3 %collective-permute-start.10 = (bf16[256,768]{1,0:T(8,128)(2,1)}, bf16[256,768]{1,0:T(8,128)(2,1)S(1)}, u32[]{:S(2)}, u32[]{:S(2)}) collective-permute-start(bf16[256,768]{1,0:T(8,128)(2,1)} %collective-permute-done.refs_6_), channel_id=1, source_target_pairs={{0,4},{1,5},{2,6},{3,7},{4,8},{5,9},{6,10},{7,11},{8,12},{9,13},{1... | collective-permute-start | bytes 1179656 | tf_op jit(solution)/shard_map/ppermute | solution.py:327
  62.4 6.2 %collective-permute-start.2 = (bf16[256,384]{1,0:T(8,128)(2,1)}, bf16[256,384]{1,0:T(8,128)(2,1)S(1)}, u32[]{:S(2)}, u32[]{:S(2)}) collective-permute-start(bf16[256,384]{1,0:T(8,128)(2,1)} %get-tuple-element.38), channel_id=1, source_target_pairs={{0,2},{1,3},{2,0},{3,1},{4,6},{5,7},{6,4},{7,5},{8,10},{9,11},{10,... | collective-permute-start | bytes 589832 | tf_op jit(solution)/shard_map/ppermute | solution.py:321
  84.6 34.7 %collective-permute-start.17 = (bf16[1536,512]{1,0:T(8,128)(2,1)S(1)}, bf16[1536,512]{1,0:T(8,128)(2,1)S(1)}, u32[]{:S(2)}, u32[]{:S(2)}) collective-permute-start(bf16[1536,512]{1,0:T(8,128)(2,1)S(1)} %constant_dynamic-slice_fusion), channel_id=1, source_target_pairs={{0,16},{16,0},{1,17},{17,1},{2,18},{18,2},{3,19},{19,3},{4,20},{20... | collective-permute-start | bytes 4718600 | tf_op jit(solution)/shard_map/ppermute | solution.py:354
  93.4 25.8 %copy-start.16 = (bf16[256,384]{1,0:T(8,128)(2,1)S(1)}, bf16[256,384]{1,0:T(8,128)(2,1)}, u32[]{:S(2)}) copy-start(bf16[256,384]{1,0:T(8,128)(2,1)} %get-tuple-element.55) | copy-start | bytes 589828
  93.5 27.8 %copy-start.15 = (bf16[256,384]{1,0:T(8,128)(2,1)S(1)}, bf16[256,384]{1,0:T(8,128)(2,1)}, u32[]{:S(2)}) copy-start(bf16[256,384]{1,0:T(8,128)(2,1)} %get-tuple-element.60) | copy-start | bytes 589828
  119.3 11.3 %copy-start = (bf16[1536,512]{1,0:T(8,128)(2,1)}, bf16[1536,512]{1,0:T(8,128)(2,1)S(1)}, u32[]{:S(2)}) copy-start(bf16[1536,512]{1,0:T(8,128)(2,1)S(1)} %collective-permute-done.17.refs_6_) | copy-start | bytes 4718596
  119.3 11.2 %collective-permute-start.18 = (bf16[1536,512]{1,0:T(8,128)(2,1)S(1)}, bf16[1536,512]{1,0:T(8,128)(2,1)S(1)}, u32[]{:S(2)}, u32[]{:S(2)}) collective-permute-start(bf16[1536,512]{1,0:T(8,128)(2,1)S(1)} %collective-permute-done.17.refs_6_), channel_id=1, source_target_pairs={{0,1},{1,0},{2,3},{3,2},{4,5},{5,4},{6,7},{7,6},{8,9},{9,8},{10,11... | collective-permute-start | bytes 4718600 | tf_op jit(solution)/shard_map/ppermute | solution.py:369
  119.3 7.8 %collective-permute-start.15 = (bf16[256,384]{1,0:T(8,128)(2,1)S(1)}, bf16[256,384]{1,0:T(8,128)(2,1)S(1)}, u32[]{:S(2)}, u32[]{:S(2)}) collective-permute-start(bf16[256,384]{1,0:T(8,128)(2,1)S(1)} %copy-done.16), channel_id=1, source_target_pairs={{0,2},{1,3},{2,0},{3,1},{4,6},{5,7},{6,4},{7,5},{8,10},{9,11},{10,... | collective-permute-start | bytes 589832 | tf_op jit(solution)/shard_map/ppermute | solution.py:321
  121.1 2.0 %collective-permute-start.14 = (bf16[256,384]{1,0:T(8,128)(2,1)}, bf16[256,384]{1,0:T(8,128)(2,1)S(1)}, u32[]{:S(2)}, u32[]{:S(2)}) collective-permute-start(bf16[256,384]{1,0:T(8,128)(2,1)} %get-tuple-element.59), channel_id=1, source_target_pairs={{0,1},{1,0},{2,3},{3,2},{4,5},{5,4},{6,7},{7,6},{8,9},{9,8},{10,11... | collective-permute-start | bytes 589832 | tf_op jit(solution)/shard_map/ppermute | solution.py:321
  121.3 9.2 %collective-permute-start.16 = (bf16[256,384]{1,0:T(8,128)(2,1)S(1)}, bf16[256,384]{1,0:T(8,128)(2,1)}, u32[]{:S(2)}, u32[]{:S(2)}) collective-permute-start(bf16[256,384]{1,0:T(8,128)(2,1)S(1)} %copy-done.15), channel_id=1, source_target_pairs={{0,3},{1,2},{2,1},{3,0},{4,7},{5,6},{6,5},{7,4},{8,11},{9,10},{10,... | collective-permute-start | bytes 589832 | tf_op jit(solution)/shard_map/ppermute | solution.py:321
  (14 other events, 63.4 us)
Sparse Core Ops, SparseCore 0:
  8.9 43.0 all-gather.2
  84.7 32.7 all-gather.4

commit v6 on v5

--- a/solution.py
+++ b/solution.py
@@ -17,6 +17,7 @@
 HC = HL * HDIM
 REACH = 4
 NEG = -1e30
+BRIEF = pl.CostEstimate(flops=1024, bytes_accessed=1024, transcendentals=0)
 TO_EXP2 = math.log2(math.e) / math.sqrt(HDIM)
 
 
@@ -185,9 +186,12 @@
     return [first, first + 1]
 
 
-def finish_kernel(group, mask, q_a, q_b, acc, stat, *refs):
-    kv_refs, o_refs, (kv, scores, weights, sems) = refs[:LANES], refs[LANES : LANES + 2], refs[LANES + 2 :]
-    rows = q_a.shape[0]
+def finish_kernel(steps, mask, *refs):
+    count = len(steps)
+    q_refs, accs, stats = refs[:count], refs[count : 2 * count], refs[2 * count : 3 * count]
+    kv_refs, o_refs = refs[3 * count : 3 * count + LANES], refs[3 * count + LANES : 4 * count + LANES]
+    kv, scores, weights, sems = refs[4 * count + LANES :]
+    rows = q_refs[0].shape[0]
     per_dev = rows // BLK
     plane = lax.axis_index("plane")
     places = [part * LANES + lane_of(step) for part in (0, 2) for step in (2, 3)]
@@ -198,15 +202,15 @@
         ],
         sems,
     )
-    for core, (q_ref, o_ref) in enumerate(zip((q_a, q_b), o_refs)):
-        tile = lane_of(2 * group + core)
+    for step, q_ref, acc, stat, o_ref in zip(steps, q_refs, accs, stats, o_refs):
+        tile = lane_of(step)
         me = plane * LANES + tile
-        devices = chunk_devices_at(group, tile, True)
+        devices = chunk_devices_at(step // 2, tile, True)
         starts = [pl.multiple_of((d - (plane - 1) * LANES) * rows, BLK) for d in devices]
         biases = biases_of(mask, me, devices, per_dev)
         for h in range(HL):
             cols = slice(h * HDIM, (h + 1) * HDIM)
-            state = (stat[core, :, h : h + 1], stat[core, :, HL + h : HL + h + 1], acc[core, :, cols])
+            state = (stat[0, :, h : h + 1], stat[0, :, HL + h : HL + h + 1], acc[0, :, cols])
             _, total, mixed = attend_head(h, q_ref[:, cols], kv, starts, biases, scores, weights, state)
             o_ref[:, cols] = (mixed / total).astype(jnp.bfloat16)
 
@@ -229,20 +233,28 @@
             pltpu.SemaphoreType.DMA((3 * LANES,)),
         ],
         compiler_params=pltpu.CompilerParams(vmem_limit_bytes=56 * 1024 * 1024),
+        cost_estimate=BRIEF,
     )(mask, *q, *kv)
 
 
-def attend_finish(group, mask, q, acc, stat, kv):
+def attend_finish(steps, mask, q, begun, kv):
     rows = kv[0].shape[0]
     span = 3 * rows
     vmem = pl.BlockSpec(memory_space=pltpu.VMEM)
+
+    def of_tile(step, width):
+        return pl.BlockSpec((1, rows, width), lambda i, step=step: (step % 2, 0, 0))
+
     return pl.pallas_call(
-        lambda *refs: finish_kernel(group, *refs),
-        out_shape=[jax.ShapeDtypeStruct((rows, HC), jnp.bfloat16)] * 2,
+        lambda *refs: finish_kernel(steps, *refs),
+        grid=(1,),
+        out_shape=[jax.ShapeDtypeStruct((rows, HC), jnp.bfloat16)] * len(steps),
         in_specs=[pl.BlockSpec(memory_space=pltpu.SMEM)]
-        + [vmem] * 4
+        + [vmem] * len(steps)
+        + [of_tile(step, HC) for step in steps]
+        + [of_tile(step, HDIM) for step in steps]
         + [pl.BlockSpec(memory_space=pl.ANY)] * LANES,
-        out_specs=[vmem] * 2,
+        out_specs=[vmem] * len(steps),
         scratch_shapes=[
             pltpu.VMEM((3 * LANES * rows, 2 * HC), jnp.bfloat16),
             pltpu.VMEM((HL, rows, span), jnp.float32),
@@ -250,7 +262,14 @@
             pltpu.SemaphoreType.DMA((LANES,)),
         ],
         compiler_params=pltpu.CompilerParams(vmem_limit_bytes=56 * 1024 * 1024),
-    )(mask, *q, acc, stat, *kv)
+        cost_estimate=BRIEF,
+    )(
+        mask,
+        *[q[step] for step in steps],
+        *[begun[step // 2] for step in steps],
+        *[begun[2 + step // 2] for step in steps],
+        *kv,
+    )
 
 
 def project_kernel(order, groups, a_refs, w_refs, o_ref, by_lane, by_shard):
@@ -339,14 +358,16 @@
     own_strip = gather(lax.dynamic_slice_in_dim(out_weight, strip_at, strip, 1))
 
     kv = pack(pack_kv_kernel, frame_index, (keys, values), 2 * HC)
+    direct_strip = gather(after(out_weight, kv[0])[:, :direct])
     across = [to_lane(kv[2], 1, 0), to_lane(kv[3], 1, 1)]
     early = {(dp, dc): to_plane(kv[dc], dp, dc) for dc in range(2) for dp in (1, -1)}
     here = [kv[0], to_lane(kv[1], 0, 1)] + across
     q = pack(pack_q_kernel, frame_index, (after(queries, across[0]),), HC)
-    late = {(dp, dc): to_plane(across[dc], dp, 0) for dc in range(2) for dp in (1, -1)}
+    onward = [after(x, *early.values(), here[1]) for x in across]
+    late = {(dp, dc): to_plane(onward[dc], dp, 0) for dc in range(2) for dp in (1, -1)}
     q = [q[0]] + [to_lane(after(q[d], *across), d // 2, d % 2) for d in range(1, LANES)]
 
-    own_strip = after(own_strip, *early.values())
+    own_strip = after(own_strip, *early.values(), q[1])
     half = strip // 2
     core_at = lax.axis_index("core") * half
     sent = lax.dynamic_slice_in_dim(own_strip, core_at, half, 1)
@@ -358,15 +379,16 @@
         after(block_mask, sent), q, here + [early[dp, dc] for dp in (1, -1) for dc in range(2)]
     )
     late = [after(late[dp, dc], begun[0]) for dp in (1, -1) for dc in range(2)]
-    direct_strip = gather(after(out_weight[:, :direct], *late))
-    mixed = attend_finish(1, block_mask, q[2:], begun[1], begun[3], late)
-    back = [to_lane(mixed[d], 1, d) for d in range(2)]
-    mixed = attend_finish(0, after(block_mask, mixed[0]), q[:2], begun[0], begun[2], late)
-    mixed = [mixed[0], to_lane(mixed[1], 0, 1)] + back
+    halves = [after(x, *late) for x in halves]
+    swapped = [lax.ppermute(x, "core", [(0, 1), (1, 0)]) for x in halves]
+    block_mask = after(block_mask, *halves)
+    mixed = attend_finish((2, 3, 1), block_mask, q, begun, late)
+    moved = [to_lane(x, step // 2, step % 2) for x, step in zip(mixed, (2, 3, 1))]
+    own = attend_finish((0,), after(block_mask, mixed[0]), q, begun, late)
+    mixed = [own[0], moved[2], moved[0], moved[1]]
     weights = [direct_strip, own_strip]
-    for x in halves:
-        x = after(x, mixed[0])
-        weights += [x, lax.ppermute(x, "core", [(0, 1), (1, 0)])]
+    for pair in zip(halves, swapped):
+        weights += pair
     return project(mixed, weights, order, groups)
 
 

time: 148 us -> 133 us (0.90)
  starting transfers between devices: 32.9 us -> 24.3 us
  waiting for transfers between devices: 52.4 us -> 45.9 us
    ppermute x1, waiting for transfers between devices: 19.3 us -> 0.01 us  [on_device(): lax.ppermute(sent, 'groups', [(g, (g + dx) % groups) for g in range(group...]
    ppermute x8, waiting for transfers between devices: 0.67 us -> 9.07 us  [to_plane(): return lax.ppermute(x, seq, pairs)]
    ppermute x8, starting transfers between devices: 21.5 us -> 15.7 us  [to_plane(): return lax.ppermute(x, seq, pairs)]
    ppermute x9, waiting for transfers between devices: 32.3 us -> 36.8 us  [to_lane(): lax.ppermute(x, seq, [(index(p, r, c), index(p, r ^ dr, c ^ dc)) for p, r...]
    ppermute x9, starting transfers between devices: 9.51 us -> 7.12 us  [to_lane(): lax.ppermute(x, seq, [(index(p, r, c), index(p, r ^ dr, c ^ dc)) for p, r...]
    dynamic_slice x0 -> x1, local copies, waits for them, and re-layouts: none -> 1.62 us  [on_device(): own_strip = gather(lax.dynamic_slice_in_dim(out_weight, strip_at, strip, 1))]
    unnamed x34 -> x38, local copies, waits for them, and re-layouts: 2.98 us -> 2.66 us
  transfers between devices with their start and end apart: 21 -> 21, of which waited for: 8 -> 11; matrix products, arithmetic and copies ran while one was open for 1% -> 2% of each run, Pallas kernels for 23% -> 25%
where the time goes in v6:
time: 133 us
  waiting for transfers between devices  45.9 us (35%)
  Pallas kernels  41.3 us (31%)
  starting transfers between devices  24.3 us (18%)
  between operations  13.7 us (10%)
  local copies, waits for them, and re-layouts  7.4 us (6%)
    ppermute x9, waiting for transfers between devices, to_lane(): lax.ppermute(x, seq, [(index(p, r, c), index(p, r ^ dr, c ^ dc)) for p, r...  36.8 us
    ppermute x8, starting transfers between devices, to_plane(): return lax.ppermute(x, seq, pairs)  15.7 us
    pallas_call x1, Pallas kernels, attend_begin(): pl.pallas_call(begin_kernel, out_shape=[jax.ShapeDtypeStruct((2, rows, HC...  14.3 us
    pallas_call x2, Pallas kernels, attend_finish(): pl.pallas_call(lambda *refs: finish_kernel(steps, *refs), grid=(1,), out_...  13.1 us
    ppermute x8, waiting for transfers between devices, to_plane(): return lax.ppermute(x, seq, pairs)  9.07 us
    pallas_call x1, Pallas kernels, project(): pl.pallas_call(lambda *refs: project_kernel(order, groups, refs[:LANES],...  8.34 us
    ppermute x9, starting transfers between devices, to_lane(): lax.ppermute(x, seq, [(index(p, r, c), index(p, r ^ dr, c ^ dc)) for p, r...  7.12 us
    pallas_call x2, Pallas kernels, pack(): pl.pallas_call(kernel, out_shape=[jax.ShapeDtypeStruct((count, width), jn...  5.55 us
  transfers between devices with their start and end apart: 21, of which 11 were waited for; matrix products, arithmetic and copies ran while one was open for 2% of the time, Pallas kernels for 25%

profile of v6, /device:TPU:0, one launch (start us, length us, event | category | flops | bytes accessed | tf_op | source)
XLA Modules:
  0.0 132.7 jit_solution(7541985188744656113)
XLA Ops:
  6.5 1.6 %constant_dynamic-slice_fusion.1 = bf16[96,1024]{1,0:T(8,128)(2,1)} fusion(bf16[96,3072]{1,0:T(8,128)(2,1)} %param.11, s32[]{:T(128)S(6)} %select_n.6), kind=kLoop, calls=%fused_computation.1 | loop fusion | bytes 393220 | tf_op jit(solution)/shard_map/dynamic_slice | solution.py:358
  8.2 3.1 %shard_map.64 = (bf16[256,768]{1,0:T(8,128)(2,1)}, bf16[256,768]{1,0:T(8,128)(2,1)}, bf16[256,768]{1,0:T(8,128)(2,1)}, bf16[256,768]{1,0:T(8,128)(2,1)}) custom-call(s32[2]{0:T(128)} %frames.3, bf16[256,1536]{1,0:T(8,128)(2,1)} %k_ref.1, bf16[256,1536]{1,0:T(8,128)(2,1)} %v_ref.1), custom_call_target="tpu_custom_call" | custom-call | tf_op jit(solution)/shard_map/pallas_call | solution.py:70
  11.3 1.6 %slice.3 = bf16[96,1024]{1,0:T(8,128)(2,1)} slice(bf16[96,3072]{1,0:T(8,128)(2,1)} %param.11), slice={[0:96], [0:1024]} | slice | bytes 393216 | tf_op jit(solution)/shard_map/slice | solution.py:361
  12.9 3.0 %collective-permute-start.4 = (bf16[256,768]{1,0:T(8,128)(2,1)}, bf16[256,768]{1,0:T(8,128)(2,1)S(1)}, u32[]{:S(2)}, u32[]{:S(2)}) collective-permute-start(bf16[256,768]{1,0:T(8,128)(2,1)} %get-tuple-element.38), channel_id=1, source_target_pairs={{0,2},{1,3},{2,0},{3,1},{4,6},{5,7},{6,4},{7,5},{8,10},{9,11},{10,... | collective-permute-start | bytes 1179656 | tf_op jit(solution)/shard_map/ppermute | solution.py:340
  16.0 3.5 %collective-permute-start = (bf16[256,768]{1,0:T(8,128)(2,1)}, bf16[256,768]{1,0:T(8,128)(2,1)S(1)}, u32[]{:S(2)}, u32[]{:S(2)}) collective-permute-start(bf16[256,768]{1,0:T(8,128)(2,1)} %get-tuple-element.36.refs_4_), channel_id=1, source_target_pairs={{0,4},{1,5},{2,6},{3,7},{4,8},{5,9},{6,10},{7,11},{8,12},{9,13},{1... | collective-permute-start | bytes 1179656 | tf_op jit(solution)/shard_map/ppermute | solution.py:346
  20.8 4.2 %collective-permute-start.2 = (bf16[256,768]{1,0:T(8,128)(2,1)}, bf16[256,768]{1,0:T(8,128)(2,1)S(1)}, u32[]{:S(2)}, u32[]{:S(2)}) collective-permute-start(bf16[256,768]{1,0:T(8,128)(2,1)} %get-tuple-element.37), channel_id=1, source_target_pairs={{0,5},{1,4},{2,7},{3,6},{4,9},{5,8},{6,11},{7,10},{8,13},{9,12},{1... | collective-permute-start | bytes 1179656 | tf_op jit(solution)/shard_map/ppermute | solution.py:346
  25.0 8.4 %collective-permute-done.4.refs_6_ = bf16[256,768]{1,0:T(8,128)(2,1)S(1)} collective-permute-done((bf16[256,768]{1,0:T(8,128)(2,1)}, bf16[256,768]{1,0:T(8,128)(2,1)S(1)}, u32[]{:S(2)}, u32[]{:S(2)}) %collective-permute-start.4) | collective-permute-done | bytes 393248 | tf_op jit(solution)/shard_map/ppermute | solution.py:340
  34.7 2.5 %shard_map.65 = (bf16[256,384]{1,0:T(8,128)(2,1)}, bf16[256,384]{1,0:T(8,128)(2,1)}, bf16[256,384]{1,0:T(8,128)(2,1)}, bf16[256,384]{1,0:T(8,128)(2,1)}) custom-call(s32[2]{0:T(128)} %frames.3, bf16[256,1536]{1,0:T(8,128)(2,1)} %q_ref), custom_call_target="tpu_custom_call" | custom-call | tf_op jit(solution)/shard_map/pallas_call | solution.py:70
  37.2 10.3 %collective-permute-done.5.refs_7_ = bf16[256,768]{1,0:T(8,128)(2,1)S(1)} collective-permute-done((bf16[256,768]{1,0:T(8,128)(2,1)}, bf16[256,768]{1,0:T(8,128)(2,1)S(1)}, u32[]{:S(2)}, u32[]{:S(2)}) %collective-permute-start.5) | collective-permute-done | bytes 393248 | tf_op jit(solution)/shard_map/ppermute | solution.py:340
  47.9 2.1 %collective-permute-done.2.refs_9_ = bf16[256,768]{1,0:T(8,128)(2,1)S(1)} collective-permute-done((bf16[256,768]{1,0:T(8,128)(2,1)}, bf16[256,768]{1,0:T(8,128)(2,1)S(1)}, u32[]{:S(2)}, u32[]{:S(2)}) %collective-permute-start.2) | collective-permute-done | bytes 393248 | tf_op jit(solution)/shard_map/ppermute | solution.py:346
  50.0 3.2 %collective-permute-done.3.refs_11_ = bf16[256,768]{1,0:T(8,128)(2,1)S(1)} collective-permute-done((bf16[256,768]{1,0:T(8,128)(2,1)}, bf16[256,768]{1,0:T(8,128)(2,1)S(1)}, u32[]{:S(2)}, u32[]{:S(2)}) %collective-permute-start.3) | collective-permute-done | bytes 393248 | tf_op jit(solution)/shard_map/ppermute | solution.py:346
  53.9 1.5 %constant_dynamic-slice_fusion = bf16[1536,512]{1,0:T(8,128)(2,1)S(1)} fusion(bf16[1536,1024]{1,0:T(8,128)(2,1)} %all-gather.3.cloned.1.call-done.refs_5_, s32[]{:T(128)S(6)} %select_n.7), kind=kLoop, calls=%fused_computation | loop fusion | bytes 3145732 | tf_op jit(solution)/shard_map/dynamic_slice | solution.py:373
  55.4 1.5 %collective-permute-start.7 = (bf16[1536,512]{1,0:T(8,128)(2,1)S(1)}, bf16[1536,512]{1,0:T(8,128)(2,1)S(1)}, u32[]{:S(2)}, u32[]{:S(2)}) collective-permute-start(bf16[1536,512]{1,0:T(8,128)(2,1)S(1)} %constant_dynamic-slice_fusion), channel_id=1, source_target_pairs={{0,16},{16,0},{1,17},{17,1},{2,18},{18,2},{3,19},{19,3},{4,20},{20... | collective-permute-start | bytes 4718600 | tf_op jit(solution)/shard_map/ppermute | solution.py:375
  56.9 1.7 %collective-permute-start.10 = (bf16[256,384]{1,0:T(8,128)(2,1)}, bf16[256,384]{1,0:T(8,128)(2,1)S(1)}, u32[]{:S(2)}, u32[]{:S(2)}) collective-permute-start(bf16[256,384]{1,0:T(8,128)(2,1)} %get-tuple-element.48), channel_id=1, source_target_pairs={{0,2},{1,3},{2,0},{3,1},{4,6},{5,7},{6,4},{7,5},{8,10},{9,11},{10,... | collective-permute-start | bytes 589832 | tf_op jit(solution)/shard_map/ppermute | solution.py:340
  61.5 7.0 %collective-permute-done.10.refs_2_.refs_1_ = bf16[256,384]{1,0:T(8,128)(2,1)S(1)} collective-permute-done((bf16[256,384]{1,0:T(8,128)(2,1)}, bf16[256,384]{1,0:T(8,128)(2,1)S(1)}, u32[]{:S(2)}, u32[]{:S(2)}) %collective-permute-start.10) | collective-permute-done | bytes 196640 | tf_op jit(solution)/shard_map/ppermute | solution.py:340
  69.8 6.3 %collective-permute-done.11.refs_3_.refs_2_ = bf16[256,384]{1,0:T(8,128)(2,1)S(1)} collective-permute-done((bf16[256,384]{1,0:T(8,128)(2,1)S(1)}, bf16[256,384]{1,0:T(8,128)(2,1)S(1)}, u32[]{:S(2)}, u32[]{:S(2)}) %collective-permute-start.11) | collective-permute-done | bytes 196640 | tf_op jit(solution)/shard_map/ppermute | solution.py:340
  76.1 1.5 %collective-permute-start.9 = (bf16[256,768]{1,0:T(8,128)(2,1)S(1)}, bf16[256,768]{1,0:T(8,128)(2,1)S(1)}, u32[]{:S(2)}, u32[]{:S(2)}) collective-permute-start(bf16[256,768]{1,0:T(8,128)(2,1)S(1)} %collective-permute-done.4.refs_6_), channel_id=1, source_target_pairs={{0,4},{1,5},{2,6},{3,7},{4,8},{5,9},{6,10},{7,11},{8,12},{9,13},{1... | collective-permute-start | bytes 1179656 | tf_op jit(solution)/shard_map/ppermute | solution.py:346
  77.7 14.3 %shard_map.66 = (f32[2,256,384]{2,1,0:T(8,128)}, f32[2,256,384]{2,1,0:T(8,128)}, f32[2,256,128]{2,1,0:T(8,128)}, f32[2,256,128]{2,1,0:T(8,128)}) custom-call(s32[32,32]{1,0:T(8,128)} %refs_0_.1, bf16[256,384]{1,0:T(8,128)(2,1)} %get-tuple-element.46.refs_0_.refs_1_, bf16[256,384]{1,0:T(8,128)(2,1)} %copy-done.6, bf16[256,384]{1,0:T(8,128)(2,1)} %copy-done.7, ...), custom_call_target="tpu_custom_call" | custom-call | flops 1024 | bytes 1024 | tf_op jit(solution)/shard_map/pallas_call | solution.py:222
  93.1 2.7 %collective-permute-done.9.refs_10_.refs_4_ = bf16[256,768]{1,0:T(8,128)(2,1)S(1)} collective-permute-done((bf16[256,768]{1,0:T(8,128)(2,1)S(1)}, bf16[256,768]{1,0:T(8,128)(2,1)S(1)}, u32[]{:S(2)}, u32[]{:S(2)}) %collective-permute-start.9) | collective-permute-done | bytes 393248 | tf_op jit(solution)/shard_map/ppermute | solution.py:346
  96.5 8.3 %shard_map.67 = (bf16[256,384]{1,0:T(8,128)(2,1)}, bf16[256,384]{1,0:T(8,128)(2,1)}, bf16[256,384]{1,0:T(8,128)(2,1)}) custom-call(s32[32,32]{1,0:T(8,128)} %refs_0_.1, bf16[256,384]{1,0:T(8,128)(2,1)} %copy-done.7, bf16[256,384]{1,0:T(8,128)(2,1)} %copy-done.8, bf16[256,384]{1,0:T(8,128)(2,1)} %copy-done.6, ...), custom_call_target="tpu_custom_call" | custom-call | flops 1024 | bytes 1024 | tf_op jit(solution)/shard_map/pallas_call | solution.py:248
  104.9 1.4 %collective-permute-start.16 = (bf16[256,384]{1,0:T(8,128)(2,1)}, bf16[256,384]{1,0:T(8,128)(2,1)S(1)}, u32[]{:S(2)}, u32[]{:S(2)}) collective-permute-start(bf16[256,384]{1,0:T(8,128)(2,1)} %get-tuple-element.62), channel_id=1, source_target_pairs={{0,2},{1,3},{2,0},{3,1},{4,6},{5,7},{6,4},{7,5},{8,10},{9,11},{10,... | collective-permute-start | bytes 589832 | tf_op jit(solution)/shard_map/ppermute | solution.py:340
  106.8 4.9 %shard_map.68.refs_0_ = bf16[256,384]{1,0:T(8,128)(2,1)} custom-call(s32[32,32]{1,0:T(8,128)} %refs_0_.1, bf16[256,384]{1,0:T(8,128)(2,1)} %get-tuple-element.46.refs_0_.refs_1_, f32[2,256,384]{2,1,0:T(8,128)} %get-tuple-element.51.refs_6_.refs_2_, f32[2,256,128]{2,1,0:T(8,128)} %get-tuple-element.61.refs_9_.refs_3_, bf16[256,768]{1,0:T(8,128)(2,1)} %copy-done.5, ...), custom_call_target="tpu_custom_call" | custom-call | flops 1024 | bytes 1024 | tf_op jit(solution)/shard_map/pallas_call | solution.py:248
  112.9 3.4 %collective-permute-done.17.refs_3_ = bf16[256,384]{1,0:T(8,128)(2,1)} collective-permute-done((bf16[256,384]{1,0:T(8,128)(2,1)}, bf16[256,384]{1,0:T(8,128)(2,1)}, u32[]{:S(2)}, u32[]{:S(2)}) %collective-permute-start.17) | collective-permute-done | bytes 196640 | tf_op jit(solution)/shard_map/ppermute | solution.py:340
  117.5 8.3 %shard_map.69 = bf16[256,3072]{1,0:T(8,128)(2,1)} custom-call(bf16[256,384]{1,0:T(8,128)(2,1)} %shard_map.68.refs_0_, bf16[256,384]{1,0:T(8,128)(2,1)} %copy-done.16, bf16[256,384]{1,0:T(8,128)(2,1)} %copy-done.17, bf16[256,384]{1,0:T(8,128)(2,1)} %collective-permute-done.17.refs_3_, bf16[1536,1024]{1,0:T(8,128)(2,1)} %all-gather.5.cloned.1.call-done.refs_4_, ...), custom_call_target="tpu_custom_call" | custom-call | tf_op jit(solution)/shard_map/pallas_call | solution.py:310
  (67 shorter events, 12.6 us)
Async XLA Ops:
  6.5 46.6 %all-gather.3.cloned.1.call-start = ((), (), s32[]{:S(2)}) async-start(), calls=%async_computation | async-start | bytes 3342336 | tf_op jit(solution)/shard_map/all_gather | solution.py:352
  8.2 103.5 %all-gather.5.cloned.1.call-start = ((), (), s32[]{:S(2)}) async-start(), calls=%async_computation.1 | async-start | bytes 3342336 | tf_op jit(solution)/shard_map/all_gather | solution.py:352
  12.9 20.5 %collective-permute-start.4 = (bf16[256,768]{1,0:T(8,128)(2,1)}, bf16[256,768]{1,0:T(8,128)(2,1)S(1)}, u32[]{:S(2)}, u32[]{:S(2)}) collective-permute-start(bf16[256,768]{1,0:T(8,128)(2,1)} %get-tuple-element.38), channel_id=1, source_target_pairs={{0,2},{1,3},{2,0},{3,1},{4,6},{5,7},{6,4},{7,5},{8,10},{9,11},{10,... | collective-permute-start | bytes 1179656 | tf_op jit(solution)/shard_map/ppermute | solution.py:340
  16.0 31.6 %collective-permute-start.5 = (bf16[256,768]{1,0:T(8,128)(2,1)}, bf16[256,768]{1,0:T(8,128)(2,1)S(1)}, u32[]{:S(2)}, u32[]{:S(2)}) collective-permute-start(bf16[256,768]{1,0:T(8,128)(2,1)} %get-tuple-element.41), channel_id=1, source_target_pairs={{0,3},{1,2},{2,1},{3,0},{4,7},{5,6},{6,5},{7,4},{8,11},{9,10},{10,... | collective-permute-start | bytes 1179656 | tf_op jit(solution)/shard_map/ppermute | solution.py:340
  16.0 31.9 %collective-permute-start = (bf16[256,768]{1,0:T(8,128)(2,1)}, bf16[256,768]{1,0:T(8,128)(2,1)S(1)}, u32[]{:S(2)}, u32[]{:S(2)}) collective-permute-start(bf16[256,768]{1,0:T(8,128)(2,1)} %get-tuple-element.36.refs_4_), channel_id=1, source_target_pairs={{0,4},{1,5},{2,6},{3,7},{4,8},{5,9},{6,10},{7,11},{8,12},{9,13},{1... | collective-permute-start | bytes 1179656 | tf_op jit(solution)/shard_map/ppermute | solution.py:346
  19.5 28.4 %collective-permute-start.1 = (bf16[256,768]{1,0:T(8,128)(2,1)}, bf16[256,768]{1,0:T(8,128)(2,1)S(1)}, u32[]{:S(2)}, u32[]{:S(2)}) collective-permute-start(bf16[256,768]{1,0:T(8,128)(2,1)} %get-tuple-element.36.refs_4_), channel_id=1, source_target_pairs={{4,0},{5,1},{6,2},{7,3},{8,4},{9,5},{10,6},{11,7},{12,8},{13,9},{1... | collective-permute-start | bytes 1179656 | tf_op jit(solution)/shard_map/ppermute | solution.py:346
  20.8 29.2 %collective-permute-start.2 = (bf16[256,768]{1,0:T(8,128)(2,1)}, bf16[256,768]{1,0:T(8,128)(2,1)S(1)}, u32[]{:S(2)}, u32[]{:S(2)}) collective-permute-start(bf16[256,768]{1,0:T(8,128)(2,1)} %get-tuple-element.37), channel_id=1, source_target_pairs={{0,5},{1,4},{2,7},{3,6},{4,9},{5,8},{6,11},{7,10},{8,13},{9,12},{1... | collective-permute-start | bytes 1179656 | tf_op jit(solution)/shard_map/ppermute | solution.py:346
  33.4 42.7 %copy-start.9 = (bf16[256,768]{1,0:T(8,128)(2,1)}, bf16[256,768]{1,0:T(8,128)(2,1)S(1)}, u32[]{:S(2)}) copy-start(bf16[256,768]{1,0:T(8,128)(2,1)S(1)} %collective-permute-done.4.refs_6_) | copy-start | bytes 1179652
  33.4 19.7 %collective-permute-start.3 = (bf16[256,768]{1,0:T(8,128)(2,1)}, bf16[256,768]{1,0:T(8,128)(2,1)S(1)}, u32[]{:S(2)}, u32[]{:S(2)}) collective-permute-start(bf16[256,768]{1,0:T(8,128)(2,1)} %get-tuple-element.37), channel_id=1, source_target_pairs={{4,1},{5,0},{6,3},{7,2},{8,5},{9,4},{10,7},{11,6},{12,9},{13,8},{1... | collective-permute-start | bytes 1179656 | tf_op jit(solution)/shard_map/ppermute | solution.py:346
  47.6 20.9 %copy-start.10 = (bf16[256,768]{1,0:T(8,128)(2,1)}, bf16[256,768]{1,0:T(8,128)(2,1)S(1)}, u32[]{:S(2)}) copy-start(bf16[256,768]{1,0:T(8,128)(2,1)S(1)} %collective-permute-done.5.refs_7_) | copy-start | bytes 1179652
  47.6 5.6 %collective-permute-start.6 = (bf16[256,384]{1,0:T(8,128)(2,1)}, bf16[256,384]{1,0:T(8,128)(2,1)S(1)}, u32[]{:S(2)}, u32[]{:S(2)}) collective-permute-start(bf16[256,384]{1,0:T(8,128)(2,1)} %get-tuple-element.42), channel_id=1, source_target_pairs={{0,1},{1,0},{2,3},{3,2},{4,5},{5,4},{6,7},{7,6},{8,9},{9,8},{10,11... | collective-permute-start | bytes 589832 | tf_op jit(solution)/shard_map/ppermute | solution.py:340
  55.4 40.4 %collective-permute-start.7 = (bf16[1536,512]{1,0:T(8,128)(2,1)S(1)}, bf16[1536,512]{1,0:T(8,128)(2,1)S(1)}, u32[]{:S(2)}, u32[]{:S(2)}) collective-permute-start(bf16[1536,512]{1,0:T(8,128)(2,1)S(1)} %constant_dynamic-slice_fusion), channel_id=1, source_target_pairs={{0,16},{16,0},{1,17},{17,1},{2,18},{18,2},{3,19},{19,3},{4,20},{20... | collective-permute-start | bytes 4718600 | tf_op jit(solution)/shard_map/ppermute | solution.py:375
  56.9 1.9 %collective-permute-start.8 = (bf16[256,768]{1,0:T(8,128)(2,1)}, bf16[256,768]{1,0:T(8,128)(2,1)S(1)}, u32[]{:S(2)}, u32[]{:S(2)}) collective-permute-start(bf16[256,768]{1,0:T(8,128)(2,1)} %get-tuple-element.37), channel_id=1, source_target_pairs={{0,1},{1,0},{2,3},{3,2},{4,5},{5,4},{6,7},{7,6},{8,9},{9,8},{10,11... | collective-permute-start | bytes 1179656 | tf_op jit(solution)/shard_map/ppermute | solution.py:340
  56.9 11.5 %collective-permute-start.10 = (bf16[256,384]{1,0:T(8,128)(2,1)}, bf16[256,384]{1,0:T(8,128)(2,1)S(1)}, u32[]{:S(2)}, u32[]{:S(2)}) collective-permute-start(bf16[256,384]{1,0:T(8,128)(2,1)} %get-tuple-element.48), channel_id=1, source_target_pairs={{0,2},{1,3},{2,0},{3,1},{4,6},{5,7},{6,4},{7,5},{8,10},{9,11},{10,... | collective-permute-start | bytes 589832 | tf_op jit(solution)/shard_map/ppermute | solution.py:340
  58.6 17.5 %collective-permute-start.11 = (bf16[256,384]{1,0:T(8,128)(2,1)S(1)}, bf16[256,384]{1,0:T(8,128)(2,1)S(1)}, u32[]{:S(2)}, u32[]{:S(2)}) collective-permute-start(bf16[256,384]{1,0:T(8,128)(2,1)S(1)} %copy-done.18), channel_id=1, source_target_pairs={{0,3},{1,2},{2,1},{3,0},{4,7},{5,6},{6,5},{7,4},{8,11},{9,10},{10,... | collective-permute-start | bytes 589832 | tf_op jit(solution)/shard_map/ppermute | solution.py:340
  58.9 18.8 %copy-start.15 = (bf16[256,768]{1,0:T(8,128)(2,1)}, bf16[256,768]{1,0:T(8,128)(2,1)S(1)}, u32[]{:S(2)}) copy-start(bf16[256,768]{1,0:T(8,128)(2,1)S(1)} %collective-permute-done.8.refs_5_) | copy-start | bytes 1179652
  58.9 33.1 %collective-permute-start.14 = (bf16[256,768]{1,0:T(8,128)(2,1)S(1)}, bf16[256,768]{1,0:T(8,128)(2,1)S(1)}, u32[]{:S(2)}, u32[]{:S(2)}) collective-permute-start(bf16[256,768]{1,0:T(8,128)(2,1)S(1)} %collective-permute-done.5.refs_7_), channel_id=1, source_target_pairs={{4,0},{5,1},{6,2},{7,3},{8,4},{9,5},{10,6},{11,7},{12,8},{13,9},{1... | collective-permute-start | bytes 1179656 | tf_op jit(solution)/shard_map/ppermute | solution.py:346
  60.2 32.9 %collective-permute-start.13 = (bf16[256,768]{1,0:T(8,128)(2,1)S(1)}, bf16[256,768]{1,0:T(8,128)(2,1)S(1)}, u32[]{:S(2)}, u32[]{:S(2)}) collective-permute-start(bf16[256,768]{1,0:T(8,128)(2,1)S(1)} %collective-permute-done.4.refs_6_), channel_id=1, source_target_pairs={{4,0},{5,1},{6,2},{7,3},{8,4},{9,5},{10,6},{11,7},{12,8},{13,9},{1... | collective-permute-start | bytes 1179656 | tf_op jit(solution)/shard_map/ppermute | solution.py:346
  68.5 24.6 %collective-permute-start.12 = (bf16[256,768]{1,0:T(8,128)(2,1)S(1)}, bf16[256,768]{1,0:T(8,128)(2,1)S(1)}, u32[]{:S(2)}, u32[]{:S(2)}) collective-permute-start(bf16[256,768]{1,0:T(8,128)(2,1)S(1)} %collective-permute-done.5.refs_7_), channel_id=1, source_target_pairs={{0,4},{1,5},{2,6},{3,7},{4,8},{5,9},{6,10},{7,11},{8,12},{9,13},{1... | collective-permute-start | bytes 1179656 | tf_op jit(solution)/shard_map/ppermute | solution.py:346
  76.1 19.7 %collective-permute-start.9 = (bf16[256,768]{1,0:T(8,128)(2,1)S(1)}, bf16[256,768]{1,0:T(8,128)(2,1)S(1)}, u32[]{:S(2)}, u32[]{:S(2)}) collective-permute-start(bf16[256,768]{1,0:T(8,128)(2,1)S(1)} %collective-permute-done.4.refs_6_), channel_id=1, source_target_pairs={{0,4},{1,5},{2,6},{3,7},{4,8},{5,9},{6,10},{7,11},{8,12},{9,13},{1... | collective-permute-start | bytes 1179656 | tf_op jit(solution)/shard_map/ppermute | solution.py:346
  95.8 20.5 %collective-permute-start.18 = (bf16[1536,512]{1,0:T(8,128)(2,1)S(1)}, bf16[1536,512]{1,0:T(8,128)(2,1)S(1)}, u32[]{:S(2)}, u32[]{:S(2)}) collective-permute-start(bf16[1536,512]{1,0:T(8,128)(2,1)S(1)} %collective-permute-done.7.refs_6_), channel_id=1, source_target_pairs={{0,1},{1,0},{2,3},{3,2},{4,5},{5,4},{6,7},{7,6},{8,9},{9,8},{10,11... | collective-permute-start | bytes 4718600 | tf_op jit(solution)/shard_map/ppermute | solution.py:383
  104.8 6.8 %collective-permute-start.15 = (bf16[256,384]{1,0:T(8,128)(2,1)}, bf16[256,384]{1,0:T(8,128)(2,1)S(1)}, u32[]{:S(2)}, u32[]{:S(2)}) collective-permute-start(bf16[256,384]{1,0:T(8,128)(2,1)} %get-tuple-element.64), channel_id=1, source_target_pairs={{0,1},{1,0},{2,3},{3,2},{4,5},{5,4},{6,7},{7,6},{8,9},{9,8},{10,11... | collective-permute-start | bytes 589832 | tf_op jit(solution)/shard_map/ppermute | solution.py:340
  104.9 8.0 %collective-permute-start.16 = (bf16[256,384]{1,0:T(8,128)(2,1)}, bf16[256,384]{1,0:T(8,128)(2,1)S(1)}, u32[]{:S(2)}, u32[]{:S(2)}) collective-permute-start(bf16[256,384]{1,0:T(8,128)(2,1)} %get-tuple-element.62), channel_id=1, source_target_pairs={{0,2},{1,3},{2,0},{3,1},{4,6},{5,7},{6,4},{7,5},{8,10},{9,11},{10,... | collective-permute-start | bytes 589832 | tf_op jit(solution)/shard_map/ppermute | solution.py:340
  106.3 10.0 %collective-permute-start.17 = (bf16[256,384]{1,0:T(8,128)(2,1)}, bf16[256,384]{1,0:T(8,128)(2,1)}, u32[]{:S(2)}, u32[]{:S(2)}) collective-permute-start(bf16[256,384]{1,0:T(8,128)(2,1)} %get-tuple-element.65), channel_id=1, source_target_pairs={{0,3},{1,2},{2,1},{3,0},{4,7},{5,6},{6,5},{7,4},{8,11},{9,10},{10,... | collective-permute-start | bytes 589832 | tf_op jit(solution)/shard_map/ppermute | solution.py:340
  (16 other events, 71.1 us)
Sparse Core Ops, SparseCore 0:
  8.9 42.9 all-gather.2
  53.5 39.5 all-gather.4

commit v7 on v6

--- a/solution.py
+++ b/solution.py
@@ -49,19 +49,20 @@
                 x = x_ref[rows, pl.ds(start, HDIM)].astype(jnp.float32)
                 partner = jnp.where(lane < half, pltpu.roll(x, HDIM - half, 1), pltpu.roll(x, half, 1))
                 turned = x * same[block, :1] + partner * other[block, :1]
-                outs[step][rows, head * HDIM : (head + 1) * HDIM] = turned.astype(jnp.bfloat16)
+                cols = slice(head * HDIM, (head + 1) * HDIM)
+                outs[step // 2][step % 2, rows, cols] = turned.astype(jnp.bfloat16)
 
 
 def pack_kv_kernel(frames, k_ref, v_ref, *rest):
-    outs, tables = rest[:LANES], rest[LANES:]
+    outs, tables = rest[:2], rest[2:]
     turn_into(frames, k_ref, outs, *tables)
     for step in range(LANES):
         start = pl.multiple_of(lane_of(step) * HC, HDIM)
-        outs[step][:, HC:] = v_ref[:, pl.ds(start, HC)]
+        outs[step // 2][step % 2, :, HC:] = v_ref[:, pl.ds(start, HC)]
 
 
 def pack_q_kernel(frames, q_ref, *rest):
-    turn_into(frames, q_ref, rest[:LANES], *rest[LANES:])
+    turn_into(frames, q_ref, rest[:2], *rest[2:])
 
 
 def pack(kernel, frames, arrays, width):
@@ -69,10 +70,10 @@
     table = pltpu.VMEM((count // BLK, 8, HDIM), jnp.float32)
     return pl.pallas_call(
         kernel,
-        out_shape=[jax.ShapeDtypeStruct((count, width), jnp.bfloat16)] * LANES,
+        out_shape=[jax.ShapeDtypeStruct((2, count, width), jnp.bfloat16)] * 2,
         in_specs=[pl.BlockSpec(memory_space=pltpu.SMEM)]
         + [pl.BlockSpec(memory_space=pltpu.VMEM) for _ in arrays],
-        out_specs=[pl.BlockSpec(memory_space=pltpu.VMEM)] * LANES,
+        out_specs=[pl.BlockSpec(memory_space=pltpu.VMEM)] * 2,
         scratch_shapes=[table, table],
         compiler_params=pltpu.CompilerParams(vmem_limit_bytes=56 * 1024 * 1024),
     )(frames, *arrays)
@@ -135,7 +136,10 @@
 
 
 def fetch(pairs, sems):
-    copies = [pltpu.make_async_copy(source, target, sems.at[i]) for i, (source, target) in enumerate(pairs)]
+    copies = []
+    for i, (source, target) in enumerate(pairs):
+        source = source.at[0] if len(source.shape) == 3 else source
+        copies.append(pltpu.make_async_copy(source, target, sems.at[i]))
     for copy in copies:
         copy.start()
     for copy in copies:
@@ -190,19 +194,17 @@
     count = len(steps)
     q_refs, accs, stats = refs[:count], refs[count : 2 * count], refs[2 * count : 3 * count]
     kv_refs, o_refs = refs[3 * count : 3 * count + LANES], refs[3 * count + LANES : 4 * count + LANES]
-    kv, scores, weights, sems = refs[4 * count + LANES :]
-    rows = q_refs[0].shape[0]
+    q_all, kv, scores, weights, sems = refs[4 * count + LANES :]
+    rows = q_all.shape[1]
     per_dev = rows // BLK
     plane = lax.axis_index("plane")
     places = [part * LANES + lane_of(step) for part in (0, 2) for step in (2, 3)]
-    fetch(
-        [
-            (ref, kv.at[pl.ds(pl.multiple_of(place * rows, BLK), rows)])
-            for ref, place in zip(kv_refs, places)
-        ],
-        sems,
-    )
-    for step, q_ref, acc, stat, o_ref in zip(steps, q_refs, accs, stats, o_refs):
+    pairs = [
+        (ref, kv.at[pl.ds(pl.multiple_of(place * rows, BLK), rows)]) for ref, place in zip(kv_refs, places)
+    ]
+    pairs += [(ref, q_all.at[i]) for i, ref in enumerate(q_refs)]
+    fetch(pairs, sems)
+    for i, (step, acc, stat, o_ref) in enumerate(zip(steps, accs, stats, o_refs)):
         tile = lane_of(step)
         me = plane * LANES + tile
         devices = chunk_devices_at(step // 2, tile, True)
@@ -211,12 +213,12 @@
         for h in range(HL):
             cols = slice(h * HDIM, (h + 1) * HDIM)
             state = (stat[0, :, h : h + 1], stat[0, :, HL + h : HL + h + 1], acc[0, :, cols])
-            _, total, mixed = attend_head(h, q_ref[:, cols], kv, starts, biases, scores, weights, state)
+            _, total, mixed = attend_head(h, q_all[i, :, cols], kv, starts, biases, scores, weights, state)
             o_ref[:, cols] = (mixed / total).astype(jnp.bfloat16)
 
 
 def attend_begin(mask, q, kv):
-    rows = kv[0].shape[0]
+    rows = kv[1].shape[0]
     span = 7 * rows
     vmem = pl.BlockSpec(memory_space=pltpu.VMEM)
     return pl.pallas_call(
@@ -238,7 +240,7 @@
 
 
 def attend_finish(steps, mask, q, begun, kv):
-    rows = kv[0].shape[0]
+    rows = begun[0].shape[1]
     span = 3 * rows
     vmem = pl.BlockSpec(memory_space=pltpu.VMEM)
 
@@ -250,16 +252,17 @@
         grid=(1,),
         out_shape=[jax.ShapeDtypeStruct((rows, HC), jnp.bfloat16)] * len(steps),
         in_specs=[pl.BlockSpec(memory_space=pltpu.SMEM)]
-        + [vmem] * len(steps)
+        + [pl.BlockSpec(memory_space=pl.ANY)] * len(steps)
         + [of_tile(step, HC) for step in steps]
         + [of_tile(step, HDIM) for step in steps]
         + [pl.BlockSpec(memory_space=pl.ANY)] * LANES,
         out_specs=[vmem] * len(steps),
         scratch_shapes=[
+            pltpu.VMEM((len(steps), rows, HC), jnp.bfloat16),
             pltpu.VMEM((3 * LANES * rows, 2 * HC), jnp.bfloat16),
             pltpu.VMEM((HL, rows, span), jnp.float32),
             pltpu.VMEM((HL, rows, span), jnp.bfloat16),
-            pltpu.SemaphoreType.DMA((LANES,)),
+            pltpu.SemaphoreType.DMA((LANES + len(steps),)),
         ],
         compiler_params=pltpu.CompilerParams(vmem_limit_bytes=56 * 1024 * 1024),
         cost_estimate=BRIEF,
@@ -339,11 +342,12 @@
     def to_lane(x, dr, dc):
         return lax.ppermute(x, seq, [(index(p, r, c), index(p, r ^ dr, c ^ dc)) for p, r, c in every])
 
-    def to_plane(x, dp, dc):
-        pairs = [
-            (index(p, r, c), index(p + dp, r, c ^ dc)) for p, r, c in every if 0 <= p + dp < planes
-        ]
+    def to_plane(x, dp):
+        pairs = [(index(p, r, c), index(p + dp, r, c)) for p, r, c in every if 0 <= p + dp < planes]
         return lax.ppermute(x, seq, pairs)
+
+    def swap(x):
+        return to_lane(x[1], 0, 1)
 
     walk = [(p, 0) for p in range(planes)] + [(p, 1) for p in reversed(range(planes))]
     order = [index(p, r, c) for p, r in walk for c in range(2)]
@@ -357,17 +361,20 @@
     strip_at = direct + lax.axis_index("groups") * strip
     own_strip = gather(lax.dynamic_slice_in_dim(out_weight, strip_at, strip, 1))
 
-    kv = pack(pack_kv_kernel, frame_index, (keys, values), 2 * HC)
-    direct_strip = gather(after(out_weight, kv[0])[:, :direct])
-    across = [to_lane(kv[2], 1, 0), to_lane(kv[3], 1, 1)]
-    early = {(dp, dc): to_plane(kv[dc], dp, dc) for dc in range(2) for dp in (1, -1)}
-    here = [kv[0], to_lane(kv[1], 0, 1)] + across
-    q = pack(pack_q_kernel, frame_index, (after(queries, across[0]),), HC)
-    onward = [after(x, *early.values(), here[1]) for x in across]
-    late = {(dp, dc): to_plane(onward[dc], dp, 0) for dc in range(2) for dp in (1, -1)}
-    q = [q[0]] + [to_lane(after(q[d], *across), d // 2, d % 2) for d in range(1, LANES)]
-
-    own_strip = after(own_strip, *early.values(), q[1])
+    own, other = pack(pack_kv_kernel, frame_index, (keys, values), 2 * HC)
+    across = to_lane(other, 1, 0)
+    early = [to_plane(own, dp) for dp in (1, -1)]
+    beside = swap(own)
+    own_q, other_q = pack(pack_q_kernel, frame_index, (after(queries, beside),), HC)
+    across_q = to_lane(other_q, 1, 0)
+    across_beside = swap(across)
+    here = [own, beside, across, across_beside]
+    q = [own_q, swap(own_q), across_q, swap(across_q)]
+    onward = after(across, *early)
+    late = [to_plane(onward, dp) for dp in (1, -1)]
+    direct_strip = gather(after(out_weight, across)[:, :direct])
+
+    own_strip = after(own_strip, *early, across_beside)
     half = strip // 2
     core_at = lax.axis_index("core") * half
     sent = lax.dynamic_slice_in_dim(own_strip, core_at, half, 1)
@@ -375,20 +382,18 @@
         lax.ppermute(sent, "groups", [(g, (g + dx) % groups) for g in range(groups)])
         for dx in range(1, groups)
     ]
-    begun = attend_begin(
-        after(block_mask, sent), q, here + [early[dp, dc] for dp in (1, -1) for dc in range(2)]
-    )
-    late = [after(late[dp, dc], begun[0]) for dp in (1, -1) for dc in range(2)]
-    halves = [after(x, *late) for x in halves]
-    swapped = [lax.ppermute(x, "core", [(0, 1), (1, 0)]) for x in halves]
-    block_mask = after(block_mask, *halves)
+    pieces = [piece for x in early for piece in (x, swap(x))]
+    begun = attend_begin(after(block_mask, sent), q, here + pieces)
+    late = [after(x, begun[0]) for x in late]
+    late = [piece for x in late for piece in (x, swap(x))]
     mixed = attend_finish((2, 3, 1), block_mask, q, begun, late)
     moved = [to_lane(x, step // 2, step % 2) for x, step in zip(mixed, (2, 3, 1))]
-    own = attend_finish((0,), after(block_mask, mixed[0]), q, begun, late)
+    halves = [after(x, mixed[0]) for x in halves]
+    own = attend_finish((0,), after(block_mask, mixed[0], *halves), q, begun, late)
     mixed = [own[0], moved[2], moved[0], moved[1]]
     weights = [direct_strip, own_strip]
-    for pair in zip(halves, swapped):
-        weights += pair
+    for x in halves:
+        weights += [x, lax.ppermute(x, "core", [(0, 1), (1, 0)])]
     return project(mixed, weights, order, groups)
 
 

time: 133 us -> 162 us (1.22)
  waiting for transfers between devices: 45.9 us -> 70.1 us
  local copies, waits for them, and re-layouts: 7.4 us -> 13.1 us
    ppermute x8 -> x4, waiting for transfers between devices: 9.07 us -> 25.3 us  [to_plane(): return lax.ppermute(x, seq, pairs)]
    ppermute x1, waiting for transfers between devices: 0.01 us -> 5.21 us  [on_device(): lax.ppermute(sent, 'groups', [(g, (g + dx) % groups) for g in range(group...]
    squeeze x0 -> x8, local copies, waits for them, and re-layouts: none -> 4.55 us  [swap(): return to_lane(x[1], 0, 1)]
    ppermute x8 -> x4, starting transfers between devices: 15.7 us -> 11.4 us  [to_plane(): return lax.ppermute(x, seq, pairs)]
    ppermute x9 -> x13, starting transfers between devices: 7.12 us -> 10 us  [to_lane(): lax.ppermute(x, seq, [(index(p, r, c), index(p, r ^ dr, c ^ dc)) for p, r...]
    ppermute x9 -> x13, waiting for transfers between devices: 36.8 us -> 39.5 us  [to_lane(): lax.ppermute(x, seq, [(index(p, r, c), index(p, r ^ dr, c ^ dc)) for p, r...]
    unnamed x38 -> x28, local copies, waits for them, and re-layouts: 2.66 us -> 3.61 us
  transfers between devices with their start and end apart: 21 -> 21, of which waited for: 11 -> 10; matrix products, arithmetic and copies ran while one was open for 2% -> 5% of each run, Pallas kernels for 25% -> 21%
where the time goes in v7:
time: 162 us
  waiting for transfers between devices  70.1 us (43%)
  Pallas kernels  41.5 us (26%)
  starting transfers between devices  23.2 us (14%)
  between operations  13.6 us (8%)
  local copies, waits for them, and re-layouts  13.1 us (8%)
    ppermute x13, waiting for transfers between devices, to_lane(): lax.ppermute(x, seq, [(index(p, r, c), index(p, r ^ dr, c ^ dc)) for p, r...  39.5 us
    ppermute x4, waiting for transfers between devices, to_plane(): return lax.ppermute(x, seq, pairs)  25.3 us
    pallas_call x1, Pallas kernels, attend_begin(): pl.pallas_call(begin_kernel, out_shape=[jax.ShapeDtypeStruct((2, rows, HC...  14.3 us
    pallas_call x2, Pallas kernels, attend_finish(): pl.pallas_call(lambda *refs: finish_kernel(steps, *refs), grid=(1,), out_...  13.1 us
    ppermute x4, starting transfers between devices, to_plane(): return lax.ppermute(x, seq, pairs)  11.4 us
    ppermute x13, starting transfers between devices, to_lane(): lax.ppermute(x, seq, [(index(p, r, c), index(p, r ^ dr, c ^ dc)) for p, r...  10 us
    pallas_call x1, Pallas kernels, project(): pl.pallas_call(lambda *refs: project_kernel(order, groups, refs[:LANES],...  8.33 us
    pallas_call x2, Pallas kernels, pack(): pl.pallas_call(kernel, out_shape=[jax.ShapeDtypeStruct((2, count, width),...  5.78 us
  transfers between devices with their start and end apart: 21, of which 10 were waited for; matrix products, arithmetic and copies ran while one was open for 5% of the time, Pallas kernels for 21%

profile of v7, /device:TPU:0, one launch (start us, length us, event | category | flops | bytes accessed | tf_op | source)
XLA Modules:
  0.0 161.5 jit_solution(9891189595972337137)
XLA Ops:
  6.5 1.6 %constant_dynamic-slice_fusion.1 = bf16[96,1024]{1,0:T(8,128)(2,1)} fusion(bf16[96,3072]{1,0:T(8,128)(2,1)} %param.11, s32[]{:T(128)S(6)} %select_n.6), kind=kLoop, calls=%fused_computation.9 | loop fusion | bytes 393220 | tf_op jit(solution)/shard_map/dynamic_slice | solution.py:362
  8.2 3.1 %shard_map.64 = (bf16[2,256,768]{2,1,0:T(8,128)(2,1)}, bf16[2,256,768]{2,1,0:T(8,128)(2,1)}) custom-call(s32[2]{0:T(128)} %frames.3, bf16[256,1536]{1,0:T(8,128)(2,1)} %k_ref.1, bf16[256,1536]{1,0:T(8,128)(2,1)} %v_ref.1), custom_call_target="tpu_custom_call" | custom-call | tf_op jit(solution)/shard_map/pallas_call | solution.py:71
  11.3 3.0 %collective-permute-start.6 = (bf16[2,256,768]{2,1,0:T(8,128)(2,1)}, bf16[2,256,768]{2,1,0:T(8,128)(2,1)S(1)}, u32[]{:S(2)}, u32[]{:S(2)}) collective-permute-start(bf16[2,256,768]{2,1,0:T(8,128)(2,1)} %get-tuple-element.29), channel_id=1, source_target_pairs={{0,2},{1,3},{2,0},{3,1},{4,6},{5,7},{6,4},{7,5},{8,10},{9,11},{10,... | collective-permute-start | bytes 2359304 | tf_op jit(solution)/shard_map/ppermute | solution.py:343
  14.3 31.3 %collective-permute-done.6.refs_6_ = bf16[2,256,768]{2,1,0:T(8,128)(2,1)S(1)} collective-permute-done((bf16[2,256,768]{2,1,0:T(8,128)(2,1)}, bf16[2,256,768]{2,1,0:T(8,128)(2,1)S(1)}, u32[]{:S(2)}, u32[]{:S(2)}) %collective-permute-start.6) | collective-permute-done | bytes 786464 | tf_op jit(solution)/shard_map/ppermute | solution.py:343
  45.6 1.8 %slice.35 = bf16[96,1024]{1,0:T(8,128)(2,1)} slice(bf16[96,3072]{1,0:T(8,128)(2,1)} %param.11), slice={[0:96], [0:1024]} | slice | bytes 393216 | tf_op jit(solution)/shard_map/slice | solution.py:375
  48.6 1.3 collective-permute-start.4
  49.9 1.3 collective-permute-start.5
  51.3 2.7 %shard_map.65 = (bf16[2,256,384]{2,1,0:T(8,128)(2,1)}, bf16[2,256,384]{2,1,0:T(8,128)(2,1)}) custom-call(s32[2]{0:T(128)} %frames.3, bf16[256,1536]{1,0:T(8,128)(2,1)} %q_ref), custom_call_target="tpu_custom_call" | custom-call | tf_op jit(solution)/shard_map/pallas_call | solution.py:71
  54.0 2.3 %collective-permute-start.1 = (bf16[2,256,384]{2,1,0:T(8,128)(2,1)}, bf16[2,256,384]{2,1,0:T(8,128)(2,1)S(1)}, u32[]{:S(2)}, u32[]{:S(2)}) collective-permute-start(bf16[2,256,384]{2,1,0:T(8,128)(2,1)} %get-tuple-element.27), channel_id=1, source_target_pairs={{0,2},{1,3},{2,0},{3,1},{4,6},{5,7},{6,4},{7,5},{8,10},{9,11},{10,... | collective-permute-start | bytes 1179656 | tf_op jit(solution)/shard_map/ppermute | solution.py:343
  56.6 1.6 %slice_bitcast_fusion.7 = bf16[256,384]{1,0:T(8,128)(2,1)} fusion(bf16[2,256,384]{2,1,0:T(8,128)(2,1)} %get-tuple-element.28.refs_0_.refs_1_), kind=kLoop, calls=%fused_computation.7 | loop fusion | bytes 393216 | tf_op jit(solution)/shard_map/squeeze | solution.py:350
  58.6 18.8 %collective-permute-done.4.refs_8_ = bf16[2,256,768]{2,1,0:T(8,128)(2,1)S(1)} collective-permute-done((bf16[2,256,768]{2,1,0:T(8,128)(2,1)}, bf16[2,256,768]{2,1,0:T(8,128)(2,1)S(1)}, u32[]{:S(2)}, u32[]{:S(2)}) %collective-permute-start.4) | collective-permute-done | bytes 786464 | tf_op jit(solution)/shard_map/ppermute | solution.py:347
  77.4 6.5 %collective-permute-done.5.refs_10_ = bf16[2,256,768]{2,1,0:T(8,128)(2,1)} collective-permute-done((bf16[2,256,768]{2,1,0:T(8,128)(2,1)}, bf16[2,256,768]{2,1,0:T(8,128)(2,1)}, u32[]{:S(2)}, u32[]{:S(2)}) %collective-permute-start.5) | collective-permute-done | bytes 786464 | tf_op jit(solution)/shard_map/ppermute | solution.py:347
  83.9 1.3 collective-permute-start.12
  85.2 7.5 %collective-permute-start.10 = (bf16[2,256,768]{2,1,0:T(8,128)(2,1)S(1)}, bf16[2,256,768]{2,1,0:T(8,128)(2,1)S(1)}, u32[]{:S(2)}, u32[]{:S(2)}) collective-permute-start(bf16[2,256,768]{2,1,0:T(8,128)(2,1)S(1)} %collective-permute-done.6.refs_6_), channel_id=1, source_target_pairs={{0,4},{1,5},{2,6},{3,7},{4,8},{5,9},{6,10},{7,11},{8,12},{9,13},{1... | collective-permute-start | bytes 2359304 | tf_op jit(solution)/shard_map/ppermute | solution.py:347
  93.5 1.5 constant_dynamic-slice_fusion
  95.1 1.6 %collective-permute-start.14 = (bf16[1536,512]{1,0:T(8,128)(2,1)S(1)}, bf16[1536,512]{1,0:T(8,128)(2,1)}, u32[]{:S(2)}, u32[]{:S(2)}) collective-permute-start(bf16[1536,512]{1,0:T(8,128)(2,1)S(1)} %constant_dynamic-slice_fusion), channel_id=1, source_target_pairs={{0,16},{16,0},{1,17},{17,1},{2,18},{18,2},{3,19},{19,3},{4,20},{20... | collective-permute-start | bytes 4718600 | tf_op jit(solution)/shard_map/ppermute | solution.py:382
  98.4 1.2 collective-permute-done.8.refs_9_
  101.1 14.3 %shard_map.66 = (f32[2,256,384]{2,1,0:T(8,128)}, f32[2,256,384]{2,1,0:T(8,128)}, f32[2,256,128]{2,1,0:T(8,128)}, f32[2,256,128]{2,1,0:T(8,128)}) custom-call(s32[32,32]{1,0:T(8,128)} %refs_0_.2, bf16[2,256,384]{2,1,0:T(8,128)(2,1)} %get-tuple-element.28.refs_0_.refs_1_, bf16[256,384]{1,0:T(8,128)(2,1)} %collective-permute-done.3.refs_1_.refs_3_, ...), custom_call_target="tpu_custom_call" | custom-call | flops 1024 | bytes 1024 | tf_op jit(solution)/shard_map/pallas_call | solution.py:224
  118.6 8.2 %shard_map.67 = (bf16[256,384]{1,0:T(8,128)(2,1)}, bf16[256,384]{1,0:T(8,128)(2,1)}, bf16[256,384]{1,0:T(8,128)(2,1)}) custom-call(s32[32,32]{1,0:T(8,128)} %refs_0_.2, bf16[2,256,384]{2,1,0:T(8,128)(2,1)} %copy-done.2, bf16[256,384]{1,0:T(8,128)(2,1)} %collective-permute-done.2.refs_3_.refs_2_, bf16[256,384]{1,0:T(8,128)(2,1)} %collective-permute-done.3.refs_1_.refs_3_, ...), custom_call_target="tpu_custom_call" | custom-call | flops 1024 | bytes 1024 | tf_op jit(solution)/shard_map/pallas_call | solution.py:250
  126.8 5.2 %collective-permute-done.14.refs_6_ = bf16[1536,512]{1,0:T(8,128)(2,1)} collective-permute-done((bf16[1536,512]{1,0:T(8,128)(2,1)S(1)}, bf16[1536,512]{1,0:T(8,128)(2,1)}, u32[]{:S(2)}, u32[]{:S(2)}) %collective-permute-start.14) | collective-permute-done | bytes 1572896 | tf_op jit(solution)/shard_map/ppermute | solution.py:382
  132.0 2.6 %collective-permute-start.16 = (bf16[256,384]{1,0:T(8,128)(2,1)}, bf16[256,384]{1,0:T(8,128)(2,1)S(1)}, u32[]{:S(2)}, u32[]{:S(2)}) collective-permute-start(bf16[256,384]{1,0:T(8,128)(2,1)} %get-tuple-element.39), channel_id=1, source_target_pairs={{0,2},{1,3},{2,0},{3,1},{4,6},{5,7},{6,4},{7,5},{8,10},{9,11},{10,... | collective-permute-start | bytes 589832 | tf_op jit(solution)/shard_map/ppermute | solution.py:343
  134.9 4.8 %shard_map.68.refs_0_ = bf16[256,384]{1,0:T(8,128)(2,1)} custom-call(s32[32,32]{1,0:T(8,128)} %refs_0_.2, bf16[2,256,384]{2,1,0:T(8,128)(2,1)} %get-tuple-element.28.refs_0_.refs_1_, f32[2,256,384]{2,1,0:T(8,128)} %get-tuple-element.33.refs_6_.refs_2_, f32[2,256,128]{2,1,0:T(8,128)} %get-tuple-element.35.refs_9_.refs_3_, bf16[2,256,768]{2,1,0:T(8,128)(2,1)} %copy-done.1, ...), custom_call_target="tpu_custom_call" | custom-call | flops 1024 | bytes 1024 | tf_op jit(solution)/shard_map/pallas_call | solution.py:250
  140.6 3.8 %collective-permute-done.17.refs_3_ = bf16[256,384]{1,0:T(8,128)(2,1)S(1)} collective-permute-done((bf16[256,384]{1,0:T(8,128)(2,1)}, bf16[256,384]{1,0:T(8,128)(2,1)S(1)}, u32[]{:S(2)}, u32[]{:S(2)}) %collective-permute-start.17) | collective-permute-done | bytes 196640 | tf_op jit(solution)/shard_map/ppermute | solution.py:343
  146.3 8.3 %shard_map.69 = bf16[256,3072]{1,0:T(8,128)(2,1)} custom-call(bf16[256,384]{1,0:T(8,128)(2,1)} %shard_map.68.refs_0_, bf16[256,384]{1,0:T(8,128)(2,1)} %copy-done.12, bf16[256,384]{1,0:T(8,128)(2,1)} %copy-done.11, bf16[256,384]{1,0:T(8,128)(2,1)} %copy-done.13, bf16[1536,1024]{1,0:T(8,128)(2,1)} %all-gather.5.cloned.1.call-done.refs_4_, ...), custom_call_target="tpu_custom_call" | custom-call | tf_op jit(solution)/shard_map/pallas_call | solution.py:313
  (65 shorter events, 11.8 us)
Async XLA Ops:
  6.5 87.0 %all-gather.3.cloned.1.call-start = ((), (), s32[]{:S(2)}) async-start(), calls=%async_computation | async-start | bytes 3342336 | tf_op jit(solution)/shard_map/all_gather | solution.py:356
  8.2 136.3 %all-gather.5.cloned.1.call-start = ((), (), s32[]{:S(2)}) async-start(), calls=%async_computation.1 | async-start | bytes 3342336 | tf_op jit(solution)/shard_map/all_gather | solution.py:356
  11.3 34.3 %collective-permute-start.6 = (bf16[2,256,768]{2,1,0:T(8,128)(2,1)}, bf16[2,256,768]{2,1,0:T(8,128)(2,1)S(1)}, u32[]{:S(2)}, u32[]{:S(2)}) collective-permute-start(bf16[2,256,768]{2,1,0:T(8,128)(2,1)} %get-tuple-element.29), channel_id=1, source_target_pairs={{0,2},{1,3},{2,0},{3,1},{4,6},{5,7},{6,4},{7,5},{8,10},{9,11},{10,... | collective-permute-start | bytes 2359304 | tf_op jit(solution)/shard_map/ppermute | solution.py:343
  45.6 39.6 %copy-start.3 = (bf16[2,256,768]{2,1,0:T(8,128)(2,1)}, bf16[2,256,768]{2,1,0:T(8,128)(2,1)S(1)}, u32[]{:S(2)}) copy-start(bf16[2,256,768]{2,1,0:T(8,128)(2,1)S(1)} %collective-permute-done.6.refs_6_) | copy-start | bytes 2359300
  48.5 2.7 %collective-permute-start = (bf16[256,768]{1,0:T(8,128)(2,1)S(1)}, bf16[256,768]{1,0:T(8,128)(2,1)S(1)}, u32[]{:S(2)}, u32[]{:S(2)}) collective-permute-start(bf16[256,768]{1,0:T(8,128)(2,1)S(1)} %slice_bitcast_fusion.5), channel_id=1, source_target_pairs={{0,1},{1,0},{2,3},{3,2},{4,5},{5,4},{6,7},{7,6},{8,9},{9,8},{10,11... | collective-permute-start | bytes 1179656 | tf_op jit(solution)/shard_map/ppermute | solution.py:343
  48.6 28.8 %collective-permute-start.4 = (bf16[2,256,768]{2,1,0:T(8,128)(2,1)}, bf16[2,256,768]{2,1,0:T(8,128)(2,1)S(1)}, u32[]{:S(2)}, u32[]{:S(2)}) collective-permute-start(bf16[2,256,768]{2,1,0:T(8,128)(2,1)} %get-tuple-element.25.refs_4_), channel_id=1, source_target_pairs={{0,4},{1,5},{2,6},{3,7},{4,8},{5,9},{6,10},{7,11},{8,12},{9,13},{1... | collective-permute-start | bytes 2359304 | tf_op jit(solution)/shard_map/ppermute | solution.py:347
  49.9 34.0 %collective-permute-start.5 = (bf16[2,256,768]{2,1,0:T(8,128)(2,1)}, bf16[2,256,768]{2,1,0:T(8,128)(2,1)}, u32[]{:S(2)}, u32[]{:S(2)}) collective-permute-start(bf16[2,256,768]{2,1,0:T(8,128)(2,1)} %get-tuple-element.25.refs_4_), channel_id=1, source_target_pairs={{4,0},{5,1},{6,2},{7,3},{8,4},{9,5},{10,6},{11,7},{12,8},{13,9},{1... | collective-permute-start | bytes 2359304 | tf_op jit(solution)/shard_map/ppermute | solution.py:347
  51.3 26.1 %copy-start.8 = (bf16[256,768]{1,0:T(8,128)(2,1)}, bf16[256,768]{1,0:T(8,128)(2,1)S(1)}, u32[]{:S(2)}) copy-start(bf16[256,768]{1,0:T(8,128)(2,1)S(1)} %collective-permute-done.refs_5_) | copy-start | bytes 1179652
  54.0 38.8 %collective-permute-start.1 = (bf16[2,256,384]{2,1,0:T(8,128)(2,1)}, bf16[2,256,384]{2,1,0:T(8,128)(2,1)S(1)}, u32[]{:S(2)}, u32[]{:S(2)}) collective-permute-start(bf16[2,256,384]{2,1,0:T(8,128)(2,1)} %get-tuple-element.27), channel_id=1, source_target_pairs={{0,2},{1,3},{2,0},{3,1},{4,6},{5,7},{6,4},{7,5},{8,10},{9,11},{10,... | collective-permute-start | bytes 1179656 | tf_op jit(solution)/shard_map/ppermute | solution.py:343
  56.4 37.2 %collective-permute-start.7 = (bf16[256,768]{1,0:T(8,128)(2,1)S(1)}, bf16[256,768]{1,0:T(8,128)(2,1)}, u32[]{:S(2)}, u32[]{:S(2)}) collective-permute-start(bf16[256,768]{1,0:T(8,128)(2,1)S(1)} %slice_bitcast_fusion.2), channel_id=1, source_target_pairs={{0,1},{1,0},{2,3},{3,2},{4,5},{5,4},{6,7},{7,6},{8,9},{9,8},{10,11... | collective-permute-start | bytes 1179656 | tf_op jit(solution)/shard_map/ppermute | solution.py:343
  58.2 39.5 %collective-permute-start.3 = (bf16[256,384]{1,0:T(8,128)(2,1)}, bf16[256,384]{1,0:T(8,128)(2,1)}, u32[]{:S(2)}, u32[]{:S(2)}) collective-permute-start(bf16[256,384]{1,0:T(8,128)(2,1)} %slice_bitcast_fusion.7), channel_id=1, source_target_pairs={{0,1},{1,0},{2,3},{3,2},{4,5},{5,4},{6,7},{7,6},{8,9},{9,8},{10,11... | collective-permute-start | bytes 589832 | tf_op jit(solution)/shard_map/ppermute | solution.py:343
  77.4 19.4 %copy-start.4 = (bf16[2,256,768]{2,1,0:T(8,128)(2,1)}, bf16[2,256,768]{2,1,0:T(8,128)(2,1)S(1)}, u32[]{:S(2)}) copy-start(bf16[2,256,768]{2,1,0:T(8,128)(2,1)S(1)} %collective-permute-done.4.refs_8_) | copy-start | bytes 2359300
  83.9 31.5 %collective-permute-start.12 = (bf16[2,256,768]{2,1,0:T(8,128)(2,1)S(1)}, bf16[2,256,768]{2,1,0:T(8,128)(2,1)S(1)}, u32[]{:S(2)}, u32[]{:S(2)}) collective-permute-start(bf16[2,256,768]{2,1,0:T(8,128)(2,1)S(1)} %collective-permute-done.6.refs_6_), channel_id=1, source_target_pairs={{4,0},{5,1},{6,2},{7,3},{8,4},{9,5},{10,6},{11,7},{12,8},{13,9},{1... | collective-permute-start | bytes 2359304 | tf_op jit(solution)/shard_map/ppermute | solution.py:347
  85.2 30.5 %collective-permute-start.10 = (bf16[2,256,768]{2,1,0:T(8,128)(2,1)S(1)}, bf16[2,256,768]{2,1,0:T(8,128)(2,1)S(1)}, u32[]{:S(2)}, u32[]{:S(2)}) collective-permute-start(bf16[2,256,768]{2,1,0:T(8,128)(2,1)S(1)} %collective-permute-done.6.refs_6_), channel_id=1, source_target_pairs={{0,4},{1,5},{2,6},{3,7},{4,8},{5,9},{6,10},{7,11},{8,12},{9,13},{1... | collective-permute-start | bytes 2359304 | tf_op jit(solution)/shard_map/ppermute | solution.py:347
  93.5 4.5 %collective-permute-start.2 = (bf16[256,384]{1,0:T(8,128)(2,1)}, bf16[256,384]{1,0:T(8,128)(2,1)}, u32[]{:S(2)}, u32[]{:S(2)}) collective-permute-start(bf16[256,384]{1,0:T(8,128)(2,1)} %slice_bitcast_fusion.6), channel_id=1, source_target_pairs={{0,1},{1,0},{2,3},{3,2},{4,5},{5,4},{6,7},{7,6},{8,9},{9,8},{10,11... | collective-permute-start | bytes 589832 | tf_op jit(solution)/shard_map/ppermute | solution.py:343
  95.1 37.0 %collective-permute-start.14 = (bf16[1536,512]{1,0:T(8,128)(2,1)S(1)}, bf16[1536,512]{1,0:T(8,128)(2,1)}, u32[]{:S(2)}, u32[]{:S(2)}) collective-permute-start(bf16[1536,512]{1,0:T(8,128)(2,1)S(1)} %constant_dynamic-slice_fusion), channel_id=1, source_target_pairs={{0,16},{16,0},{1,17},{17,1},{2,18},{18,2},{3,19},{19,3},{4,20},{20... | collective-permute-start | bytes 4718600 | tf_op jit(solution)/shard_map/ppermute | solution.py:382
  97.8 1.8 %collective-permute-start.8 = (bf16[256,768]{1,0:T(8,128)(2,1)S(1)}, bf16[256,768]{1,0:T(8,128)(2,1)S(1)}, u32[]{:S(2)}, u32[]{:S(2)}) collective-permute-start(bf16[256,768]{1,0:T(8,128)(2,1)S(1)} %slice_bitcast_fusion.1), channel_id=1, source_target_pairs={{0,1},{1,0},{2,3},{3,2},{4,5},{5,4},{6,7},{7,6},{8,9},{9,8},{10,11... | collective-permute-start | bytes 1179656 | tf_op jit(solution)/shard_map/ppermute | solution.py:343
  98.1 2.1 %collective-permute-start.9 = (bf16[256,768]{1,0:T(8,128)(2,1)S(1)}, bf16[256,768]{1,0:T(8,128)(2,1)S(1)}, u32[]{:S(2)}, u32[]{:S(2)}) collective-permute-start(bf16[256,768]{1,0:T(8,128)(2,1)S(1)} %slice_bitcast_fusion), channel_id=1, source_target_pairs={{0,1},{1,0},{2,3},{3,2},{4,5},{5,4},{6,7},{7,6},{8,9},{9,8},{10,11... | collective-permute-start | bytes 1179656 | tf_op jit(solution)/shard_map/ppermute | solution.py:343
  115.4 1.8 %collective-permute-start.13 = (bf16[256,768]{1,0:T(8,128)(2,1)S(1)}, bf16[256,768]{1,0:T(8,128)(2,1)S(1)}, u32[]{:S(2)}, u32[]{:S(2)}) collective-permute-start(bf16[256,768]{1,0:T(8,128)(2,1)S(1)} %slice_bitcast_fusion.3), channel_id=1, source_target_pairs={{0,1},{1,0},{2,3},{3,2},{4,5},{5,4},{6,7},{7,6},{8,9},{9,8},{10,11... | collective-permute-start | bytes 1179656 | tf_op jit(solution)/shard_map/ppermute | solution.py:343
  115.8 2.0 %collective-permute-start.11 = (bf16[256,768]{1,0:T(8,128)(2,1)S(1)}, bf16[256,768]{1,0:T(8,128)(2,1)S(1)}, u32[]{:S(2)}, u32[]{:S(2)}) collective-permute-start(bf16[256,768]{1,0:T(8,128)(2,1)S(1)} %slice_bitcast_fusion.4), channel_id=1, source_target_pairs={{0,1},{1,0},{2,3},{3,2},{4,5},{5,4},{6,7},{7,6},{8,9},{9,8},{10,11... | collective-permute-start | bytes 1179656 | tf_op jit(solution)/shard_map/ppermute | solution.py:343
  132.0 12.4 %collective-permute-start.18 = (bf16[1536,512]{1,0:T(8,128)(2,1)}, bf16[1536,512]{1,0:T(8,128)(2,1)S(1)}, u32[]{:S(2)}, u32[]{:S(2)}) collective-permute-start(bf16[1536,512]{1,0:T(8,128)(2,1)} %collective-permute-done.14.refs_6_), channel_id=1, source_target_pairs={{0,1},{1,0},{2,3},{3,2},{4,5},{5,4},{6,7},{7,6},{8,9},{9,8},{10,11... | collective-permute-start | bytes 4718600 | tf_op jit(solution)/shard_map/ppermute | solution.py:396
  132.0 8.6 %collective-permute-start.16 = (bf16[256,384]{1,0:T(8,128)(2,1)}, bf16[256,384]{1,0:T(8,128)(2,1)S(1)}, u32[]{:S(2)}, u32[]{:S(2)}) collective-permute-start(bf16[256,384]{1,0:T(8,128)(2,1)} %get-tuple-element.39), channel_id=1, source_target_pairs={{0,2},{1,3},{2,0},{3,1},{4,6},{5,7},{6,4},{7,5},{8,10},{9,11},{10,... | collective-permute-start | bytes 589832 | tf_op jit(solution)/shard_map/ppermute | solution.py:343
  134.7 5.1 %collective-permute-start.15 = (bf16[256,384]{1,0:T(8,128)(2,1)}, bf16[256,384]{1,0:T(8,128)(2,1)S(1)}, u32[]{:S(2)}, u32[]{:S(2)}) collective-permute-start(bf16[256,384]{1,0:T(8,128)(2,1)} %get-tuple-element.42), channel_id=1, source_target_pairs={{0,1},{1,0},{2,3},{3,2},{4,5},{5,4},{6,7},{7,6},{8,9},{9,8},{10,11... | collective-permute-start | bytes 589832 | tf_op jit(solution)/shard_map/ppermute | solution.py:343
  134.9 9.6 %collective-permute-start.17 = (bf16[256,384]{1,0:T(8,128)(2,1)}, bf16[256,384]{1,0:T(8,128)(2,1)S(1)}, u32[]{:S(2)}, u32[]{:S(2)}) collective-permute-start(bf16[256,384]{1,0:T(8,128)(2,1)} %get-tuple-element.43), channel_id=1, source_target_pairs={{0,3},{1,2},{2,1},{3,0},{4,7},{5,6},{6,5},{7,4},{8,11},{9,10},{10,... | collective-permute-start | bytes 589832 | tf_op jit(solution)/shard_map/ppermute | solution.py:343
  (11 other events, 20.3 us)
Sparse Core Ops, SparseCore 0:
  8.9 41.3 all-gather.2
  51.9 39.0 all-gather.4

commit v8 on v7

--- a/solution.py
+++ b/solution.py
@@ -372,7 +372,7 @@
     q = [own_q, swap(own_q), across_q, swap(across_q)]
     onward = after(across, *early)
     late = [to_plane(onward, dp) for dp in (1, -1)]
-    direct_strip = gather(after(out_weight, across)[:, :direct])
+    direct_strip = gather(after(out_weight, *early)[:, :direct])
 
     own_strip = after(own_strip, *early, across_beside)
     half = strip // 2

time: 162 us -> 165 us (1.019)
  waiting for transfers between devices: 70.1 us -> 76.2 us
  starting transfers between devices: 23.2 us -> 20 us
    ppermute x4, waiting for transfers between devices: 25.3 us -> 34.3 us  [to_plane(): return lax.ppermute(x, seq, pairs)]
    ppermute x13, waiting for transfers between devices: 39.5 us -> 35.6 us  [to_lane(): lax.ppermute(x, seq, [(index(p, r, c), index(p, r ^ dr, c ^ dc)) for p, r...]
    ppermute x13, starting transfers between devices: 10 us -> 6.25 us  [to_lane(): lax.ppermute(x, seq, [(index(p, r, c), index(p, r ^ dr, c ^ dc)) for p, r...]
  transfers between devices with their start and end apart: 21 -> 21, of which waited for: 10 -> 12; matrix products, arithmetic and copies ran while one was open for 5% -> 5% of each run, Pallas kernels for 21% -> 20%
where the time goes in v8:
time: 165 us; the launch traced here: 164 us
  waiting for transfers between devices  76.2 us (46%)
  Pallas kernels  41.5 us (25%)
  starting transfers between devices  20 us (12%)
  between operations  13.6 us (8%)
  local copies, waits for them, and re-layouts  13.1 us (8%)
    ppermute x13, waiting for transfers between devices, to_lane(): lax.ppermute(x, seq, [(index(p, r, c), index(p, r ^ dr, c ^ dc)) for p, r...  35.6 us
    ppermute x4, waiting for transfers between devices, to_plane(): return lax.ppermute(x, seq, pairs)  34.3 us
    pallas_call x1, Pallas kernels, attend_begin(): pl.pallas_call(begin_kernel, out_shape=[jax.ShapeDtypeStruct((2, rows, HC...  14.3 us
    pallas_call x2, Pallas kernels, attend_finish(): pl.pallas_call(lambda *refs: finish_kernel(steps, *refs), grid=(1,), out_...  13.1 us
    ppermute x4, starting transfers between devices, to_plane(): return lax.ppermute(x, seq, pairs)  12.1 us
    pallas_call x1, Pallas kernels, project(): pl.pallas_call(lambda *refs: project_kernel(order, groups, refs[:LANES],...  8.33 us
    ppermute x1, waiting for transfers between devices, on_device(): lax.ppermute(sent, 'groups', [(g, (g + dx) % groups) for g in range(group...  6.27 us
    ppermute x13, starting transfers between devices, to_lane(): lax.ppermute(x, seq, [(index(p, r, c), index(p, r ^ dr, c ^ dc)) for p, r...  6.25 us
  transfers between devices with their start and end apart: 21, of which 12 were waited for; matrix products, arithmetic and copies ran while one was open for 5% of the time, Pallas kernels for 20%

profile of v8, /device:TPU:0, one launch (start us, length us, event | category | flops | bytes accessed | tf_op | source)
XLA Modules:
  0.0 164.4 jit_solution(3971941748375590405)
XLA Ops:
  6.5 1.6 constant_dynamic-slice_fusion.1
  8.2 3.1 %shard_map.64 = (bf16[2,256,768]{2,1,0:T(8,128)(2,1)}, bf16[2,256,768]{2,1,0:T(8,128)(2,1)}) custom-call(s32[2]{0:T(128)} %frames.3, bf16[256,1536]{1,0:T(8,128)(2,1)} %k_ref.1, bf16[256,1536]{1,0:T(8,128)(2,1)} %v_ref.1), custom_call_target="tpu_custom_call" | custom-call | tf_op jit(solution)/shard_map/pallas_call | solution.py:71
  11.3 5.0 %collective-permute-start.4 = (bf16[2,256,768]{2,1,0:T(8,128)(2,1)}, bf16[2,256,768]{2,1,0:T(8,128)(2,1)S(1)}, u32[]{:S(2)}, u32[]{:S(2)}) collective-permute-start(bf16[2,256,768]{2,1,0:T(8,128)(2,1)} %get-tuple-element.25.refs_4_), channel_id=1, source_target_pairs={{0,4},{1,5},{2,6},{3,7},{4,8},{5,9},{6,10},{7,11},{8,12},{9,13},{1... | collective-permute-start | bytes 2359304 | tf_op jit(solution)/shard_map/ppermute | solution.py:347
  16.3 1.3 collective-permute-start.5
  17.6 30.5 %collective-permute-done.4.refs_8_ = bf16[2,256,768]{2,1,0:T(8,128)(2,1)S(1)} collective-permute-done((bf16[2,256,768]{2,1,0:T(8,128)(2,1)}, bf16[2,256,768]{2,1,0:T(8,128)(2,1)S(1)}, u32[]{:S(2)}, u32[]{:S(2)}) %collective-permute-start.4) | collective-permute-done | bytes 786464 | tf_op jit(solution)/shard_map/ppermute | solution.py:347
  48.1 3.8 %collective-permute-done.5.refs_10_ = bf16[2,256,768]{2,1,0:T(8,128)(2,1)S(1)} collective-permute-done((bf16[2,256,768]{2,1,0:T(8,128)(2,1)}, bf16[2,256,768]{2,1,0:T(8,128)(2,1)S(1)}, u32[]{:S(2)}, u32[]{:S(2)}) %collective-permute-start.5) | collective-permute-done | bytes 786464 | tf_op jit(solution)/shard_map/ppermute | solution.py:347
  51.8 1.8 %slice.35 = bf16[96,1024]{1,0:T(8,128)(2,1)} slice(bf16[96,3072]{1,0:T(8,128)(2,1)} %param.11), slice={[0:96], [0:1024]} | slice | bytes 393216 | tf_op jit(solution)/shard_map/slice | solution.py:375
  53.7 1.5 collective-permute-start.6
  56.3 1.7 %collective-permute-done.refs_5_ = bf16[256,768]{1,0:T(8,128)(2,1)S(1)} collective-permute-done((bf16[256,768]{1,0:T(8,128)(2,1)S(1)}, bf16[256,768]{1,0:T(8,128)(2,1)S(1)}, u32[]{:S(2)}, u32[]{:S(2)}) %collective-permute-start) | collective-permute-done | bytes 393248 | tf_op jit(solution)/shard_map/ppermute | solution.py:343
  58.0 2.7 %shard_map.65 = (bf16[2,256,384]{2,1,0:T(8,128)(2,1)}, bf16[2,256,384]{2,1,0:T(8,128)(2,1)}) custom-call(s32[2]{0:T(128)} %frames.3, bf16[256,1536]{1,0:T(8,128)(2,1)} %q_ref), custom_call_target="tpu_custom_call" | custom-call | tf_op jit(solution)/shard_map/pallas_call | solution.py:71
  61.3 25.3 %collective-permute-done.6.refs_6_ = bf16[2,256,768]{2,1,0:T(8,128)(2,1)} collective-permute-done((bf16[2,256,768]{2,1,0:T(8,128)(2,1)}, bf16[2,256,768]{2,1,0:T(8,128)(2,1)}, u32[]{:S(2)}, u32[]{:S(2)}) %collective-permute-start.6) | collective-permute-done | bytes 786464 | tf_op jit(solution)/shard_map/ppermute | solution.py:343
  87.7 1.6 slice_bitcast_fusion.7
  89.8 1.3 collective-permute-start.12
  91.1 4.6 %collective-permute-start.10 = (bf16[2,256,768]{2,1,0:T(8,128)(2,1)}, bf16[2,256,768]{2,1,0:T(8,128)(2,1)S(1)}, u32[]{:S(2)}, u32[]{:S(2)}) collective-permute-start(bf16[2,256,768]{2,1,0:T(8,128)(2,1)} %collective-permute-done.6.refs_6_), channel_id=1, source_target_pairs={{0,4},{1,5},{2,6},{3,7},{4,8},{5,9},{6,10},{7,11},{8,12},{9,13},{1... | collective-permute-start | bytes 2359304 | tf_op jit(solution)/shard_map/ppermute | solution.py:347
  97.0 1.5 constant_dynamic-slice_fusion
  98.5 1.5 collective-permute-start.14
  100.7 1.2 collective-permute-done.8.refs_9_
  103.4 14.3 %shard_map.66 = (f32[2,256,384]{2,1,0:T(8,128)}, f32[2,256,384]{2,1,0:T(8,128)}, f32[2,256,128]{2,1,0:T(8,128)}, f32[2,256,128]{2,1,0:T(8,128)}) custom-call(s32[32,32]{1,0:T(8,128)} %refs_0_.2, bf16[2,256,384]{2,1,0:T(8,128)(2,1)} %get-tuple-element.28.refs_0_.refs_1_, bf16[256,384]{1,0:T(8,128)(2,1)} %collective-permute-done.3.refs_1_.refs_3_, ...), custom_call_target="tpu_custom_call" | custom-call | flops 1024 | bytes 1024 | tf_op jit(solution)/shard_map/pallas_call | solution.py:224
  120.9 8.3 %shard_map.67 = (bf16[256,384]{1,0:T(8,128)(2,1)}, bf16[256,384]{1,0:T(8,128)(2,1)}, bf16[256,384]{1,0:T(8,128)(2,1)}) custom-call(s32[32,32]{1,0:T(8,128)} %refs_0_.2, bf16[2,256,384]{2,1,0:T(8,128)(2,1)} %copy-done.2, bf16[256,384]{1,0:T(8,128)(2,1)} %collective-permute-done.2.refs_3_.refs_2_, bf16[256,384]{1,0:T(8,128)(2,1)} %collective-permute-done.3.refs_1_.refs_3_, ...), custom_call_target="tpu_custom_call" | custom-call | flops 1024 | bytes 1024 | tf_op jit(solution)/shard_map/pallas_call | solution.py:250
  129.2 6.3 %collective-permute-done.14.refs_6_ = bf16[1536,512]{1,0:T(8,128)(2,1)} collective-permute-done((bf16[1536,512]{1,0:T(8,128)(2,1)S(1)}, bf16[1536,512]{1,0:T(8,128)(2,1)}, u32[]{:S(2)}, u32[]{:S(2)}) %collective-permute-start.14) | collective-permute-done | bytes 1572896 | tf_op jit(solution)/shard_map/ppermute | solution.py:382
  135.5 2.1 %collective-permute-start.16 = (bf16[256,384]{1,0:T(8,128)(2,1)}, bf16[256,384]{1,0:T(8,128)(2,1)S(1)}, u32[]{:S(2)}, u32[]{:S(2)}) collective-permute-start(bf16[256,384]{1,0:T(8,128)(2,1)} %get-tuple-element.39), channel_id=1, source_target_pairs={{0,2},{1,3},{2,0},{3,1},{4,6},{5,7},{6,4},{7,5},{8,10},{9,11},{10,... | collective-permute-start | bytes 589832 | tf_op jit(solution)/shard_map/ppermute | solution.py:343
  137.8 4.8 %shard_map.68.refs_0_ = bf16[256,384]{1,0:T(8,128)(2,1)} custom-call(s32[32,32]{1,0:T(8,128)} %refs_0_.2, bf16[2,256,384]{2,1,0:T(8,128)(2,1)} %get-tuple-element.28.refs_0_.refs_1_, f32[2,256,384]{2,1,0:T(8,128)} %get-tuple-element.33.refs_6_.refs_2_, f32[2,256,128]{2,1,0:T(8,128)} %get-tuple-element.35.refs_9_.refs_3_, bf16[2,256,768]{2,1,0:T(8,128)(2,1)} %copy-done.1, ...), custom_call_target="tpu_custom_call" | custom-call | flops 1024 | bytes 1024 | tf_op jit(solution)/shard_map/pallas_call | solution.py:250
  143.5 3.8 %collective-permute-done.17.refs_3_ = bf16[256,384]{1,0:T(8,128)(2,1)S(1)} collective-permute-done((bf16[256,384]{1,0:T(8,128)(2,1)}, bf16[256,384]{1,0:T(8,128)(2,1)S(1)}, u32[]{:S(2)}, u32[]{:S(2)}) %collective-permute-start.17) | collective-permute-done | bytes 196640 | tf_op jit(solution)/shard_map/ppermute | solution.py:343
  149.2 8.3 %shard_map.69 = bf16[256,3072]{1,0:T(8,128)(2,1)} custom-call(bf16[256,384]{1,0:T(8,128)(2,1)} %shard_map.68.refs_0_, bf16[256,384]{1,0:T(8,128)(2,1)} %copy-done.12, bf16[256,384]{1,0:T(8,128)(2,1)} %copy-done.11, bf16[256,384]{1,0:T(8,128)(2,1)} %copy-done.13, bf16[1536,1024]{1,0:T(8,128)(2,1)} %all-gather.5.cloned.1.call-done.refs_4_, ...), custom_call_target="tpu_custom_call" | custom-call | tf_op jit(solution)/shard_map/pallas_call | solution.py:313
  (65 shorter events, 12.8 us)
Async XLA Ops:
  6.5 90.4 %all-gather.3.cloned.1.call-start = ((), (), s32[]{:S(2)}) async-start(), calls=%async_computation | async-start | bytes 3342336 | tf_op jit(solution)/shard_map/all_gather | solution.py:356
  8.2 139.2 %all-gather.5.cloned.1.call-start = ((), (), s32[]{:S(2)}) async-start(), calls=%async_computation.1 | async-start | bytes 3342336 | tf_op jit(solution)/shard_map/all_gather | solution.py:356
  11.3 36.8 %collective-permute-start.4 = (bf16[2,256,768]{2,1,0:T(8,128)(2,1)}, bf16[2,256,768]{2,1,0:T(8,128)(2,1)S(1)}, u32[]{:S(2)}, u32[]{:S(2)}) collective-permute-start(bf16[2,256,768]{2,1,0:T(8,128)(2,1)} %get-tuple-element.25.refs_4_), channel_id=1, source_target_pairs={{0,4},{1,5},{2,6},{3,7},{4,8},{5,9},{6,10},{7,11},{8,12},{9,13},{1... | collective-permute-start | bytes 2359304 | tf_op jit(solution)/shard_map/ppermute | solution.py:347
  16.3 35.6 %collective-permute-start.5 = (bf16[2,256,768]{2,1,0:T(8,128)(2,1)}, bf16[2,256,768]{2,1,0:T(8,128)(2,1)S(1)}, u32[]{:S(2)}, u32[]{:S(2)}) collective-permute-start(bf16[2,256,768]{2,1,0:T(8,128)(2,1)} %get-tuple-element.25.refs_4_), channel_id=1, source_target_pairs={{4,0},{5,1},{6,2},{7,3},{8,4},{9,5},{10,6},{11,7},{12,8},{13,9},{1... | collective-permute-start | bytes 2359304 | tf_op jit(solution)/shard_map/ppermute | solution.py:347
  48.1 52.0 %copy-start.3 = (bf16[2,256,768]{2,1,0:T(8,128)(2,1)}, bf16[2,256,768]{2,1,0:T(8,128)(2,1)S(1)}, u32[]{:S(2)}) copy-start(bf16[2,256,768]{2,1,0:T(8,128)(2,1)S(1)} %collective-permute-done.4.refs_8_) | copy-start | bytes 2359300
  51.8 48.2 %copy-start.4 = (bf16[2,256,768]{2,1,0:T(8,128)(2,1)}, bf16[2,256,768]{2,1,0:T(8,128)(2,1)S(1)}, u32[]{:S(2)}) copy-start(bf16[2,256,768]{2,1,0:T(8,128)(2,1)S(1)} %collective-permute-done.5.refs_10_) | copy-start | bytes 2359300
  53.7 32.9 %collective-permute-start.6 = (bf16[2,256,768]{2,1,0:T(8,128)(2,1)}, bf16[2,256,768]{2,1,0:T(8,128)(2,1)}, u32[]{:S(2)}, u32[]{:S(2)}) collective-permute-start(bf16[2,256,768]{2,1,0:T(8,128)(2,1)} %get-tuple-element.29), channel_id=1, source_target_pairs={{0,2},{1,3},{2,0},{3,1},{4,6},{5,7},{6,4},{7,5},{8,10},{9,11},{10,... | collective-permute-start | bytes 2359304 | tf_op jit(solution)/shard_map/ppermute | solution.py:343
  56.2 1.8 %collective-permute-start = (bf16[256,768]{1,0:T(8,128)(2,1)S(1)}, bf16[256,768]{1,0:T(8,128)(2,1)S(1)}, u32[]{:S(2)}, u32[]{:S(2)}) collective-permute-start(bf16[256,768]{1,0:T(8,128)(2,1)S(1)} %slice_bitcast_fusion.5), channel_id=1, source_target_pairs={{0,1},{1,0},{2,3},{3,2},{4,5},{5,4},{6,7},{7,6},{8,9},{9,8},{10,11... | collective-permute-start | bytes 1179656 | tf_op jit(solution)/shard_map/ppermute | solution.py:343
  58.0 31.3 %copy-start.8 = (bf16[256,768]{1,0:T(8,128)(2,1)}, bf16[256,768]{1,0:T(8,128)(2,1)S(1)}, u32[]{:S(2)}) copy-start(bf16[256,768]{1,0:T(8,128)(2,1)S(1)} %collective-permute-done.refs_5_) | copy-start | bytes 1179652
  60.7 35.4 %collective-permute-start.1 = (bf16[2,256,384]{2,1,0:T(8,128)(2,1)}, bf16[2,256,384]{2,1,0:T(8,128)(2,1)S(1)}, u32[]{:S(2)}, u32[]{:S(2)}) collective-permute-start(bf16[2,256,384]{2,1,0:T(8,128)(2,1)} %get-tuple-element.27), channel_id=1, source_target_pairs={{0,2},{1,3},{2,0},{3,1},{4,6},{5,7},{6,4},{7,5},{8,10},{9,11},{10,... | collective-permute-start | bytes 1179656 | tf_op jit(solution)/shard_map/ppermute | solution.py:343
  87.6 9.3 %collective-permute-start.7 = (bf16[256,768]{1,0:T(8,128)(2,1)S(1)}, bf16[256,768]{1,0:T(8,128)(2,1)}, u32[]{:S(2)}, u32[]{:S(2)}) collective-permute-start(bf16[256,768]{1,0:T(8,128)(2,1)S(1)} %slice_bitcast_fusion.2), channel_id=1, source_target_pairs={{0,1},{1,0},{2,3},{3,2},{4,5},{5,4},{6,7},{7,6},{8,9},{9,8},{10,11... | collective-permute-start | bytes 1179656 | tf_op jit(solution)/shard_map/ppermute | solution.py:343
  89.3 10.8 %collective-permute-start.3 = (bf16[256,384]{1,0:T(8,128)(2,1)}, bf16[256,384]{1,0:T(8,128)(2,1)}, u32[]{:S(2)}, u32[]{:S(2)}) collective-permute-start(bf16[256,384]{1,0:T(8,128)(2,1)} %slice_bitcast_fusion.7), channel_id=1, source_target_pairs={{0,1},{1,0},{2,3},{3,2},{4,5},{5,4},{6,7},{7,6},{8,9},{9,8},{10,11... | collective-permute-start | bytes 589832 | tf_op jit(solution)/shard_map/ppermute | solution.py:343
  89.8 27.9 %collective-permute-start.12 = (bf16[2,256,768]{2,1,0:T(8,128)(2,1)}, bf16[2,256,768]{2,1,0:T(8,128)(2,1)S(1)}, u32[]{:S(2)}, u32[]{:S(2)}) collective-permute-start(bf16[2,256,768]{2,1,0:T(8,128)(2,1)} %collective-permute-done.6.refs_6_), channel_id=1, source_target_pairs={{4,0},{5,1},{6,2},{7,3},{8,4},{9,5},{10,6},{11,7},{12,8},{13,9},{1... | collective-permute-start | bytes 2359304 | tf_op jit(solution)/shard_map/ppermute | solution.py:347
  91.1 26.9 %collective-permute-start.10 = (bf16[2,256,768]{2,1,0:T(8,128)(2,1)}, bf16[2,256,768]{2,1,0:T(8,128)(2,1)S(1)}, u32[]{:S(2)}, u32[]{:S(2)}) collective-permute-start(bf16[2,256,768]{2,1,0:T(8,128)(2,1)} %collective-permute-done.6.refs_6_), channel_id=1, source_target_pairs={{0,4},{1,5},{2,6},{3,7},{4,8},{5,9},{6,10},{7,11},{8,12},{9,13},{1... | collective-permute-start | bytes 2359304 | tf_op jit(solution)/shard_map/ppermute | solution.py:347
  96.9 3.5 %collective-permute-start.2 = (bf16[256,384]{1,0:T(8,128)(2,1)}, bf16[256,384]{1,0:T(8,128)(2,1)}, u32[]{:S(2)}, u32[]{:S(2)}) collective-permute-start(bf16[256,384]{1,0:T(8,128)(2,1)} %slice_bitcast_fusion.6), channel_id=1, source_target_pairs={{0,1},{1,0},{2,3},{3,2},{4,5},{5,4},{6,7},{7,6},{8,9},{9,8},{10,11... | collective-permute-start | bytes 589832 | tf_op jit(solution)/shard_map/ppermute | solution.py:343
  98.5 37.0 %collective-permute-start.14 = (bf16[1536,512]{1,0:T(8,128)(2,1)S(1)}, bf16[1536,512]{1,0:T(8,128)(2,1)}, u32[]{:S(2)}, u32[]{:S(2)}) collective-permute-start(bf16[1536,512]{1,0:T(8,128)(2,1)S(1)} %constant_dynamic-slice_fusion), channel_id=1, source_target_pairs={{0,16},{16,0},{1,17},{17,1},{2,18},{18,2},{3,19},{19,3},{4,20},{20... | collective-permute-start | bytes 4718600 | tf_op jit(solution)/shard_map/ppermute | solution.py:382
  100.1 1.8 %collective-permute-start.8 = (bf16[256,768]{1,0:T(8,128)(2,1)S(1)}, bf16[256,768]{1,0:T(8,128)(2,1)S(1)}, u32[]{:S(2)}, u32[]{:S(2)}) collective-permute-start(bf16[256,768]{1,0:T(8,128)(2,1)S(1)} %slice_bitcast_fusion.1), channel_id=1, source_target_pairs={{0,1},{1,0},{2,3},{3,2},{4,5},{5,4},{6,7},{7,6},{8,9},{9,8},{10,11... | collective-permute-start | bytes 1179656 | tf_op jit(solution)/shard_map/ppermute | solution.py:343
  100.4 2.1 %collective-permute-start.9 = (bf16[256,768]{1,0:T(8,128)(2,1)S(1)}, bf16[256,768]{1,0:T(8,128)(2,1)S(1)}, u32[]{:S(2)}, u32[]{:S(2)}) collective-permute-start(bf16[256,768]{1,0:T(8,128)(2,1)S(1)} %slice_bitcast_fusion), channel_id=1, source_target_pairs={{0,1},{1,0},{2,3},{3,2},{4,5},{5,4},{6,7},{7,6},{8,9},{9,8},{10,11... | collective-permute-start | bytes 1179656 | tf_op jit(solution)/shard_map/ppermute | solution.py:343
  117.8 1.8 %collective-permute-start.13 = (bf16[256,768]{1,0:T(8,128)(2,1)S(1)}, bf16[256,768]{1,0:T(8,128)(2,1)S(1)}, u32[]{:S(2)}, u32[]{:S(2)}) collective-permute-start(bf16[256,768]{1,0:T(8,128)(2,1)S(1)} %slice_bitcast_fusion.3), channel_id=1, source_target_pairs={{0,1},{1,0},{2,3},{3,2},{4,5},{5,4},{6,7},{7,6},{8,9},{9,8},{10,11... | collective-permute-start | bytes 1179656 | tf_op jit(solution)/shard_map/ppermute | solution.py:343
  118.1 2.0 %collective-permute-start.11 = (bf16[256,768]{1,0:T(8,128)(2,1)S(1)}, bf16[256,768]{1,0:T(8,128)(2,1)S(1)}, u32[]{:S(2)}, u32[]{:S(2)}) collective-permute-start(bf16[256,768]{1,0:T(8,128)(2,1)S(1)} %slice_bitcast_fusion.4), channel_id=1, source_target_pairs={{0,1},{1,0},{2,3},{3,2},{4,5},{5,4},{6,7},{7,6},{8,9},{9,8},{10,11... | collective-permute-start | bytes 1179656 | tf_op jit(solution)/shard_map/ppermute | solution.py:343
  135.5 11.9 %collective-permute-start.18 = (bf16[1536,512]{1,0:T(8,128)(2,1)}, bf16[1536,512]{1,0:T(8,128)(2,1)S(1)}, u32[]{:S(2)}, u32[]{:S(2)}) collective-permute-start(bf16[1536,512]{1,0:T(8,128)(2,1)} %collective-permute-done.14.refs_6_), channel_id=1, source_target_pairs={{0,1},{1,0},{2,3},{3,2},{4,5},{5,4},{6,7},{7,6},{8,9},{9,8},{10,11... | collective-permute-start | bytes 4718600 | tf_op jit(solution)/shard_map/ppermute | solution.py:396
  135.5 8.0 %collective-permute-start.16 = (bf16[256,384]{1,0:T(8,128)(2,1)}, bf16[256,384]{1,0:T(8,128)(2,1)S(1)}, u32[]{:S(2)}, u32[]{:S(2)}) collective-permute-start(bf16[256,384]{1,0:T(8,128)(2,1)} %get-tuple-element.39), channel_id=1, source_target_pairs={{0,2},{1,3},{2,0},{3,1},{4,6},{5,7},{6,4},{7,5},{8,10},{9,11},{10,... | collective-permute-start | bytes 589832 | tf_op jit(solution)/shard_map/ppermute | solution.py:343
  137.5 5.1 %collective-permute-start.15 = (bf16[256,384]{1,0:T(8,128)(2,1)}, bf16[256,384]{1,0:T(8,128)(2,1)S(1)}, u32[]{:S(2)}, u32[]{:S(2)}) collective-permute-start(bf16[256,384]{1,0:T(8,128)(2,1)} %get-tuple-element.42), channel_id=1, source_target_pairs={{0,1},{1,0},{2,3},{3,2},{4,5},{5,4},{6,7},{7,6},{8,9},{9,8},{10,11... | collective-permute-start | bytes 589832 | tf_op jit(solution)/shard_map/ppermute | solution.py:343
  137.8 9.6 %collective-permute-start.17 = (bf16[256,384]{1,0:T(8,128)(2,1)}, bf16[256,384]{1,0:T(8,128)(2,1)S(1)}, u32[]{:S(2)}, u32[]{:S(2)}) collective-permute-start(bf16[256,384]{1,0:T(8,128)(2,1)} %get-tuple-element.43), channel_id=1, source_target_pairs={{0,3},{1,2},{2,1},{3,0},{4,7},{5,6},{6,5},{7,4},{8,11},{9,10},{10,... | collective-permute-start | bytes 589832 | tf_op jit(solution)/shard_map/ppermute | solution.py:343
  (11 other events, 20.3 us)
Sparse Core Ops, SparseCore 0:
  8.9 42.4 all-gather.2
  53.8 39.7 all-gather.4

commit v9 on v8

--- a/solution.py
+++ b/solution.py
@@ -30,6 +30,21 @@
         cosine, sine = jnp.cos(angle), jnp.sin(angle)
         same[block] = jnp.where(lane < TCH, cosine, 1.0)
         other[block] = jnp.where(lane < half, -sine, jnp.where(lane < TCH, sine, 0.0))
+
+
+def cut(own, strip_at, strip, direct):
+    def kernel(at, own_ref, strip_ref, direct_ref):
+        strip_ref[...] = own_ref[:, pl.ds(pl.multiple_of(at[0], HDIM), strip)]
+        direct_ref[...] = own_ref[:, :direct]
+
+    rows = own.shape[0]
+    vmem = pl.BlockSpec(memory_space=pltpu.VMEM)
+    return pl.pallas_call(
+        kernel,
+        out_shape=[jax.ShapeDtypeStruct((rows, width), jnp.bfloat16) for width in (strip, direct)],
+        in_specs=[pl.BlockSpec(memory_space=pltpu.SMEM), vmem],
+        out_specs=[vmem] * 2,
+    )(jnp.full((1,), strip_at, jnp.int32), own)
 
 
 def lane_of(step):
@@ -359,7 +374,7 @@
     strip = 2 * columns // 3 // (groups * 2 * HDIM) * 2 * HDIM
     direct = columns - groups * strip
     strip_at = direct + lax.axis_index("groups") * strip
-    own_strip = gather(lax.dynamic_slice_in_dim(out_weight, strip_at, strip, 1))
+    own_strip, direct_strip = [gather(x) for x in cut(out_weight, strip_at, strip, direct)]
 
     own, other = pack(pack_kv_kernel, frame_index, (keys, values), 2 * HC)
     across = to_lane(other, 1, 0)
@@ -372,7 +387,6 @@
     q = [own_q, swap(own_q), across_q, swap(across_q)]
     onward = after(across, *early)
     late = [to_plane(onward, dp) for dp in (1, -1)]
-    direct_strip = gather(after(out_weight, *early)[:, :direct])
 
     own_strip = after(own_strip, *early, across_beside)
     half = strip // 2

time: 165 us -> 131 us (0.79)
  waiting for transfers between devices: 76.2 us -> 43.5 us
  local copies, waits for them, and re-layouts: 13.1 us -> 9.8 us
  Pallas kernels: 41.5 us -> 43.4 us
    ppermute x4, waiting for transfers between devices: 34.3 us -> 11.7 us  [to_plane(): return lax.ppermute(x, seq, pairs)]
    ppermute x1, waiting for transfers between devices: 6.27 us -> 0.01 us  [on_device(): lax.ppermute(sent, 'groups', [(g, (g + dx) % groups) for g in range(group...]
    ppermute x13, waiting for transfers between devices: 35.6 us -> 31 us  [to_lane(): lax.ppermute(x, seq, [(index(p, r, c), index(p, r ^ dr, c ^ dc)) for p, r...]
    pallas_call x0 -> x1, Pallas kernels: none -> 1.84 us  [cut(): pl.pallas_call(kernel, out_shape=[jax.ShapeDtypeStruct((rows, width), jnp...]
    slice x1 -> x0, local copies, waits for them, and re-layouts: 1.82 us -> none  [on_device(): direct_strip = gather(after(out_weight, *early)[:, :direct])]
  transfers between devices with their start and end apart: 21 -> 21, of which waited for: 12 -> 9; matrix products, arithmetic and copies ran while one was open for 5% -> 5% of each run, Pallas kernels for 20% -> 26%
where the time goes in v9:
time: 131 us; the launch traced here: 130 us
  waiting for transfers between devices  43.5 us (33%)
  Pallas kernels  43.4 us (33%)
  starting transfers between devices  19.3 us (15%)
  between operations  13.7 us (10%)
  local copies, waits for them, and re-layouts  9.8 us (7%)
    ppermute x13, waiting for transfers between devices, to_lane(): lax.ppermute(x, seq, [(index(p, r, c), index(p, r ^ dr, c ^ dc)) for p, r...  31 us
    pallas_call x1, Pallas kernels, attend_begin(): pl.pallas_call(begin_kernel, out_shape=[jax.ShapeDtypeStruct((2, rows, HC...  14.3 us
    pallas_call x2, Pallas kernels, attend_finish(): pl.pallas_call(lambda *refs: finish_kernel(steps, *refs), grid=(1,), out_...  13.1 us
    ppermute x4, waiting for transfers between devices, to_plane(): return lax.ppermute(x, seq, pairs)  11.7 us
    ppermute x4, starting transfers between devices, to_plane(): return lax.ppermute(x, seq, pairs)  10.7 us
    pallas_call x1, Pallas kernels, project(): pl.pallas_call(lambda *refs: project_kernel(order, groups, refs[:LANES],...  8.33 us
    ppermute x13, starting transfers between devices, to_lane(): lax.ppermute(x, seq, [(index(p, r, c), index(p, r ^ dr, c ^ dc)) for p, r...  6.8 us
    pallas_call x2, Pallas kernels, pack(): pl.pallas_call(kernel, out_shape=[jax.ShapeDtypeStruct((2, count, width),...  5.8 us
  transfers between devices with their start and end apart: 21, of which 9 were waited for; matrix products, arithmetic and copies ran while one was open for 5% of the time, Pallas kernels for 26%

profile of v9, /device:TPU:0, one launch (start us, length us, event | category | flops | bytes accessed | tf_op | source)
XLA Modules:
  0.0 129.6 jit_solution(8331237135725273365)
XLA Ops:
  6.5 1.8 %shard_map.66 = (bf16[96,1024]{1,0:T(8,128)(2,1)}, bf16[96,1024]{1,0:T(8,128)(2,1)}) custom-call(s32[1]{0:T(128)} %bitcast.3.at, bf16[96,3072]{1,0:T(8,128)(2,1)} %own_ref.1), custom_call_target="tpu_custom_call" | custom-call | tf_op jit(solution)/shard_map/pallas_call | solution.py:42
  9.2 3.1 %shard_map.64 = (bf16[2,256,768]{2,1,0:T(8,128)(2,1)}, bf16[2,256,768]{2,1,0:T(8,128)(2,1)}) custom-call(s32[2]{0:T(128)} %frames.3, bf16[256,1536]{1,0:T(8,128)(2,1)} %k_ref.1, bf16[256,1536]{1,0:T(8,128)(2,1)} %v_ref.1), custom_call_target="tpu_custom_call" | custom-call | tf_op jit(solution)/shard_map/pallas_call | solution.py:86
  12.2 3.0 %collective-permute-start.6 = (bf16[2,256,768]{2,1,0:T(8,128)(2,1)}, bf16[2,256,768]{2,1,0:T(8,128)(2,1)S(1)}, u32[]{:S(2)}, u32[]{:S(2)}) collective-permute-start(bf16[2,256,768]{2,1,0:T(8,128)(2,1)} %get-tuple-element.31), channel_id=1, source_target_pairs={{0,2},{1,3},{2,0},{3,1},{4,6},{5,7},{6,4},{7,5},{8,10},{9,11},{10,... | collective-permute-start | bytes 2359304 | tf_op jit(solution)/shard_map/ppermute | solution.py:358
  16.3 3.5 %collective-permute-start.4 = (bf16[2,256,768]{2,1,0:T(8,128)(2,1)}, bf16[2,256,768]{2,1,0:T(8,128)(2,1)S(1)}, u32[]{:S(2)}, u32[]{:S(2)}) collective-permute-start(bf16[2,256,768]{2,1,0:T(8,128)(2,1)} %get-tuple-element.26.refs_4_), channel_id=1, source_target_pairs={{0,4},{1,5},{2,6},{3,7},{4,8},{5,9},{6,10},{7,11},{8,12},{9,13},{1... | collective-permute-start | bytes 2359304 | tf_op jit(solution)/shard_map/ppermute | solution.py:362
  19.8 1.3 collective-permute-start.5
  21.2 2.7 %shard_map.65 = (bf16[2,256,384]{2,1,0:T(8,128)(2,1)}, bf16[2,256,384]{2,1,0:T(8,128)(2,1)}) custom-call(s32[2]{0:T(128)} %frames.3, bf16[256,1536]{1,0:T(8,128)(2,1)} %q_ref), custom_call_target="tpu_custom_call" | custom-call | tf_op jit(solution)/shard_map/pallas_call | solution.py:86
  24.4 23.6 %collective-permute-done.6.refs_6_ = bf16[2,256,768]{2,1,0:T(8,128)(2,1)S(1)} collective-permute-done((bf16[2,256,768]{2,1,0:T(8,128)(2,1)}, bf16[2,256,768]{2,1,0:T(8,128)(2,1)S(1)}, u32[]{:S(2)}, u32[]{:S(2)}) %collective-permute-start.6) | collective-permute-done | bytes 786464 | tf_op jit(solution)/shard_map/ppermute | solution.py:358
  48.1 1.8 %slice_bitcast_fusion.7 = bf16[256,384]{1,0:T(8,128)(2,1)} fusion(bf16[2,256,384]{2,1,0:T(8,128)(2,1)} %get-tuple-element.29.refs_0_.refs_1_), kind=kLoop, calls=%fused_computation.7 | loop fusion | bytes 393216 | tf_op jit(solution)/shard_map/squeeze | solution.py:365
  50.2 3.2 %collective-permute-done.5.refs_10_ = bf16[2,256,768]{2,1,0:T(8,128)(2,1)} collective-permute-done((bf16[2,256,768]{2,1,0:T(8,128)(2,1)}, bf16[2,256,768]{2,1,0:T(8,128)(2,1)}, u32[]{:S(2)}, u32[]{:S(2)}) %collective-permute-start.5) | collective-permute-done | bytes 786464 | tf_op jit(solution)/shard_map/ppermute | solution.py:362
  53.4 1.3 collective-permute-start.12
  54.7 4.6 %collective-permute-start.10 = (bf16[2,256,768]{2,1,0:T(8,128)(2,1)S(1)}, bf16[2,256,768]{2,1,0:T(8,128)(2,1)S(1)}, u32[]{:S(2)}, u32[]{:S(2)}) collective-permute-start(bf16[2,256,768]{2,1,0:T(8,128)(2,1)S(1)} %collective-permute-done.6.refs_6_), channel_id=1, source_target_pairs={{0,4},{1,5},{2,6},{3,7},{4,8},{5,9},{6,10},{7,11},{8,12},{9,13},{1... | collective-permute-start | bytes 2359304 | tf_op jit(solution)/shard_map/ppermute | solution.py:362
  60.0 1.5 %constant_dynamic-slice_fusion = bf16[1536,512]{1,0:T(8,128)(2,1)S(1)} fusion(bf16[1536,1024]{1,0:T(8,128)(2,1)} %all-gather.3.cloned.1.call-done.refs_5_, s32[]{:T(128)S(6)} %select_n.3), kind=kLoop, calls=%fused_computation.8 | loop fusion | bytes 3145732 | tf_op jit(solution)/shard_map/dynamic_slice | solution.py:394
  61.6 1.5 %collective-permute-start.14 = (bf16[1536,512]{1,0:T(8,128)(2,1)S(1)}, bf16[1536,512]{1,0:T(8,128)(2,1)}, u32[]{:S(2)}, u32[]{:S(2)}) collective-permute-start(bf16[1536,512]{1,0:T(8,128)(2,1)S(1)} %constant_dynamic-slice_fusion), channel_id=1, source_target_pairs={{0,16},{16,0},{1,17},{17,1},{2,18},{18,2},{3,19},{19,3},{4,20},{20... | collective-permute-start | bytes 4718600 | tf_op jit(solution)/shard_map/ppermute | solution.py:396
  64.8 1.2 collective-permute-done.8.refs_9_
  67.5 14.3 %shard_map.67 = (f32[2,256,384]{2,1,0:T(8,128)}, f32[2,256,384]{2,1,0:T(8,128)}, f32[2,256,128]{2,1,0:T(8,128)}, f32[2,256,128]{2,1,0:T(8,128)}) custom-call(s32[32,32]{1,0:T(8,128)} %refs_0_.2, bf16[2,256,384]{2,1,0:T(8,128)(2,1)} %get-tuple-element.29.refs_0_.refs_1_, bf16[256,384]{1,0:T(8,128)(2,1)} %collective-permute-done.3.refs_1_.refs_3_, ...), custom_call_target="tpu_custom_call" | custom-call | flops 1024 | bytes 1024 | tf_op jit(solution)/shard_map/pallas_call | solution.py:239
  81.8 5.6 %collective-permute-done.12.refs_12_.refs_6_ = bf16[2,256,768]{2,1,0:T(8,128)(2,1)S(1)} collective-permute-done((bf16[2,256,768]{2,1,0:T(8,128)(2,1)S(1)}, bf16[2,256,768]{2,1,0:T(8,128)(2,1)S(1)}, u32[]{:S(2)}, u32[]{:S(2)}) %collective-permute-start.12) | collective-permute-done | bytes 786464 | tf_op jit(solution)/shard_map/ppermute | solution.py:362
  87.5 2.9 %collective-permute-done.10.refs_10_.refs_4_ = bf16[2,256,768]{2,1,0:T(8,128)(2,1)S(1)} collective-permute-done((bf16[2,256,768]{2,1,0:T(8,128)(2,1)S(1)}, bf16[2,256,768]{2,1,0:T(8,128)(2,1)S(1)}, u32[]{:S(2)}, u32[]{:S(2)}) %collective-permute-start.10) | collective-permute-done | bytes 786464 | tf_op jit(solution)/shard_map/ppermute | solution.py:362
  90.6 1.7 %collective-permute-done.11.refs_11_.refs_5_ = bf16[256,768]{1,0:T(8,128)(2,1)S(1)} collective-permute-done((bf16[256,768]{1,0:T(8,128)(2,1)S(1)}, bf16[256,768]{1,0:T(8,128)(2,1)S(1)}, u32[]{:S(2)}, u32[]{:S(2)}) %collective-permute-start.11) | collective-permute-done | bytes 393248 | tf_op jit(solution)/shard_map/ppermute | solution.py:358
  93.0 8.3 %shard_map.68 = (bf16[256,384]{1,0:T(8,128)(2,1)}, bf16[256,384]{1,0:T(8,128)(2,1)}, bf16[256,384]{1,0:T(8,128)(2,1)}) custom-call(s32[32,32]{1,0:T(8,128)} %refs_0_.2, bf16[2,256,384]{2,1,0:T(8,128)(2,1)} %copy-done.2, bf16[256,384]{1,0:T(8,128)(2,1)} %collective-permute-done.2.refs_3_.refs_2_, bf16[256,384]{1,0:T(8,128)(2,1)} %collective-permute-done.3.refs_1_.refs_3_, ...), custom_call_target="tpu_custom_call" | custom-call | flops 1024 | bytes 1024 | tf_op jit(solution)/shard_map/pallas_call | solution.py:265
  101.5 1.4 %collective-permute-start.16 = (bf16[256,384]{1,0:T(8,128)(2,1)}, bf16[256,384]{1,0:T(8,128)(2,1)S(1)}, u32[]{:S(2)}, u32[]{:S(2)}) collective-permute-start(bf16[256,384]{1,0:T(8,128)(2,1)} %get-tuple-element.41), channel_id=1, source_target_pairs={{0,2},{1,3},{2,0},{3,1},{4,6},{5,7},{6,4},{7,5},{8,10},{9,11},{10,... | collective-permute-start | bytes 589832 | tf_op jit(solution)/shard_map/ppermute | solution.py:358
  103.7 4.8 %shard_map.69.refs_0_ = bf16[256,384]{1,0:T(8,128)(2,1)} custom-call(s32[32,32]{1,0:T(8,128)} %refs_0_.2, bf16[2,256,384]{2,1,0:T(8,128)(2,1)} %get-tuple-element.29.refs_0_.refs_1_, f32[2,256,384]{2,1,0:T(8,128)} %get-tuple-element.35.refs_6_.refs_2_, f32[2,256,128]{2,1,0:T(8,128)} %get-tuple-element.37.refs_9_.refs_3_, bf16[2,256,768]{2,1,0:T(8,128)(2,1)} %copy-done.1, ...), custom_call_target="tpu_custom_call" | custom-call | flops 1024 | bytes 1024 | tf_op jit(solution)/shard_map/pallas_call | solution.py:265
  109.4 3.1 %collective-permute-done.17.refs_3_ = bf16[256,384]{1,0:T(8,128)(2,1)S(1)} collective-permute-done((bf16[256,384]{1,0:T(8,128)(2,1)}, bf16[256,384]{1,0:T(8,128)(2,1)S(1)}, u32[]{:S(2)}, u32[]{:S(2)}) %collective-permute-start.17) | collective-permute-done | bytes 196640 | tf_op jit(solution)/shard_map/ppermute | solution.py:358
  113.2 1.2 copy-done.5
  114.4 8.3 %shard_map.70 = bf16[256,3072]{1,0:T(8,128)(2,1)} custom-call(bf16[256,384]{1,0:T(8,128)(2,1)} %shard_map.69.refs_0_, bf16[256,384]{1,0:T(8,128)(2,1)} %copy-done.12, bf16[256,384]{1,0:T(8,128)(2,1)} %copy-done.11, bf16[256,384]{1,0:T(8,128)(2,1)} %copy-done.13, bf16[1536,1024]{1,0:T(8,128)(2,1)} %all-gather.5.cloned.1.call-done.refs_4_, ...), custom_call_target="tpu_custom_call" | custom-call | tf_op jit(solution)/shard_map/pallas_call | solution.py:328
  (64 shorter events, 10.2 us)
Async XLA Ops:
  6.5 53.5 %all-gather.3.cloned.1.call-start = ((), (), s32[]{:S(2)}) async-start(), calls=%async_computation | async-start | bytes 3342336 | tf_op jit(solution)/shard_map/all_gather | solution.py:371
  8.4 100.1 %all-gather.5.cloned.1.call-start = ((), (), s32[]{:S(2)}) async-start(), calls=%async_computation.1 | async-start | bytes 3342336 | tf_op jit(solution)/shard_map/all_gather | solution.py:371
  12.2 35.7 %collective-permute-start.6 = (bf16[2,256,768]{2,1,0:T(8,128)(2,1)}, bf16[2,256,768]{2,1,0:T(8,128)(2,1)S(1)}, u32[]{:S(2)}, u32[]{:S(2)}) collective-permute-start(bf16[2,256,768]{2,1,0:T(8,128)(2,1)} %get-tuple-element.31), channel_id=1, source_target_pairs={{0,2},{1,3},{2,0},{3,1},{4,6},{5,7},{6,4},{7,5},{8,10},{9,11},{10,... | collective-permute-start | bytes 2359304 | tf_op jit(solution)/shard_map/ppermute | solution.py:358
  16.2 4.9 %collective-permute-start = (bf16[256,768]{1,0:T(8,128)(2,1)S(1)}, bf16[256,768]{1,0:T(8,128)(2,1)S(1)}, u32[]{:S(2)}, u32[]{:S(2)}) collective-permute-start(bf16[256,768]{1,0:T(8,128)(2,1)S(1)} %slice_bitcast_fusion.5), channel_id=1, source_target_pairs={{0,1},{1,0},{2,3},{3,2},{4,5},{5,4},{6,7},{7,6},{8,9},{9,8},{10,11... | collective-permute-start | bytes 1179656 | tf_op jit(solution)/shard_map/ppermute | solution.py:358
  16.3 33.9 %collective-permute-start.4 = (bf16[2,256,768]{2,1,0:T(8,128)(2,1)}, bf16[2,256,768]{2,1,0:T(8,128)(2,1)S(1)}, u32[]{:S(2)}, u32[]{:S(2)}) collective-permute-start(bf16[2,256,768]{2,1,0:T(8,128)(2,1)} %get-tuple-element.26.refs_4_), channel_id=1, source_target_pairs={{0,4},{1,5},{2,6},{3,7},{4,8},{5,9},{6,10},{7,11},{8,12},{9,13},{1... | collective-permute-start | bytes 2359304 | tf_op jit(solution)/shard_map/ppermute | solution.py:362
  19.8 33.5 %collective-permute-start.5 = (bf16[2,256,768]{2,1,0:T(8,128)(2,1)}, bf16[2,256,768]{2,1,0:T(8,128)(2,1)}, u32[]{:S(2)}, u32[]{:S(2)}) collective-permute-start(bf16[2,256,768]{2,1,0:T(8,128)(2,1)} %get-tuple-element.26.refs_4_), channel_id=1, source_target_pairs={{4,0},{5,1},{6,2},{7,3},{8,4},{9,5},{10,6},{11,7},{12,8},{13,9},{1... | collective-permute-start | bytes 2359304 | tf_op jit(solution)/shard_map/ppermute | solution.py:362
  21.2 29.0 %copy-start.8 = (bf16[256,768]{1,0:T(8,128)(2,1)}, bf16[256,768]{1,0:T(8,128)(2,1)S(1)}, u32[]{:S(2)}) copy-start(bf16[256,768]{1,0:T(8,128)(2,1)S(1)} %collective-permute-done.refs_5_) | copy-start | bytes 1179652
  23.9 35.4 %collective-permute-start.1 = (bf16[2,256,384]{2,1,0:T(8,128)(2,1)}, bf16[2,256,384]{2,1,0:T(8,128)(2,1)S(1)}, u32[]{:S(2)}, u32[]{:S(2)}) collective-permute-start(bf16[2,256,384]{2,1,0:T(8,128)(2,1)} %get-tuple-element.28), channel_id=1, source_target_pairs={{0,2},{1,3},{2,0},{3,1},{4,6},{5,7},{6,4},{7,5},{8,10},{9,11},{10,... | collective-permute-start | bytes 1179656 | tf_op jit(solution)/shard_map/ppermute | solution.py:358
  48.0 13.6 %copy-start.3 = (bf16[2,256,768]{2,1,0:T(8,128)(2,1)}, bf16[2,256,768]{2,1,0:T(8,128)(2,1)S(1)}, u32[]{:S(2)}) copy-start(bf16[2,256,768]{2,1,0:T(8,128)(2,1)S(1)} %collective-permute-done.6.refs_6_) | copy-start | bytes 2359300
  48.0 12.1 %collective-permute-start.7 = (bf16[256,768]{1,0:T(8,128)(2,1)S(1)}, bf16[256,768]{1,0:T(8,128)(2,1)}, u32[]{:S(2)}, u32[]{:S(2)}) collective-permute-start(bf16[256,768]{1,0:T(8,128)(2,1)S(1)} %slice_bitcast_fusion.2), channel_id=1, source_target_pairs={{0,1},{1,0},{2,3},{3,2},{4,5},{5,4},{6,7},{7,6},{8,9},{9,8},{10,11... | collective-permute-start | bytes 1179656 | tf_op jit(solution)/shard_map/ppermute | solution.py:358
  49.9 14.3 %collective-permute-start.3 = (bf16[256,384]{1,0:T(8,128)(2,1)}, bf16[256,384]{1,0:T(8,128)(2,1)}, u32[]{:S(2)}, u32[]{:S(2)}) collective-permute-start(bf16[256,384]{1,0:T(8,128)(2,1)} %slice_bitcast_fusion.7), channel_id=1, source_target_pairs={{0,1},{1,0},{2,3},{3,2},{4,5},{5,4},{6,7},{7,6},{8,9},{9,8},{10,11... | collective-permute-start | bytes 589832 | tf_op jit(solution)/shard_map/ppermute | solution.py:358
  50.2 12.9 %copy-start.4 = (bf16[2,256,768]{2,1,0:T(8,128)(2,1)}, bf16[2,256,768]{2,1,0:T(8,128)(2,1)S(1)}, u32[]{:S(2)}) copy-start(bf16[2,256,768]{2,1,0:T(8,128)(2,1)S(1)} %collective-permute-done.4.refs_8_) | copy-start | bytes 2359300
  53.4 34.0 %collective-permute-start.12 = (bf16[2,256,768]{2,1,0:T(8,128)(2,1)S(1)}, bf16[2,256,768]{2,1,0:T(8,128)(2,1)S(1)}, u32[]{:S(2)}, u32[]{:S(2)}) collective-permute-start(bf16[2,256,768]{2,1,0:T(8,128)(2,1)S(1)} %collective-permute-done.6.refs_6_), channel_id=1, source_target_pairs={{4,0},{5,1},{6,2},{7,3},{8,4},{9,5},{10,6},{11,7},{12,8},{13,9},{1... | collective-permute-start | bytes 2359304 | tf_op jit(solution)/shard_map/ppermute | solution.py:362
  54.7 35.8 %collective-permute-start.10 = (bf16[2,256,768]{2,1,0:T(8,128)(2,1)S(1)}, bf16[2,256,768]{2,1,0:T(8,128)(2,1)S(1)}, u32[]{:S(2)}, u32[]{:S(2)}) collective-permute-start(bf16[2,256,768]{2,1,0:T(8,128)(2,1)S(1)} %collective-permute-done.6.refs_6_), channel_id=1, source_target_pairs={{0,4},{1,5},{2,6},{3,7},{4,8},{5,9},{6,10},{7,11},{8,12},{9,13},{1... | collective-permute-start | bytes 2359304 | tf_op jit(solution)/shard_map/ppermute | solution.py:362
  60.0 4.5 %collective-permute-start.2 = (bf16[256,384]{1,0:T(8,128)(2,1)}, bf16[256,384]{1,0:T(8,128)(2,1)}, u32[]{:S(2)}, u32[]{:S(2)}) collective-permute-start(bf16[256,384]{1,0:T(8,128)(2,1)} %slice_bitcast_fusion.6), channel_id=1, source_target_pairs={{0,1},{1,0},{2,3},{3,2},{4,5},{5,4},{6,7},{7,6},{8,9},{9,8},{10,11... | collective-permute-start | bytes 589832 | tf_op jit(solution)/shard_map/ppermute | solution.py:358
  61.6 39.7 %collective-permute-start.14 = (bf16[1536,512]{1,0:T(8,128)(2,1)S(1)}, bf16[1536,512]{1,0:T(8,128)(2,1)}, u32[]{:S(2)}, u32[]{:S(2)}) collective-permute-start(bf16[1536,512]{1,0:T(8,128)(2,1)S(1)} %constant_dynamic-slice_fusion), channel_id=1, source_target_pairs={{0,16},{16,0},{1,17},{17,1},{2,18},{18,2},{3,19},{19,3},{4,20},{20... | collective-permute-start | bytes 4718600 | tf_op jit(solution)/shard_map/ppermute | solution.py:396
  64.2 1.8 %collective-permute-start.8 = (bf16[256,768]{1,0:T(8,128)(2,1)S(1)}, bf16[256,768]{1,0:T(8,128)(2,1)S(1)}, u32[]{:S(2)}, u32[]{:S(2)}) collective-permute-start(bf16[256,768]{1,0:T(8,128)(2,1)S(1)} %slice_bitcast_fusion.1), channel_id=1, source_target_pairs={{0,1},{1,0},{2,3},{3,2},{4,5},{5,4},{6,7},{7,6},{8,9},{9,8},{10,11... | collective-permute-start | bytes 1179656 | tf_op jit(solution)/shard_map/ppermute | solution.py:358
  64.5 2.0 %collective-permute-start.9 = (bf16[256,768]{1,0:T(8,128)(2,1)S(1)}, bf16[256,768]{1,0:T(8,128)(2,1)S(1)}, u32[]{:S(2)}, u32[]{:S(2)}) collective-permute-start(bf16[256,768]{1,0:T(8,128)(2,1)S(1)} %slice_bitcast_fusion), channel_id=1, source_target_pairs={{0,1},{1,0},{2,3},{3,2},{4,5},{5,4},{6,7},{7,6},{8,9},{9,8},{10,11... | collective-permute-start | bytes 1179656 | tf_op jit(solution)/shard_map/ppermute | solution.py:358
  87.5 3.1 %collective-permute-start.13 = (bf16[256,768]{1,0:T(8,128)(2,1)S(1)}, bf16[256,768]{1,0:T(8,128)(2,1)S(1)}, u32[]{:S(2)}, u32[]{:S(2)}) collective-permute-start(bf16[256,768]{1,0:T(8,128)(2,1)S(1)} %slice_bitcast_fusion.3), channel_id=1, source_target_pairs={{0,1},{1,0},{2,3},{3,2},{4,5},{5,4},{6,7},{7,6},{8,9},{9,8},{10,11... | collective-permute-start | bytes 1179656 | tf_op jit(solution)/shard_map/ppermute | solution.py:358
  90.5 1.8 %collective-permute-start.11 = (bf16[256,768]{1,0:T(8,128)(2,1)S(1)}, bf16[256,768]{1,0:T(8,128)(2,1)S(1)}, u32[]{:S(2)}, u32[]{:S(2)}) collective-permute-start(bf16[256,768]{1,0:T(8,128)(2,1)S(1)} %slice_bitcast_fusion.4), channel_id=1, source_target_pairs={{0,1},{1,0},{2,3},{3,2},{4,5},{5,4},{6,7},{7,6},{8,9},{9,8},{10,11... | collective-permute-start | bytes 1179656 | tf_op jit(solution)/shard_map/ppermute | solution.py:358
  101.3 11.3 %collective-permute-start.18 = (bf16[1536,512]{1,0:T(8,128)(2,1)}, bf16[1536,512]{1,0:T(8,128)(2,1)S(1)}, u32[]{:S(2)}, u32[]{:S(2)}) collective-permute-start(bf16[1536,512]{1,0:T(8,128)(2,1)} %collective-permute-done.14.refs_6_), channel_id=1, source_target_pairs={{0,1},{1,0},{2,3},{3,2},{4,5},{5,4},{6,7},{7,6},{8,9},{9,8},{10,11... | collective-permute-start | bytes 4718600 | tf_op jit(solution)/shard_map/ppermute | solution.py:410
  101.5 7.9 %collective-permute-start.16 = (bf16[256,384]{1,0:T(8,128)(2,1)}, bf16[256,384]{1,0:T(8,128)(2,1)S(1)}, u32[]{:S(2)}, u32[]{:S(2)}) collective-permute-start(bf16[256,384]{1,0:T(8,128)(2,1)} %get-tuple-element.41), channel_id=1, source_target_pairs={{0,2},{1,3},{2,0},{3,1},{4,6},{5,7},{6,4},{7,5},{8,10},{9,11},{10,... | collective-permute-start | bytes 589832 | tf_op jit(solution)/shard_map/ppermute | solution.py:358
  102.9 5.7 %collective-permute-start.15 = (bf16[256,384]{1,0:T(8,128)(2,1)}, bf16[256,384]{1,0:T(8,128)(2,1)S(1)}, u32[]{:S(2)}, u32[]{:S(2)}) collective-permute-start(bf16[256,384]{1,0:T(8,128)(2,1)} %get-tuple-element.44), channel_id=1, source_target_pairs={{0,1},{1,0},{2,3},{3,2},{4,5},{5,4},{6,7},{7,6},{8,9},{9,8},{10,11... | collective-permute-start | bytes 589832 | tf_op jit(solution)/shard_map/ppermute | solution.py:358
  102.9 9.6 %collective-permute-start.17 = (bf16[256,384]{1,0:T(8,128)(2,1)}, bf16[256,384]{1,0:T(8,128)(2,1)S(1)}, u32[]{:S(2)}, u32[]{:S(2)}) collective-permute-start(bf16[256,384]{1,0:T(8,128)(2,1)} %get-tuple-element.45), channel_id=1, source_target_pairs={{0,3},{1,2},{2,1},{3,0},{4,7},{5,6},{6,5},{7,4},{8,11},{9,10},{10,... | collective-permute-start | bytes 589832 | tf_op jit(solution)/shard_map/ppermute | solution.py:358
  (11 other events, 21.9 us)
Sparse Core Ops, SparseCore 0:
  8.9 43.0 all-gather.2
  53.6 38.8 all-gather.4

commit v10 on v8

--- a/solution.py
+++ b/solution.py
@@ -30,6 +30,23 @@
         cosine, sine = jnp.cos(angle), jnp.sin(angle)
         same[block] = jnp.where(lane < TCH, cosine, 1.0)
         other[block] = jnp.where(lane < half, -sine, jnp.where(lane < TCH, sine, 0.0))
+
+
+def cut(own, start, widths):
+    def kernel(at, own_ref, *refs):
+        begin = 0
+        for ref, width in zip(refs, widths):
+            ref[...] = own_ref[:, pl.ds(pl.multiple_of(at[0] + begin, HDIM), width)]
+            begin += width
+
+    rows = own.shape[0]
+    vmem = pl.BlockSpec(memory_space=pltpu.VMEM)
+    return pl.pallas_call(
+        kernel,
+        out_shape=[jax.ShapeDtypeStruct((rows, width), jnp.bfloat16) for width in widths],
+        in_specs=[pl.BlockSpec(memory_space=pltpu.SMEM), vmem],
+        out_specs=[vmem] * len(widths),
+    )(jnp.full((1,), start, jnp.int32), own)
 
 
 def lane_of(step):
@@ -275,7 +292,7 @@
     )
 
 
-def project_kernel(order, groups, a_refs, w_refs, o_ref, by_lane, by_shard):
+def project_kernel(order, groups, steps, a_refs, w_refs, o_ref, by_lane, by_shard):
     step = pl.program_id(0)
     depth = by_shard.shape[1]
     shard = depth // len(order)
@@ -291,27 +308,34 @@
         by_shard[...] = jnp.concatenate(parts, axis=1)
 
     mine, core = lax.axis_index("groups"), lax.axis_index("core")
-    widths = [w.shape[1] for w in w_refs]
-    steps = o_ref.shape[1] // (widths[0] + groups * widths[1])
-    direct, strip, half = widths[0] * steps, widths[1] * steps, widths[1] * steps // 2
-    places = [0, direct + mine * strip]
-    for dx in range(1, groups):
-        start = direct + lax.rem(mine + groups - dx, groups) * strip
-        places += [start + core * half, start + (1 - core) * half]
-    for w_ref, place, width in zip(w_refs, places, widths):
-        out = jnp.dot(by_shard[...], w_ref[...], preferred_element_type=jnp.float32)
-        at = pl.multiple_of(place + step * width, HDIM)
+    strip = o_ref.shape[1] // groups
+    per_part = 2 * groups - 1
+    begin = 0
+    for part in range(len(w_refs) // per_part):
+        own_ref, *half_refs = w_refs[part * per_part : (part + 1) * per_part]
+        width = own_ref.shape[1]
+        half = width // 2
+        out = jnp.dot(by_shard[...], own_ref[...], preferred_element_type=jnp.float32)
+        at = pl.multiple_of(mine * strip + begin + step * width, HDIM)
         o_ref[:, pl.ds(at, width)] = out.astype(jnp.bfloat16)
+        for dx in range(1, groups):
+            both = jnp.concatenate([ref[...] for ref in half_refs[2 * dx - 2 : 2 * dx]], axis=1)
+            out = jnp.dot(by_shard[...], both, preferred_element_type=jnp.float32).astype(jnp.bfloat16)
+            base = lax.rem(mine + groups - dx, groups) * strip + begin
+            for i, which in enumerate((core, 1 - core)):
+                at = pl.multiple_of(base + which * (half * steps) + step * half, HDIM)
+                o_ref[:, pl.ds(at, half)] = out[:, i * half : (i + 1) * half]
+        begin += width * steps
 
 
 def project(attended, weights, order, groups):
     count, depth = attended[0].shape
     channels = weights[0].shape[0]
     steps = weights[-1].shape[1] // HDIM
-    columns = weights[0].shape[1] + groups * weights[1].shape[1]
+    columns = groups * sum(w.shape[1] for w in weights[:: 2 * groups - 1])
     whole = pl.BlockSpec((count, depth), lambda n: (0, 0))
     return pl.pallas_call(
-        lambda *refs: project_kernel(order, groups, refs[:LANES], refs[LANES:-3], *refs[-3:]),
+        lambda *refs: project_kernel(order, groups, steps, refs[:LANES], refs[LANES:-3], *refs[-3:]),
         out_shape=jax.ShapeDtypeStruct((count, columns), jnp.bfloat16),
         grid=(steps,),
         in_specs=[whole] * LANES
@@ -355,11 +379,16 @@
     def gather(part):
         return lax.all_gather(part, seq, axis=0, tiled=True, axis_index_groups=[order])
 
-    columns = out_weight.shape[1]
-    strip = 2 * columns // 3 // (groups * 2 * HDIM) * 2 * HDIM
-    direct = columns - groups * strip
-    strip_at = direct + lax.axis_index("groups") * strip
-    own_strip = gather(lax.dynamic_slice_in_dim(out_weight, strip_at, strip, 1))
+    strip = out_weight.shape[1] // groups
+    second = strip // 3 // (2 * HDIM) * 2 * HDIM
+    strips = cut(out_weight, lax.axis_index("groups") * strip, (strip - second, second))
+    strips = [gather(x) for x in strips]
+
+    def exchange(part):
+        half = part.shape[1] // 2
+        sent = lax.dynamic_slice_in_dim(part, lax.axis_index("core") * half, half, 1)
+        turns = [[(g, (g + dx) % groups) for g in range(groups)] for dx in range(1, groups)]
+        return sent, [lax.ppermute(sent, "groups", turn) for turn in turns]
 
     own, other = pack(pack_kv_kernel, frame_index, (keys, values), 2 * HC)
     across = to_lane(other, 1, 0)
@@ -372,18 +401,13 @@
     q = [own_q, swap(own_q), across_q, swap(across_q)]
     onward = after(across, *early)
     late = [to_plane(onward, dp) for dp in (1, -1)]
-    direct_strip = gather(after(out_weight, *early)[:, :direct])
-
-    own_strip = after(own_strip, *early, across_beside)
-    half = strip // 2
-    core_at = lax.axis_index("core") * half
-    sent = lax.dynamic_slice_in_dim(own_strip, core_at, half, 1)
-    halves = [
-        lax.ppermute(sent, "groups", [(g, (g + dx) % groups) for g in range(groups)])
-        for dx in range(1, groups)
-    ]
+
+    strips[0] = after(strips[0], *early, across_beside)
+    sent, halves = exchange(strips[0])
     pieces = [piece for x in early for piece in (x, swap(x))]
     begun = attend_begin(after(block_mask, sent), q, here + pieces)
+    strips[1] = after(strips[1], begun[0])
+    _, second_halves = exchange(strips[1])
     late = [after(x, begun[0]) for x in late]
     late = [piece for x in late for piece in (x, swap(x))]
     mixed = attend_finish((2, 3, 1), block_mask, q, begun, late)
@@ -391,9 +415,12 @@
     halves = [after(x, mixed[0]) for x in halves]
     own = attend_finish((0,), after(block_mask, mixed[0], *halves), q, begun, late)
     mixed = [own[0], moved[2], moved[0], moved[1]]
-    weights = [direct_strip, own_strip]
-    for x in halves:
-        weights += [x, lax.ppermute(x, "core", [(0, 1), (1, 0)])]
+    second_halves = [after(x, own[0], *moved) for x in second_halves]
+    weights = []
+    for part, received in zip(strips, (halves, second_halves)):
+        weights.append(part)
+        for x in received:
+            weights += [x, lax.ppermute(x, "core", [(0, 1), (1, 0)])]
     return project(mixed, weights, order, groups)
 
 

time: 165 us -> 136 us (0.82)
  waiting for transfers between devices: 76.2 us -> 46.7 us
    ppermute x4, waiting for transfers between devices: 34.3 us -> 4.92 us  [to_plane(): return lax.ppermute(x, seq, pairs)]
    ppermute x13, waiting for transfers between devices: 35.6 us -> 29.3 us  [to_lane(): lax.ppermute(x, seq, [(index(p, r, c), index(p, r ^ dr, c ^ dc)) for p, r...]
    all_gather x2, waiting for transfers between devices: 0.01 us -> 2.69 us  [gather(): lax.all_gather(part, seq, axis=0, tiled=True, axis_index_groups=[order])]
    ppermute x1 -> x2, waiting for transfers between devices: 0.01 us -> 2.29 us  [on_device(): weights += [x, lax.ppermute(x, 'core', [(0, 1), (1, 0)])]]
    slice x1 -> x0, local copies, waits for them, and re-layouts: 1.82 us -> none  [on_device(): direct_strip = gather(after(out_weight, *early)[:, :direct])]
    ppermute x1 -> x2, waiting for transfers between devices: 6.27 us -> 7.5 us  [exchange(): return (sent, [lax.ppermute(sent, 'groups', turn) for turn in turns])]
    unnamed x28 -> x36, local copies, waits for them, and re-layouts: 3.61 us -> 4.74 us
    pallas_call x1 -> x2, Pallas kernels: 8.33 us -> 9.11 us  [the longest x1 7.31 us: project(): pl.pallas_call(lambda *refs: project_kernel(order, groups, steps, refs[:L...]
  transfers between devices with their start and end apart: 21 -> 23, of which waited for: 12 -> 12; matrix products, arithmetic and copies ran while one was open for 5% -> 6% of each run, Pallas kernels for 20% -> 24%
where the time goes in v10:
time: 136 us
  waiting for transfers between devices  46.7 us (34%)
  Pallas kernels  42.3 us (31%)
  starting transfers between devices  20.7 us (15%)
  between operations  13.7 us (10%)
  local copies, waits for them, and re-layouts  12.4 us (9%)
    ppermute x13, waiting for transfers between devices, to_lane(): lax.ppermute(x, seq, [(index(p, r, c), index(p, r ^ dr, c ^ dc)) for p, r...  29.3 us
    pallas_call x1, Pallas kernels, attend_begin(): pl.pallas_call(begin_kernel, out_shape=[jax.ShapeDtypeStruct((2, rows, HC...  14.3 us
    pallas_call x2, Pallas kernels, attend_finish(): pl.pallas_call(lambda *refs: finish_kernel(steps, *refs), grid=(1,), out_...  13.1 us
    ppermute x4, starting transfers between devices, to_plane(): return lax.ppermute(x, seq, pairs)  10.7 us
    ppermute x2, waiting for transfers between devices, exchange(): return (sent, [lax.ppermute(sent, 'groups', turn) for turn in turns])  7.5 us
    pallas_call x1, Pallas kernels, project(): pl.pallas_call(lambda *refs: project_kernel(order, groups, steps, refs[:L...  7.31 us
    ppermute x13, starting transfers between devices, to_lane(): lax.ppermute(x, seq, [(index(p, r, c), index(p, r ^ dr, c ^ dc)) for p, r...  6.99 us
    pallas_call x2, Pallas kernels, pack(): pl.pallas_call(kernel, out_shape=[jax.ShapeDtypeStruct((2, count, width),...  5.76 us
  transfers between devices with their start and end apart: 23, of which 12 were waited for; matrix products, arithmetic and copies ran while one was open for 6% of the time, Pallas kernels for 24%

profile of v10, /device:TPU:0, one launch (start us, length us, event | category | flops | bytes accessed | tf_op | source)
XLA Modules:
  0.0 135.8 jit_solution(15903905837575017758)
XLA Ops:
  6.5 1.8 %shard_map.66 = (bf16[96,1024]{1,0:T(8,128)(2,1)}, bf16[96,512]{1,0:T(8,128)(2,1)}) custom-call(s32[1]{0:T(128)} %bitcast.3.at, bf16[96,3072]{1,0:T(8,128)(2,1)} %own_ref.1), custom_call_target="tpu_custom_call" | custom-call | tf_op jit(solution)/shard_map/pallas_call | solution.py:44
  8.4 3.1 %shard_map.64 = (bf16[2,256,768]{2,1,0:T(8,128)(2,1)}, bf16[2,256,768]{2,1,0:T(8,128)(2,1)}) custom-call(s32[2]{0:T(128)} %frames.3, bf16[256,1536]{1,0:T(8,128)(2,1)} %k_ref.1, bf16[256,1536]{1,0:T(8,128)(2,1)} %v_ref.1), custom_call_target="tpu_custom_call" | custom-call | tf_op jit(solution)/shard_map/pallas_call | solution.py:88
  11.5 3.0 %collective-permute-start.6 = (bf16[2,256,768]{2,1,0:T(8,128)(2,1)}, bf16[2,256,768]{2,1,0:T(8,128)(2,1)S(1)}, u32[]{:S(2)}, u32[]{:S(2)}) collective-permute-start(bf16[2,256,768]{2,1,0:T(8,128)(2,1)} %get-tuple-element.33), channel_id=1, source_target_pairs={{0,2},{1,3},{2,0},{3,1},{4,6},{5,7},{6,4},{7,5},{8,10},{9,11},{10,... | collective-permute-start | bytes 2359304 | tf_op jit(solution)/shard_map/ppermute | solution.py:367
  15.6 3.5 %collective-permute-start.4 = (bf16[2,256,768]{2,1,0:T(8,128)(2,1)}, bf16[2,256,768]{2,1,0:T(8,128)(2,1)S(1)}, u32[]{:S(2)}, u32[]{:S(2)}) collective-permute-start(bf16[2,256,768]{2,1,0:T(8,128)(2,1)} %get-tuple-element.28.refs_4_), channel_id=1, source_target_pairs={{0,4},{1,5},{2,6},{3,7},{4,8},{5,9},{6,10},{7,11},{8,12},{9,13},{1... | collective-permute-start | bytes 2359304 | tf_op jit(solution)/shard_map/ppermute | solution.py:371
  19.1 1.3 collective-permute-start.5
  20.4 2.7 %shard_map.65 = (bf16[2,256,384]{2,1,0:T(8,128)(2,1)}, bf16[2,256,384]{2,1,0:T(8,128)(2,1)}) custom-call(s32[2]{0:T(128)} %frames.3, bf16[256,1536]{1,0:T(8,128)(2,1)} %q_ref), custom_call_target="tpu_custom_call" | custom-call | tf_op jit(solution)/shard_map/pallas_call | solution.py:88
  23.6 23.1 %collective-permute-done.6.refs_6_ = bf16[2,256,768]{2,1,0:T(8,128)(2,1)S(1)} collective-permute-done((bf16[2,256,768]{2,1,0:T(8,128)(2,1)}, bf16[2,256,768]{2,1,0:T(8,128)(2,1)S(1)}, u32[]{:S(2)}, u32[]{:S(2)}) %collective-permute-start.6) | collective-permute-done | bytes 786464 | tf_op jit(solution)/shard_map/ppermute | solution.py:367
  46.9 1.8 %slice_bitcast_fusion.7 = bf16[256,384]{1,0:T(8,128)(2,1)} fusion(bf16[2,256,384]{2,1,0:T(8,128)(2,1)} %get-tuple-element.31.refs_0_.refs_1_), kind=kLoop, calls=%fused_computation.7 | loop fusion | bytes 393216 | tf_op jit(solution)/shard_map/squeeze | solution.py:374
  49.8 3.4 %collective-permute-done.5.refs_10_ = bf16[2,256,768]{2,1,0:T(8,128)(2,1)S(1)} collective-permute-done((bf16[2,256,768]{2,1,0:T(8,128)(2,1)}, bf16[2,256,768]{2,1,0:T(8,128)(2,1)S(1)}, u32[]{:S(2)}, u32[]{:S(2)}) %collective-permute-start.5) | collective-permute-done | bytes 786464 | tf_op jit(solution)/shard_map/ppermute | solution.py:371
  54.0 1.3 collective-permute-start.12
  55.3 4.6 %collective-permute-start.10 = (bf16[2,256,768]{2,1,0:T(8,128)(2,1)S(1)}, bf16[2,256,768]{2,1,0:T(8,128)(2,1)S(1)}, u32[]{:S(2)}, u32[]{:S(2)}) collective-permute-start(bf16[2,256,768]{2,1,0:T(8,128)(2,1)S(1)} %collective-permute-done.6.refs_6_), channel_id=1, source_target_pairs={{0,4},{1,5},{2,6},{3,7},{4,8},{5,9},{6,10},{7,11},{8,12},{9,13},{1... | collective-permute-start | bytes 2359304 | tf_op jit(solution)/shard_map/ppermute | solution.py:371
  60.7 2.7 %constant_dynamic-slice_fusion.1 = bf16[1536,512]{1,0:T(8,128)(2,1)} fusion(bf16[1536,1024]{1,0:T(8,128)(2,1)} %all-gather.3.cloned.1.call-done.refs_4_, s32[]{:T(128)S(6)} %select_n.6), kind=kLoop, calls=%fused_computation.9 | loop fusion | bytes 3145732 | tf_op jit(solution)/shard_map/dynamic_slice | solution.py:389
  63.4 1.5 %collective-permute-start.14 = (bf16[1536,512]{1,0:T(8,128)(2,1)}, bf16[1536,512]{1,0:T(8,128)(2,1)}, u32[]{:S(2)}, u32[]{:S(2)}) collective-permute-start(bf16[1536,512]{1,0:T(8,128)(2,1)} %constant_dynamic-slice_fusion.1), channel_id=1, source_target_pairs={{0,16},{16,0},{1,17},{17,1},{2,18},{18,2},{3,19},{19,3},{4,20},{20... | collective-permute-start | bytes 4718600 | tf_op jit(solution)/shard_map/ppermute | solution.py:391
  65.5 1.2 collective-permute-done.8.refs_9_
  68.2 14.3 %shard_map.67 = (f32[2,256,384]{2,1,0:T(8,128)}, f32[2,256,384]{2,1,0:T(8,128)}, f32[2,256,128]{2,1,0:T(8,128)}, f32[2,256,128]{2,1,0:T(8,128)}) custom-call(s32[32,32]{1,0:T(8,128)} %refs_0_.2, bf16[2,256,384]{2,1,0:T(8,128)(2,1)} %get-tuple-element.31.refs_0_.refs_1_, bf16[256,384]{1,0:T(8,128)(2,1)} %collective-permute-done.3.refs_1_.refs_3_, ...), custom_call_target="tpu_custom_call" | custom-call | flops 1024 | bytes 1024 | tf_op jit(solution)/shard_map/pallas_call | solution.py:241
  83.9 2.7 %all-gather.5.cloned.1.call-done.refs_7_ = bf16[1536,512]{1,0:T(8,128)(2,1)} async-done(((bf16[96,512]{1,0:T(8,128)(2,1)}), bf16[1536,512]{1,0:T(8,128)(2,1)}) %all-gather.5.cloned.1.call-update) | async-done | bytes 1572880 | tf_op jit(solution)/shard_map/all_gather | solution.py:380
  87.8 1.5 %collective-permute-start.19 = (bf16[1536,256]{1,0:T(8,128)(2,1)S(1)}, bf16[1536,256]{1,0:T(8,128)(2,1)S(1)}, u32[]{:S(2)}, u32[]{:S(2)}) collective-permute-start(bf16[1536,256]{1,0:T(8,128)(2,1)S(1)} %constant_dynamic-slice_fusion), channel_id=1, source_target_pairs={{0,16},{16,0},{1,17},{17,1},{2,18},{18,2},{3,19},{19,3},{4,20},{20... | collective-permute-start | bytes 2359304 | tf_op jit(solution)/shard_map/ppermute | solution.py:391
  90.1 8.3 %shard_map.68 = (bf16[256,384]{1,0:T(8,128)(2,1)}, bf16[256,384]{1,0:T(8,128)(2,1)}, bf16[256,384]{1,0:T(8,128)(2,1)}) custom-call(s32[32,32]{1,0:T(8,128)} %refs_0_.2, bf16[2,256,384]{2,1,0:T(8,128)(2,1)} %copy-done.2, bf16[256,384]{1,0:T(8,128)(2,1)} %collective-permute-done.2.refs_3_.refs_2_, bf16[256,384]{1,0:T(8,128)(2,1)} %collective-permute-done.3.refs_1_.refs_3_, ...), custom_call_target="tpu_custom_call" | custom-call | flops 1024 | bytes 1024 | tf_op jit(solution)/shard_map/pallas_call | solution.py:267
  98.4 2.5 %collective-permute-done.14.refs_5_ = bf16[1536,512]{1,0:T(8,128)(2,1)} collective-permute-done((bf16[1536,512]{1,0:T(8,128)(2,1)}, bf16[1536,512]{1,0:T(8,128)(2,1)}, u32[]{:S(2)}, u32[]{:S(2)}) %collective-permute-start.14) | collective-permute-done | bytes 1572896 | tf_op jit(solution)/shard_map/ppermute | solution.py:391
  103.1 4.8 %shard_map.69.refs_0_ = bf16[256,384]{1,0:T(8,128)(2,1)} custom-call(s32[32,32]{1,0:T(8,128)} %refs_0_.2, bf16[2,256,384]{2,1,0:T(8,128)(2,1)} %get-tuple-element.31.refs_0_.refs_1_, f32[2,256,384]{2,1,0:T(8,128)} %get-tuple-element.37.refs_6_.refs_2_, f32[2,256,128]{2,1,0:T(8,128)} %get-tuple-element.39.refs_9_.refs_3_, bf16[2,256,768]{2,1,0:T(8,128)(2,1)} %copy-done.1, ...), custom_call_target="tpu_custom_call" | custom-call | flops 1024 | bytes 1024 | tf_op jit(solution)/shard_map/pallas_call | solution.py:267
  108.8 3.4 %collective-permute-done.17.refs_3_ = bf16[256,384]{1,0:T(8,128)(2,1)S(1)} collective-permute-done((bf16[256,384]{1,0:T(8,128)(2,1)}, bf16[256,384]{1,0:T(8,128)(2,1)S(1)}, u32[]{:S(2)}, u32[]{:S(2)}) %collective-permute-start.17) | collective-permute-done | bytes 196640 | tf_op jit(solution)/shard_map/ppermute | solution.py:367
  112.3 5.0 %collective-permute-done.19.refs_8_ = bf16[1536,256]{1,0:T(8,128)(2,1)S(1)} collective-permute-done((bf16[1536,256]{1,0:T(8,128)(2,1)S(1)}, bf16[1536,256]{1,0:T(8,128)(2,1)S(1)}, u32[]{:S(2)}, u32[]{:S(2)}) %collective-permute-start.19) | collective-permute-done | bytes 786464 | tf_op jit(solution)/shard_map/ppermute | solution.py:391
  117.3 2.3 %collective-permute-done.20.refs_9_ = bf16[1536,256]{1,0:T(8,128)(2,1)S(1)} collective-permute-done((bf16[1536,256]{1,0:T(8,128)(2,1)S(1)}, bf16[1536,256]{1,0:T(8,128)(2,1)S(1)}, u32[]{:S(2)}, u32[]{:S(2)}) %collective-permute-start.20) | collective-permute-done | bytes 786464 | tf_op jit(solution)/shard_map/ppermute | solution.py:423
  121.6 7.3 %shard_map.70 = bf16[256,3072]{1,0:T(8,128)(2,1)} custom-call(bf16[256,384]{1,0:T(8,128)(2,1)} %shard_map.69.refs_0_, bf16[256,384]{1,0:T(8,128)(2,1)} %copy-done.16, bf16[256,384]{1,0:T(8,128)(2,1)} %copy-done.15, bf16[256,384]{1,0:T(8,128)(2,1)} %copy-done.17, bf16[1536,1024]{1,0:T(8,128)(2,1)} %all-gather.3.cloned.1.call-done.refs_4_, ...), custom_call_target="tpu_custom_call" | custom-call | tf_op jit(solution)/shard_map/pallas_call | solution.py:337
  (77 shorter events, 15.0 us)
Async XLA Ops:
  6.5 54.1 %all-gather.3.cloned.1.call-start = ((), (), s32[]{:S(2)}) async-start(), calls=%async_computation | async-start | bytes 3342336 | tf_op jit(solution)/shard_map/all_gather | solution.py:380
  8.4 78.2 %all-gather.5.cloned.1.call-start = ((), (), s32[]{:S(2)}) async-start(), calls=%async_computation.1 | async-start | bytes 1671168 | tf_op jit(solution)/shard_map/all_gather | solution.py:380
  11.5 35.3 %collective-permute-start.6 = (bf16[2,256,768]{2,1,0:T(8,128)(2,1)}, bf16[2,256,768]{2,1,0:T(8,128)(2,1)S(1)}, u32[]{:S(2)}, u32[]{:S(2)}) collective-permute-start(bf16[2,256,768]{2,1,0:T(8,128)(2,1)} %get-tuple-element.33), channel_id=1, source_target_pairs={{0,2},{1,3},{2,0},{3,1},{4,6},{5,7},{6,4},{7,5},{8,10},{9,11},{10,... | collective-permute-start | bytes 2359304 | tf_op jit(solution)/shard_map/ppermute | solution.py:367
  15.5 4.9 %collective-permute-start = (bf16[256,768]{1,0:T(8,128)(2,1)S(1)}, bf16[256,768]{1,0:T(8,128)(2,1)S(1)}, u32[]{:S(2)}, u32[]{:S(2)}) collective-permute-start(bf16[256,768]{1,0:T(8,128)(2,1)S(1)} %slice_bitcast_fusion.5), channel_id=1, source_target_pairs={{0,1},{1,0},{2,3},{3,2},{4,5},{5,4},{6,7},{7,6},{8,9},{9,8},{10,11... | collective-permute-start | bytes 1179656 | tf_op jit(solution)/shard_map/ppermute | solution.py:367
  15.6 34.2 %collective-permute-start.4 = (bf16[2,256,768]{2,1,0:T(8,128)(2,1)}, bf16[2,256,768]{2,1,0:T(8,128)(2,1)S(1)}, u32[]{:S(2)}, u32[]{:S(2)}) collective-permute-start(bf16[2,256,768]{2,1,0:T(8,128)(2,1)} %get-tuple-element.28.refs_4_), channel_id=1, source_target_pairs={{0,4},{1,5},{2,6},{3,7},{4,8},{5,9},{6,10},{7,11},{8,12},{9,13},{1... | collective-permute-start | bytes 2359304 | tf_op jit(solution)/shard_map/ppermute | solution.py:371
  19.1 34.0 %collective-permute-start.5 = (bf16[2,256,768]{2,1,0:T(8,128)(2,1)}, bf16[2,256,768]{2,1,0:T(8,128)(2,1)S(1)}, u32[]{:S(2)}, u32[]{:S(2)}) collective-permute-start(bf16[2,256,768]{2,1,0:T(8,128)(2,1)} %get-tuple-element.28.refs_4_), channel_id=1, source_target_pairs={{4,0},{5,1},{6,2},{7,3},{8,4},{9,5},{10,6},{11,7},{12,8},{13,9},{1... | collective-permute-start | bytes 2359304 | tf_op jit(solution)/shard_map/ppermute | solution.py:371
  20.4 29.3 %copy-start.12 = (bf16[256,768]{1,0:T(8,128)(2,1)}, bf16[256,768]{1,0:T(8,128)(2,1)S(1)}, u32[]{:S(2)}) copy-start(bf16[256,768]{1,0:T(8,128)(2,1)S(1)} %collective-permute-done.refs_5_) | copy-start | bytes 1179652
  23.1 36.8 %collective-permute-start.1 = (bf16[2,256,384]{2,1,0:T(8,128)(2,1)}, bf16[2,256,384]{2,1,0:T(8,128)(2,1)S(1)}, u32[]{:S(2)}, u32[]{:S(2)}) collective-permute-start(bf16[2,256,384]{2,1,0:T(8,128)(2,1)} %get-tuple-element.30), channel_id=1, source_target_pairs={{0,2},{1,3},{2,0},{3,1},{4,6},{5,7},{6,4},{7,5},{8,10},{9,11},{10,... | collective-permute-start | bytes 1179656 | tf_op jit(solution)/shard_map/ppermute | solution.py:367
  46.8 13.9 %collective-permute-start.7 = (bf16[256,768]{1,0:T(8,128)(2,1)S(1)}, bf16[256,768]{1,0:T(8,128)(2,1)}, u32[]{:S(2)}, u32[]{:S(2)}) collective-permute-start(bf16[256,768]{1,0:T(8,128)(2,1)S(1)} %slice_bitcast_fusion.2), channel_id=1, source_target_pairs={{0,1},{1,0},{2,3},{3,2},{4,5},{5,4},{6,7},{7,6},{8,9},{9,8},{10,11... | collective-permute-start | bytes 1179656 | tf_op jit(solution)/shard_map/ppermute | solution.py:367
  48.7 16.2 %collective-permute-start.3 = (bf16[256,384]{1,0:T(8,128)(2,1)}, bf16[256,384]{1,0:T(8,128)(2,1)}, u32[]{:S(2)}, u32[]{:S(2)}) collective-permute-start(bf16[256,384]{1,0:T(8,128)(2,1)} %slice_bitcast_fusion.7), channel_id=1, source_target_pairs={{0,1},{1,0},{2,3},{3,2},{4,5},{5,4},{6,7},{7,6},{8,9},{9,8},{10,11... | collective-permute-start | bytes 589832 | tf_op jit(solution)/shard_map/ppermute | solution.py:367
  54.0 28.6 %collective-permute-start.12 = (bf16[2,256,768]{2,1,0:T(8,128)(2,1)S(1)}, bf16[2,256,768]{2,1,0:T(8,128)(2,1)S(1)}, u32[]{:S(2)}, u32[]{:S(2)}) collective-permute-start(bf16[2,256,768]{2,1,0:T(8,128)(2,1)S(1)} %collective-permute-done.6.refs_6_), channel_id=1, source_target_pairs={{4,0},{5,1},{6,2},{7,3},{8,4},{9,5},{10,6},{11,7},{12,8},{13,9},{1... | collective-permute-start | bytes 2359304 | tf_op jit(solution)/shard_map/ppermute | solution.py:371
  55.3 28.5 %collective-permute-start.10 = (bf16[2,256,768]{2,1,0:T(8,128)(2,1)S(1)}, bf16[2,256,768]{2,1,0:T(8,128)(2,1)S(1)}, u32[]{:S(2)}, u32[]{:S(2)}) collective-permute-start(bf16[2,256,768]{2,1,0:T(8,128)(2,1)S(1)} %collective-permute-done.6.refs_6_), channel_id=1, source_target_pairs={{0,4},{1,5},{2,6},{3,7},{4,8},{5,9},{6,10},{7,11},{8,12},{9,13},{1... | collective-permute-start | bytes 2359304 | tf_op jit(solution)/shard_map/ppermute | solution.py:371
  60.7 4.6 %collective-permute-start.2 = (bf16[256,384]{1,0:T(8,128)(2,1)}, bf16[256,384]{1,0:T(8,128)(2,1)}, u32[]{:S(2)}, u32[]{:S(2)}) collective-permute-start(bf16[256,384]{1,0:T(8,128)(2,1)} %slice_bitcast_fusion.6), channel_id=1, source_target_pairs={{0,1},{1,0},{2,3},{3,2},{4,5},{5,4},{6,7},{7,6},{8,9},{9,8},{10,11... | collective-permute-start | bytes 589832 | tf_op jit(solution)/shard_map/ppermute | solution.py:367
  63.4 37.5 %collective-permute-start.14 = (bf16[1536,512]{1,0:T(8,128)(2,1)}, bf16[1536,512]{1,0:T(8,128)(2,1)}, u32[]{:S(2)}, u32[]{:S(2)}) collective-permute-start(bf16[1536,512]{1,0:T(8,128)(2,1)} %constant_dynamic-slice_fusion.1), channel_id=1, source_target_pairs={{0,16},{16,0},{1,17},{17,1},{2,18},{18,2},{3,19},{19,3},{4,20},{20... | collective-permute-start | bytes 4718600 | tf_op jit(solution)/shard_map/ppermute | solution.py:391
  65.0 1.8 %collective-permute-start.8 = (bf16[256,768]{1,0:T(8,128)(2,1)S(1)}, bf16[256,768]{1,0:T(8,128)(2,1)S(1)}, u32[]{:S(2)}, u32[]{:S(2)}) collective-permute-start(bf16[256,768]{1,0:T(8,128)(2,1)S(1)} %slice_bitcast_fusion.1), channel_id=1, source_target_pairs={{0,1},{1,0},{2,3},{3,2},{4,5},{5,4},{6,7},{7,6},{8,9},{9,8},{10,11... | collective-permute-start | bytes 1179656 | tf_op jit(solution)/shard_map/ppermute | solution.py:367
  65.3 2.1 %collective-permute-start.9 = (bf16[256,768]{1,0:T(8,128)(2,1)S(1)}, bf16[256,768]{1,0:T(8,128)(2,1)S(1)}, u32[]{:S(2)}, u32[]{:S(2)}) collective-permute-start(bf16[256,768]{1,0:T(8,128)(2,1)S(1)} %slice_bitcast_fusion), channel_id=1, source_target_pairs={{0,1},{1,0},{2,3},{3,2},{4,5},{5,4},{6,7},{7,6},{8,9},{9,8},{10,11... | collective-permute-start | bytes 1179656 | tf_op jit(solution)/shard_map/ppermute | solution.py:367
  82.6 6.6 %collective-permute-start.13 = (bf16[256,768]{1,0:T(8,128)(2,1)S(1)}, bf16[256,768]{1,0:T(8,128)(2,1)S(1)}, u32[]{:S(2)}, u32[]{:S(2)}) collective-permute-start(bf16[256,768]{1,0:T(8,128)(2,1)S(1)} %slice_bitcast_fusion.3), channel_id=1, source_target_pairs={{0,1},{1,0},{2,3},{3,2},{4,5},{5,4},{6,7},{7,6},{8,9},{9,8},{10,11... | collective-permute-start | bytes 1179656 | tf_op jit(solution)/shard_map/ppermute | solution.py:367
  83.8 5.5 %collective-permute-start.11 = (bf16[256,768]{1,0:T(8,128)(2,1)S(1)}, bf16[256,768]{1,0:T(8,128)(2,1)S(1)}, u32[]{:S(2)}, u32[]{:S(2)}) collective-permute-start(bf16[256,768]{1,0:T(8,128)(2,1)S(1)} %slice_bitcast_fusion.4), channel_id=1, source_target_pairs={{0,1},{1,0},{2,3},{3,2},{4,5},{5,4},{6,7},{7,6},{8,9},{9,8},{10,11... | collective-permute-start | bytes 1179656 | tf_op jit(solution)/shard_map/ppermute | solution.py:367
  87.8 29.5 %collective-permute-start.19 = (bf16[1536,256]{1,0:T(8,128)(2,1)S(1)}, bf16[1536,256]{1,0:T(8,128)(2,1)S(1)}, u32[]{:S(2)}, u32[]{:S(2)}) collective-permute-start(bf16[1536,256]{1,0:T(8,128)(2,1)S(1)} %constant_dynamic-slice_fusion), channel_id=1, source_target_pairs={{0,16},{16,0},{1,17},{17,1},{2,18},{18,2},{3,19},{19,3},{4,20},{20... | collective-permute-start | bytes 2359304 | tf_op jit(solution)/shard_map/ppermute | solution.py:391
  100.9 18.6 %collective-permute-start.18 = (bf16[1536,512]{1,0:T(8,128)(2,1)}, bf16[1536,512]{1,0:T(8,128)(2,1)S(1)}, u32[]{:S(2)}, u32[]{:S(2)}) collective-permute-start(bf16[1536,512]{1,0:T(8,128)(2,1)} %collective-permute-done.14.refs_5_), channel_id=1, source_target_pairs={{0,1},{1,0},{2,3},{3,2},{4,5},{5,4},{6,7},{7,6},{8,9},{9,8},{10,11... | collective-permute-start | bytes 4718600 | tf_op jit(solution)/shard_map/ppermute | solution.py:423
  100.9 7.9 %collective-permute-start.16 = (bf16[256,384]{1,0:T(8,128)(2,1)}, bf16[256,384]{1,0:T(8,128)(2,1)S(1)}, u32[]{:S(2)}, u32[]{:S(2)}) collective-permute-start(bf16[256,384]{1,0:T(8,128)(2,1)} %get-tuple-element.43), channel_id=1, source_target_pairs={{0,2},{1,3},{2,0},{3,1},{4,6},{5,7},{6,4},{7,5},{8,10},{9,11},{10,... | collective-permute-start | bytes 589832 | tf_op jit(solution)/shard_map/ppermute | solution.py:367
  101.8 6.1 %collective-permute-start.15 = (bf16[256,384]{1,0:T(8,128)(2,1)}, bf16[256,384]{1,0:T(8,128)(2,1)S(1)}, u32[]{:S(2)}, u32[]{:S(2)}) collective-permute-start(bf16[256,384]{1,0:T(8,128)(2,1)} %get-tuple-element.46), channel_id=1, source_target_pairs={{0,1},{1,0},{2,3},{3,2},{4,5},{5,4},{6,7},{7,6},{8,9},{9,8},{10,11... | collective-permute-start | bytes 589832 | tf_op jit(solution)/shard_map/ppermute | solution.py:367
  102.1 10.2 %collective-permute-start.17 = (bf16[256,384]{1,0:T(8,128)(2,1)}, bf16[256,384]{1,0:T(8,128)(2,1)S(1)}, u32[]{:S(2)}, u32[]{:S(2)}) collective-permute-start(bf16[256,384]{1,0:T(8,128)(2,1)} %get-tuple-element.47), channel_id=1, source_target_pairs={{0,3},{1,2},{2,1},{3,0},{4,7},{5,6},{6,5},{7,4},{8,11},{9,10},{10,... | collective-permute-start | bytes 589832 | tf_op jit(solution)/shard_map/ppermute | solution.py:367
  117.3 2.3 %collective-permute-start.20 = (bf16[1536,256]{1,0:T(8,128)(2,1)S(1)}, bf16[1536,256]{1,0:T(8,128)(2,1)S(1)}, u32[]{:S(2)}, u32[]{:S(2)}) collective-permute-start(bf16[1536,256]{1,0:T(8,128)(2,1)S(1)} %collective-permute-done.19.refs_8_), channel_id=1, source_target_pairs={{0,1},{1,0},{2,3},{3,2},{4,5},{5,4},{6,7},{7,6},{8,9},{9,8},{10,11... | collective-permute-start | bytes 2359304 | tf_op jit(solution)/shard_map/ppermute | solution.py:423
  (17 other events, 88.3 us)
Sparse Core Ops, SparseCore 0:
  8.9 42.9 all-gather.2
  53.6 32.9 all-gather.4

commit v11 on v9

--- a/solution.py
+++ b/solution.py
@@ -69,15 +69,17 @@
 
 
 def pack_kv_kernel(frames, k_ref, v_ref, *rest):
-    outs, tables = rest[:2], rest[2:]
+    outs, tables = rest[:3], rest[3:]
     turn_into(frames, k_ref, outs, *tables)
     for step in range(LANES):
         start = pl.multiple_of(lane_of(step) * HC, HDIM)
         outs[step // 2][step % 2, :, HC:] = v_ref[:, pl.ds(start, HC)]
+    outs[2][...] = outs[0][1]
 
 
 def pack_q_kernel(frames, q_ref, *rest):
-    turn_into(frames, q_ref, rest[:2], *rest[2:])
+    turn_into(frames, q_ref, rest[:3], *rest[3:])
+    rest[2][...] = rest[0][1]
 
 
 def pack(kernel, frames, arrays, width):
@@ -85,10 +87,11 @@
     table = pltpu.VMEM((count // BLK, 8, HDIM), jnp.float32)
     return pl.pallas_call(
         kernel,
-        out_shape=[jax.ShapeDtypeStruct((2, count, width), jnp.bfloat16)] * 2,
+        out_shape=[jax.ShapeDtypeStruct((2, count, width), jnp.bfloat16)] * 2
+        + [jax.ShapeDtypeStruct((count, width), jnp.bfloat16)],
         in_specs=[pl.BlockSpec(memory_space=pltpu.SMEM)]
         + [pl.BlockSpec(memory_space=pltpu.VMEM) for _ in arrays],
-        out_specs=[pl.BlockSpec(memory_space=pltpu.VMEM)] * 2,
+        out_specs=[pl.BlockSpec(memory_space=pltpu.VMEM)] * 3,
         scratch_shapes=[table, table],
         compiler_params=pltpu.CompilerParams(vmem_limit_bytes=56 * 1024 * 1024),
     )(frames, *arrays)
@@ -290,15 +293,14 @@
     )
 
 
-def project_kernel(order, groups, a_refs, w_refs, o_ref, by_lane, by_shard):
+def project_kernel(order, groups, a_refs, w_refs, o_ref, by_lane, by_shard, sems):
     step = pl.program_id(0)
     depth = by_shard.shape[1]
     shard = depth // len(order)
 
     @pl.when(step == 0)
     def _():
-        for d in range(LANES):
-            by_lane[lane_of(d)] = a_refs[d][...]
+        fetch([(a_refs[d], by_lane.at[lane_of(d)]) for d in range(LANES)], sems)
         parts = []
         for place in order:
             lane, at = place * shard // HC, place * shard % HC
@@ -309,14 +311,18 @@
     widths = [w.shape[1] for w in w_refs]
     steps = o_ref.shape[1] // (widths[0] + groups * widths[1])
     direct, strip, half = widths[0] * steps, widths[1] * steps, widths[1] * steps // 2
-    places = [0, direct + mine * strip]
+    for w_ref, place in zip(w_refs, (0, direct + mine * strip)):
+        width = w_ref.shape[1]
+        out = jnp.dot(by_shard[...], w_ref[...], preferred_element_type=jnp.float32)
+        o_ref[:, pl.ds(pl.multiple_of(place + step * width, HDIM), width)] = out.astype(jnp.bfloat16)
+    width = half // steps
     for dx in range(1, groups):
-        start = direct + lax.rem(mine + groups - dx, groups) * strip
-        places += [start + core * half, start + (1 - core) * half]
-    for w_ref, place, width in zip(w_refs, places, widths):
-        out = jnp.dot(by_shard[...], w_ref[...], preferred_element_type=jnp.float32)
-        at = pl.multiple_of(place + step * width, HDIM)
-        o_ref[:, pl.ds(at, width)] = out.astype(jnp.bfloat16)
+        both = jnp.concatenate([ref[...] for ref in w_refs[2 * dx : 2 * dx + 2]], axis=1)
+        out = jnp.dot(by_shard[...], both, preferred_element_type=jnp.float32).astype(jnp.bfloat16)
+        start = direct + lax.rem(mine + groups - dx, groups) * strip + step * width
+        for i, which in enumerate((core, 1 - core)):
+            at = pl.multiple_of(start + which * half, HDIM)
+            o_ref[:, pl.ds(at, width)] = out[:, i * width : (i + 1) * width]
 
 
 def project(attended, weights, order, groups):
@@ -324,17 +330,17 @@
     channels = weights[0].shape[0]
     steps = weights[-1].shape[1] // HDIM
     columns = weights[0].shape[1] + groups * weights[1].shape[1]
-    whole = pl.BlockSpec((count, depth), lambda n: (0, 0))
     return pl.pallas_call(
-        lambda *refs: project_kernel(order, groups, refs[:LANES], refs[LANES:-3], *refs[-3:]),
+        lambda *refs: project_kernel(order, groups, refs[:LANES], refs[LANES:-4], *refs[-4:]),
         out_shape=jax.ShapeDtypeStruct((count, columns), jnp.bfloat16),
         grid=(steps,),
-        in_specs=[whole] * LANES
+        in_specs=[pl.BlockSpec(memory_space=pltpu.HBM)] * LANES
         + [pl.BlockSpec((channels, w.shape[1] // steps), lambda n: (0, n)) for w in weights],
         out_specs=pl.BlockSpec((count, columns), lambda n: (0, 0)),
         scratch_shapes=[
             pltpu.VMEM((LANES, count, depth), jnp.bfloat16),
             pltpu.VMEM((count, channels), jnp.bfloat16),
+            pltpu.SemaphoreType.DMA((LANES,)),
         ],
         compiler_params=pltpu.CompilerParams(vmem_limit_bytes=56 * 1024 * 1024),
     )(*attended, *weights)
@@ -376,15 +382,15 @@
     strip_at = direct + lax.axis_index("groups") * strip
     own_strip, direct_strip = [gather(x) for x in cut(out_weight, strip_at, strip, direct)]
 
-    own, other = pack(pack_kv_kernel, frame_index, (keys, values), 2 * HC)
+    own, other, own_beside = pack(pack_kv_kernel, frame_index, (keys, values), 2 * HC)
     across = to_lane(other, 1, 0)
     early = [to_plane(own, dp) for dp in (1, -1)]
-    beside = swap(own)
-    own_q, other_q = pack(pack_q_kernel, frame_index, (after(queries, beside),), HC)
+    beside = to_lane(own_beside, 0, 1)
+    own_q, other_q, own_q_beside = pack(pack_q_kernel, frame_index, (after(queries, beside),), HC)
     across_q = to_lane(other_q, 1, 0)
     across_beside = swap(across)
     here = [own, beside, across, across_beside]
-    q = [own_q, swap(own_q), across_q, swap(across_q)]
+    q = [own_q, to_lane(own_q_beside, 0, 1), across_q, swap(across_q)]
     onward = after(across, *early)
     late = [to_plane(onward, dp) for dp in (1, -1)]
 

time: 131 us -> 130 us (level)
  local copies, waits for them, and re-layouts: 9.8 us -> 7.6 us
  waiting for transfers between devices: 43.5 us -> 45.4 us
    squeeze x8 -> x6, local copies, waits for them, and re-layouts: 4.71 us -> 2.67 us  [swap(): return to_lane(x[1], 0, 1)]
    ppermute x13, waiting for transfers between devices: 31 us -> 32.4 us  [to_lane(): lax.ppermute(x, seq, [(index(p, r, c), index(p, r ^ dr, c ^ dc)) for p, r...]
    unnamed x28 -> x26, local copies, waits for them, and re-layouts: 3.58 us -> 3.41 us
  transfers between devices with their start and end apart: 21 -> 21, of which waited for: 9 -> 10; matrix products, arithmetic and copies ran while one was open for 5% -> 3% of each run, Pallas kernels for 26% -> 26%
where the time goes in v11:
time: 130 us
  waiting for transfers between devices  45.4 us (35%)
  Pallas kernels  43.7 us (34%)
  starting transfers between devices  19.5 us (15%)
  between operations  13.6 us (10%)
  local copies, waits for them, and re-layouts  7.6 us (6%)
    ppermute x13, waiting for transfers between devices, to_lane(): lax.ppermute(x, seq, [(index(p, r, c), index(p, r ^ dr, c ^ dc)) for p, r...  32.4 us
    pallas_call x1, Pallas kernels, attend_begin(): pl.pallas_call(begin_kernel, out_shape=[jax.ShapeDtypeStruct((2, rows, HC...  14.3 us
    pallas_call x2, Pallas kernels, attend_finish(): pl.pallas_call(lambda *refs: finish_kernel(steps, *refs), grid=(1,), out_...  13.1 us
    ppermute x4, waiting for transfers between devices, to_plane(): return lax.ppermute(x, seq, pairs)  12.2 us
    ppermute x4, starting transfers between devices, to_plane(): return lax.ppermute(x, seq, pairs)  10.9 us
    pallas_call x1, Pallas kernels, project(): pl.pallas_call(lambda *refs: project_kernel(order, groups, refs[:LANES],...  8.51 us
    ppermute x13, starting transfers between devices, to_lane(): lax.ppermute(x, seq, [(index(p, r, c), index(p, r ^ dr, c ^ dc)) for p, r...  6.88 us
    pallas_call x2, Pallas kernels, pack(): pl.pallas_call(kernel, out_shape=[jax.ShapeDtypeStruct((2, count, width),...  5.94 us
  transfers between devices with their start and end apart: 21, of which 10 were waited for; matrix products, arithmetic and copies ran while one was open for 3% of the time, Pallas kernels for 26%

profile of v11, /device:TPU:0, one launch (start us, length us, event | category | flops | bytes accessed | tf_op | source)
XLA Modules:
  0.0 129.9 jit_solution(8501472418723955238)
XLA Ops:
  6.5 1.8 %shard_map.66 = (bf16[96,1024]{1,0:T(8,128)(2,1)}, bf16[96,1024]{1,0:T(8,128)(2,1)}) custom-call(s32[1]{0:T(128)} %bitcast.1.at, bf16[96,3072]{1,0:T(8,128)(2,1)} %own_ref.1), custom_call_target="tpu_custom_call" | custom-call | tf_op jit(solution)/shard_map/pallas_call | solution.py:42
  9.2 3.3 %shard_map.64 = (bf16[2,256,768]{2,1,0:T(8,128)(2,1)}, bf16[2,256,768]{2,1,0:T(8,128)(2,1)}, bf16[256,768]{1,0:T(8,128)(2,1)}) custom-call(s32[2]{0:T(128)} %frames.3, bf16[256,1536]{1,0:T(8,128)(2,1)} %k_ref.1, bf16[256,1536]{1,0:T(8,128)(2,1)} %v_ref.1), custom_call_target="tpu_custom_call" | custom-call | tf_op jit(solution)/shard_map/pallas_call | solution.py:88
  12.4 3.0 %collective-permute-start.6 = (bf16[2,256,768]{2,1,0:T(8,128)(2,1)}, bf16[2,256,768]{2,1,0:T(8,128)(2,1)S(1)}, u32[]{:S(2)}, u32[]{:S(2)}) collective-permute-start(bf16[2,256,768]{2,1,0:T(8,128)(2,1)} %get-tuple-element.34), channel_id=1, source_target_pairs={{0,2},{1,3},{2,0},{3,1},{4,6},{5,7},{6,4},{7,5},{8,10},{9,11},{10,... | collective-permute-start | bytes 2359304 | tf_op jit(solution)/shard_map/ppermute | solution.py:364
  15.4 3.5 %collective-permute-start.4 = (bf16[2,256,768]{2,1,0:T(8,128)(2,1)}, bf16[2,256,768]{2,1,0:T(8,128)(2,1)S(1)}, u32[]{:S(2)}, u32[]{:S(2)}) collective-permute-start(bf16[2,256,768]{2,1,0:T(8,128)(2,1)} %get-tuple-element.33.refs_4_), channel_id=1, source_target_pairs={{0,4},{1,5},{2,6},{3,7},{4,8},{5,9},{6,10},{7,11},{8,12},{9,13},{1... | collective-permute-start | bytes 2359304 | tf_op jit(solution)/shard_map/ppermute | solution.py:368
  18.9 1.3 collective-permute-start.5
  20.2 2.7 %shard_map.65 = (bf16[2,256,384]{2,1,0:T(8,128)(2,1)}, bf16[2,256,384]{2,1,0:T(8,128)(2,1)}, bf16[256,384]{1,0:T(8,128)(2,1)}) custom-call(s32[2]{0:T(128)} %frames.3, bf16[256,1536]{1,0:T(8,128)(2,1)} %q_ref), custom_call_target="tpu_custom_call" | custom-call | tf_op jit(solution)/shard_map/pallas_call | solution.py:88
  23.4 24.9 %collective-permute-done.6.refs_6_ = bf16[2,256,768]{2,1,0:T(8,128)(2,1)S(1)} collective-permute-done((bf16[2,256,768]{2,1,0:T(8,128)(2,1)}, bf16[2,256,768]{2,1,0:T(8,128)(2,1)S(1)}, u32[]{:S(2)}, u32[]{:S(2)}) %collective-permute-start.6) | collective-permute-done | bytes 786464 | tf_op jit(solution)/shard_map/ppermute | solution.py:364
  49.8 3.4 %collective-permute-done.5.refs_10_ = bf16[2,256,768]{2,1,0:T(8,128)(2,1)} collective-permute-done((bf16[2,256,768]{2,1,0:T(8,128)(2,1)}, bf16[2,256,768]{2,1,0:T(8,128)(2,1)}, u32[]{:S(2)}, u32[]{:S(2)}) %collective-permute-start.5) | collective-permute-done | bytes 786464 | tf_op jit(solution)/shard_map/ppermute | solution.py:368
  53.2 1.3 collective-permute-start.12
  54.5 4.8 %collective-permute-start.10 = (bf16[2,256,768]{2,1,0:T(8,128)(2,1)S(1)}, bf16[2,256,768]{2,1,0:T(8,128)(2,1)S(1)}, u32[]{:S(2)}, u32[]{:S(2)}) collective-permute-start(bf16[2,256,768]{2,1,0:T(8,128)(2,1)S(1)} %collective-permute-done.6.refs_6_), channel_id=1, source_target_pairs={{0,4},{1,5},{2,6},{3,7},{4,8},{5,9},{6,10},{7,11},{8,12},{9,13},{1... | collective-permute-start | bytes 2359304 | tf_op jit(solution)/shard_map/ppermute | solution.py:368
  60.0 1.5 %constant_dynamic-slice_fusion = bf16[1536,512]{1,0:T(8,128)(2,1)S(1)} fusion(bf16[1536,1024]{1,0:T(8,128)(2,1)} %all-gather.3.cloned.1.call-done.refs_5_, s32[]{:T(128)S(6)} %select_n.3), kind=kLoop, calls=%fused_computation.6 | loop fusion | bytes 3145732 | tf_op jit(solution)/shard_map/dynamic_slice | solution.py:400
  61.6 1.6 %collective-permute-start.14 = (bf16[1536,512]{1,0:T(8,128)(2,1)S(1)}, bf16[1536,512]{1,0:T(8,128)(2,1)}, u32[]{:S(2)}, u32[]{:S(2)}) collective-permute-start(bf16[1536,512]{1,0:T(8,128)(2,1)S(1)} %constant_dynamic-slice_fusion), channel_id=1, source_target_pairs={{0,16},{16,0},{1,17},{17,1},{2,18},{18,2},{3,19},{19,3},{4,20},{20... | collective-permute-start | bytes 4718600 | tf_op jit(solution)/shard_map/ppermute | solution.py:402
  63.2 1.0 slice_bitcast_fusion
  64.8 1.3 collective-permute-done.8.refs_9_
  67.4 14.3 %shard_map.67 = (f32[2,256,384]{2,1,0:T(8,128)}, f32[2,256,384]{2,1,0:T(8,128)}, f32[2,256,128]{2,1,0:T(8,128)}, f32[2,256,128]{2,1,0:T(8,128)}) custom-call(s32[32,32]{1,0:T(8,128)} %refs_0_.2, bf16[2,256,384]{2,1,0:T(8,128)(2,1)} %get-tuple-element.37.refs_0_.refs_1_, bf16[256,384]{1,0:T(8,128)(2,1)} %collective-permute-done.3.refs_1_.refs_3_, ...), custom_call_target="tpu_custom_call" | custom-call | flops 1024 | bytes 1024 | tf_op jit(solution)/shard_map/pallas_call | solution.py:242
  81.7 5.3 %collective-permute-done.12.refs_12_.refs_6_ = bf16[2,256,768]{2,1,0:T(8,128)(2,1)S(1)} collective-permute-done((bf16[2,256,768]{2,1,0:T(8,128)(2,1)S(1)}, bf16[2,256,768]{2,1,0:T(8,128)(2,1)S(1)}, u32[]{:S(2)}, u32[]{:S(2)}) %collective-permute-start.12) | collective-permute-done | bytes 786464 | tf_op jit(solution)/shard_map/ppermute | solution.py:368
  87.1 3.4 %collective-permute-done.10.refs_10_.refs_4_ = bf16[2,256,768]{2,1,0:T(8,128)(2,1)S(1)} collective-permute-done((bf16[2,256,768]{2,1,0:T(8,128)(2,1)S(1)}, bf16[2,256,768]{2,1,0:T(8,128)(2,1)S(1)}, u32[]{:S(2)}, u32[]{:S(2)}) %collective-permute-start.10) | collective-permute-done | bytes 786464 | tf_op jit(solution)/shard_map/ppermute | solution.py:368
  90.6 1.7 %collective-permute-done.11.refs_11_.refs_5_ = bf16[256,768]{1,0:T(8,128)(2,1)S(1)} collective-permute-done((bf16[256,768]{1,0:T(8,128)(2,1)S(1)}, bf16[256,768]{1,0:T(8,128)(2,1)S(1)}, u32[]{:S(2)}, u32[]{:S(2)}) %collective-permute-start.11) | collective-permute-done | bytes 393248 | tf_op jit(solution)/shard_map/ppermute | solution.py:364
  93.1 8.3 %shard_map.68 = (bf16[256,384]{1,0:T(8,128)(2,1)}, bf16[256,384]{1,0:T(8,128)(2,1)}, bf16[256,384]{1,0:T(8,128)(2,1)}) custom-call(s32[32,32]{1,0:T(8,128)} %refs_0_.2, bf16[2,256,384]{2,1,0:T(8,128)(2,1)} %copy-done.2, bf16[256,384]{1,0:T(8,128)(2,1)} %collective-permute-done.2.refs_3_.refs_2_, bf16[256,384]{1,0:T(8,128)(2,1)} %collective-permute-done.3.refs_1_.refs_3_, ...), custom_call_target="tpu_custom_call" | custom-call | flops 1024 | bytes 1024 | tf_op jit(solution)/shard_map/pallas_call | solution.py:268
  102.2 1.6 %collective-permute-start.17 = (bf16[256,384]{1,0:T(8,128)(2,1)}, bf16[256,384]{1,0:T(8,128)(2,1)S(1)}, u32[]{:S(2)}, u32[]{:S(2)}) collective-permute-start(bf16[256,384]{1,0:T(8,128)(2,1)} %get-tuple-element.49), channel_id=1, source_target_pairs={{0,3},{1,2},{2,1},{3,0},{4,7},{5,6},{6,5},{7,4},{8,11},{9,10},{10,... | collective-permute-start | bytes 589832 | tf_op jit(solution)/shard_map/ppermute | solution.py:364
  103.7 4.8 %shard_map.69.refs_0_ = bf16[256,384]{1,0:T(8,128)(2,1)} custom-call(s32[32,32]{1,0:T(8,128)} %refs_0_.2, bf16[2,256,384]{2,1,0:T(8,128)(2,1)} %get-tuple-element.37.refs_0_.refs_1_, f32[2,256,384]{2,1,0:T(8,128)} %get-tuple-element.39.refs_6_.refs_2_, f32[2,256,128]{2,1,0:T(8,128)} %get-tuple-element.41.refs_9_.refs_3_, bf16[2,256,768]{2,1,0:T(8,128)(2,1)} %copy-done.1, ...), custom_call_target="tpu_custom_call" | custom-call | flops 1024 | bytes 1024 | tf_op jit(solution)/shard_map/pallas_call | solution.py:268
  109.5 3.1 %collective-permute-done.17.refs_3_ = bf16[256,384]{1,0:T(8,128)(2,1)S(1)} collective-permute-done((bf16[256,384]{1,0:T(8,128)(2,1)}, bf16[256,384]{1,0:T(8,128)(2,1)S(1)}, u32[]{:S(2)}, u32[]{:S(2)}) %collective-permute-start.17) | collective-permute-done | bytes 196640 | tf_op jit(solution)/shard_map/ppermute | solution.py:364
  113.3 1.2 copy-done.5
  114.5 8.5 %shard_map.70 = bf16[256,3072]{1,0:T(8,128)(2,1)} custom-call(bf16[256,384]{1,0:T(8,128)(2,1)} %shard_map.69.refs_0_, bf16[256,384]{1,0:T(8,128)(2,1)} %copy-done.11, bf16[256,384]{1,0:T(8,128)(2,1)} %copy-done.10, bf16[256,384]{1,0:T(8,128)(2,1)} %copy-done.12, bf16[1536,1024]{1,0:T(8,128)(2,1)} %all-gather.5.cloned.1.call-done.refs_4_, ...), custom_call_target="tpu_custom_call" | custom-call | tf_op jit(solution)/shard_map/pallas_call | solution.py:333
  (60 shorter events, 8.8 us)
Async XLA Ops:
  6.5 53.5 %all-gather.3.cloned.1.call-start = ((), (), s32[]{:S(2)}) async-start(), calls=%async_computation | async-start | bytes 3342336 | tf_op jit(solution)/shard_map/all_gather | solution.py:377
  8.4 100.2 %all-gather.5.cloned.1.call-start = ((), (), s32[]{:S(2)}) async-start(), calls=%async_computation.1 | async-start | bytes 3342336 | tf_op jit(solution)/shard_map/all_gather | solution.py:377
  12.4 35.9 %collective-permute-start.6 = (bf16[2,256,768]{2,1,0:T(8,128)(2,1)}, bf16[2,256,768]{2,1,0:T(8,128)(2,1)S(1)}, u32[]{:S(2)}, u32[]{:S(2)}) collective-permute-start(bf16[2,256,768]{2,1,0:T(8,128)(2,1)} %get-tuple-element.34), channel_id=1, source_target_pairs={{0,2},{1,3},{2,0},{3,1},{4,6},{5,7},{6,4},{7,5},{8,10},{9,11},{10,... | collective-permute-start | bytes 2359304 | tf_op jit(solution)/shard_map/ppermute | solution.py:364
  15.4 4.8 %collective-permute-start = (bf16[256,768]{1,0:T(8,128)(2,1)}, bf16[256,768]{1,0:T(8,128)(2,1)}, u32[]{:S(2)}, u32[]{:S(2)}) collective-permute-start(bf16[256,768]{1,0:T(8,128)(2,1)} %get-tuple-element.28), channel_id=1, source_target_pairs={{0,1},{1,0},{2,3},{3,2},{4,5},{5,4},{6,7},{7,6},{8,9},{9,8},{10,11... | collective-permute-start | bytes 1179656 | tf_op jit(solution)/shard_map/ppermute | solution.py:364
  15.4 34.4 %collective-permute-start.4 = (bf16[2,256,768]{2,1,0:T(8,128)(2,1)}, bf16[2,256,768]{2,1,0:T(8,128)(2,1)S(1)}, u32[]{:S(2)}, u32[]{:S(2)}) collective-permute-start(bf16[2,256,768]{2,1,0:T(8,128)(2,1)} %get-tuple-element.33.refs_4_), channel_id=1, source_target_pairs={{0,4},{1,5},{2,6},{3,7},{4,8},{5,9},{6,10},{7,11},{8,12},{9,13},{1... | collective-permute-start | bytes 2359304 | tf_op jit(solution)/shard_map/ppermute | solution.py:368
  18.9 34.3 %collective-permute-start.5 = (bf16[2,256,768]{2,1,0:T(8,128)(2,1)}, bf16[2,256,768]{2,1,0:T(8,128)(2,1)}, u32[]{:S(2)}, u32[]{:S(2)}) collective-permute-start(bf16[2,256,768]{2,1,0:T(8,128)(2,1)} %get-tuple-element.33.refs_4_), channel_id=1, source_target_pairs={{4,0},{5,1},{6,2},{7,3},{8,4},{9,5},{10,6},{11,7},{12,8},{13,9},{1... | collective-permute-start | bytes 2359304 | tf_op jit(solution)/shard_map/ppermute | solution.py:368
  22.9 36.4 %collective-permute-start.1 = (bf16[2,256,384]{2,1,0:T(8,128)(2,1)}, bf16[2,256,384]{2,1,0:T(8,128)(2,1)S(1)}, u32[]{:S(2)}, u32[]{:S(2)}) collective-permute-start(bf16[2,256,384]{2,1,0:T(8,128)(2,1)} %get-tuple-element.30), channel_id=1, source_target_pairs={{0,2},{1,3},{2,0},{3,1},{4,6},{5,7},{6,4},{7,5},{8,10},{9,11},{10,... | collective-permute-start | bytes 1179656 | tf_op jit(solution)/shard_map/ppermute | solution.py:364
  48.3 13.3 %copy-start.3 = (bf16[2,256,768]{2,1,0:T(8,128)(2,1)}, bf16[2,256,768]{2,1,0:T(8,128)(2,1)S(1)}, u32[]{:S(2)}) copy-start(bf16[2,256,768]{2,1,0:T(8,128)(2,1)S(1)} %collective-permute-done.6.refs_6_) | copy-start | bytes 2359300
  49.1 10.9 %collective-permute-start.7 = (bf16[256,768]{1,0:T(8,128)(2,1)}, bf16[256,768]{1,0:T(8,128)(2,1)}, u32[]{:S(2)}, u32[]{:S(2)}) collective-permute-start(bf16[256,768]{1,0:T(8,128)(2,1)} %slice_bitcast_fusion.2), channel_id=1, source_target_pairs={{0,1},{1,0},{2,3},{3,2},{4,5},{5,4},{6,7},{7,6},{8,9},{9,8},{10,11... | collective-permute-start | bytes 1179656 | tf_op jit(solution)/shard_map/ppermute | solution.py:364
  49.1 15.1 %collective-permute-start.3 = (bf16[256,384]{1,0:T(8,128)(2,1)}, bf16[256,384]{1,0:T(8,128)(2,1)}, u32[]{:S(2)}, u32[]{:S(2)}) collective-permute-start(bf16[256,384]{1,0:T(8,128)(2,1)} %get-tuple-element.31), channel_id=1, source_target_pairs={{0,1},{1,0},{2,3},{3,2},{4,5},{5,4},{6,7},{7,6},{8,9},{9,8},{10,11... | collective-permute-start | bytes 589832 | tf_op jit(solution)/shard_map/ppermute | solution.py:364
  49.8 13.4 %copy-start.4 = (bf16[2,256,768]{2,1,0:T(8,128)(2,1)}, bf16[2,256,768]{2,1,0:T(8,128)(2,1)S(1)}, u32[]{:S(2)}) copy-start(bf16[2,256,768]{2,1,0:T(8,128)(2,1)S(1)} %collective-permute-done.4.refs_8_) | copy-start | bytes 2359300
  53.2 33.8 %collective-permute-start.12 = (bf16[2,256,768]{2,1,0:T(8,128)(2,1)S(1)}, bf16[2,256,768]{2,1,0:T(8,128)(2,1)S(1)}, u32[]{:S(2)}, u32[]{:S(2)}) collective-permute-start(bf16[2,256,768]{2,1,0:T(8,128)(2,1)S(1)} %collective-permute-done.6.refs_6_), channel_id=1, source_target_pairs={{4,0},{5,1},{6,2},{7,3},{8,4},{9,5},{10,6},{11,7},{12,8},{13,9},{1... | collective-permute-start | bytes 2359304 | tf_op jit(solution)/shard_map/ppermute | solution.py:368
  54.5 36.0 %collective-permute-start.10 = (bf16[2,256,768]{2,1,0:T(8,128)(2,1)S(1)}, bf16[2,256,768]{2,1,0:T(8,128)(2,1)S(1)}, u32[]{:S(2)}, u32[]{:S(2)}) collective-permute-start(bf16[2,256,768]{2,1,0:T(8,128)(2,1)S(1)} %collective-permute-done.6.refs_6_), channel_id=1, source_target_pairs={{0,4},{1,5},{2,6},{3,7},{4,8},{5,9},{6,10},{7,11},{8,12},{9,13},{1... | collective-permute-start | bytes 2359304 | tf_op jit(solution)/shard_map/ppermute | solution.py:368
  60.0 4.5 %collective-permute-start.2 = (bf16[256,384]{1,0:T(8,128)(2,1)}, bf16[256,384]{1,0:T(8,128)(2,1)}, u32[]{:S(2)}, u32[]{:S(2)}) collective-permute-start(bf16[256,384]{1,0:T(8,128)(2,1)} %slice_bitcast_fusion.5), channel_id=1, source_target_pairs={{0,1},{1,0},{2,3},{3,2},{4,5},{5,4},{6,7},{7,6},{8,9},{9,8},{10,11... | collective-permute-start | bytes 589832 | tf_op jit(solution)/shard_map/ppermute | solution.py:364
  61.6 39.8 %collective-permute-start.14 = (bf16[1536,512]{1,0:T(8,128)(2,1)S(1)}, bf16[1536,512]{1,0:T(8,128)(2,1)}, u32[]{:S(2)}, u32[]{:S(2)}) collective-permute-start(bf16[1536,512]{1,0:T(8,128)(2,1)S(1)} %constant_dynamic-slice_fusion), channel_id=1, source_target_pairs={{0,16},{16,0},{1,17},{17,1},{2,18},{18,2},{3,19},{19,3},{4,20},{20... | collective-permute-start | bytes 4718600 | tf_op jit(solution)/shard_map/ppermute | solution.py:402
  64.2 1.9 %collective-permute-start.8 = (bf16[256,768]{1,0:T(8,128)(2,1)S(1)}, bf16[256,768]{1,0:T(8,128)(2,1)S(1)}, u32[]{:S(2)}, u32[]{:S(2)}) collective-permute-start(bf16[256,768]{1,0:T(8,128)(2,1)S(1)} %slice_bitcast_fusion.1), channel_id=1, source_target_pairs={{0,1},{1,0},{2,3},{3,2},{4,5},{5,4},{6,7},{7,6},{8,9},{9,8},{10,11... | collective-permute-start | bytes 1179656 | tf_op jit(solution)/shard_map/ppermute | solution.py:364
  64.5 2.1 %collective-permute-start.9 = (bf16[256,768]{1,0:T(8,128)(2,1)S(1)}, bf16[256,768]{1,0:T(8,128)(2,1)S(1)}, u32[]{:S(2)}, u32[]{:S(2)}) collective-permute-start(bf16[256,768]{1,0:T(8,128)(2,1)S(1)} %slice_bitcast_fusion), channel_id=1, source_target_pairs={{0,1},{1,0},{2,3},{3,2},{4,5},{5,4},{6,7},{7,6},{8,9},{9,8},{10,11... | collective-permute-start | bytes 1179656 | tf_op jit(solution)/shard_map/ppermute | solution.py:364
  87.0 5.3 %copy-start = (bf16[2,256,768]{2,1,0:T(8,128)(2,1)}, bf16[2,256,768]{2,1,0:T(8,128)(2,1)S(1)}, u32[]{:S(2)}) copy-start(bf16[2,256,768]{2,1,0:T(8,128)(2,1)S(1)} %collective-permute-done.12.refs_12_.refs_6_) | copy-start | bytes 2359300
  87.0 3.6 %collective-permute-start.13 = (bf16[256,768]{1,0:T(8,128)(2,1)S(1)}, bf16[256,768]{1,0:T(8,128)(2,1)S(1)}, u32[]{:S(2)}, u32[]{:S(2)}) collective-permute-start(bf16[256,768]{1,0:T(8,128)(2,1)S(1)} %slice_bitcast_fusion.3), channel_id=1, source_target_pairs={{0,1},{1,0},{2,3},{3,2},{4,5},{5,4},{6,7},{7,6},{8,9},{9,8},{10,11... | collective-permute-start | bytes 1179656 | tf_op jit(solution)/shard_map/ppermute | solution.py:364
  90.5 1.8 %collective-permute-start.11 = (bf16[256,768]{1,0:T(8,128)(2,1)S(1)}, bf16[256,768]{1,0:T(8,128)(2,1)S(1)}, u32[]{:S(2)}, u32[]{:S(2)}) collective-permute-start(bf16[256,768]{1,0:T(8,128)(2,1)S(1)} %slice_bitcast_fusion.4), channel_id=1, source_target_pairs={{0,1},{1,0},{2,3},{3,2},{4,5},{5,4},{6,7},{7,6},{8,9},{9,8},{10,11... | collective-permute-start | bytes 1179656 | tf_op jit(solution)/shard_map/ppermute | solution.py:364
  101.4 11.3 %collective-permute-start.18 = (bf16[1536,512]{1,0:T(8,128)(2,1)}, bf16[1536,512]{1,0:T(8,128)(2,1)S(1)}, u32[]{:S(2)}, u32[]{:S(2)}) collective-permute-start(bf16[1536,512]{1,0:T(8,128)(2,1)} %collective-permute-done.14.refs_6_), channel_id=1, source_target_pairs={{0,1},{1,0},{2,3},{3,2},{4,5},{5,4},{6,7},{7,6},{8,9},{9,8},{10,11... | collective-permute-start | bytes 4718600 | tf_op jit(solution)/shard_map/ppermute | solution.py:416
  101.6 7.9 %collective-permute-start.16 = (bf16[256,384]{1,0:T(8,128)(2,1)}, bf16[256,384]{1,0:T(8,128)(2,1)S(1)}, u32[]{:S(2)}, u32[]{:S(2)}) collective-permute-start(bf16[256,384]{1,0:T(8,128)(2,1)} %get-tuple-element.45), channel_id=1, source_target_pairs={{0,2},{1,3},{2,0},{3,1},{4,6},{5,7},{6,4},{7,5},{8,10},{9,11},{10,... | collective-permute-start | bytes 589832 | tf_op jit(solution)/shard_map/ppermute | solution.py:364
  102.1 6.5 %collective-permute-start.15 = (bf16[256,384]{1,0:T(8,128)(2,1)}, bf16[256,384]{1,0:T(8,128)(2,1)S(1)}, u32[]{:S(2)}, u32[]{:S(2)}) collective-permute-start(bf16[256,384]{1,0:T(8,128)(2,1)} %get-tuple-element.48), channel_id=1, source_target_pairs={{0,1},{1,0},{2,3},{3,2},{4,5},{5,4},{6,7},{7,6},{8,9},{9,8},{10,11... | collective-permute-start | bytes 589832 | tf_op jit(solution)/shard_map/ppermute | solution.py:364
  102.2 10.5 %collective-permute-start.17 = (bf16[256,384]{1,0:T(8,128)(2,1)}, bf16[256,384]{1,0:T(8,128)(2,1)S(1)}, u32[]{:S(2)}, u32[]{:S(2)}) collective-permute-start(bf16[256,384]{1,0:T(8,128)(2,1)} %get-tuple-element.49), channel_id=1, source_target_pairs={{0,3},{1,2},{2,1},{3,0},{4,7},{5,6},{6,5},{7,4},{8,11},{9,10},{10,... | collective-permute-start | bytes 589832 | tf_op jit(solution)/shard_map/ppermute | solution.py:364
  (10 other events, 17.2 us)
Sparse Core Ops, SparseCore 0:
  8.9 42.9 all-gather.2
  53.5 39.0 all-gather.4

commit v12 on v11

--- a/solution.py
+++ b/solution.py
@@ -406,11 +406,11 @@
     begun = attend_begin(after(block_mask, sent), q, here + pieces)
     late = [after(x, begun[0]) for x in late]
     late = [piece for x in late for piece in (x, swap(x))]
-    mixed = attend_finish((2, 3, 1), block_mask, q, begun, late)
-    moved = [to_lane(x, step // 2, step % 2) for x, step in zip(mixed, (2, 3, 1))]
+    mixed = attend_finish((2, 3), block_mask, q, begun, late)
+    back = [to_lane(x, 1, d) for d, x in enumerate(mixed)]
     halves = [after(x, mixed[0]) for x in halves]
-    own = attend_finish((0,), after(block_mask, mixed[0], *halves), q, begun, late)
-    mixed = [own[0], moved[2], moved[0], moved[1]]
+    rest = attend_finish((0, 1), after(block_mask, mixed[0], *halves), q, begun, late)
+    mixed = [rest[0], to_lane(after(rest[1], back[0]), 0, 1)] + back
     weights = [direct_strip, own_strip]
     for x in halves:
         weights += [x, lax.ppermute(x, "core", [(0, 1), (1, 0)])]

time: 130 us -> 129 us (level)
    ppermute x13, waiting for transfers between devices: 32.4 us -> 30.9 us  [to_lane(): lax.ppermute(x, seq, [(index(p, r, c), index(p, r ^ dr, c ^ dc)) for p, r...]
  transfers between devices with their start and end apart: 21 -> 21, of which waited for: 10 -> 9; matrix products, arithmetic and copies ran while one was open for 3% -> 3% of each run, Pallas kernels for 26% -> 26%
where the time goes in v12:
time: 129 us; the launch traced here: 128 us
  waiting for transfers between devices  44.1 us (34%)
  Pallas kernels  43.8 us (34%)
  starting transfers between devices  19.4 us (15%)
  between operations  13.6 us (11%)
  local copies, waits for them, and re-layouts  7.03 us (5%)
    ppermute x13, waiting for transfers between devices, to_lane(): lax.ppermute(x, seq, [(index(p, r, c), index(p, r ^ dr, c ^ dc)) for p, r...  30.9 us
    pallas_call x1, Pallas kernels, attend_begin(): pl.pallas_call(begin_kernel, out_shape=[jax.ShapeDtypeStruct((2, rows, HC...  14.3 us
    pallas_call x2, Pallas kernels, attend_finish(): pl.pallas_call(lambda *refs: finish_kernel(steps, *refs), grid=(1,), out_...  13.3 us
    ppermute x4, waiting for transfers between devices, to_plane(): return lax.ppermute(x, seq, pairs)  12.4 us
    ppermute x4, starting transfers between devices, to_plane(): return lax.ppermute(x, seq, pairs)  10.7 us
    pallas_call x1, Pallas kernels, project(): pl.pallas_call(lambda *refs: project_kernel(order, groups, refs[:LANES],...  8.51 us
    ppermute x13, starting transfers between devices, to_lane(): lax.ppermute(x, seq, [(index(p, r, c), index(p, r ^ dr, c ^ dc)) for p, r...  6.93 us
    pallas_call x2, Pallas kernels, pack(): pl.pallas_call(kernel, out_shape=[jax.ShapeDtypeStruct((2, count, width),...  5.89 us
  transfers between devices with their start and end apart: 21, of which 9 were waited for; matrix products, arithmetic and copies ran while one was open for 3% of the time, Pallas kernels for 26%

profile of v12, /device:TPU:0, one launch (start us, length us, event | category | flops | bytes accessed | tf_op | source)
XLA Modules:
  0.0 128.0 jit_solution(4099926094414721769)
XLA Ops:
  6.5 1.8 %shard_map.66 = (bf16[96,1024]{1,0:T(8,128)(2,1)}, bf16[96,1024]{1,0:T(8,128)(2,1)}) custom-call(s32[1]{0:T(128)} %bitcast.1.at, bf16[96,3072]{1,0:T(8,128)(2,1)} %own_ref.1), custom_call_target="tpu_custom_call" | custom-call | tf_op jit(solution)/shard_map/pallas_call | solution.py:42
  9.2 3.3 %shard_map.64 = (bf16[2,256,768]{2,1,0:T(8,128)(2,1)}, bf16[2,256,768]{2,1,0:T(8,128)(2,1)}, bf16[256,768]{1,0:T(8,128)(2,1)}) custom-call(s32[2]{0:T(128)} %frames.3, bf16[256,1536]{1,0:T(8,128)(2,1)} %k_ref.1, bf16[256,1536]{1,0:T(8,128)(2,1)} %v_ref.1), custom_call_target="tpu_custom_call" | custom-call | tf_op jit(solution)/shard_map/pallas_call | solution.py:88
  12.4 3.0 %collective-permute-start.5 = (bf16[2,256,768]{2,1,0:T(8,128)(2,1)}, bf16[2,256,768]{2,1,0:T(8,128)(2,1)S(1)}, u32[]{:S(2)}, u32[]{:S(2)}) collective-permute-start(bf16[2,256,768]{2,1,0:T(8,128)(2,1)} %get-tuple-element.35), channel_id=1, source_target_pairs={{0,2},{1,3},{2,0},{3,1},{4,6},{5,7},{6,4},{7,5},{8,10},{9,11},{10,... | collective-permute-start | bytes 2359304 | tf_op jit(solution)/shard_map/ppermute | solution.py:364
  15.4 3.5 %collective-permute-start.3 = (bf16[2,256,768]{2,1,0:T(8,128)(2,1)}, bf16[2,256,768]{2,1,0:T(8,128)(2,1)S(1)}, u32[]{:S(2)}, u32[]{:S(2)}) collective-permute-start(bf16[2,256,768]{2,1,0:T(8,128)(2,1)} %get-tuple-element.34.refs_4_), channel_id=1, source_target_pairs={{0,4},{1,5},{2,6},{3,7},{4,8},{5,9},{6,10},{7,11},{8,12},{9,13},{1... | collective-permute-start | bytes 2359304 | tf_op jit(solution)/shard_map/ppermute | solution.py:368
  18.9 1.3 %collective-permute-start.4 = (bf16[2,256,768]{2,1,0:T(8,128)(2,1)}, bf16[2,256,768]{2,1,0:T(8,128)(2,1)}, u32[]{:S(2)}, u32[]{:S(2)}) collective-permute-start(bf16[2,256,768]{2,1,0:T(8,128)(2,1)} %get-tuple-element.34.refs_4_), channel_id=1, source_target_pairs={{4,0},{5,1},{6,2},{7,3},{8,4},{9,5},{10,6},{11,7},{12,8},{13,9},{1... | collective-permute-start | bytes 2359304 | tf_op jit(solution)/shard_map/ppermute | solution.py:368
  20.2 2.6 %shard_map.65 = (bf16[2,256,384]{2,1,0:T(8,128)(2,1)}, bf16[2,256,384]{2,1,0:T(8,128)(2,1)}, bf16[256,384]{1,0:T(8,128)(2,1)}) custom-call(s32[2]{0:T(128)} %frames.3, bf16[256,1536]{1,0:T(8,128)(2,1)} %q_ref), custom_call_target="tpu_custom_call" | custom-call | tf_op jit(solution)/shard_map/pallas_call | solution.py:88
  23.4 24.9 %collective-permute-done.5.refs_6_ = bf16[2,256,768]{2,1,0:T(8,128)(2,1)S(1)} collective-permute-done((bf16[2,256,768]{2,1,0:T(8,128)(2,1)}, bf16[2,256,768]{2,1,0:T(8,128)(2,1)S(1)}, u32[]{:S(2)}, u32[]{:S(2)}) %collective-permute-start.5) | collective-permute-done | bytes 786464 | tf_op jit(solution)/shard_map/ppermute | solution.py:364
  48.3 0.8 slice_bitcast_fusion.2
  49.8 3.4 %collective-permute-done.4.refs_10_ = bf16[2,256,768]{2,1,0:T(8,128)(2,1)} collective-permute-done((bf16[2,256,768]{2,1,0:T(8,128)(2,1)}, bf16[2,256,768]{2,1,0:T(8,128)(2,1)}, u32[]{:S(2)}, u32[]{:S(2)}) %collective-permute-start.4) | collective-permute-done | bytes 786464 | tf_op jit(solution)/shard_map/ppermute | solution.py:368
  53.2 1.3 %collective-permute-start.12 = (bf16[2,256,768]{2,1,0:T(8,128)(2,1)S(1)}, bf16[2,256,768]{2,1,0:T(8,128)(2,1)S(1)}, u32[]{:S(2)}, u32[]{:S(2)}) collective-permute-start(bf16[2,256,768]{2,1,0:T(8,128)(2,1)S(1)} %collective-permute-done.5.refs_6_), channel_id=1, source_target_pairs={{4,0},{5,1},{6,2},{7,3},{8,4},{9,5},{10,6},{11,7},{12,8},{13,9},{1... | collective-permute-start | bytes 2359304 | tf_op jit(solution)/shard_map/ppermute | solution.py:368
  54.5 4.6 %collective-permute-start.10 = (bf16[2,256,768]{2,1,0:T(8,128)(2,1)S(1)}, bf16[2,256,768]{2,1,0:T(8,128)(2,1)S(1)}, u32[]{:S(2)}, u32[]{:S(2)}) collective-permute-start(bf16[2,256,768]{2,1,0:T(8,128)(2,1)S(1)} %collective-permute-done.5.refs_6_), channel_id=1, source_target_pairs={{0,4},{1,5},{2,6},{3,7},{4,8},{5,9},{6,10},{7,11},{8,12},{9,13},{1... | collective-permute-start | bytes 2359304 | tf_op jit(solution)/shard_map/ppermute | solution.py:368
  59.9 1.5 %constant_dynamic-slice_fusion = bf16[1536,512]{1,0:T(8,128)(2,1)S(1)} fusion(bf16[1536,1024]{1,0:T(8,128)(2,1)} %all-gather.3.cloned.1.call-done.refs_5_, s32[]{:T(128)S(6)} %select_n.3), kind=kLoop, calls=%fused_computation.6 | loop fusion | bytes 3145732 | tf_op jit(solution)/shard_map/dynamic_slice | solution.py:400
  61.4 1.6 %collective-permute-start.14 = (bf16[1536,512]{1,0:T(8,128)(2,1)S(1)}, bf16[1536,512]{1,0:T(8,128)(2,1)}, u32[]{:S(2)}, u32[]{:S(2)}) collective-permute-start(bf16[1536,512]{1,0:T(8,128)(2,1)S(1)} %constant_dynamic-slice_fusion), channel_id=1, source_target_pairs={{0,16},{16,0},{1,17},{17,1},{2,18},{18,2},{3,19},{19,3},{4,20},{20... | collective-permute-start | bytes 4718600 | tf_op jit(solution)/shard_map/ppermute | solution.py:402
  63.0 1.0 slice_bitcast_fusion
  64.6 1.2 collective-permute-done.8.refs_9_
  67.2 14.3 %shard_map.67 = (f32[2,256,384]{2,1,0:T(8,128)}, f32[2,256,384]{2,1,0:T(8,128)}, f32[2,256,128]{2,1,0:T(8,128)}, f32[2,256,128]{2,1,0:T(8,128)}) custom-call(s32[32,32]{1,0:T(8,128)} %refs_0_.2, bf16[2,256,384]{2,1,0:T(8,128)(2,1)} %get-tuple-element.38.refs_0_.refs_1_, bf16[256,384]{1,0:T(8,128)(2,1)} %collective-permute-done.7.refs_1_.refs_2_, ...), custom_call_target="tpu_custom_call" | custom-call | flops 1024 | bytes 1024 | tf_op jit(solution)/shard_map/pallas_call | solution.py:242
  81.6 5.4 %collective-permute-done.12.refs_9_ = bf16[2,256,768]{2,1,0:T(8,128)(2,1)S(1)} collective-permute-done((bf16[2,256,768]{2,1,0:T(8,128)(2,1)S(1)}, bf16[2,256,768]{2,1,0:T(8,128)(2,1)S(1)}, u32[]{:S(2)}, u32[]{:S(2)}) %collective-permute-start.12) | collective-permute-done | bytes 786464 | tf_op jit(solution)/shard_map/ppermute | solution.py:368
  87.1 3.4 %collective-permute-done.10.refs_7_ = bf16[2,256,768]{2,1,0:T(8,128)(2,1)S(1)} collective-permute-done((bf16[2,256,768]{2,1,0:T(8,128)(2,1)S(1)}, bf16[2,256,768]{2,1,0:T(8,128)(2,1)S(1)}, u32[]{:S(2)}, u32[]{:S(2)}) %collective-permute-start.10) | collective-permute-done | bytes 786464 | tf_op jit(solution)/shard_map/ppermute | solution.py:368
  90.6 1.7 %collective-permute-done.11.refs_8_ = bf16[256,768]{1,0:T(8,128)(2,1)S(1)} collective-permute-done((bf16[256,768]{1,0:T(8,128)(2,1)S(1)}, bf16[256,768]{1,0:T(8,128)(2,1)S(1)}, u32[]{:S(2)}, u32[]{:S(2)}) %collective-permute-start.11) | collective-permute-done | bytes 393248 | tf_op jit(solution)/shard_map/ppermute | solution.py:364
  93.1 7.0 %shard_map.68 = (bf16[256,384]{1,0:T(8,128)(2,1)}, bf16[256,384]{1,0:T(8,128)(2,1)}) custom-call(s32[32,32]{1,0:T(8,128)} %refs_0_.2, bf16[2,256,384]{2,1,0:T(8,128)(2,1)} %copy-done.2, bf16[256,384]{1,0:T(8,128)(2,1)} %collective-permute-done.2.refs_3_.refs_2_, f32[2,256,384]{2,1,0:T(8,128)} %get-tuple-element.40.refs_3_.refs_4_, ...), custom_call_target="tpu_custom_call" | custom-call | flops 1024 | bytes 1024 | tf_op jit(solution)/shard_map/pallas_call | solution.py:268
  100.8 1.2 collective-permute-start.17
  102.0 6.3 %shard_map.69 = (bf16[256,384]{1,0:T(8,128)(2,1)}, bf16[256,384]{1,0:T(8,128)(2,1)}) custom-call(s32[32,32]{1,0:T(8,128)} %refs_0_.2, bf16[2,256,384]{2,1,0:T(8,128)(2,1)} %get-tuple-element.38.refs_0_.refs_1_, bf16[256,384]{1,0:T(8,128)(2,1)} %collective-permute-done.7.refs_1_.refs_2_, f32[2,256,384]{2,1,0:T(8,128)} %get-tuple-element.43.refs_3_.refs_4_, ...), custom_call_target="tpu_custom_call" | custom-call | flops 1024 | bytes 1024 | tf_op jit(solution)/shard_map/pallas_call | solution.py:268
  108.8 2.5 %collective-permute-done.17.refs_3_ = bf16[256,384]{1,0:T(8,128)(2,1)S(1)} collective-permute-done((bf16[256,384]{1,0:T(8,128)(2,1)}, bf16[256,384]{1,0:T(8,128)(2,1)S(1)}, u32[]{:S(2)}, u32[]{:S(2)}) %collective-permute-start.17) | collective-permute-done | bytes 196640 | tf_op jit(solution)/shard_map/ppermute | solution.py:364
  112.6 8.5 %shard_map.70 = bf16[256,3072]{1,0:T(8,128)(2,1)} custom-call(bf16[256,384]{1,0:T(8,128)(2,1)} %get-tuple-element.50.refs_0_, bf16[256,384]{1,0:T(8,128)(2,1)} %copy-done.12, bf16[256,384]{1,0:T(8,128)(2,1)} %copy-done.10, bf16[256,384]{1,0:T(8,128)(2,1)} %copy-done.11, bf16[1536,1024]{1,0:T(8,128)(2,1)} %all-gather.5.cloned.1.call-done.refs_4_, ...), custom_call_target="tpu_custom_call" | custom-call | tf_op jit(solution)/shard_map/pallas_call | solution.py:333
  (60 shorter events, 8.2 us)
Async XLA Ops:
  6.5 53.3 %all-gather.3.cloned.1.call-start = ((), (), s32[]{:S(2)}) async-start(), calls=%async_computation | async-start | bytes 3342336 | tf_op jit(solution)/shard_map/all_gather | solution.py:377
  8.4 100.4 %all-gather.5.cloned.1.call-start = ((), (), s32[]{:S(2)}) async-start(), calls=%async_computation.1 | async-start | bytes 3342336 | tf_op jit(solution)/shard_map/all_gather | solution.py:377
  12.4 35.8 %collective-permute-start.5 = (bf16[2,256,768]{2,1,0:T(8,128)(2,1)}, bf16[2,256,768]{2,1,0:T(8,128)(2,1)S(1)}, u32[]{:S(2)}, u32[]{:S(2)}) collective-permute-start(bf16[2,256,768]{2,1,0:T(8,128)(2,1)} %get-tuple-element.35), channel_id=1, source_target_pairs={{0,2},{1,3},{2,0},{3,1},{4,6},{5,7},{6,4},{7,5},{8,10},{9,11},{10,... | collective-permute-start | bytes 2359304 | tf_op jit(solution)/shard_map/ppermute | solution.py:364
  15.4 4.8 %collective-permute-start = (bf16[256,768]{1,0:T(8,128)(2,1)}, bf16[256,768]{1,0:T(8,128)(2,1)}, u32[]{:S(2)}, u32[]{:S(2)}) collective-permute-start(bf16[256,768]{1,0:T(8,128)(2,1)} %get-tuple-element.30), channel_id=1, source_target_pairs={{0,1},{1,0},{2,3},{3,2},{4,5},{5,4},{6,7},{7,6},{8,9},{9,8},{10,11... | collective-permute-start | bytes 1179656 | tf_op jit(solution)/shard_map/ppermute | solution.py:364
  15.4 34.4 %collective-permute-start.3 = (bf16[2,256,768]{2,1,0:T(8,128)(2,1)}, bf16[2,256,768]{2,1,0:T(8,128)(2,1)S(1)}, u32[]{:S(2)}, u32[]{:S(2)}) collective-permute-start(bf16[2,256,768]{2,1,0:T(8,128)(2,1)} %get-tuple-element.34.refs_4_), channel_id=1, source_target_pairs={{0,4},{1,5},{2,6},{3,7},{4,8},{5,9},{6,10},{7,11},{8,12},{9,13},{1... | collective-permute-start | bytes 2359304 | tf_op jit(solution)/shard_map/ppermute | solution.py:368
  18.9 34.3 %collective-permute-start.4 = (bf16[2,256,768]{2,1,0:T(8,128)(2,1)}, bf16[2,256,768]{2,1,0:T(8,128)(2,1)}, u32[]{:S(2)}, u32[]{:S(2)}) collective-permute-start(bf16[2,256,768]{2,1,0:T(8,128)(2,1)} %get-tuple-element.34.refs_4_), channel_id=1, source_target_pairs={{4,0},{5,1},{6,2},{7,3},{8,4},{9,5},{10,6},{11,7},{12,8},{13,9},{1... | collective-permute-start | bytes 2359304 | tf_op jit(solution)/shard_map/ppermute | solution.py:368
  22.9 36.2 %collective-permute-start.1 = (bf16[2,256,384]{2,1,0:T(8,128)(2,1)}, bf16[2,256,384]{2,1,0:T(8,128)(2,1)S(1)}, u32[]{:S(2)}, u32[]{:S(2)}) collective-permute-start(bf16[2,256,384]{2,1,0:T(8,128)(2,1)} %get-tuple-element.32), channel_id=1, source_target_pairs={{0,2},{1,3},{2,0},{3,1},{4,6},{5,7},{6,4},{7,5},{8,10},{9,11},{10,... | collective-permute-start | bytes 1179656 | tf_op jit(solution)/shard_map/ppermute | solution.py:364
  48.3 13.2 %copy-start.3 = (bf16[2,256,768]{2,1,0:T(8,128)(2,1)}, bf16[2,256,768]{2,1,0:T(8,128)(2,1)S(1)}, u32[]{:S(2)}) copy-start(bf16[2,256,768]{2,1,0:T(8,128)(2,1)S(1)} %collective-permute-done.5.refs_6_) | copy-start | bytes 2359300
  49.1 10.8 %collective-permute-start.6 = (bf16[256,768]{1,0:T(8,128)(2,1)}, bf16[256,768]{1,0:T(8,128)(2,1)}, u32[]{:S(2)}, u32[]{:S(2)}) collective-permute-start(bf16[256,768]{1,0:T(8,128)(2,1)} %slice_bitcast_fusion.2), channel_id=1, source_target_pairs={{0,1},{1,0},{2,3},{3,2},{4,5},{5,4},{6,7},{7,6},{8,9},{9,8},{10,11... | collective-permute-start | bytes 1179656 | tf_op jit(solution)/shard_map/ppermute | solution.py:364
  49.1 15.0 %collective-permute-start.7 = (bf16[256,384]{1,0:T(8,128)(2,1)}, bf16[256,384]{1,0:T(8,128)(2,1)}, u32[]{:S(2)}, u32[]{:S(2)}) collective-permute-start(bf16[256,384]{1,0:T(8,128)(2,1)} %get-tuple-element.39), channel_id=1, source_target_pairs={{0,1},{1,0},{2,3},{3,2},{4,5},{5,4},{6,7},{7,6},{8,9},{9,8},{10,11... | collective-permute-start | bytes 589832 | tf_op jit(solution)/shard_map/ppermute | solution.py:364
  49.8 13.2 %copy-start.4 = (bf16[2,256,768]{2,1,0:T(8,128)(2,1)}, bf16[2,256,768]{2,1,0:T(8,128)(2,1)S(1)}, u32[]{:S(2)}) copy-start(bf16[2,256,768]{2,1,0:T(8,128)(2,1)S(1)} %collective-permute-done.3.refs_8_) | copy-start | bytes 2359300
  53.2 33.8 %collective-permute-start.12 = (bf16[2,256,768]{2,1,0:T(8,128)(2,1)S(1)}, bf16[2,256,768]{2,1,0:T(8,128)(2,1)S(1)}, u32[]{:S(2)}, u32[]{:S(2)}) collective-permute-start(bf16[2,256,768]{2,1,0:T(8,128)(2,1)S(1)} %collective-permute-done.5.refs_6_), channel_id=1, source_target_pairs={{4,0},{5,1},{6,2},{7,3},{8,4},{9,5},{10,6},{11,7},{12,8},{13,9},{1... | collective-permute-start | bytes 2359304 | tf_op jit(solution)/shard_map/ppermute | solution.py:368
  54.5 36.0 %collective-permute-start.10 = (bf16[2,256,768]{2,1,0:T(8,128)(2,1)S(1)}, bf16[2,256,768]{2,1,0:T(8,128)(2,1)S(1)}, u32[]{:S(2)}, u32[]{:S(2)}) collective-permute-start(bf16[2,256,768]{2,1,0:T(8,128)(2,1)S(1)} %collective-permute-done.5.refs_6_), channel_id=1, source_target_pairs={{0,4},{1,5},{2,6},{3,7},{4,8},{5,9},{6,10},{7,11},{8,12},{9,13},{1... | collective-permute-start | bytes 2359304 | tf_op jit(solution)/shard_map/ppermute | solution.py:368
  59.9 4.5 %collective-permute-start.2 = (bf16[256,384]{1,0:T(8,128)(2,1)}, bf16[256,384]{1,0:T(8,128)(2,1)}, u32[]{:S(2)}, u32[]{:S(2)}) collective-permute-start(bf16[256,384]{1,0:T(8,128)(2,1)} %slice_bitcast_fusion.5), channel_id=1, source_target_pairs={{0,1},{1,0},{2,3},{3,2},{4,5},{5,4},{6,7},{7,6},{8,9},{9,8},{10,11... | collective-permute-start | bytes 589832 | tf_op jit(solution)/shard_map/ppermute | solution.py:364
  61.4 38.6 %collective-permute-start.14 = (bf16[1536,512]{1,0:T(8,128)(2,1)S(1)}, bf16[1536,512]{1,0:T(8,128)(2,1)}, u32[]{:S(2)}, u32[]{:S(2)}) collective-permute-start(bf16[1536,512]{1,0:T(8,128)(2,1)S(1)} %constant_dynamic-slice_fusion), channel_id=1, source_target_pairs={{0,16},{16,0},{1,17},{17,1},{2,18},{18,2},{3,19},{19,3},{4,20},{20... | collective-permute-start | bytes 4718600 | tf_op jit(solution)/shard_map/ppermute | solution.py:402
  64.1 1.8 %collective-permute-start.8 = (bf16[256,768]{1,0:T(8,128)(2,1)S(1)}, bf16[256,768]{1,0:T(8,128)(2,1)S(1)}, u32[]{:S(2)}, u32[]{:S(2)}) collective-permute-start(bf16[256,768]{1,0:T(8,128)(2,1)S(1)} %slice_bitcast_fusion.1), channel_id=1, source_target_pairs={{0,1},{1,0},{2,3},{3,2},{4,5},{5,4},{6,7},{7,6},{8,9},{9,8},{10,11... | collective-permute-start | bytes 1179656 | tf_op jit(solution)/shard_map/ppermute | solution.py:364
  64.3 2.1 %collective-permute-start.9 = (bf16[256,768]{1,0:T(8,128)(2,1)S(1)}, bf16[256,768]{1,0:T(8,128)(2,1)S(1)}, u32[]{:S(2)}, u32[]{:S(2)}) collective-permute-start(bf16[256,768]{1,0:T(8,128)(2,1)S(1)} %slice_bitcast_fusion), channel_id=1, source_target_pairs={{0,1},{1,0},{2,3},{3,2},{4,5},{5,4},{6,7},{7,6},{8,9},{9,8},{10,11... | collective-permute-start | bytes 1179656 | tf_op jit(solution)/shard_map/ppermute | solution.py:364
  87.0 5.3 %copy-start = (bf16[2,256,768]{2,1,0:T(8,128)(2,1)}, bf16[2,256,768]{2,1,0:T(8,128)(2,1)S(1)}, u32[]{:S(2)}) copy-start(bf16[2,256,768]{2,1,0:T(8,128)(2,1)S(1)} %collective-permute-done.12.refs_9_) | copy-start | bytes 2359300
  87.0 3.6 %collective-permute-start.13 = (bf16[256,768]{1,0:T(8,128)(2,1)S(1)}, bf16[256,768]{1,0:T(8,128)(2,1)S(1)}, u32[]{:S(2)}, u32[]{:S(2)}) collective-permute-start(bf16[256,768]{1,0:T(8,128)(2,1)S(1)} %slice_bitcast_fusion.3), channel_id=1, source_target_pairs={{0,1},{1,0},{2,3},{3,2},{4,5},{5,4},{6,7},{7,6},{8,9},{9,8},{10,11... | collective-permute-start | bytes 1179656 | tf_op jit(solution)/shard_map/ppermute | solution.py:364
  90.5 1.8 %collective-permute-start.11 = (bf16[256,768]{1,0:T(8,128)(2,1)S(1)}, bf16[256,768]{1,0:T(8,128)(2,1)S(1)}, u32[]{:S(2)}, u32[]{:S(2)}) collective-permute-start(bf16[256,768]{1,0:T(8,128)(2,1)S(1)} %slice_bitcast_fusion.4), channel_id=1, source_target_pairs={{0,1},{1,0},{2,3},{3,2},{4,5},{5,4},{6,7},{7,6},{8,9},{9,8},{10,11... | collective-permute-start | bytes 1179656 | tf_op jit(solution)/shard_map/ppermute | solution.py:364
  100.1 11.3 %collective-permute-start.18 = (bf16[1536,512]{1,0:T(8,128)(2,1)}, bf16[1536,512]{1,0:T(8,128)(2,1)S(1)}, u32[]{:S(2)}, u32[]{:S(2)}) collective-permute-start(bf16[1536,512]{1,0:T(8,128)(2,1)} %collective-permute-done.14.refs_6_), channel_id=1, source_target_pairs={{0,1},{1,0},{2,3},{3,2},{4,5},{5,4},{6,7},{7,6},{8,9},{9,8},{10,11... | collective-permute-start | bytes 4718600 | tf_op jit(solution)/shard_map/ppermute | solution.py:416
  100.3 8.0 %collective-permute-start.15 = (bf16[256,384]{1,0:T(8,128)(2,1)}, bf16[256,384]{1,0:T(8,128)(2,1)S(1)}, u32[]{:S(2)}, u32[]{:S(2)}) collective-permute-start(bf16[256,384]{1,0:T(8,128)(2,1)} %get-tuple-element.46), channel_id=1, source_target_pairs={{0,2},{1,3},{2,0},{3,1},{4,6},{5,7},{6,4},{7,5},{8,10},{9,11},{10,... | collective-permute-start | bytes 589832 | tf_op jit(solution)/shard_map/ppermute | solution.py:364
  100.8 10.5 %collective-permute-start.17 = (bf16[256,384]{1,0:T(8,128)(2,1)}, bf16[256,384]{1,0:T(8,128)(2,1)S(1)}, u32[]{:S(2)}, u32[]{:S(2)}) collective-permute-start(bf16[256,384]{1,0:T(8,128)(2,1)} %get-tuple-element.53), channel_id=1, source_target_pairs={{0,3},{1,2},{2,1},{3,0},{4,7},{5,6},{6,5},{7,4},{8,11},{9,10},{10,... | collective-permute-start | bytes 589832 | tf_op jit(solution)/shard_map/ppermute | solution.py:364
  108.3 3.0 %collective-permute-start.16 = (bf16[256,384]{1,0:T(8,128)(2,1)}, bf16[256,384]{1,0:T(8,128)(2,1)S(1)}, u32[]{:S(2)}, u32[]{:S(2)}) collective-permute-start(bf16[256,384]{1,0:T(8,128)(2,1)} %get-tuple-element.52), channel_id=1, source_target_pairs={{0,1},{1,0},{2,3},{3,2},{4,5},{5,4},{6,7},{7,6},{8,9},{9,8},{10,11... | collective-permute-start | bytes 589832 | tf_op jit(solution)/shard_map/ppermute | solution.py:364
  (10 other events, 13.9 us)
Sparse Core Ops, SparseCore 0:
  8.9 42.9 all-gather.2
  53.6 39.0 all-gather.4

commit v13 on v12

--- a/solution.py
+++ b/solution.py
@@ -328,7 +328,7 @@
 def project(attended, weights, order, groups):
     count, depth = attended[0].shape
     channels = weights[0].shape[0]
-    steps = weights[-1].shape[1] // HDIM
+    steps = weights[-1].shape[1] // (2 * HDIM)
     columns = weights[0].shape[1] + groups * weights[1].shape[1]
     return pl.pallas_call(
         lambda *refs: project_kernel(order, groups, refs[:LANES], refs[LANES:-4], *refs[-4:]),

time: 129 us -> 128 us (level)
  no operation moved by 1% of the time
where the time goes in v13:
time: 128 us
  waiting for transfers between devices  44.1 us (34%)
  Pallas kernels  43.6 us (34%)
  starting transfers between devices  19.4 us (15%)
  between operations  13.6 us (11%)
  local copies, waits for them, and re-layouts  7.03 us (5%)
    ppermute x13, waiting for transfers between devices, to_lane(): lax.ppermute(x, seq, [(index(p, r, c), index(p, r ^ dr, c ^ dc)) for p, r...  30.9 us
    pallas_call x1, Pallas kernels, attend_begin(): pl.pallas_call(begin_kernel, out_shape=[jax.ShapeDtypeStruct((2, rows, HC...  14.3 us
    pallas_call x2, Pallas kernels, attend_finish(): pl.pallas_call(lambda *refs: finish_kernel(steps, *refs), grid=(1,), out_...  13.3 us
    ppermute x4, waiting for transfers between devices, to_plane(): return lax.ppermute(x, seq, pairs)  12.4 us
    ppermute x4, starting transfers between devices, to_plane(): return lax.ppermute(x, seq, pairs)  10.7 us
    pallas_call x1, Pallas kernels, project(): pl.pallas_call(lambda *refs: project_kernel(order, groups, refs[:LANES],...  8.25 us
    ppermute x13, starting transfers between devices, to_lane(): lax.ppermute(x, seq, [(index(p, r, c), index(p, r ^ dr, c ^ dc)) for p, r...  6.93 us
    pallas_call x2, Pallas kernels, pack(): pl.pallas_call(kernel, out_shape=[jax.ShapeDtypeStruct((2, count, width),...  5.89 us
  transfers between devices with their start and end apart: 21, of which 9 were waited for; matrix products, arithmetic and copies ran while one was open for 3% of the time, Pallas kernels for 26%

profile of v13, /device:TPU:0, one launch (start us, length us, event | category | flops | bytes accessed | tf_op | source)
XLA Modules:
  0.0 127.7 jit_solution(874357490521367976)
XLA Ops:
  6.5 1.8 %shard_map.66 = (bf16[96,1024]{1,0:T(8,128)(2,1)}, bf16[96,1024]{1,0:T(8,128)(2,1)}) custom-call(s32[1]{0:T(128)} %bitcast.1.at, bf16[96,3072]{1,0:T(8,128)(2,1)} %own_ref.1), custom_call_target="tpu_custom_call" | custom-call | tf_op jit(solution)/shard_map/pallas_call | solution.py:42
  9.2 3.3 %shard_map.64 = (bf16[2,256,768]{2,1,0:T(8,128)(2,1)}, bf16[2,256,768]{2,1,0:T(8,128)(2,1)}, bf16[256,768]{1,0:T(8,128)(2,1)}) custom-call(s32[2]{0:T(128)} %frames.3, bf16[256,1536]{1,0:T(8,128)(2,1)} %k_ref.1, bf16[256,1536]{1,0:T(8,128)(2,1)} %v_ref.1), custom_call_target="tpu_custom_call" | custom-call | tf_op jit(solution)/shard_map/pallas_call | solution.py:88
  12.4 3.0 %collective-permute-start.5 = (bf16[2,256,768]{2,1,0:T(8,128)(2,1)}, bf16[2,256,768]{2,1,0:T(8,128)(2,1)S(1)}, u32[]{:S(2)}, u32[]{:S(2)}) collective-permute-start(bf16[2,256,768]{2,1,0:T(8,128)(2,1)} %get-tuple-element.35), channel_id=1, source_target_pairs={{0,2},{1,3},{2,0},{3,1},{4,6},{5,7},{6,4},{7,5},{8,10},{9,11},{10,... | collective-permute-start | bytes 2359304 | tf_op jit(solution)/shard_map/ppermute | solution.py:364
  15.4 3.5 %collective-permute-start.3 = (bf16[2,256,768]{2,1,0:T(8,128)(2,1)}, bf16[2,256,768]{2,1,0:T(8,128)(2,1)S(1)}, u32[]{:S(2)}, u32[]{:S(2)}) collective-permute-start(bf16[2,256,768]{2,1,0:T(8,128)(2,1)} %get-tuple-element.34.refs_4_), channel_id=1, source_target_pairs={{0,4},{1,5},{2,6},{3,7},{4,8},{5,9},{6,10},{7,11},{8,12},{9,13},{1... | collective-permute-start | bytes 2359304 | tf_op jit(solution)/shard_map/ppermute | solution.py:368
  18.9 1.3 %collective-permute-start.4 = (bf16[2,256,768]{2,1,0:T(8,128)(2,1)}, bf16[2,256,768]{2,1,0:T(8,128)(2,1)}, u32[]{:S(2)}, u32[]{:S(2)}) collective-permute-start(bf16[2,256,768]{2,1,0:T(8,128)(2,1)} %get-tuple-element.34.refs_4_), channel_id=1, source_target_pairs={{4,0},{5,1},{6,2},{7,3},{8,4},{9,5},{10,6},{11,7},{12,8},{13,9},{1... | collective-permute-start | bytes 2359304 | tf_op jit(solution)/shard_map/ppermute | solution.py:368
  20.2 2.6 %shard_map.65 = (bf16[2,256,384]{2,1,0:T(8,128)(2,1)}, bf16[2,256,384]{2,1,0:T(8,128)(2,1)}, bf16[256,384]{1,0:T(8,128)(2,1)}) custom-call(s32[2]{0:T(128)} %frames.3, bf16[256,1536]{1,0:T(8,128)(2,1)} %q_ref), custom_call_target="tpu_custom_call" | custom-call | tf_op jit(solution)/shard_map/pallas_call | solution.py:88
  23.4 24.9 %collective-permute-done.5.refs_6_ = bf16[2,256,768]{2,1,0:T(8,128)(2,1)S(1)} collective-permute-done((bf16[2,256,768]{2,1,0:T(8,128)(2,1)}, bf16[2,256,768]{2,1,0:T(8,128)(2,1)S(1)}, u32[]{:S(2)}, u32[]{:S(2)}) %collective-permute-start.5) | collective-permute-done | bytes 786464 | tf_op jit(solution)/shard_map/ppermute | solution.py:364
  48.3 0.8 slice_bitcast_fusion.2
  49.8 3.4 %collective-permute-done.4.refs_10_ = bf16[2,256,768]{2,1,0:T(8,128)(2,1)} collective-permute-done((bf16[2,256,768]{2,1,0:T(8,128)(2,1)}, bf16[2,256,768]{2,1,0:T(8,128)(2,1)}, u32[]{:S(2)}, u32[]{:S(2)}) %collective-permute-start.4) | collective-permute-done | bytes 786464 | tf_op jit(solution)/shard_map/ppermute | solution.py:368
  53.2 1.3 %collective-permute-start.12 = (bf16[2,256,768]{2,1,0:T(8,128)(2,1)S(1)}, bf16[2,256,768]{2,1,0:T(8,128)(2,1)S(1)}, u32[]{:S(2)}, u32[]{:S(2)}) collective-permute-start(bf16[2,256,768]{2,1,0:T(8,128)(2,1)S(1)} %collective-permute-done.5.refs_6_), channel_id=1, source_target_pairs={{4,0},{5,1},{6,2},{7,3},{8,4},{9,5},{10,6},{11,7},{12,8},{13,9},{1... | collective-permute-start | bytes 2359304 | tf_op jit(solution)/shard_map/ppermute | solution.py:368
  54.5 4.6 %collective-permute-start.10 = (bf16[2,256,768]{2,1,0:T(8,128)(2,1)S(1)}, bf16[2,256,768]{2,1,0:T(8,128)(2,1)S(1)}, u32[]{:S(2)}, u32[]{:S(2)}) collective-permute-start(bf16[2,256,768]{2,1,0:T(8,128)(2,1)S(1)} %collective-permute-done.5.refs_6_), channel_id=1, source_target_pairs={{0,4},{1,5},{2,6},{3,7},{4,8},{5,9},{6,10},{7,11},{8,12},{9,13},{1... | collective-permute-start | bytes 2359304 | tf_op jit(solution)/shard_map/ppermute | solution.py:368
  59.9 1.5 %constant_dynamic-slice_fusion = bf16[1536,512]{1,0:T(8,128)(2,1)S(1)} fusion(bf16[1536,1024]{1,0:T(8,128)(2,1)} %all-gather.3.cloned.1.call-done.refs_5_, s32[]{:T(128)S(6)} %select_n.3), kind=kLoop, calls=%fused_computation.6 | loop fusion | bytes 3145732 | tf_op jit(solution)/shard_map/dynamic_slice | solution.py:400
  61.4 1.6 %collective-permute-start.14 = (bf16[1536,512]{1,0:T(8,128)(2,1)S(1)}, bf16[1536,512]{1,0:T(8,128)(2,1)}, u32[]{:S(2)}, u32[]{:S(2)}) collective-permute-start(bf16[1536,512]{1,0:T(8,128)(2,1)S(1)} %constant_dynamic-slice_fusion), channel_id=1, source_target_pairs={{0,16},{16,0},{1,17},{17,1},{2,18},{18,2},{3,19},{19,3},{4,20},{20... | collective-permute-start | bytes 4718600 | tf_op jit(solution)/shard_map/ppermute | solution.py:402
  63.0 1.0 slice_bitcast_fusion
  64.6 1.2 collective-permute-done.8.refs_9_
  67.2 14.3 %shard_map.67 = (f32[2,256,384]{2,1,0:T(8,128)}, f32[2,256,384]{2,1,0:T(8,128)}, f32[2,256,128]{2,1,0:T(8,128)}, f32[2,256,128]{2,1,0:T(8,128)}) custom-call(s32[32,32]{1,0:T(8,128)} %refs_0_.2, bf16[2,256,384]{2,1,0:T(8,128)(2,1)} %get-tuple-element.38.refs_0_.refs_1_, bf16[256,384]{1,0:T(8,128)(2,1)} %collective-permute-done.7.refs_1_.refs_2_, ...), custom_call_target="tpu_custom_call" | custom-call | flops 1024 | bytes 1024 | tf_op jit(solution)/shard_map/pallas_call | solution.py:242
  81.6 5.4 %collective-permute-done.12.refs_9_ = bf16[2,256,768]{2,1,0:T(8,128)(2,1)S(1)} collective-permute-done((bf16[2,256,768]{2,1,0:T(8,128)(2,1)S(1)}, bf16[2,256,768]{2,1,0:T(8,128)(2,1)S(1)}, u32[]{:S(2)}, u32[]{:S(2)}) %collective-permute-start.12) | collective-permute-done | bytes 786464 | tf_op jit(solution)/shard_map/ppermute | solution.py:368
  87.1 3.4 %collective-permute-done.10.refs_7_ = bf16[2,256,768]{2,1,0:T(8,128)(2,1)S(1)} collective-permute-done((bf16[2,256,768]{2,1,0:T(8,128)(2,1)S(1)}, bf16[2,256,768]{2,1,0:T(8,128)(2,1)S(1)}, u32[]{:S(2)}, u32[]{:S(2)}) %collective-permute-start.10) | collective-permute-done | bytes 786464 | tf_op jit(solution)/shard_map/ppermute | solution.py:368
  90.6 1.7 %collective-permute-done.11.refs_8_ = bf16[256,768]{1,0:T(8,128)(2,1)S(1)} collective-permute-done((bf16[256,768]{1,0:T(8,128)(2,1)S(1)}, bf16[256,768]{1,0:T(8,128)(2,1)S(1)}, u32[]{:S(2)}, u32[]{:S(2)}) %collective-permute-start.11) | collective-permute-done | bytes 393248 | tf_op jit(solution)/shard_map/ppermute | solution.py:364
  93.1 7.0 %shard_map.68 = (bf16[256,384]{1,0:T(8,128)(2,1)}, bf16[256,384]{1,0:T(8,128)(2,1)}) custom-call(s32[32,32]{1,0:T(8,128)} %refs_0_.2, bf16[2,256,384]{2,1,0:T(8,128)(2,1)} %copy-done.2, bf16[256,384]{1,0:T(8,128)(2,1)} %collective-permute-done.2.refs_3_.refs_2_, f32[2,256,384]{2,1,0:T(8,128)} %get-tuple-element.40.refs_3_.refs_4_, ...), custom_call_target="tpu_custom_call" | custom-call | flops 1024 | bytes 1024 | tf_op jit(solution)/shard_map/pallas_call | solution.py:268
  100.8 1.2 collective-permute-start.17
  102.0 6.3 %shard_map.69 = (bf16[256,384]{1,0:T(8,128)(2,1)}, bf16[256,384]{1,0:T(8,128)(2,1)}) custom-call(s32[32,32]{1,0:T(8,128)} %refs_0_.2, bf16[2,256,384]{2,1,0:T(8,128)(2,1)} %get-tuple-element.38.refs_0_.refs_1_, bf16[256,384]{1,0:T(8,128)(2,1)} %collective-permute-done.7.refs_1_.refs_2_, f32[2,256,384]{2,1,0:T(8,128)} %get-tuple-element.43.refs_3_.refs_4_, ...), custom_call_target="tpu_custom_call" | custom-call | flops 1024 | bytes 1024 | tf_op jit(solution)/shard_map/pallas_call | solution.py:268
  108.8 2.5 %collective-permute-done.17.refs_3_ = bf16[256,384]{1,0:T(8,128)(2,1)S(1)} collective-permute-done((bf16[256,384]{1,0:T(8,128)(2,1)}, bf16[256,384]{1,0:T(8,128)(2,1)S(1)}, u32[]{:S(2)}, u32[]{:S(2)}) %collective-permute-start.17) | collective-permute-done | bytes 196640 | tf_op jit(solution)/shard_map/ppermute | solution.py:364
  112.6 8.3 %shard_map.70 = bf16[256,3072]{1,0:T(8,128)(2,1)} custom-call(bf16[256,384]{1,0:T(8,128)(2,1)} %get-tuple-element.50.refs_0_, bf16[256,384]{1,0:T(8,128)(2,1)} %copy-done.12, bf16[256,384]{1,0:T(8,128)(2,1)} %copy-done.10, bf16[256,384]{1,0:T(8,128)(2,1)} %copy-done.11, bf16[1536,1024]{1,0:T(8,128)(2,1)} %all-gather.5.cloned.1.call-done.refs_4_, ...), custom_call_target="tpu_custom_call" | custom-call | tf_op jit(solution)/shard_map/pallas_call | solution.py:333
  (60 shorter events, 8.2 us)
Async XLA Ops:
  6.5 53.3 %all-gather.3.cloned.1.call-start = ((), (), s32[]{:S(2)}) async-start(), calls=%async_computation | async-start | bytes 3342336 | tf_op jit(solution)/shard_map/all_gather | solution.py:377
  8.4 100.4 %all-gather.5.cloned.1.call-start = ((), (), s32[]{:S(2)}) async-start(), calls=%async_computation.1 | async-start | bytes 3342336 | tf_op jit(solution)/shard_map/all_gather | solution.py:377
  12.4 35.8 %collective-permute-start.5 = (bf16[2,256,768]{2,1,0:T(8,128)(2,1)}, bf16[2,256,768]{2,1,0:T(8,128)(2,1)S(1)}, u32[]{:S(2)}, u32[]{:S(2)}) collective-permute-start(bf16[2,256,768]{2,1,0:T(8,128)(2,1)} %get-tuple-element.35), channel_id=1, source_target_pairs={{0,2},{1,3},{2,0},{3,1},{4,6},{5,7},{6,4},{7,5},{8,10},{9,11},{10,... | collective-permute-start | bytes 2359304 | tf_op jit(solution)/shard_map/ppermute | solution.py:364
  15.4 4.8 %collective-permute-start = (bf16[256,768]{1,0:T(8,128)(2,1)}, bf16[256,768]{1,0:T(8,128)(2,1)}, u32[]{:S(2)}, u32[]{:S(2)}) collective-permute-start(bf16[256,768]{1,0:T(8,128)(2,1)} %get-tuple-element.30), channel_id=1, source_target_pairs={{0,1},{1,0},{2,3},{3,2},{4,5},{5,4},{6,7},{7,6},{8,9},{9,8},{10,11... | collective-permute-start | bytes 1179656 | tf_op jit(solution)/shard_map/ppermute | solution.py:364
  15.4 34.4 %collective-permute-start.3 = (bf16[2,256,768]{2,1,0:T(8,128)(2,1)}, bf16[2,256,768]{2,1,0:T(8,128)(2,1)S(1)}, u32[]{:S(2)}, u32[]{:S(2)}) collective-permute-start(bf16[2,256,768]{2,1,0:T(8,128)(2,1)} %get-tuple-element.34.refs_4_), channel_id=1, source_target_pairs={{0,4},{1,5},{2,6},{3,7},{4,8},{5,9},{6,10},{7,11},{8,12},{9,13},{1... | collective-permute-start | bytes 2359304 | tf_op jit(solution)/shard_map/ppermute | solution.py:368
  18.9 34.3 %collective-permute-start.4 = (bf16[2,256,768]{2,1,0:T(8,128)(2,1)}, bf16[2,256,768]{2,1,0:T(8,128)(2,1)}, u32[]{:S(2)}, u32[]{:S(2)}) collective-permute-start(bf16[2,256,768]{2,1,0:T(8,128)(2,1)} %get-tuple-element.34.refs_4_), channel_id=1, source_target_pairs={{4,0},{5,1},{6,2},{7,3},{8,4},{9,5},{10,6},{11,7},{12,8},{13,9},{1... | collective-permute-start | bytes 2359304 | tf_op jit(solution)/shard_map/ppermute | solution.py:368
  22.9 36.2 %collective-permute-start.1 = (bf16[2,256,384]{2,1,0:T(8,128)(2,1)}, bf16[2,256,384]{2,1,0:T(8,128)(2,1)S(1)}, u32[]{:S(2)}, u32[]{:S(2)}) collective-permute-start(bf16[2,256,384]{2,1,0:T(8,128)(2,1)} %get-tuple-element.32), channel_id=1, source_target_pairs={{0,2},{1,3},{2,0},{3,1},{4,6},{5,7},{6,4},{7,5},{8,10},{9,11},{10,... | collective-permute-start | bytes 1179656 | tf_op jit(solution)/shard_map/ppermute | solution.py:364
  48.3 13.2 %copy-start.3 = (bf16[2,256,768]{2,1,0:T(8,128)(2,1)}, bf16[2,256,768]{2,1,0:T(8,128)(2,1)S(1)}, u32[]{:S(2)}) copy-start(bf16[2,256,768]{2,1,0:T(8,128)(2,1)S(1)} %collective-permute-done.5.refs_6_) | copy-start | bytes 2359300
  49.1 10.8 %collective-permute-start.6 = (bf16[256,768]{1,0:T(8,128)(2,1)}, bf16[256,768]{1,0:T(8,128)(2,1)}, u32[]{:S(2)}, u32[]{:S(2)}) collective-permute-start(bf16[256,768]{1,0:T(8,128)(2,1)} %slice_bitcast_fusion.2), channel_id=1, source_target_pairs={{0,1},{1,0},{2,3},{3,2},{4,5},{5,4},{6,7},{7,6},{8,9},{9,8},{10,11... | collective-permute-start | bytes 1179656 | tf_op jit(solution)/shard_map/ppermute | solution.py:364
  49.1 15.0 %collective-permute-start.7 = (bf16[256,384]{1,0:T(8,128)(2,1)}, bf16[256,384]{1,0:T(8,128)(2,1)}, u32[]{:S(2)}, u32[]{:S(2)}) collective-permute-start(bf16[256,384]{1,0:T(8,128)(2,1)} %get-tuple-element.39), channel_id=1, source_target_pairs={{0,1},{1,0},{2,3},{3,2},{4,5},{5,4},{6,7},{7,6},{8,9},{9,8},{10,11... | collective-permute-start | bytes 589832 | tf_op jit(solution)/shard_map/ppermute | solution.py:364
  49.8 13.2 %copy-start.4 = (bf16[2,256,768]{2,1,0:T(8,128)(2,1)}, bf16[2,256,768]{2,1,0:T(8,128)(2,1)S(1)}, u32[]{:S(2)}) copy-start(bf16[2,256,768]{2,1,0:T(8,128)(2,1)S(1)} %collective-permute-done.3.refs_8_) | copy-start | bytes 2359300
  53.2 33.8 %collective-permute-start.12 = (bf16[2,256,768]{2,1,0:T(8,128)(2,1)S(1)}, bf16[2,256,768]{2,1,0:T(8,128)(2,1)S(1)}, u32[]{:S(2)}, u32[]{:S(2)}) collective-permute-start(bf16[2,256,768]{2,1,0:T(8,128)(2,1)S(1)} %collective-permute-done.5.refs_6_), channel_id=1, source_target_pairs={{4,0},{5,1},{6,2},{7,3},{8,4},{9,5},{10,6},{11,7},{12,8},{13,9},{1... | collective-permute-start | bytes 2359304 | tf_op jit(solution)/shard_map/ppermute | solution.py:368
  54.5 36.0 %collective-permute-start.10 = (bf16[2,256,768]{2,1,0:T(8,128)(2,1)S(1)}, bf16[2,256,768]{2,1,0:T(8,128)(2,1)S(1)}, u32[]{:S(2)}, u32[]{:S(2)}) collective-permute-start(bf16[2,256,768]{2,1,0:T(8,128)(2,1)S(1)} %collective-permute-done.5.refs_6_), channel_id=1, source_target_pairs={{0,4},{1,5},{2,6},{3,7},{4,8},{5,9},{6,10},{7,11},{8,12},{9,13},{1... | collective-permute-start | bytes 2359304 | tf_op jit(solution)/shard_map/ppermute | solution.py:368
  59.9 4.5 %collective-permute-start.2 = (bf16[256,384]{1,0:T(8,128)(2,1)}, bf16[256,384]{1,0:T(8,128)(2,1)}, u32[]{:S(2)}, u32[]{:S(2)}) collective-permute-start(bf16[256,384]{1,0:T(8,128)(2,1)} %slice_bitcast_fusion.5), channel_id=1, source_target_pairs={{0,1},{1,0},{2,3},{3,2},{4,5},{5,4},{6,7},{7,6},{8,9},{9,8},{10,11... | collective-permute-start | bytes 589832 | tf_op jit(solution)/shard_map/ppermute | solution.py:364
  61.4 38.6 %collective-permute-start.14 = (bf16[1536,512]{1,0:T(8,128)(2,1)S(1)}, bf16[1536,512]{1,0:T(8,128)(2,1)}, u32[]{:S(2)}, u32[]{:S(2)}) collective-permute-start(bf16[1536,512]{1,0:T(8,128)(2,1)S(1)} %constant_dynamic-slice_fusion), channel_id=1, source_target_pairs={{0,16},{16,0},{1,17},{17,1},{2,18},{18,2},{3,19},{19,3},{4,20},{20... | collective-permute-start | bytes 4718600 | tf_op jit(solution)/shard_map/ppermute | solution.py:402
  64.1 1.8 %collective-permute-start.8 = (bf16[256,768]{1,0:T(8,128)(2,1)S(1)}, bf16[256,768]{1,0:T(8,128)(2,1)S(1)}, u32[]{:S(2)}, u32[]{:S(2)}) collective-permute-start(bf16[256,768]{1,0:T(8,128)(2,1)S(1)} %slice_bitcast_fusion.1), channel_id=1, source_target_pairs={{0,1},{1,0},{2,3},{3,2},{4,5},{5,4},{6,7},{7,6},{8,9},{9,8},{10,11... | collective-permute-start | bytes 1179656 | tf_op jit(solution)/shard_map/ppermute | solution.py:364
  64.3 2.1 %collective-permute-start.9 = (bf16[256,768]{1,0:T(8,128)(2,1)S(1)}, bf16[256,768]{1,0:T(8,128)(2,1)S(1)}, u32[]{:S(2)}, u32[]{:S(2)}) collective-permute-start(bf16[256,768]{1,0:T(8,128)(2,1)S(1)} %slice_bitcast_fusion), channel_id=1, source_target_pairs={{0,1},{1,0},{2,3},{3,2},{4,5},{5,4},{6,7},{7,6},{8,9},{9,8},{10,11... | collective-permute-start | bytes 1179656 | tf_op jit(solution)/shard_map/ppermute | solution.py:364
  87.0 5.3 %copy-start = (bf16[2,256,768]{2,1,0:T(8,128)(2,1)}, bf16[2,256,768]{2,1,0:T(8,128)(2,1)S(1)}, u32[]{:S(2)}) copy-start(bf16[2,256,768]{2,1,0:T(8,128)(2,1)S(1)} %collective-permute-done.12.refs_9_) | copy-start | bytes 2359300
  87.0 3.6 %collective-permute-start.13 = (bf16[256,768]{1,0:T(8,128)(2,1)S(1)}, bf16[256,768]{1,0:T(8,128)(2,1)S(1)}, u32[]{:S(2)}, u32[]{:S(2)}) collective-permute-start(bf16[256,768]{1,0:T(8,128)(2,1)S(1)} %slice_bitcast_fusion.3), channel_id=1, source_target_pairs={{0,1},{1,0},{2,3},{3,2},{4,5},{5,4},{6,7},{7,6},{8,9},{9,8},{10,11... | collective-permute-start | bytes 1179656 | tf_op jit(solution)/shard_map/ppermute | solution.py:364
  90.5 1.8 %collective-permute-start.11 = (bf16[256,768]{1,0:T(8,128)(2,1)S(1)}, bf16[256,768]{1,0:T(8,128)(2,1)S(1)}, u32[]{:S(2)}, u32[]{:S(2)}) collective-permute-start(bf16[256,768]{1,0:T(8,128)(2,1)S(1)} %slice_bitcast_fusion.4), channel_id=1, source_target_pairs={{0,1},{1,0},{2,3},{3,2},{4,5},{5,4},{6,7},{7,6},{8,9},{9,8},{10,11... | collective-permute-start | bytes 1179656 | tf_op jit(solution)/shard_map/ppermute | solution.py:364
  100.1 11.3 %collective-permute-start.18 = (bf16[1536,512]{1,0:T(8,128)(2,1)}, bf16[1536,512]{1,0:T(8,128)(2,1)S(1)}, u32[]{:S(2)}, u32[]{:S(2)}) collective-permute-start(bf16[1536,512]{1,0:T(8,128)(2,1)} %collective-permute-done.14.refs_6_), channel_id=1, source_target_pairs={{0,1},{1,0},{2,3},{3,2},{4,5},{5,4},{6,7},{7,6},{8,9},{9,8},{10,11... | collective-permute-start | bytes 4718600 | tf_op jit(solution)/shard_map/ppermute | solution.py:416
  100.3 8.0 %collective-permute-start.15 = (bf16[256,384]{1,0:T(8,128)(2,1)}, bf16[256,384]{1,0:T(8,128)(2,1)S(1)}, u32[]{:S(2)}, u32[]{:S(2)}) collective-permute-start(bf16[256,384]{1,0:T(8,128)(2,1)} %get-tuple-element.46), channel_id=1, source_target_pairs={{0,2},{1,3},{2,0},{3,1},{4,6},{5,7},{6,4},{7,5},{8,10},{9,11},{10,... | collective-permute-start | bytes 589832 | tf_op jit(solution)/shard_map/ppermute | solution.py:364
  100.8 10.5 %collective-permute-start.17 = (bf16[256,384]{1,0:T(8,128)(2,1)}, bf16[256,384]{1,0:T(8,128)(2,1)S(1)}, u32[]{:S(2)}, u32[]{:S(2)}) collective-permute-start(bf16[256,384]{1,0:T(8,128)(2,1)} %get-tuple-element.53), channel_id=1, source_target_pairs={{0,3},{1,2},{2,1},{3,0},{4,7},{5,6},{6,5},{7,4},{8,11},{9,10},{10,... | collective-permute-start | bytes 589832 | tf_op jit(solution)/shard_map/ppermute | solution.py:364
  108.3 3.0 %collective-permute-start.16 = (bf16[256,384]{1,0:T(8,128)(2,1)}, bf16[256,384]{1,0:T(8,128)(2,1)S(1)}, u32[]{:S(2)}, u32[]{:S(2)}) collective-permute-start(bf16[256,384]{1,0:T(8,128)(2,1)} %get-tuple-element.52), channel_id=1, source_target_pairs={{0,1},{1,0},{2,3},{3,2},{4,5},{5,4},{6,7},{7,6},{8,9},{9,8},{10,11... | collective-permute-start | bytes 589832 | tf_op jit(solution)/shard_map/ppermute | solution.py:364
  (10 other events, 13.9 us)
Sparse Core Ops, SparseCore 0:
  8.9 42.9 all-gather.2
  53.6 39.0 all-gather.4
